TPU v7x, 512 devices: a whole 4x8x8 slice. The times are simulated.
512 devices in a mesh: img: 64 (over y_lo, x, z), vol: 8 (over y_hi, core).
Axes of the slice: x: 4, y: 8 (y_hi: 4, y_lo: 2; y = y_hi * 2 + y_lo), z: 8, core: 2. Of those that a mesh axis runs over, the one named last changes fastest.
Arguments:
- images: bfloat16 [512, 512, 512], P(('img', 'vol')), may hold values from -6 to 6
- defocus: float32 [512], P(('img', 'vol')), may hold values from 40 to 400
- noise: float32 [512], P(('img', 'vol')), may hold values from 102.4 to 1024
- orient: int32 [512, 4], P(('img', 'vol')), may hold values from 0 to 767
- planes: int32 [2, 768, 512], P(None, None, 'img'), may hold values from 0 to 31, as said below
- weights: bfloat16 [2, 768, 512], P(None, None, 'img'), may hold values from 0.099609375 to 0.8984375
- volume: bfloat16 [32, 512, 1024], P('vol', 'img'), may hold values from -6 to 6
- data_old: float32 [32, 512, 1024], P('vol', 'img'), may hold values from -6 to 6
- weight_old: float32 [32, 512, 512], P('vol', 'img'), may hold values from 1 to 20
Outputs:
- probs: float32 [512, 4], P(('img', 'vol'))
- data_acc: float32 [32, 512, 1024], P('vol', 'img')
- weight_acc: float32 [32, 512, 512], P('vol', 'img')
Inputs may be any that keep to these rules, and one draw needn't show every extreme that they name: `planes`: for every direction and row the two plane indices differ.
All inputs are finite; a program needn't handle non-finite values.
Results may differ from a plain program's by a relative error of at most 0.01325.
Values may be sent and summed in bfloat16 or wider, within the bound.
No kernel may reach another device: no remote copies, remote signals or barrier semaphores. Data moves between devices by JAX's collectives and lax.ppermute only.
A program may use at most 64 MiB of HBM per device.

v0:
```python
import math

import jax
import jax.numpy as jnp
from jax import lax
from jax.sharding import PartitionSpec as P

AMP = 0.1
PHASE_PART = math.sqrt(0.99)


def dft_tables(npix):
    index = jnp.arange(npix, dtype=jnp.int32)
    product = index[:, None] * index[None, :] % npix
    angle = product.astype(jnp.float32) * (2.0 * math.pi / npix)
    scale = 1.0 / math.sqrt(npix)
    return (
        (jnp.cos(angle) * scale).astype(jnp.bfloat16),
        (jnp.sin(angle) * scale).astype(jnp.bfloat16),
    )


def frequency(index, npix):
    return ((index + npix // 2) % npix - npix // 2).astype(jnp.float32) / npix


def contrast(defocus, row_index, npix):
    freq_y = frequency(row_index, npix)
    freq_x = frequency(jnp.arange(npix, dtype=jnp.int32), npix)
    shell = freq_y[:, None] * freq_y[:, None] + freq_x[None, :] * freq_x[None, :]
    phase = defocus[:, None, None] * shell[None]
    return -(PHASE_PART * jnp.sin(phase) + AMP * jnp.cos(phase))


def on_device(images, defocus, noise, orient, planes, weights, volume, data_old, weight_old):
    count = images.shape[0]
    npix = images.shape[1]
    n_img = lax.axis_size("img")
    rows = npix // n_img
    highest = lax.Precision.HIGHEST
    cosine, sine = dft_tables(npix)
    first = jnp.einsum(
        "nyx,xk->nyk",
        images,
        jnp.concatenate([cosine, -sine], 1),
        preferred_element_type=jnp.float32,
    ).astype(jnp.bfloat16)
    swapped = jnp.concatenate([first[..., npix:], -first[..., :npix]], -1)
    fourier = (
        jnp.einsum("yj,njk->nyk", cosine, first, preferred_element_type=jnp.float32)
        + jnp.einsum("yj,njk->nyk", sine, swapped, preferred_element_type=jnp.float32)
    ).astype(jnp.bfloat16)
    rowsets = lax.all_to_all(fourier, "img", split_axis=1, concat_axis=0, tiled=True)
    labels = lax.all_gather(orient, "img", axis=0, tiled=True)
    defocus_all, noise_all = (
        lax.all_gather(defocus, "img", axis=0, tiled=True),
        lax.all_gather(noise, "img", axis=0, tiled=True),
    )
    vol_rows = lax.all_gather(volume, "vol", axis=0, tiled=True)
    depth = vol_rows.shape[0]
    row_start = lax.axis_index("img") * rows
    row_index = row_start + jnp.arange(rows, dtype=jnp.int32)
    ctf = contrast(defocus_all, row_index, npix)
    ctf_full = jnp.concatenate([ctf, ctf], -1)
    filtered = (ctf_full * rowsets.astype(jnp.float32)).astype(jnp.bfloat16)
    picked = planes[:, labels, :]
    picked_w = weights[:, labels, :].astype(jnp.float32)
    levels = jnp.arange(depth, dtype=jnp.int32)
    zero = jnp.zeros((), jnp.float32)
    onehot = (
        jnp.where(picked[0][..., None] == levels, picked_w[0][..., None], zero)
        + jnp.where(picked[1][..., None] == levels, picked_w[1][..., None], zero)
    ).astype(jnp.bfloat16)
    mix_f = onehot.astype(jnp.float32)
    local_rows = jnp.arange(rows, dtype=jnp.int32)[None, None, :]
    section = picked_w[0][..., None] * vol_rows[picked[0], local_rows].astype(
        jnp.float32
    ) + picked_w[1][..., None] * vol_rows[picked[1], local_rows].astype(jnp.float32)
    cross = jnp.sum(filtered.astype(jnp.float32)[:, None] * section, axis=(2, 3))
    power = jnp.sum((ctf_full * ctf_full)[:, None] * section * section, axis=(2, 3))
    own_start = lax.axis_index("img") * count
    cross, power = lax.psum((cross, power), "img")
    every = jax.nn.softmax((cross - 0.5 * power) / noise_all[:, None], axis=1)
    mine = lax.dynamic_slice_in_dim(every, own_start, count, 0)
    share = jnp.einsum("no,norz->rnz", every, mix_f, precision=highest).astype(jnp.bfloat16)
    ctf_square = (ctf * ctf).astype(jnp.bfloat16)
    data_part = jnp.einsum("rnz,nrc->zrc", share, filtered, preferred_element_type=jnp.float32)
    weight_part = jnp.einsum("rnz,nrc->zrc", share, ctf_square, preferred_element_type=jnp.float32)
    data_sum, weight_sum = (
        lax.psum_scatter(
            data_part.astype(jnp.bfloat16), "vol", scatter_dimension=0, tiled=True
        ).astype(jnp.float32),
        lax.psum_scatter(
            weight_part.astype(jnp.bfloat16), "vol", scatter_dimension=0, tiled=True
        ).astype(jnp.float32),
    )
    return (mine, data_old + data_sum, weight_old + weight_sum)


def solution(mesh):
    placed = (
        P(("img", "vol"), None, None),
        P(("img", "vol")),
        P(("img", "vol")),
        P(("img", "vol"), None),
        P(None, None, "img"),
        P(None, None, "img"),
        P("vol", "img", None),
        P("vol", "img", None),
        P("vol", "img", None),
    )
    return jax.shard_map(
        on_device,
        mesh=mesh,
        in_specs=placed,
        out_specs=(P(("img", "vol"), None), P("vol", "img", None), P("vol", "img", None)),
        check_vma=False,
    )
```

profile of v0, /device:TPU:1, one launch (start us, length us, event | category | flops | bytes accessed | tf_op | source)
XLA Modules:
  0.0 876.9 jit_solution(5868541020546762116)
XLA Ops:
  7.2 4.0 fusion.28
  11.2 4.0 multiply_convert_fusion.1
  15.2 0.8 convolution_convert_fusion
  15.9 5.6 fusion.31
  21.7 5.4 fusion.5
  27.1 4.9 copy.46
  32.0 0.5 broadcast.271
  32.5 7.8 reduce
  40.3 2.6 reshape.242
  42.9 15.7 %all-to-all-start = ((bf16[64,2,4096]{2,1,0:T(2,128)(2,1)}), bf16[64,2,4096]{2,1,0:T(2,128)(2,1)}, u32[]{:S(2)}, u32[]{:S(2)}) async-start(bf16[64,2,4096]{2,1,0:T(2,128)(2,1)} %reshape.242), calls=%async_computation | async-start | bytes 2097152 | tf_op jit(solution)/shard_map/all_to_all | solution.py:53
  59.3 142.7 %all-gather = s32[64,1,4]{2,1,0:T(1,128)S(1)} all-gather(s32[1,1,4]{2,1,0:T(1,128)S(1)} %bitcast.77), channel_id=1, replica_groups=mesh['img'=64,'vol'=8] {'img'}, dimensions={0}, use_global_device_ids=true | all-gather | bytes 1040 | tf_op jit(solution)/shard_map/all_gather | solution.py:54
  202.0 0.1 reshape.195
  202.2 0.5 copy.51
  202.6 1.0 gather_fusion.1
  203.6 0.1 fusion.34
  203.8 0.2 reshape.209
  203.9 0.2 reshape.215
  204.1 44.6 %all_gather.14 = bf16[32,8,1024]{2,1,0:T(8,128)(2,1)S(1)} all-gather(bf16[4,8,1024]{2,1,0:T(8,128)(2,1)S(1)} %copy-done.6), channel_id=1, replica_groups=mesh['img'=64,'vol'=8] {'vol'}, dimensions={0}, use_global_device_ids=true | all-gather | bytes 589824 | tf_op jit(solution)/shard_map/all_gather | solution.py:59
  248.7 29.6 %gather_fusion.2 = bf16[2048,1024]{1,0:T(8,128)(2,1)} fusion(bf16[32,8,1024]{2,1,0:T(8,128)(2,1)S(1)} %all_gather.14, s32[2048]{0:T(1024)S(1)} %reshape.209), kind=kCustom, calls=%fused_computation.2 | custom fusion | bytes 8404992 | tf_op jit(solution)/shard_map/gather | solution.py:76
  278.4 29.6 %gather_fusion.3 = bf16[2048,1024]{1,0:T(8,128)(2,1)} fusion(bf16[32,8,1024]{2,1,0:T(8,128)(2,1)S(1)} %all_gather.14, s32[2048]{0:T(1024)S(1)} %reshape.215), kind=kCustom, calls=%fused_computation.3 | custom fusion | bytes 8404992 | tf_op jit(solution)/shard_map/gather | solution.py:78
  307.9 0.4 copy.48
  308.3 0.9 gather_fusion
  309.3 0.1 copy.50
  310.1 1.3 dynamic-slice
  311.4 0.8 dynamic-update-slice
  312.2 0.8 dynamic-update-slice.1
  312.9 124.7 %all-reduce = f32[64]{0:T(128)S(1)} all-reduce(f32[64]{0:T(128)S(1)} %dynamic-update-slice), channel_id=1, replica_groups=mesh['img'=64,'vol'=8] {'img'}, use_global_device_ids=true, to_apply=%add | all-reduce | flops 64 | bytes 512
  437.8 4.9 fusion.13
  442.7 2.3 add_convert_fusion.1
  445.0 6.5 reshape.243
  451.5 3.6 fusion.66
  455.1 0.9 copy-done.2
  456.0 7.2 fusion
  463.1 249.1 %all-reduce.2 = (f32[64,4]{1,0:T(8,128)S(1)}, f32[64,4]{1,0:T(8,128)S(1)}, f32[64]{0:T(128)S(1)}) all-reduce(f32[64,4]{1,0:T(8,128)S(1)} %get-tuple-element.10, f32[64,4]{1,0:T(8,128)S(1)} %get-tuple-element.9, f32[64]{0:T(128)S(1)} %dynamic-update-slice.1), channel_id=1, replica_groups=mesh['img'=64,'vol'=8] {'img'}, use_global_device_ids=true, to_apply=%region_1.2 | all-reduce | flops 576 | bytes 4608 | tf_op jit(solution)/shard_map/psum | solution.py:82
  712.3 0.2 fusion.65
  712.5 0.2 fusion.42
  712.6 0.1 fusion.41
  712.8 1.0 fusion.29
  713.8 0.2 copy.59
  713.9 0.3 fusion.7
  714.3 0.8 copy.56
  715.2 1.3 fusion.6
  716.5 1.1 copy.54
  717.6 0.5 constant_dynamic-slice_fusion
  718.1 108.4 %reduce-scatter.5.cloned.1.call-done = bf16[4,8,512]{2,1,0:T(8,128)(2,1)} async-done(((bf16[32,8,512]{2,1,0:T(8,128)(2,1)}), bf16[4,8,512]{2,1,0:T(8,128)(2,1)}) %reduce-scatter.5.cloned.1.call-update) | async-done | bytes 32784 | tf_op jit(solution)/shard_map/reduce_scatter | solution.py:93
  826.5 1.4 convert_add_fusion.1
  827.9 40.6 %reduce-scatter.3.cloned.1.call-done = bf16[4,8,1024]{2,1,0:T(8,128)(2,1)} async-done(((bf16[32,8,1024]{2,1,0:T(8,128)(2,1)}), bf16[4,8,1024]{2,1,0:T(8,128)(2,1)}) %reduce-scatter.3.cloned.1.call-update) | async-done | bytes 65552 | tf_op jit(solution)/shard_map/reduce_scatter | solution.py:90
  868.5 1.5 convert_add_fusion
  (38 shorter events, 0.5 us)
Async XLA Ops:
  7.2 8.0 copy-start
  40.3 19.0 %copy-start.10 = (s32[1,4]{1,0:T(1,128)S(1)}, s32[1,4]{1,0:T(1,128)}, u32[]{:S(2)}) copy-start(s32[1,4]{1,0:T(1,128)} %param.12) | copy-start | bytes 52
  40.3 161.9 %copy-start.8 = (s32[2,768,8]{1,2,0:T(8,128)S(1)}, s32[2,768,8]{1,2,0:T(8,128)}, u32[]{:S(2)}) copy-start(s32[2,768,8]{1,2,0:T(8,128)} %param.13) | copy-start | bytes 147460
  42.9 161.2 %copy-start.6 = (bf16[4,8,1024]{2,1,0:T(8,128)(2,1)S(1)}, bf16[4,8,1024]{2,1,0:T(8,128)(2,1)}, u32[]{:S(2)}) copy-start(bf16[4,8,1024]{2,1,0:T(8,128)(2,1)} %param.15) | copy-start | bytes 196612
  42.9 402.1 %all-to-all-start = ((bf16[64,2,4096]{2,1,0:T(2,128)(2,1)}), bf16[64,2,4096]{2,1,0:T(2,128)(2,1)}, u32[]{:S(2)}, u32[]{:S(2)}) async-start(bf16[64,2,4096]{2,1,0:T(2,128)(2,1)} %reshape.242), calls=%async_computation | async-start | bytes 2097152 | tf_op jit(solution)/shard_map/all_to_all | solution.py:53
  58.6 767.9 %reduce-scatter.5.cloned.1.call-start = ((), (), s32[]{:S(2)}) async-start(), calls=%async_computation.4 | async-start | bytes 294912 | tf_op jit(solution)/shard_map/reduce_scatter | solution.py:93
  278.4 29.6 %copy-start.9 = (bf16[2,768,8]{1,2,0:T(8,128)(2,1)S(1)}, bf16[2,768,8]{1,2,0:T(8,128)(2,1)}, u32[]{:S(2)}) copy-start(bf16[2,768,8]{1,2,0:T(8,128)(2,1)} %param.14) | copy-start | bytes 73732
  451.5 3.6 copy-start.1
  451.5 4.5 copy-start.2
  456.0 256.8 %copy-start.4 = (bf16[64,4,8,32]{3,2,1,0:T(8,128)(2,1)S(1)}, bf16[64,4,8,32]{3,2,1,0:T(8,128)(2,1)}, u32[]{:S(2)}) copy-start(bf16[64,4,8,32]{3,2,1,0:T(8,128)(2,1)} %add_convert_fusion.1) | copy-start | bytes 393220
  463.1 252.0 %copy-start.3 = (bf16[64,8,1024]{2,1,0:T(8,128)(2,1)S(1)}, bf16[64,8,1024]{2,1,0:T(8,128)(2,1)}, u32[]{:S(2)}) copy-start(bf16[64,8,1024]{2,1,0:T(8,128)(2,1)} %get-tuple-element.17) | copy-start | bytes 3145732
  714.2 112.3 %copy-start.7 = (f32[4,8,512]{2,1,0:T(8,128)S(1)}, f32[4,8,512]{2,1,0:T(8,128)}, u32[]{:S(2)}) copy-start(f32[4,8,512]{2,1,0:T(8,128)} %param.17) | copy-start | bytes 196612
  714.2 154.3 %copy-start.5 = (f32[4,8,1024]{2,1,0:T(8,128)S(1)}, f32[4,8,1024]{2,1,0:T(8,128)}, u32[]{:S(2)}) copy-start(f32[4,8,1024]{2,1,0:T(8,128)} %param.16) | copy-start | bytes 393220
  715.1 153.4 %reduce-scatter.3.cloned.1.call-start = ((), (), s32[]{:S(2)}) async-start(), calls=%async_computation.3 | async-start | bytes 589824 | tf_op jit(solution)/shard_map/reduce_scatter | solution.py:90
Sparse Core Ops, SparseCore 0:
  715.2 111.2 reduce-scatter.4
  829.6 38.9 reduce-scatter.2
where the time goes:
time: 878 us; the launch traced here: 877 us
  blocking collectives  561 us (64%)
  waiting for transfers between devices  149 us (17%)
  local copies, waits for them, and re-layouts  83.5 us (10%)
  other arithmetic  37.3 us (4%)
  starting transfers between devices  15.8 us (2%)
  between operations  15.6 us (2%)
  matrix products  14.4 us (2%)
    psum x1, blocking collectives, on_device(): cross, power = lax.psum((cross, power), 'img')  249 us
    all_gather x1, blocking collectives, on_device(): labels = lax.all_gather(orient, 'img', axis=0, tiled=True)  143 us
    unnamed x1, blocking collectives  125 us
    reduce_scatter x1, waiting for transfers between devices, on_device(): lax.psum_scatter(weight_part.astype(jnp.bfloat16), 'vol', scatter_dimensi...  108 us
    all_gather x1, blocking collectives, on_device(): vol_rows = lax.all_gather(volume, 'vol', axis=0, tiled=True)  44.6 us
    reduce_scatter x1, waiting for transfers between devices, on_device(): lax.psum_scatter(data_part.astype(jnp.bfloat16), 'vol', scatter_dimension...  40.6 us
    gather x1, local copies, waits for them, and re-layouts, on_device(): vol_rows[picked[0], local_rows].astype(jnp.float32)  29.6 us
    gather x1, local copies, waits for them, and re-layouts, on_device(): vol_rows[picked[1], local_rows].astype(jnp.float32)  29.6 us
  transfers between devices with their start and end apart: 3, of which 2 were waited for; matrix products, arithmetic and copies ran while one was open for 9% of the time, Pallas kernels for 0%

commit v1 on v0

v1 whole, which is shorter than its diff:
```python
import functools
import math

import jax
import jax.numpy as jnp
import ml_dtypes
import numpy as np
from jax import lax
from jax.experimental import pallas as pl
from jax.experimental.pallas import tpu as pltpu
from jax.sharding import PartitionSpec as P

AMP = 0.1
TILT = math.asin(AMP)
PI_HIGH = float(np.float32(math.floor(math.pi * 4096) / 4096))
PI_LOW = math.pi - PI_HIGH
VMEM = 32 * 1024 * 1024


def dft_table(npix):
    index = np.arange(npix)
    angle = (index[:, None] * index[None, :] % npix) * (2.0 * math.pi / npix)
    scale = 1.0 / math.sqrt(npix)
    both = np.concatenate([np.cos(angle) * scale, np.sin(angle) * scale], 1)
    return both.astype(np.float32).astype(ml_dtypes.bfloat16)


def frequency(index, npix):
    return ((index + npix // 2) % npix - npix // 2).astype(jnp.float32) / npix


def params():
    return pltpu.CompilerParams(vmem_limit_bytes=VMEM)


def transform_kernel(block, image_ref, table_ref, out_ref, both_ref):
    npix = image_ref.shape[0]
    steps = npix // block

    @pl.loop(0, steps)
    def _(step):
        at = pl.multiple_of(step * block, block)
        first = jnp.dot(
            image_ref[pl.ds(at, block), :], table_ref[...], preferred_element_type=jnp.float32
        )
        real = first[:, :npix].astype(jnp.bfloat16)
        negative = first[:, npix:].astype(jnp.bfloat16)
        below = pl.multiple_of(npix + step * block, block)
        both_ref[pl.ds(at, block), :npix] = real
        both_ref[pl.ds(at, block), npix:] = -negative
        both_ref[pl.ds(below, block), :npix] = -negative
        both_ref[pl.ds(below, block), npix:] = -real

    @pl.loop(0, steps)
    def _(step):
        at = pl.multiple_of(step * block, block)
        out_ref[pl.ds(at, block), :] = jnp.dot(
            table_ref[pl.ds(at, block), :], both_ref[...], preferred_element_type=jnp.float32
        ).astype(jnp.bfloat16)


def transform(image, table):
    npix = image.shape[0]
    return pl.pallas_call(
        functools.partial(transform_kernel, 128),
        out_shape=jax.ShapeDtypeStruct((npix, 2 * npix), jnp.bfloat16),
        scratch_shapes=[pltpu.VMEM((2 * npix, 2 * npix), jnp.bfloat16)],
        compiler_params=params(),
        cost_estimate=pl.CostEstimate(
            flops=6 * npix**3, bytes_accessed=5 * npix * npix * 2, transcendentals=0
        ),
        name="transform",
    )(image, table)


def prepare_kernel(spots_ref, weights_ref, defocus_ref, row_ref, col_ref, mix_ref, turned_ref, ctf_ref, square_ref):
    ori, deep, many = turned_ref.shape
    level = lax.broadcasted_iota(jnp.int32, (deep, many), 0)
    for o in range(ori):
        total = jnp.zeros((deep, many), jnp.float32)
        for k in range(2):
            spot = spots_ref[2 * o + k : 2 * o + k + 1, :]
            weight = weights_ref[2 * o + k : 2 * o + k + 1, :]
            total = total + jnp.where(level == spot, weight, 0.0)
        turned_ref[o] = total.astype(jnp.bfloat16)
        mix_ref[o] = jnp.transpose(total).astype(jnp.bfloat16)
    chi = defocus_ref[...] * (row_ref[...] + col_ref[...])
    turns = jnp.floor((chi + TILT) * (1.0 / math.pi) + 0.5)
    angle = ((chi - turns * PI_HIGH) - turns * PI_LOW) + TILT
    half = turns * 0.5
    sign = 4.0 * (half - jnp.floor(half)) - 1.0
    square = angle * angle
    series = -1.0 / 39916800.0
    for term in (1.0 / 362880.0, -1.0 / 5040.0, 1.0 / 120.0, -1.0 / 6.0, 1.0):
        series = series * square + term
    ctf = sign * (series * angle)
    ctf_ref[...] = ctf
    square_ref[...] = (ctf * ctf).astype(jnp.bfloat16)


def prepare(spots, weights, defocus, row_square, col_square, deep):
    ori = spots.shape[0] // 2
    many = spots.shape[1]
    npix = col_square.shape[1]
    return pl.pallas_call(
        prepare_kernel,
        out_shape=(
            jax.ShapeDtypeStruct((ori, many, deep), jnp.bfloat16),
            jax.ShapeDtypeStruct((ori, deep, many), jnp.bfloat16),
            jax.ShapeDtypeStruct((many, npix), jnp.float32),
            jax.ShapeDtypeStruct((many, npix), jnp.bfloat16),
        ),
        compiler_params=params(),
        cost_estimate=pl.CostEstimate(flops=1 << 25, bytes_accessed=4 << 20, transcendentals=0),
        name="prepare",
    )(spots, weights, defocus, row_square, col_square)


def compare_kernel(steps, rows, step_rows, fourier_ref, ctf_ref, mix_ref, volume_ref, filtered_ref, part_ref, section_ref, total_ref):
    ori, block, deep = mix_ref.shape
    npix = ctf_ref.shape[1]
    step = pl.program_id(0)
    section_ref[...] = jnp.dot(
        mix_ref[...].reshape(ori * block, deep), volume_ref[...], preferred_element_type=jnp.float32
    )

    @pl.loop(0, block // step_rows)
    def _(piece):
        at = pl.multiple_of(piece * step_rows, step_rows)
        ctf = ctf_ref[pl.ds(at, step_rows), :]
        fourier = fourier_ref[pl.ds(at, step_rows), :].astype(jnp.float32)
        real = (ctf * fourier[:, :npix]).astype(jnp.bfloat16)
        imag = (ctf * fourier[:, npix:]).astype(jnp.bfloat16)
        filtered_ref[pl.ds(at, step_rows), :npix] = real
        filtered_ref[pl.ds(at, step_rows), npix:] = imag
        real = real.astype(jnp.float32)
        imag = imag.astype(jnp.float32)
        minus = -0.5 * ctf * ctf
        for o in range(ori):
            below = pl.multiple_of(o * block + at, step_rows)
            s_real = section_ref[pl.ds(below, step_rows), :npix]
            s_imag = section_ref[pl.ds(below, step_rows), npix:]
            score = (
                real * s_real + imag * s_imag + minus * (s_real * s_real + s_imag * s_imag)
            )
            lanes = score[:, :128]
            for chunk in range(1, npix // 128):
                lanes = lanes + score[:, chunk * 128 : (chunk + 1) * 128]
            images = step_rows // rows
            sums = jnp.sum(lanes.reshape(images, rows, 128), axis=1)
            first = pl.multiple_of(step * (block // rows) + piece * images, images)
            total_ref[pl.ds(o * (steps * block // rows) + first, images), :] = sums

    @pl.when(step == steps - 1)
    def _():
        half = total_ref.shape[0] // 2
        upper = jnp.sum(jnp.transpose(total_ref[:half, :]), axis=0, keepdims=True)
        lower = jnp.sum(jnp.transpose(total_ref[half:, :]), axis=0, keepdims=True)
        even = lax.broadcasted_iota(jnp.int32, part_ref.shape, 0) % 2 == 0
        part_ref[...] = jnp.where(even, upper, lower)


def compare(fourier, ctf, mix, volume, rows, copies):
    many, wide = fourier.shape
    ori, _, deep = mix.shape
    steps = 4
    block = many // steps
    images = many // rows
    return pl.pallas_call(
        functools.partial(compare_kernel, steps, rows, 8 * rows),
        grid=(steps,),
        in_specs=[
            pl.BlockSpec((block, wide), lambda i: (i, 0)),
            pl.BlockSpec((block, wide // 2), lambda i: (i, 0)),
            pl.BlockSpec((ori, block, deep), lambda i: (0, i, 0)),
            pl.BlockSpec((deep, wide), lambda i: (0, 0)),
        ],
        out_specs=(
            pl.BlockSpec((block, wide), lambda i: (i, 0)),
            pl.BlockSpec((copies * 2, 2 * images), lambda i: (0, 0)),
        ),
        out_shape=(
            jax.ShapeDtypeStruct((many, wide), jnp.bfloat16),
            jax.ShapeDtypeStruct((copies * 2, 2 * images), jnp.float32),
        ),
        scratch_shapes=[
            pltpu.VMEM((ori * block, wide), jnp.float32),
            pltpu.VMEM((ori * images, 128), jnp.float32),
        ],
        compiler_params=params(),
        cost_estimate=pl.CostEstimate(flops=1 << 30, bytes_accessed=5 << 20, transcendentals=0),
        name="compare",
    )(fourier, ctf, mix, volume)


def project_kernel(rows, part_ref, noise_ref, mix_ref, filtered_ref, square_ref, probs_ref, out_ref):
    ori, deep, many = mix_ref.shape
    wide = filtered_ref.shape[1]
    lanes = part_ref.shape[1]
    images = lanes // 2
    sums = jnp.sum(part_ref[...].reshape(part_ref.shape[0] // 8, 8, lanes), axis=0)
    sums = sums + pltpu.roll(sums, 4, 0)
    sums = sums + pltpu.roll(sums, 2, 0)
    score = sums / noise_ref[...]
    top = jnp.maximum(score, pltpu.roll(score, 1, 0))
    top = jnp.maximum(top, pltpu.roll(top, images, 1))
    power = jnp.exp(score - top)
    whole = power + pltpu.roll(power, 1, 0)
    whole = whole + pltpu.roll(whole, images, 1)
    probs = power / whole
    probs_ref[...] = probs
    image = lax.broadcasted_iota(jnp.int32, (lanes, many), 0)
    owner = lax.broadcasted_iota(jnp.int32, (lanes, many), 1) // rows
    share = jnp.zeros((deep, many), jnp.float32)
    for half in range(2):
        spread = jnp.where(image == owner + half * images, 1.0, 0.0)
        along = jnp.dot(
            probs, spread, preferred_element_type=jnp.float32, precision=lax.Precision.HIGHEST
        )
        for row in range(2):
            share = share + along[row : row + 1, :] * mix_ref[2 * row + half].astype(jnp.float32)
    share = share.astype(jnp.bfloat16)
    out_ref[:, :wide] = jnp.dot(
        share, filtered_ref[...], preferred_element_type=jnp.float32
    ).astype(jnp.bfloat16)
    out_ref[:, wide:] = jnp.dot(
        share, square_ref[...], preferred_element_type=jnp.float32
    ).astype(jnp.bfloat16)


def project(part, noise, mix, filtered, square, rows):
    _, deep, many = mix.shape
    wide = filtered.shape[1]
    return pl.pallas_call(
        functools.partial(project_kernel, rows),
        out_shape=(
            jax.ShapeDtypeStruct((8, part.shape[1]), jnp.float32),
            jax.ShapeDtypeStruct((deep, wide + wide // 2), jnp.bfloat16),
        ),
        compiler_params=params(),
        cost_estimate=pl.CostEstimate(flops=1 << 29, bytes_accessed=4 << 20, transcendentals=0),
        name="project",
    )(part, noise, mix, filtered, square)


def finish_kernel(part_ref, data_ref, weight_ref, data_out, weight_out):
    wide = data_ref.shape[1]
    data = part_ref[0, :, :wide].astype(jnp.float32)
    weight = part_ref[0, :, wide:].astype(jnp.float32)
    for source in range(1, part_ref.shape[0]):
        data = data + part_ref[source, :, :wide].astype(jnp.float32)
        weight = weight + part_ref[source, :, wide:].astype(jnp.float32)
    data_out[...] = data_ref[...] + data
    weight_out[...] = weight_ref[...] + weight


def finish(parts, data_old, weight_old):
    return pl.pallas_call(
        finish_kernel,
        out_shape=(
            jax.ShapeDtypeStruct(data_old.shape, jnp.float32),
            jax.ShapeDtypeStruct(weight_old.shape, jnp.float32),
        ),
        compiler_params=params(),
        cost_estimate=pl.CostEstimate(flops=1 << 20, bytes_accessed=2 << 20, transcendentals=0),
        name="finish",
    )(parts, data_old, weight_old)


def on_device(images, defocus, noise, orient, planes, weights, volume, data_old, weight_old):
    npix = images.shape[1]
    ori = orient.shape[1]
    n_img = lax.axis_size("img")
    n_vol = lax.axis_size("vol")
    rows = npix // n_img
    slab = volume.shape[0]
    deep = n_vol * slab * rows
    many = n_img * rows

    about = jnp.concatenate(
        [orient[0].astype(jnp.float32), defocus, noise, jnp.zeros((2,), jnp.float32)]
    )
    about = jnp.broadcast_to(about[None, None, :], (n_img, 1, ori + 4))
    about = lax.all_to_all(about, "img", split_axis=0, concat_axis=0, tiled=True)[:, 0, :]
    vol_rows = lax.all_to_all(
        jnp.broadcast_to(volume.reshape(1, slab * rows, 2 * npix), (n_vol, slab * rows, 2 * npix)),
        "vol",
        split_axis=0,
        concat_axis=0,
        tiled=True,
    ).reshape(deep, 2 * npix)

    fourier = transform(images[0], jnp.asarray(dft_table(npix)))
    fourier = lax.all_to_all(
        fourier.reshape(n_img, rows, 2 * npix), "img", split_axis=0, concat_axis=0, tiled=True
    ).reshape(many, 2 * npix)

    labels = about[:, :ori].astype(jnp.int32)
    defocus_all = about[:, ori]
    noise_all = about[:, ori + 1]
    local = jnp.arange(rows, dtype=jnp.int32)
    spots = planes[:, labels, :] * rows + local
    spots = jnp.transpose(spots, (2, 0, 1, 3)).reshape(2 * ori, many)
    picked = jnp.transpose(weights[:, labels, :], (2, 0, 1, 3)).reshape(2 * ori, many)
    freq_y = frequency(lax.axis_index("img") * rows + local, npix)
    row_square = jnp.tile(freq_y * freq_y, n_img)[:, None]
    freq_x = frequency(jnp.arange(npix, dtype=jnp.int32), npix)
    mix, turned, ctf, square = prepare(
        spots,
        picked.astype(jnp.float32),
        jnp.repeat(defocus_all, rows)[:, None],
        row_square,
        (freq_x * freq_x)[None, :],
        deep,
    )
    filtered, part = compare(fourier, ctf, mix, vol_rows, rows, n_img)
    part = lax.all_to_all(
        part.reshape(n_img, 2, 2 * n_img), "img", split_axis=0, concat_axis=0, tiled=True
    ).reshape(2 * n_img, 2 * n_img)
    probs, sums = project(part, jnp.tile(noise_all, 2)[None, :], turned, filtered, square, rows)
    sums = lax.all_to_all(
        sums.reshape(n_vol, slab * rows, 3 * npix), "vol", split_axis=0, concat_axis=0, tiled=True
    )
    mine = lax.dynamic_slice_in_dim(
        probs[:2].reshape(2 * 2, n_img), lax.axis_index("img"), 1, 1
    ).reshape(1, ori)
    data, weight = finish(
        sums,
        data_old.reshape(slab * rows, 2 * npix),
        weight_old.reshape(slab * rows, npix),
    )
    return (mine, data.reshape(data_old.shape), weight.reshape(weight_old.shape))


def solution(mesh):
    placed = (
        P(("img", "vol"), None, None),
        P(("img", "vol")),
        P(("img", "vol")),
        P(("img", "vol"), None),
        P(None, None, "img"),
        P(None, None, "img"),
        P("vol", "img", None),
        P("vol", "img", None),
        P("vol", "img", None),
    )
    return jax.shard_map(
        on_device,
        mesh=mesh,
        in_specs=placed,
        out_specs=(P(("img", "vol"), None), P("vol", "img", None), P("vol", "img", None)),
        check_vma=False,
    )
```

time: 878 us -> 143 us (0.16)
  blocking collectives: 561 us -> 24.4 us
  waiting for transfers between devices: 149 us -> 58.6 us
  local copies, waits for them, and re-layouts: 83.5 us -> 16.7 us
  other arithmetic: 37.3 us -> 0.84 us
  matrix products: 14.4 us -> 0 us
  between operations: 15.6 us -> 2.24 us
  Pallas kernels: 0 us -> 12.3 us
  starting transfers between devices: 15.8 us -> 25.9 us
    psum x1 -> x0, blocking collectives: 249 us -> none  [on_device(): cross, power = lax.psum((cross, power), 'img')]
    all_gather x2 -> x0, blocking collectives: 187 us -> none  [the longest x1 143 us: on_device(): labels = lax.all_gather(orient, 'img', axis=0, tiled=True)]
    reduce_scatter x2 -> x0, waiting for transfers between devices: 149 us -> none  [the longest x1 108 us: on_device(): lax.psum_scatter(weight_part.astype(jnp.bfloat16), 'vol', scatter_dimensi...]
    unnamed x1 -> x0, blocking collectives: 125 us -> none
    gather x6 -> x4, local copies, waits for them, and re-layouts: 61.2 us -> 2.07 us  [the longest x2 1.07 us: on_device(): spots = planes[:, labels, :] * rows + local]
    all_to_all x1 -> x4, waiting for transfers between devices: 0.01 us -> 58.6 us  [the longest x1 19.9 us: on_device(): lax.all_to_all(sums.reshape(n_vol, slab * rows, 3 * npix), 'vol', split_a...]
    all_to_all x0 -> x1, blocking collectives: none -> 24.4 us  [on_device(): lax.all_to_all(about, 'img', split_axis=0, concat_axis=0, tiled=True)]
    dot_general x6 -> x0, matrix products: 14.4 us -> none  [the longest x1 5.64 us: on_device(): jnp.einsum('yj,njk->nyk', cosine, first, preferred_element_type=jnp.float32)]
  transfers between devices with their start and end apart: 3 -> 4, of which waited for: 2 -> 4; matrix products, arithmetic and copies ran while one was open for 9% -> 4% of each run, Pallas kernels for 0% -> 4%
where the time goes in v1:
time: 143 us; the launch traced here: 141 us
  waiting for transfers between devices  58.6 us (41%)
  starting transfers between devices  25.9 us (18%)
  blocking collectives  24.4 us (17%)
  local copies, waits for them, and re-layouts  16.7 us (12%)
  Pallas kernels  12.3 us (9%)
  between operations  2.24 us (2%)
    all_to_all x1, blocking collectives, on_device(): lax.all_to_all(about, 'img', split_axis=0, concat_axis=0, tiled=True)  24.4 us
    all_to_all x1, waiting for transfers between devices, on_device(): lax.all_to_all(sums.reshape(n_vol, slab * rows, 3 * npix), 'vol', split_a...  19.9 us
    all_to_all x1, waiting for transfers between devices, on_device(): lax.all_to_all(fourier.reshape(n_img, rows, 2 * npix), 'img', split_axis=...  18.4 us
    unnamed x33, local copies, waits for them, and re-layouts  11.4 us
    all_to_all x1, waiting for transfers between devices, on_device(): lax.all_to_all(jnp.broadcast_to(volume.reshape(1, slab * rows, 2 * npix),...  11.1 us
    all_to_all x1, waiting for transfers between devices, on_device(): lax.all_to_all(part.reshape(n_img, 2, 2 * n_img), 'img', split_axis=0, co...  9.27 us
    all_to_all x1, starting transfers between devices, on_device(): lax.all_to_all(jnp.broadcast_to(volume.reshape(1, slab * rows, 2 * npix),...  8.43 us
    all_to_all x1, starting transfers between devices, on_device(): lax.all_to_all(part.reshape(n_img, 2, 2 * n_img), 'img', split_axis=0, co...  6.82 us
  transfers between devices with their start and end apart: 4, of which 4 were waited for; matrix products, arithmetic and copies ran while one was open for 4% of the time, Pallas kernels for 4%

profile of v1, /device:TPU:1, one launch (start us, length us, event | category | flops | bytes accessed | tf_op | source)
XLA Modules:
  0.0 141.0 jit_solution(1522392688006608471)
XLA Ops:
  0.6 0.0 copy-start.12
  2.0 0.7 convert_bitcast_fusion
  2.7 0.1 pad_maximum_fusion
  2.8 24.4 %all_to_all.25 = f32[64,1,8]{2,1,0:T(1,128)S(1)} all-to-all(f32[64,1,8]{2,1,0:T(1,128)S(1)} %broadcast_in_dim.10), channel_id=1, replica_groups=mesh['img'=64,'vol'=8] {'img'}, dimensions={0} | all-to-all | bytes 4096 | tf_op jit(solution)/shard_map/all_to_all | solution.py:284
  27.2 1.7 %broadcast_in_dim.26 = bf16[8,32,1024]{2,1,0:T(8,128)(2,1)} broadcast(bf16[32,1024]{1,0:T(8,128)(2,1)} %bitcast.37), dimensions={1,2} | broadcast | bytes 589824 | tf_op jit(solution)/shard_map/broadcast_in_dim | solution.py:286
  28.9 8.4 %all-to-all-start.2 = ((bf16[8,32,1024]{2,1,0:T(8,128)(2,1)}), bf16[8,32,1024]{2,1,0:T(8,128)(2,1)S(1)}, u32[]{:S(2)}, u32[]{:S(2)}) async-start(bf16[8,32,1024]{2,1,0:T(8,128)(2,1)} %broadcast_in_dim.26), calls=%async_computation.2 | async-start | bytes 1048576 | tf_op jit(solution)/shard_map/all_to_all | solution.py:285
  37.4 4.2 %transform.1 = bf16[512,1024]{1,0:T(8,128)(2,1)} custom-call(bf16[512,512]{1,0:T(8,128)(2,1)S(1)} %bitcast.32, bf16[512,1024]{1,0:T(8,128)(2,1)S(1)} %copy-done.12), custom_call_target="tpu_custom_call" | custom-call | flops 805306368 | bytes 2621440 | tf_op jit(solution)/shard_map/transform/pallas_call | solution.py:64
  41.5 11.1 %all-to-all-done.2 = bf16[8,32,1024]{2,1,0:T(8,128)(2,1)S(1)} async-done(((bf16[8,32,1024]{2,1,0:T(8,128)(2,1)}), bf16[8,32,1024]{2,1,0:T(8,128)(2,1)S(1)}, u32[]{:S(2)}, u32[]{:S(2)}) %all-to-all-start.2) | async-done | bytes 524320 | tf_op jit(solution)/shard_map/all_to_all | solution.py:285
  52.6 0.8 copy-done.1
  53.4 4.7 %all-to-all-start = ((bf16[64,8,1024]{2,1,0:T(8,128)(2,1)}), bf16[64,8,1024]{2,1,0:T(8,128)(2,1)S(1)}, u32[]{:S(2)}, u32[]{:S(2)}) async-start(bf16[64,8,1024]{2,1,0:T(8,128)(2,1)} %bitcast.1), calls=%async_computation | async-start | bytes 2097152 | tf_op jit(solution)/shard_map/all_to_all | solution.py:294
  58.1 0.1 broadcast_in_dim_tile.8.row_ref
  58.2 0.6 copy-done.14
  58.8 0.4 copy.48
  59.2 0.4 copy-done.13
  59.6 0.4 copy.44
  60.1 0.1 reshape.143
  60.2 0.2 slice_reduce_fusion
  60.4 0.1 broadcast_in_dim.24
  60.5 0.1 broadcast_in_dim_reshape.4.defocus_ref
  60.6 0.9 gather_fusion.1
  61.6 0.1 copy.49
  61.6 0.1 copy.50
  61.8 0.2 reshape.140.weights_ref
  62.0 1.0 gather_fusion
  63.0 0.1 copy.45
  63.1 0.1 copy.46
  63.3 0.2 reshape.129.spots_ref
  63.5 1.8 %prepare.1 = (bf16[4,512,256]{2,1,0:T(8,128)(2,1)S(1)}, bf16[4,256,512]{2,1,0:T(8,128)(2,1)S(1)}, f32[512,512]{1,0:T(8,128)S(1)}, bf16[512,512]{1,0:T(8,128)(2,1)S(1)}) custom-call(s32[8,512]{1,0:T(8,128)S(1)} %reshape.129.spots_ref, f32[8,512]{1,0:T(8,128)S(1)} %reshape.140.weights_ref, f32[512,1]{1,0:T(8,128)S(1)} %broadcast_in_dim_reshape.4.defocus_ref, ...), custom_call_target="tpu_custom_call" | custom-call | flops 33554432 | bytes 4194304 | tf_op jit(solution)/shard_map/prepare/pallas_call | solution.py:105
  65.2 0.8 copy-done.3
  66.0 1.0 copy-done.7
  67.0 1.0 copy-done.9
  68.0 18.4 %all-to-all-done = bf16[64,8,1024]{2,1,0:T(8,128)(2,1)S(1)} async-done(((bf16[64,8,1024]{2,1,0:T(8,128)(2,1)}), bf16[64,8,1024]{2,1,0:T(8,128)(2,1)S(1)}, u32[]{:S(2)}, u32[]{:S(2)}) %all-to-all-start) | async-done | bytes 1048608 | tf_op jit(solution)/shard_map/all_to_all | solution.py:294
  86.3 1.0 copy-done.2
  87.4 1.2 copy-done.8
  88.6 1.2 copy-done.10
  89.8 4.6 %compare.12 = (bf16[512,1024]{1,0:T(8,128)(2,1)S(1)}, f32[128,128]{1,0:T(8,128)}) custom-call(bf16[512,1024]{1,0:T(8,128)(2,1)S(1)} %bitcast.26, f32[512,512]{1,0:T(8,128)S(1)} %copy-done.10, bf16[4,512,256]{2,1,0:T(8,128)(2,1)S(1)} %copy-done.8, bf16[256,1024]{1,0:T(8,128)(2,1)S(1)} %bitcast.28), custom_call_target="tpu_custom_call" | custom-call | flops 1073741824 | bytes 5242880 | tf_op jit(solution)/shard_map/compare/pallas_call | solution.py:169
  94.4 6.8 %all-to-all-start.3 = ((f32[64,2,128]{2,1,0:T(2,128)}), f32[64,2,128]{2,1,0:T(2,128)S(1)}, u32[]{:S(2)}, u32[]{:S(2)}) async-start(f32[64,2,128]{2,1,0:T(2,128)} %bitcast.11), calls=%async_computation.3 | async-start | bytes 131072 | tf_op jit(solution)/shard_map/all_to_all | solution.py:317
  101.3 0.1 broadcast_in_dim_tile.7.noise_ref
  101.3 9.3 %all-to-all-done.3 = f32[64,2,128]{2,1,0:T(2,128)S(1)} async-done(((f32[64,2,128]{2,1,0:T(2,128)}), f32[64,2,128]{2,1,0:T(2,128)S(1)}, u32[]{:S(2)}, u32[]{:S(2)}) %all-to-all-start.3) | async-done | bytes 65568 | tf_op jit(solution)/shard_map/all_to_all | solution.py:317
  110.6 1.0 copy-done.4
  111.7 1.0 project.1
  112.7 0.9 copy-done
  113.6 6.0 %all-to-all-start.4 = ((bf16[8,32,1536]{2,1,0:T(8,128)(2,1)}), bf16[8,32,1536]{2,1,0:T(8,128)(2,1)S(1)}, u32[]{:S(2)}, u32[]{:S(2)}) async-start(bf16[8,32,1536]{2,1,0:T(8,128)(2,1)} %bitcast.27), calls=%async_computation.4 | async-start | bytes 1572864 | tf_op jit(solution)/shard_map/all_to_all | solution.py:321
  119.6 0.1 reshape.133
  119.7 0.1 constant_dynamic-slice_fusion
  119.7 0.6 copy.55
  120.3 19.9 %all-to-all-done.4.part_ref = bf16[8,32,1536]{2,1,0:T(8,128)(2,1)S(1)} async-done(((bf16[8,32,1536]{2,1,0:T(8,128)(2,1)}), bf16[8,32,1536]{2,1,0:T(8,128)(2,1)S(1)}, u32[]{:S(2)}, u32[]{:S(2)}) %all-to-all-start.4) | async-done | bytes 786464 | tf_op jit(solution)/shard_map/all_to_all | solution.py:321
  140.3 0.7 finish.1
  (31 shorter events, 0.2 us)
Async XLA Ops:
  0.6 36.7 %copy-start.12 = (bf16[512,1024]{1,0:T(8,128)(2,1)S(1)}, bf16[512,1024]{1,0:T(8,128)(2,1)}, u32[]{:S(2)}) copy-start(bf16[512,1024]{1,0:T(8,128)(2,1)} %constant.53.clone.table_ref) | copy-start | bytes 3145732
  28.9 8.4 %copy-start.11 = (bf16[1,512,512]{2,1,0:T(8,128)(2,1)S(1)}, bf16[1,512,512]{2,1,0:T(8,128)(2,1)}, u32[]{:S(2)}) copy-start(bf16[1,512,512]{2,1,0:T(8,128)(2,1)} %param.10) | copy-start | bytes 1572868
  28.9 23.7 %all-to-all-start.2 = ((bf16[8,32,1024]{2,1,0:T(8,128)(2,1)}), bf16[8,32,1024]{2,1,0:T(8,128)(2,1)S(1)}, u32[]{:S(2)}, u32[]{:S(2)}) async-start(bf16[8,32,1024]{2,1,0:T(8,128)(2,1)} %broadcast_in_dim.26), calls=%async_computation.2 | async-start | bytes 1048576 | tf_op jit(solution)/shard_map/all_to_all | solution.py:285
  52.6 0.8 copy-start.1
  53.4 32.9 %all-to-all-start = ((bf16[64,8,1024]{2,1,0:T(8,128)(2,1)}), bf16[64,8,1024]{2,1,0:T(8,128)(2,1)S(1)}, u32[]{:S(2)}, u32[]{:S(2)}) async-start(bf16[64,8,1024]{2,1,0:T(8,128)(2,1)} %bitcast.1), calls=%async_computation | async-start | bytes 2097152 | tf_op jit(solution)/shard_map/all_to_all | solution.py:294
  58.1 0.7 copy-start.14
  58.8 0.8 copy-start.13
  65.2 0.8 copy-start.3
  66.0 1.0 copy-start.7
  67.0 1.0 copy-start.9
  86.3 1.0 copy-start.2
  87.4 1.2 copy-start.8
  88.6 1.2 copy-start.10
  94.4 16.2 %all-to-all-start.3 = ((f32[64,2,128]{2,1,0:T(2,128)}), f32[64,2,128]{2,1,0:T(2,128)S(1)}, u32[]{:S(2)}, u32[]{:S(2)}) async-start(f32[64,2,128]{2,1,0:T(2,128)} %bitcast.11), calls=%async_computation.3 | async-start | bytes 131072 | tf_op jit(solution)/shard_map/all_to_all | solution.py:317
  110.6 1.0 copy-start.4
  112.7 0.9 copy-start
  113.6 26.7 %copy-start.5 = (f32[4,8,1024]{2,1,0:T(8,128)S(1)}, f32[4,8,1024]{2,1,0:T(8,128)}, u32[]{:S(2)}) copy-start(f32[4,8,1024]{2,1,0:T(8,128)} %param.17) | copy-start | bytes 393220
  113.6 26.7 %copy-start.6 = (f32[4,8,512]{2,1,0:T(8,128)S(1)}, f32[4,8,512]{2,1,0:T(8,128)}, u32[]{:S(2)}) copy-start(f32[4,8,512]{2,1,0:T(8,128)} %param.18) | copy-start | bytes 196612
  113.6 26.7 %all-to-all-start.4 = ((bf16[8,32,1536]{2,1,0:T(8,128)(2,1)}), bf16[8,32,1536]{2,1,0:T(8,128)(2,1)S(1)}, u32[]{:S(2)}, u32[]{:S(2)}) async-start(bf16[8,32,1536]{2,1,0:T(8,128)(2,1)} %bitcast.27), calls=%async_computation.4 | async-start | bytes 1572864 | tf_op jit(solution)/shard_map/all_to_all | solution.py:321

commit v2 on v0

v2 whole, which is shorter than its diff:
```python
import functools
import math

import jax
import jax.numpy as jnp
import ml_dtypes
import numpy as np
from jax import lax
from jax.experimental import pallas as pl
from jax.experimental.pallas import tpu as pltpu
from jax.sharding import PartitionSpec as P

AMP = 0.1
TILT = math.asin(AMP)
PI_HIGH = float(np.float32(math.floor(math.pi * 4096) / 4096))
PI_LOW = math.pi - PI_HIGH
VMEM = 56 * 1024 * 1024
LARGE = 32 * 1024 * 1024
SMALL = 16 * 1024 * 1024
META = 128


def dft_table(npix):
    index = np.arange(npix)
    angle = (index[:, None] * index[None, :] % npix) * (2.0 * math.pi / npix)
    scale = 1.0 / math.sqrt(npix)
    both = np.concatenate([np.cos(angle) * scale, np.sin(angle) * scale], 1)
    return both.astype(np.float32).astype(ml_dtypes.bfloat16)


def frequency(index, npix):
    return ((index + npix // 2) % npix - npix // 2).astype(jnp.float32) / npix


def params(size=VMEM):
    return pltpu.CompilerParams(vmem_limit_bytes=size)


def cost(flops, size):
    return pl.CostEstimate(flops=flops, bytes_accessed=size, transcendentals=0)


def whole():
    return pl.BlockSpec(memory_space=pltpu.VMEM)


def scalar():
    return pl.BlockSpec(memory_space=pltpu.SMEM)


def same(a, b):
    return lax.dot_general(a, b, (((1,), (1,)), ((), ())), preferred_element_type=jnp.float32)


def three_parts(value):
    parts = []
    for _ in range(3):
        part = value.astype(jnp.bfloat16).astype(jnp.float32)
        parts.append(part)
        value = value - part
    return parts


def transform_kernel(chunk, orient_ref, defocus_ref, noise_ref, image_ref, table_ref, out_ref, both_ref):
    npix = image_ref.shape[0]
    ori = orient_ref.shape[1]
    lane = lax.broadcasted_iota(jnp.int32, (8, META), 1)
    codes = jnp.zeros((8, META), jnp.int32)
    for o in range(ori):
        label = orient_ref[0, o]
        codes = jnp.where(lane == o, label & 255, codes)
        codes = jnp.where(lane == ori + o, label >> 8, codes)
    about = codes.astype(jnp.float32)
    place = 2 * ori
    for scalar_ref in (defocus_ref, noise_ref):
        for part in three_parts(jnp.full((8, META), scalar_ref[0], jnp.float32)):
            about = jnp.where(lane == place, part, about)
            place += 1
    out_ref[:, 2 * npix :] = jnp.broadcast_to(about[:1], (npix, META)).astype(jnp.bfloat16)
    for start in range(0, npix, chunk):
        real = jnp.dot(
            image_ref[...], table_ref[:, start : start + chunk], preferred_element_type=jnp.float32
        ).astype(jnp.bfloat16)
        both_ref[:npix, start : start + chunk] = real
        both_ref[npix:, npix + start : npix + start + chunk] = -real
        imag = -jnp.dot(
            image_ref[...],
            table_ref[:, npix + start : npix + start + chunk],
            preferred_element_type=jnp.float32,
        ).astype(jnp.bfloat16)
        both_ref[:npix, npix + start : npix + start + chunk] = imag
        both_ref[npix:, start : start + chunk] = imag
    for start in range(0, 2 * npix, chunk):
        out_ref[:, start : start + chunk] = jnp.dot(
            table_ref[...], both_ref[:, start : start + chunk], preferred_element_type=jnp.float32
        ).astype(jnp.bfloat16)


def transform(orient, defocus, noise, image, table):
    npix = image.shape[0]
    return pl.pallas_call(
        functools.partial(transform_kernel, 256),
        in_specs=[scalar(), scalar(), scalar(), whole(), whole()],
        out_specs=whole(),
        out_shape=jax.ShapeDtypeStruct((npix, 2 * npix + META), jnp.bfloat16),
        scratch_shapes=[pltpu.VMEM((2 * npix, 2 * npix), jnp.bfloat16)],
        compiler_params=params(),
        cost_estimate=cost(12 * npix**3, 10 * npix * npix),
        name="transform",
    )(orient, defocus, noise, image, table)


def prepare_kernel(planes_ref, weights_ref, lookup_ref):
    deep, labels = lookup_ref.shape
    rows = planes_ref.shape[1]
    level = lax.broadcasted_iota(jnp.int32, (deep // rows, rows, labels), 0)
    total = jnp.zeros((deep // rows, rows, labels), jnp.float32)
    for k in range(2):
        weight = weights_ref[k].astype(jnp.float32)
        total = total + jnp.where(level == planes_ref[k][None], weight[None], 0.0)
    lookup_ref[...] = total.reshape(deep, labels).astype(jnp.bfloat16)


def prepare(planes, weights, deep):
    labels = planes.shape[2]
    return pl.pallas_call(
        prepare_kernel,
        in_specs=[whole(), whole()],
        out_specs=whole(),
        out_shape=jax.ShapeDtypeStruct((deep, labels), jnp.bfloat16),
        compiler_params=params(SMALL),
        cost_estimate=cost(1 << 22, 1 << 20),
        name="prepare",
    )(planes, weights)


def contrast(defocus, row_square, npix):
    column = lax.broadcasted_iota(jnp.int32, (1, npix), 1)
    freq_x = frequency(column, npix)
    chi = defocus * (row_square + freq_x * freq_x)
    turns = jnp.floor((chi + TILT) * (1.0 / math.pi) + 0.5)
    angle = ((chi - turns * PI_HIGH) - turns * PI_LOW) + TILT
    half = turns * 0.5
    sign = 4.0 * (half - jnp.floor(half)) - 1.0
    square = angle * angle
    series = -1.0 / 39916800.0
    for term in (1.0 / 362880.0, -1.0 / 5040.0, 1.0 / 120.0, -1.0 / 6.0, 1.0):
        series = series * square + term
    return sign * (series * angle)


def compare_kernel(ori, rows, slot_ref, fourier_ref, lookup_ref, volume_ref, filtered_ref, square_ref, picks_ref, part_ref, noise_ref, mix_ref, total_ref, defocus_ref):
    many, npix = square_ref.shape
    deep = volume_ref.shape[0]
    images = many // rows
    batches, block, _ = mix_ref.shape
    lines = block // ori
    group = lines // rows

    meta = fourier_ref[:, 2 * npix :]
    here = lax.broadcasted_iota(jnp.int32, (images, many), 0) * rows
    there = lax.broadcasted_iota(jnp.int32, (images, many), 1)
    pick = jnp.where(here == there, 1.0, 0.0).astype(jnp.bfloat16)
    about = jnp.dot(pick, meta, preferred_element_type=jnp.float32)
    label = lax.broadcasted_iota(jnp.int32, (images, lookup_ref.shape[1]), 1).astype(jnp.float32)
    owner = lax.broadcasted_iota(jnp.int32, (many, images), 0) // rows
    image = lax.broadcasted_iota(jnp.int32, (many, images), 1)
    spread = jnp.where(owner == image, 1.0, 0.0).astype(jnp.bfloat16)
    row = lax.broadcasted_iota(jnp.int32, (many, deep), 0) % rows
    at_row = row == lax.broadcasted_iota(jnp.int32, (many, deep), 1) % rows
    for o in range(ori):
        mine = about[:, o : o + 1] + 256.0 * about[:, ori + o : ori + o + 1]
        found = same(jnp.where(label == mine, 1.0, 0.0).astype(jnp.bfloat16), lookup_ref[...])
        found = found.astype(jnp.bfloat16)
        picks_ref[o * images : (o + 1) * images, :] = found
        every = jnp.dot(spread, found, preferred_element_type=jnp.float32)
        every = jnp.where(at_row, every, 0.0).astype(jnp.bfloat16)
        for batch in range(batches):
            mix_ref[batch, o * lines : (o + 1) * lines, :] = every[batch * lines : (batch + 1) * lines]
    place = 2 * ori
    defocus = meta.astype(jnp.float32)
    defocus_ref[...] = (
        defocus[:, place : place + 1]
        + defocus[:, place + 1 : place + 2]
        + defocus[:, place + 2 : place + 3]
    )
    turned = jnp.transpose(jnp.concatenate([about, about], 0))
    noise_ref[...] = (
        turned[place + 3 : place + 4] + turned[place + 4 : place + 5] + turned[place + 5 : place + 6]
    )
    index = lax.broadcasted_iota(jnp.int32, (lines, 1), 0) % rows + slot_ref[0] * rows
    freq_y = frequency(index, npix)

    @pl.loop(0, batches)
    def _(batch):
        at = pl.multiple_of(batch * lines, lines)
        section = jnp.dot(mix_ref[batch], volume_ref[...], preferred_element_type=jnp.float32)
        ctf = contrast(defocus_ref[pl.ds(at, lines), :], freq_y * freq_y, npix)
        for part in range(2):
            fourier = fourier_ref[pl.ds(at, lines), part * npix : (part + 1) * npix]
            filtered_ref[pl.ds(at, lines), part * npix : (part + 1) * npix] = (
                ctf * fourier.astype(jnp.float32)
            ).astype(jnp.bfloat16)
        square = ctf * ctf
        square_ref[pl.ds(at, lines), :] = square.astype(jnp.bfloat16)
        for o in range(ori):
            real = section[o * lines : (o + 1) * lines, :npix]
            imag = section[o * lines : (o + 1) * lines, npix:]
            power = square * (real * real + imag * imag)
            lanes = power[:, :128]
            for chunk in range(1, npix // 128):
                lanes = lanes + power[:, chunk * 128 : (chunk + 1) * 128]
            sums = jnp.sum(lanes.reshape(group, rows, 128), axis=1)
            first = pl.multiple_of(o * images + batch * group, group)
            total_ref[pl.ds(first, group), :] = sums

    found = jnp.where(at_row, same(filtered_ref[...], volume_ref[...]), 0.0)
    found = jnp.sum(found.reshape(images, rows, deep), axis=1)
    halves = []
    for o in range(ori):
        cross = found * picks_ref[o * images : (o + 1) * images, :].astype(jnp.float32)
        lanes = cross[:, :128]
        for chunk in range(1, deep // 128):
            lanes = lanes + cross[:, chunk * 128 : (chunk + 1) * 128]
        halves.append(lanes - 0.5 * total_ref[o * images : (o + 1) * images, :])
    upper = jnp.concatenate(halves[: ori // 2], 0)
    lower = jnp.concatenate(halves[ori // 2 :], 0)
    upper = jnp.sum(jnp.transpose(upper), axis=0, keepdims=True)
    lower = jnp.sum(jnp.transpose(lower), axis=0, keepdims=True)
    even = lax.broadcasted_iota(jnp.int32, part_ref.shape, 0) % 2 == 0
    part_ref[...] = jnp.where(even, upper, lower)


def compare(slot, fourier, lookup, volume, ori, rows, copies):
    many = fourier.shape[0]
    deep, wide = volume.shape
    images = many // rows
    lines = 8 * rows
    return pl.pallas_call(
        functools.partial(compare_kernel, ori, rows),
        in_specs=[scalar()] + [whole()] * 3,
        out_specs=(whole(),) * 5,
        out_shape=(
            jax.ShapeDtypeStruct((many, wide), jnp.bfloat16),
            jax.ShapeDtypeStruct((many, wide // 2), jnp.bfloat16),
            jax.ShapeDtypeStruct((ori * images, deep), jnp.bfloat16),
            jax.ShapeDtypeStruct((copies * 2, 2 * images), jnp.float32),
            jax.ShapeDtypeStruct((1, 2 * images), jnp.float32),
        ),
        scratch_shapes=[
            pltpu.VMEM((many // lines, ori * lines, deep), jnp.bfloat16),
            pltpu.VMEM((ori * images, 128), jnp.float32),
            pltpu.VMEM((many, 1), jnp.float32),
        ],
        compiler_params=params(LARGE),
        cost_estimate=cost(1 << 31, 5 << 20),
        name="compare",
    )(slot, fourier, lookup, volume)


def project_kernel(rows, ori, core_ref, part_ref, noise_ref, picks_ref, filtered_ref, square_ref, probs_ref, keep_ref, send_ref):
    many, wide = filtered_ref.shape
    deep = picks_ref.shape[1]
    lanes = part_ref.shape[1]
    images = lanes // 2
    sums = jnp.sum(part_ref[...].reshape(part_ref.shape[0] // 8, 8, lanes), axis=0)
    sums = sums + pltpu.roll(sums, 4, 0)
    sums = sums + pltpu.roll(sums, 2, 0)
    score = sums / noise_ref[...]
    top = jnp.maximum(score, pltpu.roll(score, 1, 0))
    top = jnp.maximum(top, pltpu.roll(top, images, 1))
    power = jnp.exp(score - top)
    total = power + pltpu.roll(power, 1, 0)
    total = total + pltpu.roll(total, images, 1)
    probs = power / total
    probs_ref[...] = probs
    column = jnp.transpose(jnp.concatenate([probs] * (lanes // 8), 0))
    share = jnp.zeros((images, deep), jnp.float32)
    for o in range(ori):
        half = o % 2
        chance = column[half * images : (half + 1) * images, o // 2 : o // 2 + 1]
        share = share + chance * picks_ref[o * images : (o + 1) * images, :].astype(jnp.float32)
    image = lax.broadcasted_iota(jnp.int32, (images, many), 0)
    owner = lax.broadcasted_iota(jnp.int32, (images, many), 1) // rows
    spread = jnp.where(owner == image, 1.0, 0.0).astype(jnp.bfloat16)
    row = lax.broadcasted_iota(jnp.int32, (deep, many), 0) % rows
    at_row = row == lax.broadcasted_iota(jnp.int32, (deep, many), 1) % rows
    share = jnp.dot(
        jnp.transpose(share).astype(jnp.bfloat16), spread, preferred_element_type=jnp.float32
    )
    share = jnp.where(at_row, share, 0.0).astype(jnp.bfloat16)
    first = core_ref[0] == 0
    for source_ref, start, size in ((filtered_ref, 0, wide), (square_ref, wide, wide // 2)):
        sums = jnp.dot(share, source_ref[...], preferred_element_type=jnp.float32)
        sums = sums.reshape(keep_ref.shape[0], 2, keep_ref.shape[1], size)
        keep_ref[:, :, start : start + size] = jnp.where(first, sums[:, 0], sums[:, 1]).astype(jnp.bfloat16)
        send_ref[:, :, start : start + size] = jnp.where(first, sums[:, 1], sums[:, 0]).astype(jnp.bfloat16)


def project(core, part, noise, picks, filtered, square, rows, ori, pairs):
    many, wide = filtered.shape
    deep = picks.shape[1]
    half = jax.ShapeDtypeStruct((pairs, deep // (2 * pairs), wide + wide // 2), jnp.bfloat16)
    return pl.pallas_call(
        functools.partial(project_kernel, rows, ori),
        in_specs=[scalar()] + [whole()] * 5,
        out_specs=(whole(), whole(), whole()),
        out_shape=(jax.ShapeDtypeStruct((8, part.shape[1]), jnp.float32), half, half),
        compiler_params=params(LARGE),
        cost_estimate=cost(1 << 29, 4 << 20),
        name="project",
    )(core, part, noise, picks, filtered, square)


def middle_kernel(high_ref, keep_ref, got_ref, own_ref, *send_refs):
    pairs = keep_ref.shape[0]
    for ahead in range(pairs):
        at = (high_ref[0] + ahead) % pairs
        total = keep_ref[at].astype(jnp.float32) + got_ref[at].astype(jnp.float32)
        if ahead == 0:
            own_ref[...] = total
        else:
            send_refs[ahead - 1][...] = total.astype(jnp.bfloat16)


def middle(high, keep, got):
    pairs, slab, wide = keep.shape
    return pl.pallas_call(
        middle_kernel,
        in_specs=[scalar(), whole(), whole()],
        out_specs=(whole(),) * pairs,
        out_shape=(jax.ShapeDtypeStruct((slab, wide), jnp.float32),)
        + (jax.ShapeDtypeStruct((slab, wide), jnp.bfloat16),) * (pairs - 1),
        compiler_params=params(SMALL),
        cost_estimate=cost(1 << 20, 2 << 20),
        name="middle",
    )(high, keep, got)


def finish_kernel(own_ref, *refs):
    data_ref, weight_ref, data_out, weight_out = refs[-4:]
    wide = data_ref.shape[1]
    total = own_ref[...]
    for part_ref in refs[:-4]:
        total = total + part_ref[...].astype(jnp.float32)
    data_out[...] = data_ref[...] + total[:, :wide]
    weight_out[...] = weight_ref[...] + total[:, wide:]


def finish(own, parts, data_old, weight_old):
    return pl.pallas_call(
        finish_kernel,
        out_shape=(
            jax.ShapeDtypeStruct(data_old.shape, jnp.float32),
            jax.ShapeDtypeStruct(weight_old.shape, jnp.float32),
        ),
        compiler_params=params(SMALL),
        cost_estimate=cost(1 << 20, 2 << 20),
        name="finish",
    )(own, *parts, data_old, weight_old)


def on_device(images, defocus, noise, orient, planes, weights, volume, data_old, weight_old):
    npix = images.shape[1]
    ori = orient.shape[1]
    n_img = lax.axis_size("img")
    n_vol = lax.axis_size("vol")
    rows = npix // n_img
    slab = volume.shape[0]
    deep = n_vol * slab * rows
    many = n_img * rows
    pairs = n_vol // 2
    slot = lax.axis_index("img").astype(jnp.int32).reshape(1)
    place = lax.axis_index("vol").astype(jnp.int32)

    fourier = transform(orient, defocus, noise, images[0], jnp.asarray(dft_table(npix)))
    fourier = lax.all_to_all(
        fourier.reshape(n_img, rows, 2 * npix + META), "img", split_axis=0, concat_axis=0, tiled=True
    ).reshape(many, 2 * npix + META)
    vol_rows = lax.all_gather(volume.reshape(slab * rows, 2 * npix), "vol", axis=0, tiled=True)
    lookup = prepare(jnp.swapaxes(planes, 1, 2), jnp.swapaxes(weights, 1, 2), deep)
    filtered, square, picks, part, noise_all = compare(
        slot, fourier, lookup, vol_rows, ori, rows, n_img
    )
    part = lax.all_to_all(
        part.reshape(n_img, 2, 2 * n_img), "img", split_axis=0, concat_axis=0, tiled=True
    ).reshape(2 * n_img, 2 * n_img)
    probs, keep, send = project(
        (place % 2).reshape(1), part, noise_all, picks, filtered, square, rows, ori, pairs
    )
    mine = lax.dynamic_slice_in_dim(
        probs[:2].reshape(2 * 2, n_img), lax.axis_index("img"), 1, 1
    ).reshape(1, ori)
    got = lax.ppermute(send, "vol", [(v, v ^ 1) for v in range(n_vol)])
    own, *sends = middle((place // 2).reshape(1), keep, got)
    parts = [
        lax.ppermute(part, "vol", [(v, (v + 2 * ahead) % n_vol) for v in range(n_vol)])
        for ahead, part in enumerate(sends, 1)
    ]
    data, weight = finish(
        own,
        parts,
        data_old.reshape(slab * rows, 2 * npix),
        weight_old.reshape(slab * rows, npix),
    )
    return (mine, data.reshape(data_old.shape), weight.reshape(weight_old.shape))


def solution(mesh):
    placed = (
        P(("img", "vol"), None, None),
        P(("img", "vol")),
        P(("img", "vol")),
        P(("img", "vol"), None),
        P(None, None, "img"),
        P(None, None, "img"),
        P("vol", "img", None),
        P("vol", "img", None),
        P("vol", "img", None),
    )
    return jax.shard_map(
        on_device,
        mesh=mesh,
        in_specs=placed,
        out_specs=(P(("img", "vol"), None), P("vol", "img", None), P("vol", "img", None)),
        check_vma=False,
    )
```

time: 878 us -> 105 us (0.12)
  blocking collectives: 561 us -> 26.5 us
  waiting for transfers between devices: 149 us -> 19.9 us
  local copies, waits for them, and re-layouts: 83.5 us -> 2.63 us
  other arithmetic: 37.3 us -> 0 us
  starting transfers between devices: 15.8 us -> 40 us
  matrix products: 14.4 us -> 0 us
  between operations: 15.6 us -> 2.06 us
  Pallas kernels: 0 us -> 13 us
    psum x1 -> x0, blocking collectives: 249 us -> none  [on_device(): cross, power = lax.psum((cross, power), 'img')]
    all_gather x2 -> x1, blocking collectives: 187 us -> 26.5 us  [on_device(): lax.all_gather(volume.reshape(slab * rows, 2 * npix), 'vol', axis=0, tile...]
    reduce_scatter x2 -> x0, waiting for transfers between devices: 149 us -> none  [the longest x1 108 us: on_device(): lax.psum_scatter(weight_part.astype(jnp.bfloat16), 'vol', scatter_dimensi...]
    unnamed x1 -> x0, blocking collectives: 125 us -> none
    gather x6 -> x0, local copies, waits for them, and re-layouts: 61.2 us -> none  [the longest x1 29.6 us: on_device(): vol_rows[picked[0], local_rows].astype(jnp.float32)]
    ppermute x0 -> x4, starting transfers between devices: none -> 17.8 us  [the longest x3 13.9 us: on_device(): lax.ppermute(part, 'vol', [(v, (v + 2 * ahead) % n_vol) for v in range(n_...]
    convert_element_type x4 -> x0, other arithmetic: 14.7 us -> none  [the longest x1 4.87 us: on_device(): ctf_square = (ctf * ctf).astype(jnp.bfloat16)]
    dot_general x6 -> x0, matrix products: 14.4 us -> none  [the longest x1 5.64 us: on_device(): jnp.einsum('yj,njk->nyk', cosine, first, preferred_element_type=jnp.float32)]
  transfers between devices with their start and end apart: 3 -> 6, of which waited for: 2 -> 5; matrix products, arithmetic and copies ran while one was open for 9% -> 1% of each run, Pallas kernels for 0% -> 0%
where the time goes in v2:
time: 105 us; the launch traced here: 104 us
  starting transfers between devices  40 us (38%)
  blocking collectives  26.5 us (25%)
  waiting for transfers between devices  19.9 us (19%)
  Pallas kernels  13 us (12%)
  local copies, waits for them, and re-layouts  2.63 us (3%)
  between operations  2.06 us (2%)
    all_gather x1, blocking collectives, on_device(): lax.all_gather(volume.reshape(slab * rows, 2 * npix), 'vol', axis=0, tile...  26.5 us
    all_to_all x1, starting transfers between devices, on_device(): lax.all_to_all(fourier.reshape(n_img, rows, 2 * npix + META), 'img', spli...  15.5 us
    ppermute x3, starting transfers between devices, on_device(): lax.ppermute(part, 'vol', [(v, (v + 2 * ahead) % n_vol) for v in range(n_...  13.9 us
    all_to_all x1, waiting for transfers between devices, on_device(): lax.all_to_all(part.reshape(n_img, 2, 2 * n_img), 'img', split_axis=0, co...  9.35 us
    all_to_all x1, starting transfers between devices, on_device(): lax.all_to_all(part.reshape(n_img, 2, 2 * n_img), 'img', split_axis=0, co...  6.75 us
    pallas_call x1, Pallas kernels, compare(): pl.pallas_call(functools.partial(compare_kernel, ori, rows), in_specs=[sc...  6.69 us
    ppermute x3, waiting for transfers between devices, on_device(): lax.ppermute(part, 'vol', [(v, (v + 2 * ahead) % n_vol) for v in range(n_...  4.85 us
    all_to_all x1, waiting for transfers between devices, on_device(): lax.all_to_all(fourier.reshape(n_img, rows, 2 * npix + META), 'img', spli...  4.49 us
  transfers between devices with their start and end apart: 6, of which 5 were waited for; matrix products, arithmetic and copies ran while one was open for 1% of the time, Pallas kernels for 0%

profile of v2, /device:TPU:1, one launch (start us, length us, event | category | flops | bytes accessed | tf_op | source)
XLA Modules:
  0.0 104.1 jit_solution(14972459417179301549)
XLA Ops:
  1.9 4.3 %transform.1 = bf16[512,1152]{1,0:T(8,128)(2,1)} custom-call(s32[1,4]{1,0:T(1,128)} %orient_ref.1, f32[1]{0:T(128)S(6)} %copy.15.defocus_ref, f32[1]{0:T(128)S(6)} %copy.16.noise_ref, bf16[512,512]{1,0:T(8,128)(2,1)} %bitcast.25, bf16[512,1024]{1,0:T(8,128)(2,1)} %constant.38.clone.table_ref), custom_call_target="tpu_custom_call" | custom-call | flops 1610612736 | bytes 2621440 | tf_op jit(solution)/shard_map/transform/pallas_call | solution.py:101
  6.2 0.0 copy-start.2
  6.2 0.0 copy-start.3
  6.2 0.0 copy-start.6
  6.2 15.5 %all-to-all-start = ((bf16[64,8,1152]{2,1,0:T(8,128)(2,1)}), bf16[64,8,1152]{2,1,0:T(8,128)(2,1)S(1)}, u32[]{:S(2)}, u32[]{:S(2)}) async-start(bf16[64,8,1152]{2,1,0:T(8,128)(2,1)} %bitcast.22), calls=%async_computation | async-start | bytes 2359296 | tf_op jit(solution)/shard_map/all_to_all | solution.py:377
  21.7 0.0 copy-done.2
  21.7 0.0 copy-done.3
  21.8 0.1 prepare.1.lookup_ref
  21.9 0.0 copy-done.6
  21.9 26.5 %all_gather.3.volume_ref = bf16[256,1024]{1,0:T(8,128)(2,1)S(1)} all-gather(bf16[32,1024]{1,0:T(8,128)(2,1)S(1)} %bitcast.23), channel_id=1, replica_groups=mesh['img'=64,'vol'=8] {'vol'}, dimensions={0}, use_global_device_ids=true | all-gather | bytes 589824 | tf_op jit(solution)/shard_map/all_gather | solution.py:380
  48.4 4.5 %all-to-all-done = bf16[64,8,1152]{2,1,0:T(8,128)(2,1)S(1)} async-done(((bf16[64,8,1152]{2,1,0:T(8,128)(2,1)}), bf16[64,8,1152]{2,1,0:T(8,128)(2,1)S(1)}, u32[]{:S(2)}, u32[]{:S(2)}) %all-to-all-start) | async-done | bytes 1179680 | tf_op jit(solution)/shard_map/all_to_all | solution.py:377
  52.9 6.7 %compare.4 = (bf16[512,1024]{1,0:T(8,128)(2,1)S(1)}, bf16[512,512]{1,0:T(8,128)(2,1)S(1)}, bf16[256,256]{1,0:T(8,128)(2,1)S(1)}, f32[128,128]{1,0:T(8,128)}, f32[1,128]{1,0:T(1,128)S(1)}) custom-call(s32[1]{0:T(128)} %bitcast.1.slot_ref, bf16[512,1152]{1,0:T(8,128)(2,1)S(1)} %bitcast.16, bf16[256,768]{1,0:T(8,128)(2,1)S(1)} %prepare.1.lookup_ref, ...), custom_call_target="tpu_custom_call" | custom-call | flops 2147483648 | bytes 5242880 | tf_op jit(solution)/shard_map/compare/pallas_call | solution.py:239
  59.6 0.0 copy-start.4
  59.6 0.8 copy-done.4
  60.4 6.8 %all-to-all-start.1 = ((f32[64,2,128]{2,1,0:T(2,128)}), f32[64,2,128]{2,1,0:T(2,128)S(1)}, u32[]{:S(2)}, u32[]{:S(2)}) async-start(f32[64,2,128]{2,1,0:T(2,128)} %bitcast.8), calls=%async_computation.1 | async-start | bytes 131072 | tf_op jit(solution)/shard_map/all_to_all | solution.py:385
  67.2 9.4 %all-to-all-done.1 = f32[64,2,128]{2,1,0:T(2,128)S(1)} async-done(((f32[64,2,128]{2,1,0:T(2,128)}), f32[64,2,128]{2,1,0:T(2,128)S(1)}, u32[]{:S(2)}, u32[]{:S(2)}) %all-to-all-start.1) | async-done | bytes 65568 | tf_op jit(solution)/shard_map/all_to_all | solution.py:385
  76.5 0.0 copy-start.5
  76.5 1.0 copy-done.5
  77.6 0.0 copy-start
  77.6 0.0 copy-start.1
  77.6 1.1 %project.1 = (f32[8,128]{1,0:T(8,128)S(1)}, bf16[4,32,1536]{2,1,0:T(8,128)(2,1)S(1)}, bf16[4,32,1536]{2,1,0:T(8,128)(2,1)S(1)}) custom-call(s32[1]{0:T(128)} %bitcast.core_ref, f32[128,128]{1,0:T(8,128)S(1)} %bitcast.18, f32[1,128]{1,0:T(1,128)S(1)} %get-tuple-element.18.noise_ref, bf16[256,256]{1,0:T(8,128)(2,1)S(1)} %get-tuple-element.19.picks_ref, ...), custom_call_target="tpu_custom_call" | custom-call | flops 536870912 | bytes 4194304 | tf_op jit(solution)/shard_map/project/pallas_call | solution.py:304
  78.7 3.8 %collective-permute-start = (bf16[4,32,1536]{2,1,0:T(8,128)(2,1)S(1)}, bf16[4,32,1536]{2,1,0:T(8,128)(2,1)S(1)}, u32[]{:S(2)}, u32[]{:S(2)}) collective-permute-start(bf16[4,32,1536]{2,1,0:T(8,128)(2,1)S(1)} %get-tuple-element.24), channel_id=1, source_target_pairs={{0,1},{1,0},{2,3},{3,2},{4,5},{5,4},{6,7},{7,6},{8,9},{9,8},{10,11... | collective-permute-start | bytes 1179656 | tf_op jit(solution)/shard_map/ppermute | solution.py:394
  82.5 0.1 reshape.55
  82.6 1.2 %collective-permute-done.got_ref = bf16[4,32,1536]{2,1,0:T(8,128)(2,1)S(1)} collective-permute-done((bf16[4,32,1536]{2,1,0:T(8,128)(2,1)S(1)}, bf16[4,32,1536]{2,1,0:T(8,128)(2,1)S(1)}, u32[]{:S(2)}, u32[]{:S(2)}) %collective-permute-start) | collective-permute-done | bytes 393248 | tf_op jit(solution)/shard_map/ppermute | solution.py:394
  83.8 0.1 middle.1
  83.9 4.2 %collective-permute-start.1 = (bf16[32,1536]{1,0:T(8,128)(2,1)S(1)}, bf16[32,1536]{1,0:T(8,128)(2,1)S(1)}, u32[]{:S(2)}, u32[]{:S(2)}) collective-permute-start(bf16[32,1536]{1,0:T(8,128)(2,1)S(1)} %get-tuple-element.26), channel_id=1, source_target_pairs={{0,2},{1,3},{2,4},{3,5},{4,6},{5,7},{6,0},{7,1},{8,10},{9,11},{10,... | collective-permute-start | bytes 294920 | tf_op jit(solution)/shard_map/ppermute | solution.py:397
  88.2 4.7 %collective-permute-start.2 = (bf16[32,1536]{1,0:T(8,128)(2,1)S(1)}, bf16[32,1536]{1,0:T(8,128)(2,1)S(1)}, u32[]{:S(2)}, u32[]{:S(2)}) collective-permute-start(bf16[32,1536]{1,0:T(8,128)(2,1)S(1)} %get-tuple-element.27), channel_id=1, source_target_pairs={{0,4},{1,5},{2,6},{3,7},{4,0},{5,1},{6,2},{7,3},{8,12},{9,13},{10,... | collective-permute-start | bytes 294920 | tf_op jit(solution)/shard_map/ppermute | solution.py:397
  92.9 5.0 %collective-permute-start.3 = (bf16[32,1536]{1,0:T(8,128)(2,1)S(1)}, bf16[32,1536]{1,0:T(8,128)(2,1)S(1)}, u32[]{:S(2)}, u32[]{:S(2)}) collective-permute-start(bf16[32,1536]{1,0:T(8,128)(2,1)S(1)} %get-tuple-element.28), channel_id=1, source_target_pairs={{0,6},{1,7},{2,0},{3,1},{4,2},{5,3},{6,4},{7,5},{8,14},{9,15},{10,... | collective-permute-start | bytes 294920 | tf_op jit(solution)/shard_map/ppermute | solution.py:397
  97.9 0.1 constant_dynamic-slice_fusion
  98.0 0.6 copy.14
  98.6 0.0 collective-permute-done.1.refs_0_
  98.6 1.2 %collective-permute-done.2.refs_1_ = bf16[32,1536]{1,0:T(8,128)(2,1)S(1)} collective-permute-done((bf16[32,1536]{1,0:T(8,128)(2,1)S(1)}, bf16[32,1536]{1,0:T(8,128)(2,1)S(1)}, u32[]{:S(2)}, u32[]{:S(2)}) %collective-permute-start.2) | collective-permute-done | bytes 98336 | tf_op jit(solution)/shard_map/ppermute | solution.py:397
  99.8 3.6 %collective-permute-done.3.refs_2_ = bf16[32,1536]{1,0:T(8,128)(2,1)S(1)} collective-permute-done((bf16[32,1536]{1,0:T(8,128)(2,1)S(1)}, bf16[32,1536]{1,0:T(8,128)(2,1)S(1)}, u32[]{:S(2)}, u32[]{:S(2)}) %collective-permute-start.3) | collective-permute-done | bytes 98336 | tf_op jit(solution)/shard_map/ppermute | solution.py:397
  103.4 0.0 copy-done
  103.4 0.0 copy-done.1
  103.4 0.7 finish.1
  (1 shorter events, 0.0 us)
Async XLA Ops:
  6.2 15.5 %copy-start.2 = (s32[2,768,8]{1,2,0:T(8,128)S(1)}, s32[2,768,8]{1,2,0:T(8,128)}, u32[]{:S(2)}) copy-start(s32[2,768,8]{1,2,0:T(8,128)} %param.14) | copy-start | bytes 147460
  6.2 15.5 %copy-start.3 = (bf16[2,768,8]{1,2,0:T(8,128)(2,1)S(1)}, bf16[2,768,8]{1,2,0:T(8,128)(2,1)}, u32[]{:S(2)}) copy-start(bf16[2,768,8]{1,2,0:T(8,128)(2,1)} %param.15) | copy-start | bytes 73732
  6.2 15.7 %copy-start.6 = (bf16[4,8,1024]{2,1,0:T(8,128)(2,1)S(1)}, bf16[4,8,1024]{2,1,0:T(8,128)(2,1)}, u32[]{:S(2)}) copy-start(bf16[4,8,1024]{2,1,0:T(8,128)(2,1)} %param.16) | copy-start | bytes 196612
  6.2 46.7 %all-to-all-start = ((bf16[64,8,1152]{2,1,0:T(8,128)(2,1)}), bf16[64,8,1152]{2,1,0:T(8,128)(2,1)S(1)}, u32[]{:S(2)}, u32[]{:S(2)}) async-start(bf16[64,8,1152]{2,1,0:T(8,128)(2,1)} %bitcast.22), calls=%async_computation | async-start | bytes 2359296 | tf_op jit(solution)/shard_map/all_to_all | solution.py:377
  59.6 0.8 copy-start.4
  60.4 16.1 %all-to-all-start.1 = ((f32[64,2,128]{2,1,0:T(2,128)}), f32[64,2,128]{2,1,0:T(2,128)S(1)}, u32[]{:S(2)}, u32[]{:S(2)}) async-start(f32[64,2,128]{2,1,0:T(2,128)} %bitcast.8), calls=%async_computation.1 | async-start | bytes 131072 | tf_op jit(solution)/shard_map/all_to_all | solution.py:385
  76.5 1.0 %copy-start.5 = (bf16[512,512]{1,0:T(8,128)(2,1)S(1)}, bf16[512,512]{1,0:T(8,128)(2,1)}, u32[]{:S(2)}) copy-start(bf16[512,512]{1,0:T(8,128)(2,1)} %copy-done.4) | copy-start | bytes 1572868
  77.6 25.9 %copy-start = (f32[4,8,1024]{2,1,0:T(8,128)S(1)}, f32[4,8,1024]{2,1,0:T(8,128)}, u32[]{:S(2)}) copy-start(f32[4,8,1024]{2,1,0:T(8,128)} %param.17) | copy-start | bytes 393220
  77.6 25.9 %copy-start.1 = (f32[4,8,512]{2,1,0:T(8,128)S(1)}, f32[4,8,512]{2,1,0:T(8,128)}, u32[]{:S(2)}) copy-start(f32[4,8,512]{2,1,0:T(8,128)} %param.18) | copy-start | bytes 196612
  78.7 5.2 %collective-permute-start = (bf16[4,32,1536]{2,1,0:T(8,128)(2,1)S(1)}, bf16[4,32,1536]{2,1,0:T(8,128)(2,1)S(1)}, u32[]{:S(2)}, u32[]{:S(2)}) collective-permute-start(bf16[4,32,1536]{2,1,0:T(8,128)(2,1)S(1)} %get-tuple-element.24), channel_id=1, source_target_pairs={{0,1},{1,0},{2,3},{3,2},{4,5},{5,4},{6,7},{7,6},{8,9},{9,8},{10,11... | collective-permute-start | bytes 1179656 | tf_op jit(solution)/shard_map/ppermute | solution.py:394
  83.9 14.6 %collective-permute-start.1 = (bf16[32,1536]{1,0:T(8,128)(2,1)S(1)}, bf16[32,1536]{1,0:T(8,128)(2,1)S(1)}, u32[]{:S(2)}, u32[]{:S(2)}) collective-permute-start(bf16[32,1536]{1,0:T(8,128)(2,1)S(1)} %get-tuple-element.26), channel_id=1, source_target_pairs={{0,2},{1,3},{2,4},{3,5},{4,6},{5,7},{6,0},{7,1},{8,10},{9,11},{10,... | collective-permute-start | bytes 294920 | tf_op jit(solution)/shard_map/ppermute | solution.py:397
  88.2 11.7 %collective-permute-start.2 = (bf16[32,1536]{1,0:T(8,128)(2,1)S(1)}, bf16[32,1536]{1,0:T(8,128)(2,1)S(1)}, u32[]{:S(2)}, u32[]{:S(2)}) collective-permute-start(bf16[32,1536]{1,0:T(8,128)(2,1)S(1)} %get-tuple-element.27), channel_id=1, source_target_pairs={{0,4},{1,5},{2,6},{3,7},{4,0},{5,1},{6,2},{7,3},{8,12},{9,13},{10,... | collective-permute-start | bytes 294920 | tf_op jit(solution)/shard_map/ppermute | solution.py:397
  92.9 10.5 %collective-permute-start.3 = (bf16[32,1536]{1,0:T(8,128)(2,1)S(1)}, bf16[32,1536]{1,0:T(8,128)(2,1)S(1)}, u32[]{:S(2)}, u32[]{:S(2)}) collective-permute-start(bf16[32,1536]{1,0:T(8,128)(2,1)S(1)} %get-tuple-element.28), channel_id=1, source_target_pairs={{0,6},{1,7},{2,0},{3,1},{4,2},{5,3},{6,4},{7,5},{8,14},{9,15},{10,... | collective-permute-start | bytes 294920 | tf_op jit(solution)/shard_map/ppermute | solution.py:397

commit v3 on v2

v3 whole, which is shorter than its diff:
```python
import functools
import math

import jax
import jax.numpy as jnp
import ml_dtypes
import numpy as np
from jax import lax
from jax.experimental import pallas as pl
from jax.experimental.pallas import tpu as pltpu
from jax.sharding import PartitionSpec as P

AMP = 0.1
TILT = math.asin(AMP)
TURN = 2.0 * math.pi
TURN_HIGH = math.floor(TURN * 4096) / 4096
TURN_LOW = TURN - TURN_HIGH
SINE = tuple(
    factor / TURN ** (2 * power + 1)
    for power, factor in enumerate(
        (
            6.283185272722434,
            -41.341697068956265,
            81.60502462257806,
            -76.70155117622761,
            42.01616582127327,
            -14.868610992503873,
            3.199693654235983,
        )
    )
)
LARGE = 32 * 1024 * 1024
SMALL = 16 * 1024 * 1024
META = 128


def dft_table(npix):
    index = np.arange(npix)
    angle = (index[:, None] * index[None, :] % npix) * (2.0 * math.pi / npix)
    scale = 1.0 / math.sqrt(npix)
    both = np.concatenate([np.cos(angle) * scale, np.sin(angle) * scale], 1)
    return both.astype(np.float32).astype(ml_dtypes.bfloat16)


def frequency(index, npix):
    return ((index + npix // 2) % npix - npix // 2).astype(jnp.float32) / npix


def params(size):
    return pltpu.CompilerParams(vmem_limit_bytes=size)


def cost(flops, size):
    return pl.CostEstimate(flops=flops, bytes_accessed=size, transcendentals=0)


def whole():
    return pl.BlockSpec(memory_space=pltpu.VMEM)


def scalar():
    return pl.BlockSpec(memory_space=pltpu.SMEM)


def same(a, b):
    return lax.dot_general(a, b, (((1,), (1,)), ((), ())), preferred_element_type=jnp.float32)


def three_parts(value):
    parts = []
    for _ in range(3):
        part = value.astype(jnp.bfloat16).astype(jnp.float32)
        parts.append(part)
        value = value - part
    return parts


def bits(rows):
    assert rows & (rows - 1) == 0
    return rows.bit_length() - 1


def spread_over(rows, shape, image_axis):
    image = lax.broadcasted_iota(jnp.int32, shape, image_axis)
    owner = lax.broadcasted_iota(jnp.int32, shape, 1 - image_axis) >> bits(rows)
    return jnp.where(owner == image, 1.0, 0.0).astype(jnp.bfloat16)


def own_row(values, rows):
    height, width = values.shape
    sublane = lax.broadcasted_iota(jnp.int32, (rows, width), 0)
    lane = lax.broadcasted_iota(jnp.int32, (rows, width), 1) & (rows - 1)
    return jnp.where((sublane == lane)[None], values.reshape(height // rows, rows, width), 0.0)


def transform_kernel(chunk, orient_ref, defocus_ref, noise_ref, image_ref, table_hbm, out_hbm, table_ref, both_ref, out_ref, in_sems, out_sems):
    npix = image_ref.shape[0]
    ori = orient_ref.shape[1]
    starts = list(range(0, 2 * npix, chunk))
    loads = []
    for number, start in enumerate(starts):
        at = pl.ds(start, chunk)
        load = pltpu.make_async_copy(table_hbm.at[:, at], table_ref.at[:, at], in_sems.at[number])
        load.start()
        loads.append(load)
    lane = lax.broadcasted_iota(jnp.int32, (8, META), 1)
    codes = jnp.zeros((8, META), jnp.int32)
    for o in range(ori):
        label = orient_ref[0, o]
        codes = jnp.where(lane == o, label & 255, codes)
        codes = jnp.where(lane == ori + o, label >> 8, codes)
    about = codes.astype(jnp.float32)
    place = 2 * ori
    for scalar_ref in (defocus_ref, noise_ref):
        for part in three_parts(jnp.full((8, META), scalar_ref[0, 0], jnp.float32)):
            about = jnp.where(lane == place, part, about)
            place += 1
    out_ref[:, 2 * npix :] = jnp.broadcast_to(about[:1], (npix, META)).astype(jnp.bfloat16)
    saves = []

    def save(start, size):
        at = pl.ds(start, size)
        copy = pltpu.make_async_copy(out_ref.at[:, at], out_hbm.at[:, at], out_sems.at[len(saves)])
        copy.start()
        saves.append(copy)

    save(2 * npix, META)
    for number, start in enumerate(starts):
        loads[number].wait()
        first = jnp.dot(
            image_ref[...], table_ref[:, start : start + chunk], preferred_element_type=jnp.float32
        ).astype(jnp.bfloat16)
        if start < npix:
            both_ref[:npix, start : start + chunk] = first
            both_ref[npix:, npix + start : npix + start + chunk] = -first
        else:
            both_ref[:npix, start : start + chunk] = -first
            both_ref[npix:, start - npix : start - npix + chunk] = -first
    for start in starts:
        out_ref[:, start : start + chunk] = jnp.dot(
            table_ref[...], both_ref[:, start : start + chunk], preferred_element_type=jnp.float32
        ).astype(jnp.bfloat16)
        save(start, chunk)
    for copy in saves:
        copy.wait()


def transform(orient, defocus, noise, image, table):
    npix = image.shape[0]
    chunk = 256
    pieces = 2 * npix // chunk
    return pl.pallas_call(
        functools.partial(transform_kernel, chunk),
        in_specs=[scalar(), scalar(), scalar(), whole(), pl.BlockSpec(memory_space=pl.ANY)],
        out_specs=pl.BlockSpec(memory_space=pl.ANY),
        out_shape=jax.ShapeDtypeStruct((npix, 2 * npix + META), jnp.bfloat16),
        scratch_shapes=[
            pltpu.VMEM((npix, 2 * npix), jnp.bfloat16),
            pltpu.VMEM((2 * npix, 2 * npix), jnp.bfloat16),
            pltpu.VMEM((npix, 2 * npix + META), jnp.bfloat16),
            pltpu.SemaphoreType.DMA((pieces,)),
            pltpu.SemaphoreType.DMA((pieces + 1,)),
        ],
        compiler_params=params(LARGE),
        cost_estimate=cost(12 * npix**3, 10 * npix * npix),
        name="transform",
    )(orient, defocus, noise, image, table)


def prepare_kernel(planes_ref, weights_ref, lookup_ref):
    deep, labels = lookup_ref.shape
    rows = planes_ref.shape[1]
    level = lax.broadcasted_iota(jnp.int32, (deep // rows, rows, labels), 0)
    total = jnp.zeros((deep // rows, rows, labels), jnp.float32)
    for k in range(2):
        weight = weights_ref[k].astype(jnp.float32)
        total = total + jnp.where(level == planes_ref[k][None], weight[None], 0.0)
    lookup_ref[...] = total.reshape(deep, labels).astype(jnp.bfloat16)


def prepare(planes, weights, deep):
    labels = planes.shape[2]
    return pl.pallas_call(
        prepare_kernel,
        in_specs=[whole(), whole()],
        out_specs=whole(),
        out_shape=jax.ShapeDtypeStruct((deep, labels), jnp.bfloat16),
        compiler_params=params(SMALL),
        cost_estimate=cost(1 << 22, 1 << 20),
        name="prepare",
    )(planes, weights)


def contrast(defocus, row_square, start, width, npix):
    column = start + lax.broadcasted_iota(jnp.int32, (1, width), 1)
    freq_x = frequency(column, npix)
    chi = defocus * (row_square + freq_x * freq_x)
    turns = jnp.floor(chi * (1.0 / TURN) + (TILT / TURN + 0.5))
    angle = ((chi - turns * TURN_HIGH) - turns * TURN_LOW) + TILT
    square = angle * angle
    series = -SINE[-1]
    for term in SINE[-2::-1]:
        series = series * square - term
    return series * angle


def line_geometry(meta, ori, rows, many, npix, slot):
    place = 2 * ori
    defocus = meta[:, place : place + 1] + meta[:, place + 1 : place + 2] + meta[:, place + 2 : place + 3]
    index = (lax.broadcasted_iota(jnp.int32, (many, 1), 0) & (rows - 1)) + slot * rows
    freq_y = jnp.where(index < npix // 2, index, index - npix).astype(jnp.float32) / npix
    return defocus, freq_y * freq_y


def compare_kernel(ori, rows, slot_ref, fourier_ref, lookup_ref, volume_ref, filtered_ref, picks_ref, part_ref, about_ref, mix_ref, section_ref, power_ref):
    many, wide = filtered_ref.shape
    npix = wide // 2
    deep = volume_ref.shape[0]
    images = many // rows

    meta = fourier_ref[:, wide:]
    here = lax.broadcasted_iota(jnp.int32, (images, many), 0) << bits(rows)
    there = lax.broadcasted_iota(jnp.int32, (images, many), 1)
    pick = jnp.where(here == there, 1.0, 0.0).astype(jnp.bfloat16)
    about = jnp.dot(pick, meta, preferred_element_type=jnp.float32)
    about_ref[...] = about
    label = lax.broadcasted_iota(jnp.int32, (images, lookup_ref.shape[1]), 1).astype(jnp.float32)
    found = []
    for o in range(ori):
        mine = about[:, o : o + 1] + 256.0 * about[:, ori + o : ori + o + 1]
        found.append(jnp.where(label == mine, 1.0, 0.0).astype(jnp.bfloat16))
    found = same(jnp.concatenate(found, 0), lookup_ref[...]).astype(jnp.bfloat16)
    picks_ref[...] = found
    spread = spread_over(rows, (many, images), 1)
    for o in range(ori):
        every = jnp.dot(
            spread, found[o * images : (o + 1) * images], preferred_element_type=jnp.float32
        )
        mix_ref[o * many : (o + 1) * many, :] = (
            own_row(every, rows).reshape(many, deep).astype(jnp.bfloat16)
        )
    defocus, row_square = line_geometry(meta.astype(jnp.float32), ori, rows, many, npix, slot_ref[0])
    for number, start in enumerate(range(0, npix, 128)):
        real = slice(start, start + 128)
        imag = slice(npix + start, npix + start + 128)
        slot = number % 2
        section_ref[slot] = jnp.dot(
            mix_ref[...],
            jnp.concatenate([volume_ref[:, real], volume_ref[:, imag]], 1),
            preferred_element_type=jnp.float32,
        )
        ctf = contrast(defocus, row_square, start, 128, npix)
        for part in (real, imag):
            filtered_ref[:, part] = (ctf * fourier_ref[:, part].astype(jnp.float32)).astype(jnp.bfloat16)
        square = ctf * ctf
        for o in range(ori):
            s_real = section_ref[slot, o * many : (o + 1) * many, :128]
            s_imag = section_ref[slot, o * many : (o + 1) * many, 128:]
            power = square * (s_real * s_real + s_imag * s_imag)
            if number:
                power = power + power_ref[o]
            power_ref[o] = power

    found = own_row(same(filtered_ref[...], volume_ref[...]), rows)
    found = jnp.sum(found, axis=1)
    halves = []
    for o in range(ori):
        cross = found * picks_ref[o * images : (o + 1) * images, :].astype(jnp.float32)
        lanes = cross[:, :128]
        for start in range(128, deep, 128):
            lanes = lanes + cross[:, start : start + 128]
        power = jnp.sum(power_ref[o].reshape(images, rows, 128), axis=1)
        halves.append(lanes - 0.5 * power)
    upper = jnp.concatenate(halves[: ori // 2], 0)
    lower = jnp.concatenate(halves[ori // 2 :], 0)
    upper = jnp.sum(jnp.transpose(upper), axis=0, keepdims=True)
    lower = jnp.sum(jnp.transpose(lower), axis=0, keepdims=True)
    even = (lax.broadcasted_iota(jnp.int32, part_ref.shape, 0) & 1) == 0
    part_ref[...] = jnp.where(even, upper, lower)


def compare(slot, fourier, lookup, volume, ori, rows, copies):
    many = fourier.shape[0]
    deep, wide = volume.shape
    images = many // rows
    return pl.pallas_call(
        functools.partial(compare_kernel, ori, rows),
        in_specs=[scalar()] + [whole()] * 3,
        out_specs=(whole(),) * 4,
        out_shape=(
            jax.ShapeDtypeStruct((many, wide), jnp.bfloat16),
            jax.ShapeDtypeStruct((ori * images, deep), jnp.bfloat16),
            jax.ShapeDtypeStruct((copies * 2, 2 * images), jnp.float32),
            jax.ShapeDtypeStruct((images, META), jnp.float32),
        ),
        scratch_shapes=[
            pltpu.VMEM((ori * many, deep), jnp.bfloat16),
            pltpu.VMEM((2, ori * many, 256), jnp.float32),
            pltpu.VMEM((ori, many, 128), jnp.float32),
        ],
        compiler_params=params(LARGE),
        cost_estimate=cost(1 << 31, 5 << 20),
        name="compare",
    )(slot, fourier, lookup, volume)


def squares_kernel(ori, rows, slot_ref, about_ref, square_ref, noise_ref):
    many, npix = square_ref.shape
    images = many // rows
    about = about_ref[...]
    meta = jnp.dot(
        spread_over(rows, (many, images), 1),
        about.astype(jnp.bfloat16),
        preferred_element_type=jnp.float32,
    )
    defocus, row_square = line_geometry(meta, ori, rows, many, npix, slot_ref[0])
    for start in range(0, npix, 128):
        ctf = contrast(defocus, row_square, start, 128, npix)
        square_ref[:, start : start + 128] = (ctf * ctf).astype(jnp.bfloat16)
    place = 2 * ori + 3
    turned = jnp.transpose(jnp.concatenate([about, about], 0))
    noise_ref[...] = turned[place : place + 1] + turned[place + 1 : place + 2] + turned[place + 2 : place + 3]


def squares(slot, about, ori, rows, npix):
    images = about.shape[0]
    return pl.pallas_call(
        functools.partial(squares_kernel, ori, rows),
        in_specs=[scalar(), whole()],
        out_specs=(whole(), whole()),
        out_shape=(
            jax.ShapeDtypeStruct((images * rows, npix), jnp.bfloat16),
            jax.ShapeDtypeStruct((1, 2 * images), jnp.float32),
        ),
        compiler_params=params(SMALL),
        cost_estimate=cost(1 << 27, 1 << 20),
        name="squares",
    )(slot, about)


def project_kernel(rows, ori, core_ref, part_ref, noise_ref, picks_ref, filtered_ref, square_ref, probs_ref, keep_ref, send_ref):
    many, wide = filtered_ref.shape
    deep = picks_ref.shape[1]
    lanes = part_ref.shape[1]
    images = lanes // 2
    sums = jnp.sum(part_ref[...].reshape(part_ref.shape[0] // 8, 8, lanes), axis=0)
    sums = sums + pltpu.roll(sums, 4, 0)
    sums = sums + pltpu.roll(sums, 2, 0)
    score = sums / noise_ref[...]
    top = jnp.maximum(score, pltpu.roll(score, 1, 0))
    top = jnp.maximum(top, pltpu.roll(top, images, 1))
    power = jnp.exp(score - top)
    total = power + pltpu.roll(power, 1, 0)
    total = total + pltpu.roll(total, images, 1)
    probs = power / total
    probs_ref[...] = probs
    column = jnp.transpose(jnp.concatenate([probs] * (lanes // 8), 0))
    share = jnp.zeros((images, deep), jnp.float32)
    for o in range(ori):
        half = o % 2
        chance = column[half * images : (half + 1) * images, o // 2 : o // 2 + 1]
        share = share + chance * picks_ref[o * images : (o + 1) * images, :].astype(jnp.float32)
    share = jnp.dot(
        jnp.transpose(share).astype(jnp.bfloat16),
        spread_over(rows, (images, many), 0),
        preferred_element_type=jnp.float32,
    )
    share = own_row(share, rows).reshape(deep, many).astype(jnp.bfloat16)
    first = core_ref[0] == 0
    for source_ref, start, size in ((filtered_ref, 0, wide), (square_ref, wide, wide // 2)):
        sums = jnp.dot(share, source_ref[...], preferred_element_type=jnp.float32)
        sums = sums.reshape(keep_ref.shape[0], 2, keep_ref.shape[1], size)
        keep_ref[:, :, start : start + size] = jnp.where(first, sums[:, 0], sums[:, 1]).astype(jnp.bfloat16)
        send_ref[:, :, start : start + size] = jnp.where(first, sums[:, 1], sums[:, 0]).astype(jnp.bfloat16)


def project(core, part, noise, picks, filtered, square, rows, ori, pairs):
    many, wide = filtered.shape
    deep = picks.shape[1]
    half = jax.ShapeDtypeStruct((pairs, deep // (2 * pairs), wide + wide // 2), jnp.bfloat16)
    return pl.pallas_call(
        functools.partial(project_kernel, rows, ori),
        in_specs=[scalar()] + [whole()] * 5,
        out_specs=(whole(), whole(), whole()),
        out_shape=(jax.ShapeDtypeStruct((8, part.shape[1]), jnp.float32), half, half),
        compiler_params=params(LARGE),
        cost_estimate=cost(1 << 29, 4 << 20),
        name="project",
    )(core, part, noise, picks, filtered, square)


def middle_kernel(keep_ref, got_ref, out_ref):
    out_ref[...] = (keep_ref[...].astype(jnp.float32) + got_ref[...].astype(jnp.float32)).astype(jnp.bfloat16)


def middle(keep, got):
    return pl.pallas_call(
        middle_kernel,
        out_shape=jax.ShapeDtypeStruct(keep.shape, jnp.bfloat16),
        compiler_params=params(SMALL),
        cost_estimate=cost(1 << 20, 2 << 20),
        name="middle",
    )(keep, got)


def finish_kernel(parts_ref, data_ref, weight_ref, data_out, weight_out):
    wide = data_ref.shape[1]
    total = parts_ref[0].astype(jnp.float32)
    for source in range(1, parts_ref.shape[0]):
        total = total + parts_ref[source].astype(jnp.float32)
    data_out[...] = data_ref[...] + total[:, :wide]
    weight_out[...] = weight_ref[...] + total[:, wide:]


def finish(parts, data_old, weight_old):
    return pl.pallas_call(
        finish_kernel,
        out_shape=(
            jax.ShapeDtypeStruct(data_old.shape, jnp.float32),
            jax.ShapeDtypeStruct(weight_old.shape, jnp.float32),
        ),
        compiler_params=params(SMALL),
        cost_estimate=cost(1 << 20, 2 << 20),
        name="finish",
    )(parts, data_old, weight_old)


def on_device(images, defocus, noise, orient, planes, weights, volume, data_old, weight_old):
    npix = images.shape[1]
    ori = orient.shape[1]
    n_img = lax.axis_size("img")
    n_vol = lax.axis_size("vol")
    rows = npix // n_img
    slab = volume.shape[0]
    deep = n_vol * slab * rows
    many = n_img * rows
    pairs = n_vol // 2
    slot = lax.axis_index("img").astype(jnp.int32).reshape(1)
    place = lax.axis_index("vol").astype(jnp.int32)

    fourier = transform(
        orient, defocus.reshape(1, 1), noise.reshape(1, 1), images[0], jnp.asarray(dft_table(npix))
    )
    fourier = lax.all_to_all(
        fourier.reshape(n_img, rows, 2 * npix + META), "img", split_axis=0, concat_axis=0, tiled=True
    ).reshape(many, 2 * npix + META)
    vol_rows = lax.all_gather(volume.reshape(slab * rows, 2 * npix), "vol", axis=0, tiled=True)
    lookup = prepare(jnp.swapaxes(planes, 1, 2), jnp.swapaxes(weights, 1, 2), deep)
    filtered, picks, part, about = compare(slot, fourier, lookup, vol_rows, ori, rows, n_img)
    square, noise_all = squares(slot, about, ori, rows, npix)
    part = lax.all_to_all(
        part.reshape(n_img, 2, 2 * n_img), "img", split_axis=0, concat_axis=0, tiled=True
    ).reshape(2 * n_img, 2 * n_img)
    probs, keep, send = project(
        (place % 2).reshape(1), part, noise_all, picks, filtered, square, rows, ori, pairs
    )
    mine = lax.dynamic_slice_in_dim(
        probs[:2].reshape(2 * 2, n_img), lax.axis_index("img"), 1, 1
    ).reshape(1, ori)
    got = lax.ppermute(send, "vol", [(v, v ^ 1) for v in range(n_vol)])
    parts = lax.all_to_all(
        middle(keep, got),
        "vol",
        split_axis=0,
        concat_axis=0,
        axis_index_groups=[list(range(core, n_vol, 2)) for core in range(2)],
        tiled=True,
    )
    data, weight = finish(
        parts,
        data_old.reshape(slab * rows, 2 * npix),
        weight_old.reshape(slab * rows, npix),
    )
    return (mine, data.reshape(data_old.shape), weight.reshape(weight_old.shape))


def solution(mesh):
    placed = (
        P(("img", "vol"), None, None),
        P(("img", "vol")),
        P(("img", "vol")),
        P(("img", "vol"), None),
        P(None, None, "img"),
        P(None, None, "img"),
        P("vol", "img", None),
        P("vol", "img", None),
        P("vol", "img", None),
    )
    return jax.shard_map(
        on_device,
        mesh=mesh,
        in_specs=placed,
        out_specs=(P(("img", "vol"), None), P("vol", "img", None), P("vol", "img", None)),
        check_vma=False,
    )
```

time: 105 us -> 104 us (level); the launches traced: 104 us -> 101 us
  starting transfers between devices: 40 us -> 32.1 us
  waiting for transfers between devices: 19.9 us -> 24.3 us
  local copies, waits for them, and re-layouts: 2.63 us -> 3.7 us
    ppermute x3 -> x0, starting transfers between devices: 13.9 us -> none  [on_device(): lax.ppermute(part, 'vol', [(v, (v + 2 * ahead) % n_vol) for v in range(n_...]
    all_to_all x0 -> x1, waiting for transfers between devices: none -> 10.4 us  [on_device(): lax.all_to_all(middle(keep, got), 'vol', split_axis=0, concat_axis=0, axi...]
    all_to_all x0 -> x1, starting transfers between devices: none -> 5.92 us  [on_device(): lax.all_to_all(middle(keep, got), 'vol', split_axis=0, concat_axis=0, axi...]
    ppermute x3 -> x0, waiting for transfers between devices: 4.85 us -> none  [on_device(): lax.ppermute(part, 'vol', [(v, (v + 2 * ahead) % n_vol) for v in range(n_...]
    pallas_call x1, Pallas kernels: 6.69 us -> 4.31 us  [compare(): pl.pallas_call(functools.partial(compare_kernel, ori, rows), in_specs=[sc...]
    pallas_call x2 -> x3, Pallas kernels: 4.39 us -> 6.48 us  [the longest x1 4.34 us: transform(): pl.pallas_call(functools.partial(transform_kernel, chunk), in_specs=[scal...]
    all_to_all x1, waiting for transfers between devices: 9.35 us -> 8.06 us  [on_device(): lax.all_to_all(part.reshape(n_img, 2, 2 * n_img), 'img', split_axis=0, co...]
    unnamed x15 -> x17, local copies, waits for them, and re-layouts: 2.47 us -> 3.54 us
  transfers between devices with their start and end apart: 6 -> 4, of which waited for: 5 -> 4; matrix products, arithmetic and copies ran while one was open for 1% -> 1% of each run, Pallas kernels for 0% -> 1%
where the time goes in v3:
time: 104 us; the launch traced here: 101 us
  starting transfers between devices  32.1 us (31%)
  blocking collectives  26.5 us (25%)
  waiting for transfers between devices  24.3 us (23%)
  Pallas kernels  12.7 us (12%)
  local copies, waits for them, and re-layouts  3.7 us (4%)
  between operations  2.07 us (2%)
    all_gather x1, blocking collectives, on_device(): lax.all_gather(volume.reshape(slab * rows, 2 * npix), 'vol', axis=0, tile...  26.5 us
    all_to_all x1, starting transfers between devices, on_device(): lax.all_to_all(fourier.reshape(n_img, rows, 2 * npix + META), 'img', spli...  15.5 us
    all_to_all x1, waiting for transfers between devices, on_device(): lax.all_to_all(middle(keep, got), 'vol', split_axis=0, concat_axis=0, axi...  10.4 us
    all_to_all x1, waiting for transfers between devices, on_device(): lax.all_to_all(part.reshape(n_img, 2, 2 * n_img), 'img', split_axis=0, co...  8.06 us
    all_to_all x1, starting transfers between devices, on_device(): lax.all_to_all(part.reshape(n_img, 2, 2 * n_img), 'img', split_axis=0, co...  6.77 us
    all_to_all x1, starting transfers between devices, on_device(): lax.all_to_all(middle(keep, got), 'vol', split_axis=0, concat_axis=0, axi...  5.92 us
    all_to_all x1, waiting for transfers between devices, on_device(): lax.all_to_all(fourier.reshape(n_img, rows, 2 * npix + META), 'img', spli...  4.49 us
    pallas_call x1, Pallas kernels, transform(): pl.pallas_call(functools.partial(transform_kernel, chunk), in_specs=[scal...  4.34 us
  transfers between devices with their start and end apart: 4, of which 4 were waited for; matrix products, arithmetic and copies ran while one was open for 1% of the time, Pallas kernels for 1%

profile of v3, /device:TPU:1, one launch (start us, length us, event | category | flops | bytes accessed | tf_op | source)
XLA Modules:
  0.0 101.4 jit_solution(10540605589512968780)
XLA Ops:
  1.9 0.0 copy-start.4
  1.9 1.0 %copy-done.4 = bf16[1,512,512]{2,1,0:T(8,128)(2,1)S(1)} copy-done((bf16[1,512,512]{2,1,0:T(8,128)(2,1)S(1)}, bf16[1,512,512]{2,1,0:T(8,128)(2,1)}, u32[]{:S(2)}) %copy-start.4) | copy-done | bytes 524312
  3.0 0.0 copy-start.5
  3.0 0.7 copy-done.5
  3.6 0.0 copy-start.6
  3.6 1.2 %copy-done.6 = bf16[512,1024]{1,0:T(8,128)(2,1)S(1)} copy-done((bf16[512,1024]{1,0:T(8,128)(2,1)S(1)}, bf16[512,1024]{1,0:T(8,128)(2,1)}, u32[]{:S(2)}) %copy-start.6) | copy-done | bytes 1048600
  4.8 4.3 %transform.1 = bf16[512,1152]{1,0:T(8,128)(2,1)} custom-call(s32[1,4]{1,0:T(1,128)S(1)} %copy-done.5, f32[1,1]{1,0:T(1,128)} %bitcast.17.defocus_ref, f32[1,1]{1,0:T(1,128)} %bitcast.18.noise_ref, bf16[512,512]{1,0:T(8,128)(2,1)S(1)} %bitcast.25, bf16[512,1024]{1,0:T(8,128)(2,1)S(1)} %copy-done.6), custom_call_target="tpu_custom_call" | custom-call | flops 1610612736 | bytes 2621440 | tf_op jit(solution)/shard_map/transform/pallas_call | solution.py:152
  9.2 0.0 copy-start.2
  9.2 0.0 copy-start.3
  9.2 0.0 copy-start.7
  9.2 15.5 %all-to-all-start = ((bf16[64,8,1152]{2,1,0:T(8,128)(2,1)}), bf16[64,8,1152]{2,1,0:T(8,128)(2,1)S(1)}, u32[]{:S(2)}, u32[]{:S(2)}) async-start(bf16[64,8,1152]{2,1,0:T(8,128)(2,1)} %bitcast.5), calls=%async_computation | async-start | bytes 2359296 | tf_op jit(solution)/shard_map/all_to_all | solution.py:444
  24.7 0.0 copy-done.2
  24.7 0.0 copy-done.3
  24.8 0.1 prepare.1.lookup_ref
  24.9 0.0 copy-done.7
  24.9 26.5 %all_gather.3.volume_ref = bf16[256,1024]{1,0:T(8,128)(2,1)S(1)} all-gather(bf16[32,1024]{1,0:T(8,128)(2,1)S(1)} %bitcast.26), channel_id=1, replica_groups=mesh['img'=64,'vol'=8] {'vol'}, dimensions={0}, use_global_device_ids=true | all-gather | bytes 589824 | tf_op jit(solution)/shard_map/all_gather | solution.py:447
  51.4 4.5 %all-to-all-done = bf16[64,8,1152]{2,1,0:T(8,128)(2,1)S(1)} async-done(((bf16[64,8,1152]{2,1,0:T(8,128)(2,1)}), bf16[64,8,1152]{2,1,0:T(8,128)(2,1)S(1)}, u32[]{:S(2)}, u32[]{:S(2)}) %all-to-all-start) | async-done | bytes 1179680 | tf_op jit(solution)/shard_map/all_to_all | solution.py:444
  55.9 4.3 %compare.2 = (bf16[512,1024]{1,0:T(8,128)(2,1)S(1)}, bf16[256,256]{1,0:T(8,128)(2,1)S(1)}, f32[128,128]{1,0:T(8,128)}, f32[64,128]{1,0:T(8,128)S(1)}) custom-call(s32[1]{0:T(128)} %bitcast.1.slot_ref, bf16[512,1152]{1,0:T(8,128)(2,1)S(1)} %bitcast.19, bf16[256,768]{1,0:T(8,128)(2,1)S(1)} %prepare.1.lookup_ref, bf16[256,1024]{1,0:T(8,128)(2,1)S(1)} %all_gather.3.volume_ref), custom_call_target="tpu_custom_call" | custom-call | flops 2147483648 | bytes 5242880 | tf_op jit(solution)/shard_map/compare/pallas_call | solution.py:286
  60.2 6.8 %all-to-all-start.1 = ((f32[64,2,128]{2,1,0:T(2,128)}), f32[64,2,128]{2,1,0:T(2,128)S(1)}, u32[]{:S(2)}, u32[]{:S(2)}) async-start(f32[64,2,128]{2,1,0:T(2,128)} %bitcast.10), calls=%async_computation.1 | async-start | bytes 131072 | tf_op jit(solution)/shard_map/all_to_all | solution.py:451
  67.0 1.3 %squares.1 = (bf16[512,512]{1,0:T(8,128)(2,1)S(1)}, f32[1,128]{1,0:T(1,128)S(1)}) custom-call(s32[1]{0:T(128)} %bitcast.1.slot_ref, f32[64,128]{1,0:T(8,128)S(1)} %get-tuple-element.15.about_ref), custom_call_target="tpu_custom_call" | custom-call | flops 134217728 | bytes 1048576 | tf_op jit(solution)/shard_map/squares/pallas_call | solution.py:327
  68.3 8.1 %all-to-all-done.1 = f32[64,2,128]{2,1,0:T(2,128)S(1)} async-done(((f32[64,2,128]{2,1,0:T(2,128)}), f32[64,2,128]{2,1,0:T(2,128)S(1)}, u32[]{:S(2)}, u32[]{:S(2)}) %all-to-all-start.1) | async-done | bytes 65568 | tf_op jit(solution)/shard_map/all_to_all | solution.py:451
  76.3 1.1 %project.1 = (f32[8,128]{1,0:T(8,128)S(1)}, bf16[4,32,1536]{2,1,0:T(8,128)(2,1)S(1)}, bf16[4,32,1536]{2,1,0:T(8,128)(2,1)S(1)}) custom-call(s32[1]{0:T(128)} %bitcast.core_ref, f32[128,128]{1,0:T(8,128)S(1)} %bitcast.22, f32[1,128]{1,0:T(1,128)S(1)} %get-tuple-element.16.noise_ref, bf16[256,256]{1,0:T(8,128)(2,1)S(1)} %get-tuple-element.17.picks_ref, ...), custom_call_target="tpu_custom_call" | custom-call | flops 536870912 | bytes 4194304 | tf_op jit(solution)/shard_map/project/pallas_call | solution.py:381
  77.4 0.0 copy-start
  77.4 0.0 copy-start.1
  77.5 4.0 %collective-permute-start = (bf16[4,32,1536]{2,1,0:T(8,128)(2,1)S(1)}, bf16[4,32,1536]{2,1,0:T(8,128)(2,1)S(1)}, u32[]{:S(2)}, u32[]{:S(2)}) collective-permute-start(bf16[4,32,1536]{2,1,0:T(8,128)(2,1)S(1)} %get-tuple-element.22), channel_id=1, source_target_pairs={{0,1},{1,0},{2,3},{3,2},{4,5},{5,4},{6,7},{7,6},{8,9},{9,8},{10,11... | collective-permute-start | bytes 1179656 | tf_op jit(solution)/shard_map/ppermute | solution.py:460
  81.4 1.3 %collective-permute-done.got_ref = bf16[4,32,1536]{2,1,0:T(8,128)(2,1)S(1)} collective-permute-done((bf16[4,32,1536]{2,1,0:T(8,128)(2,1)S(1)}, bf16[4,32,1536]{2,1,0:T(8,128)(2,1)S(1)}, u32[]{:S(2)}, u32[]{:S(2)}) %collective-permute-start) | collective-permute-done | bytes 393248 | tf_op jit(solution)/shard_map/ppermute | solution.py:460
  82.8 0.9 middle.1
  83.6 5.9 %all-to-all-start.2 = ((bf16[4,32,1536]{2,1,0:T(8,128)(2,1)}), bf16[4,32,1536]{2,1,0:T(8,128)(2,1)S(1)}, u32[]{:S(2)}, u32[]{:S(2)}) async-start(bf16[4,32,1536]{2,1,0:T(8,128)(2,1)} %middle.1), calls=%async_computation.2 | async-start | bytes 786432 | tf_op jit(solution)/shard_map/all_to_all | solution.py:461
  89.5 0.1 reshape.60
  89.6 0.1 constant_dynamic-slice_fusion
  89.7 0.6 copy.14
  90.3 10.4 %all-to-all-done.2.parts_ref = bf16[4,32,1536]{2,1,0:T(8,128)(2,1)S(1)} async-done(((bf16[4,32,1536]{2,1,0:T(8,128)(2,1)}), bf16[4,32,1536]{2,1,0:T(8,128)(2,1)S(1)}, u32[]{:S(2)}, u32[]{:S(2)}) %all-to-all-start.2) | async-done | bytes 393248 | tf_op jit(solution)/shard_map/all_to_all | solution.py:461
  100.7 0.0 copy-done
  100.7 0.0 copy-done.1
  100.7 0.7 finish.1
  (1 shorter events, 0.0 us)
Async XLA Ops:
  1.9 1.0 %copy-start.4 = (bf16[1,512,512]{2,1,0:T(8,128)(2,1)S(1)}, bf16[1,512,512]{2,1,0:T(8,128)(2,1)}, u32[]{:S(2)}) copy-start(bf16[1,512,512]{2,1,0:T(8,128)(2,1)} %param.10) | copy-start | bytes 1572868
  3.0 0.7 copy-start.5
  3.6 1.2 %copy-start.6 = (bf16[512,1024]{1,0:T(8,128)(2,1)S(1)}, bf16[512,1024]{1,0:T(8,128)(2,1)}, u32[]{:S(2)}) copy-start(bf16[512,1024]{1,0:T(8,128)(2,1)} %constant.27.clone.table_hbm) | copy-start | bytes 3145732
  9.2 15.5 %copy-start.2 = (s32[2,768,8]{1,2,0:T(8,128)S(1)}, s32[2,768,8]{1,2,0:T(8,128)}, u32[]{:S(2)}) copy-start(s32[2,768,8]{1,2,0:T(8,128)} %param.14) | copy-start | bytes 147460
  9.2 15.5 %copy-start.3 = (bf16[2,768,8]{1,2,0:T(8,128)(2,1)S(1)}, bf16[2,768,8]{1,2,0:T(8,128)(2,1)}, u32[]{:S(2)}) copy-start(bf16[2,768,8]{1,2,0:T(8,128)(2,1)} %param.15) | copy-start | bytes 73732
  9.2 15.7 %copy-start.7 = (bf16[4,8,1024]{2,1,0:T(8,128)(2,1)S(1)}, bf16[4,8,1024]{2,1,0:T(8,128)(2,1)}, u32[]{:S(2)}) copy-start(bf16[4,8,1024]{2,1,0:T(8,128)(2,1)} %param.16) | copy-start | bytes 196612
  9.2 46.7 %all-to-all-start = ((bf16[64,8,1152]{2,1,0:T(8,128)(2,1)}), bf16[64,8,1152]{2,1,0:T(8,128)(2,1)S(1)}, u32[]{:S(2)}, u32[]{:S(2)}) async-start(bf16[64,8,1152]{2,1,0:T(8,128)(2,1)} %bitcast.5), calls=%async_computation | async-start | bytes 2359296 | tf_op jit(solution)/shard_map/all_to_all | solution.py:444
  60.2 16.1 %all-to-all-start.1 = ((f32[64,2,128]{2,1,0:T(2,128)}), f32[64,2,128]{2,1,0:T(2,128)S(1)}, u32[]{:S(2)}, u32[]{:S(2)}) async-start(f32[64,2,128]{2,1,0:T(2,128)} %bitcast.10), calls=%async_computation.1 | async-start | bytes 131072 | tf_op jit(solution)/shard_map/all_to_all | solution.py:451
  77.4 23.3 %copy-start = (f32[4,8,1024]{2,1,0:T(8,128)S(1)}, f32[4,8,1024]{2,1,0:T(8,128)}, u32[]{:S(2)}) copy-start(f32[4,8,1024]{2,1,0:T(8,128)} %param.17) | copy-start | bytes 393220
  77.4 23.3 %copy-start.1 = (f32[4,8,512]{2,1,0:T(8,128)S(1)}, f32[4,8,512]{2,1,0:T(8,128)}, u32[]{:S(2)}) copy-start(f32[4,8,512]{2,1,0:T(8,128)} %param.18) | copy-start | bytes 196612
  77.5 5.3 %collective-permute-start = (bf16[4,32,1536]{2,1,0:T(8,128)(2,1)S(1)}, bf16[4,32,1536]{2,1,0:T(8,128)(2,1)S(1)}, u32[]{:S(2)}, u32[]{:S(2)}) collective-permute-start(bf16[4,32,1536]{2,1,0:T(8,128)(2,1)S(1)} %get-tuple-element.22), channel_id=1, source_target_pairs={{0,1},{1,0},{2,3},{3,2},{4,5},{5,4},{6,7},{7,6},{8,9},{9,8},{10,11... | collective-permute-start | bytes 1179656 | tf_op jit(solution)/shard_map/ppermute | solution.py:460
  83.6 17.1 %all-to-all-start.2 = ((bf16[4,32,1536]{2,1,0:T(8,128)(2,1)}), bf16[4,32,1536]{2,1,0:T(8,128)(2,1)S(1)}, u32[]{:S(2)}, u32[]{:S(2)}) async-start(bf16[4,32,1536]{2,1,0:T(8,128)(2,1)} %middle.1), calls=%async_computation.2 | async-start | bytes 786432 | tf_op jit(solution)/shard_map/all_to_all | solution.py:461

commit v4 on v3

--- a/solution.py
+++ b/solution.py
@@ -29,6 +29,7 @@
         )
     )
 )
+HUGE = 56 * 1024 * 1024
 LARGE = 32 * 1024 * 1024
 SMALL = 16 * 1024 * 1024
 META = 128
@@ -93,16 +94,40 @@
     return jnp.where((sublane == lane)[None], values.reshape(height // rows, rows, width), 0.0)
 
 
-def transform_kernel(chunk, orient_ref, defocus_ref, noise_ref, image_ref, table_hbm, out_hbm, table_ref, both_ref, out_ref, in_sems, out_sems):
+def transform_kernel(chunk, orient_hbm, defocus_hbm, noise_hbm, image_hbm, table_hbm, out_hbm, orient_ref, defocus_ref, noise_ref, image_ref, table_ref, both_ref, out_ref, in_sems, out_sems):
     npix = image_ref.shape[0]
     ori = orient_ref.shape[1]
     starts = list(range(0, 2 * npix, chunk))
+    pairs = [(image_hbm, image_ref)]
+    pairs += [(table_hbm.at[:, pl.ds(start, chunk)], table_ref.at[:, pl.ds(start, chunk)]) for start in starts]
+    pairs += [(orient_hbm, orient_ref), (defocus_hbm, defocus_ref), (noise_hbm, noise_ref)]
     loads = []
-    for number, start in enumerate(starts):
-        at = pl.ds(start, chunk)
-        load = pltpu.make_async_copy(table_hbm.at[:, at], table_ref.at[:, at], in_sems.at[number])
+    for number, (source, target) in enumerate(pairs):
+        load = pltpu.make_async_copy(source, target, in_sems.at[number])
         load.start()
         loads.append(load)
+    loads[0].wait()
+    for number, start in enumerate(starts):
+        loads[1 + number].wait()
+        first = jnp.dot(
+            image_ref[...], table_ref[:, start : start + chunk], preferred_element_type=jnp.float32
+        ).astype(jnp.bfloat16)
+        if start < npix:
+            both_ref[:npix, start : start + chunk] = first
+            both_ref[npix:, npix + start : npix + start + chunk] = -first
+        else:
+            both_ref[:npix, start : start + chunk] = -first
+            both_ref[npix:, start - npix : start - npix + chunk] = -first
+    for load in loads[1 + len(starts) :]:
+        load.wait()
+    saves = []
+
+    def save(start, size):
+        at = pl.ds(start, size)
+        copy = pltpu.make_async_copy(out_ref.at[:, at], out_hbm.at[:, at], out_sems.at[len(saves)])
+        copy.start()
+        saves.append(copy)
+
     lane = lax.broadcasted_iota(jnp.int32, (8, META), 1)
     codes = jnp.zeros((8, META), jnp.int32)
     for o in range(ori):
@@ -112,30 +137,11 @@
     about = codes.astype(jnp.float32)
     place = 2 * ori
     for scalar_ref in (defocus_ref, noise_ref):
-        for part in three_parts(jnp.full((8, META), scalar_ref[0, 0], jnp.float32)):
+        for part in three_parts(jnp.full((8, META), scalar_ref[0], jnp.float32)):
             about = jnp.where(lane == place, part, about)
             place += 1
     out_ref[:, 2 * npix :] = jnp.broadcast_to(about[:1], (npix, META)).astype(jnp.bfloat16)
-    saves = []
-
-    def save(start, size):
-        at = pl.ds(start, size)
-        copy = pltpu.make_async_copy(out_ref.at[:, at], out_hbm.at[:, at], out_sems.at[len(saves)])
-        copy.start()
-        saves.append(copy)
-
     save(2 * npix, META)
-    for number, start in enumerate(starts):
-        loads[number].wait()
-        first = jnp.dot(
-            image_ref[...], table_ref[:, start : start + chunk], preferred_element_type=jnp.float32
-        ).astype(jnp.bfloat16)
-        if start < npix:
-            both_ref[:npix, start : start + chunk] = first
-            both_ref[npix:, npix + start : npix + start + chunk] = -first
-        else:
-            both_ref[:npix, start : start + chunk] = -first
-            both_ref[npix:, start - npix : start - npix + chunk] = -first
     for start in starts:
         out_ref[:, start : start + chunk] = jnp.dot(
             table_ref[...], both_ref[:, start : start + chunk], preferred_element_type=jnp.float32
@@ -147,21 +153,25 @@
 
 def transform(orient, defocus, noise, image, table):
     npix = image.shape[0]
-    chunk = 256
+    chunk = npix
     pieces = 2 * npix // chunk
     return pl.pallas_call(
         functools.partial(transform_kernel, chunk),
-        in_specs=[scalar(), scalar(), scalar(), whole(), pl.BlockSpec(memory_space=pl.ANY)],
+        in_specs=[pl.BlockSpec(memory_space=pl.ANY)] * 5,
         out_specs=pl.BlockSpec(memory_space=pl.ANY),
         out_shape=jax.ShapeDtypeStruct((npix, 2 * npix + META), jnp.bfloat16),
         scratch_shapes=[
+            pltpu.SMEM(orient.shape, jnp.int32),
+            pltpu.SMEM(defocus.shape, jnp.float32),
+            pltpu.SMEM(noise.shape, jnp.float32),
+            pltpu.VMEM((npix, npix), jnp.bfloat16),
             pltpu.VMEM((npix, 2 * npix), jnp.bfloat16),
             pltpu.VMEM((2 * npix, 2 * npix), jnp.bfloat16),
             pltpu.VMEM((npix, 2 * npix + META), jnp.bfloat16),
-            pltpu.SemaphoreType.DMA((pieces,)),
+            pltpu.SemaphoreType.DMA((pieces + 4,)),
             pltpu.SemaphoreType.DMA((pieces + 1,)),
         ],
-        compiler_params=params(LARGE),
+        compiler_params=params(HUGE),
         cost_estimate=cost(12 * npix**3, 10 * npix * npix),
         name="transform",
     )(orient, defocus, noise, image, table)
@@ -389,30 +399,42 @@
     )(core, part, noise, picks, filtered, square)
 
 
-def middle_kernel(keep_ref, got_ref, out_ref):
-    out_ref[...] = (keep_ref[...].astype(jnp.float32) + got_ref[...].astype(jnp.float32)).astype(jnp.bfloat16)
-
-
-def middle(keep, got):
+def middle_kernel(high_ref, keep_ref, got_ref, own_ref, *send_refs):
+    pairs = keep_ref.shape[0]
+    for ahead in range(pairs):
+        at = (high_ref[0] + ahead) % pairs
+        total = keep_ref[at].astype(jnp.float32) + got_ref[at].astype(jnp.float32)
+        if ahead == 0:
+            own_ref[...] = total
+        else:
+            send_refs[ahead - 1][...] = total.astype(jnp.bfloat16)
+
+
+def middle(high, keep, got):
+    pairs, slab, wide = keep.shape
     return pl.pallas_call(
         middle_kernel,
-        out_shape=jax.ShapeDtypeStruct(keep.shape, jnp.bfloat16),
+        in_specs=[scalar(), whole(), whole()],
+        out_specs=(whole(),) * pairs,
+        out_shape=(jax.ShapeDtypeStruct((slab, wide), jnp.float32),)
+        + (jax.ShapeDtypeStruct((slab, wide), jnp.bfloat16),) * (pairs - 1),
         compiler_params=params(SMALL),
         cost_estimate=cost(1 << 20, 2 << 20),
         name="middle",
-    )(keep, got)
-
-
-def finish_kernel(parts_ref, data_ref, weight_ref, data_out, weight_out):
+    )(high, keep, got)
+
+
+def finish_kernel(own_ref, *refs):
+    data_ref, weight_ref, data_out, weight_out = refs[-4:]
     wide = data_ref.shape[1]
-    total = parts_ref[0].astype(jnp.float32)
-    for source in range(1, parts_ref.shape[0]):
-        total = total + parts_ref[source].astype(jnp.float32)
+    total = own_ref[...]
+    for part_ref in refs[:-4]:
+        total = total + part_ref[...].astype(jnp.float32)
     data_out[...] = data_ref[...] + total[:, :wide]
     weight_out[...] = weight_ref[...] + total[:, wide:]
 
 
-def finish(parts, data_old, weight_old):
+def finish(own, parts, data_old, weight_old):
     return pl.pallas_call(
         finish_kernel,
         out_shape=(
@@ -422,7 +444,7 @@
         compiler_params=params(SMALL),
         cost_estimate=cost(1 << 20, 2 << 20),
         name="finish",
-    )(parts, data_old, weight_old)
+    )(own, *parts, data_old, weight_old)
 
 
 def on_device(images, defocus, noise, orient, planes, weights, volume, data_old, weight_old):
@@ -438,9 +460,7 @@
     slot = lax.axis_index("img").astype(jnp.int32).reshape(1)
     place = lax.axis_index("vol").astype(jnp.int32)
 
-    fourier = transform(
-        orient, defocus.reshape(1, 1), noise.reshape(1, 1), images[0], jnp.asarray(dft_table(npix))
-    )
+    fourier = transform(orient, defocus, noise, images[0], jnp.asarray(dft_table(npix)))
     fourier = lax.all_to_all(
         fourier.reshape(n_img, rows, 2 * npix + META), "img", split_axis=0, concat_axis=0, tiled=True
     ).reshape(many, 2 * npix + META)
@@ -458,15 +478,13 @@
         probs[:2].reshape(2 * 2, n_img), lax.axis_index("img"), 1, 1
     ).reshape(1, ori)
     got = lax.ppermute(send, "vol", [(v, v ^ 1) for v in range(n_vol)])
-    parts = lax.all_to_all(
-        middle(keep, got),
-        "vol",
-        split_axis=0,
-        concat_axis=0,
-        axis_index_groups=[list(range(core, n_vol, 2)) for core in range(2)],
-        tiled=True,
-    )
+    own, *sends = middle((place // 2).reshape(1), keep, got)
+    parts = [
+        lax.ppermute(part, "vol", [(v, (v + 2 * ahead) % n_vol) for v in range(n_vol)])
+        for ahead, part in enumerate(sends, 1)
+    ]
     data, weight = finish(
+        own,
         parts,
         data_old.reshape(slab * rows, 2 * npix),
         weight_old.reshape(slab * rows, npix),

time: 104 us -> 100 us (0.962); the launches traced: 101 us -> 99.9 us
  starting transfers between devices: 32.1 us -> 40 us
  waiting for transfers between devices: 24.3 us -> 18.6 us
  local copies, waits for them, and re-layouts: 3.7 us -> 0.79 us
    ppermute x0 -> x3, starting transfers between devices: none -> 13.9 us  [on_device(): lax.ppermute(part, 'vol', [(v, (v + 2 * ahead) % n_vol) for v in range(n_...]
    all_to_all x1 -> x0, waiting for transfers between devices: 10.4 us -> none  [on_device(): lax.all_to_all(middle(keep, got), 'vol', split_axis=0, concat_axis=0, axi...]
    all_to_all x1 -> x0, starting transfers between devices: 5.92 us -> none  [on_device(): lax.all_to_all(middle(keep, got), 'vol', split_axis=0, concat_axis=0, axi...]
    ppermute x0 -> x3, waiting for transfers between devices: none -> 4.85 us  [on_device(): lax.ppermute(part, 'vol', [(v, (v + 2 * ahead) % n_vol) for v in range(n_...]
    unnamed x17 -> x11, local copies, waits for them, and re-layouts: 3.54 us -> 0.63 us
  transfers between devices with their start and end apart: 4 -> 6, of which waited for: 4 -> 5; matrix products, arithmetic and copies ran while one was open for 1% -> 1% of each run, Pallas kernels for 1% -> 1%
where the time goes in v4:
time: 100 us; the launch traced here: 99.9 us
  starting transfers between devices  40 us (40%)
  blocking collectives  26.5 us (26%)
  waiting for transfers between devices  18.6 us (19%)
  Pallas kernels  11.9 us (12%)
  between operations  2.1 us (2%)
    all_gather x1, blocking collectives, on_device(): lax.all_gather(volume.reshape(slab * rows, 2 * npix), 'vol', axis=0, tile...  26.5 us
    all_to_all x1, starting transfers between devices, on_device(): lax.all_to_all(fourier.reshape(n_img, rows, 2 * npix + META), 'img', spli...  15.5 us
    ppermute x3, starting transfers between devices, on_device(): lax.ppermute(part, 'vol', [(v, (v + 2 * ahead) % n_vol) for v in range(n_...  13.9 us
    all_to_all x1, waiting for transfers between devices, on_device(): lax.all_to_all(part.reshape(n_img, 2, 2 * n_img), 'img', split_axis=0, co...  8.06 us
    all_to_all x1, starting transfers between devices, on_device(): lax.all_to_all(part.reshape(n_img, 2, 2 * n_img), 'img', split_axis=0, co...  6.77 us
    ppermute x3, waiting for transfers between devices, on_device(): lax.ppermute(part, 'vol', [(v, (v + 2 * ahead) % n_vol) for v in range(n_...  4.85 us
    all_to_all x1, waiting for transfers between devices, on_device(): lax.all_to_all(fourier.reshape(n_img, rows, 2 * npix + META), 'img', spli...  4.48 us
    pallas_call x1, Pallas kernels, compare(): pl.pallas_call(functools.partial(compare_kernel, ori, rows), in_specs=[sc...  4.31 us
  transfers between devices with their start and end apart: 6, of which 5 were waited for; matrix products, arithmetic and copies ran while one was open for 1% of the time, Pallas kernels for 1%

profile of v4, /device:TPU:1, one launch (start us, length us, event | category | flops | bytes accessed | tf_op | source)
XLA Modules:
  0.0 99.9 jit_solution(15441564623459099648)
XLA Ops:
  1.9 4.3 %transform.1 = bf16[512,1152]{1,0:T(8,128)(2,1)} custom-call(s32[1,4]{1,0:T(1,128)} %orient_hbm.1, f32[1]{0:T(128)S(6)} %copy.15.defocus_hbm, f32[1]{0:T(128)S(6)} %copy.16.noise_hbm, bf16[512,512]{1,0:T(8,128)(2,1)} %bitcast.25, bf16[512,1024]{1,0:T(8,128)(2,1)} %constant.38.clone.table_hbm), custom_call_target="tpu_custom_call" | custom-call | flops 1610612736 | bytes 2621440 | tf_op jit(solution)/shard_map/transform/pallas_call | solution.py:158
  6.2 0.0 copy-start.2
  6.2 0.0 copy-start.3
  6.2 0.0 copy-start.4
  6.2 15.5 %all-to-all-start = ((bf16[64,8,1152]{2,1,0:T(8,128)(2,1)}), bf16[64,8,1152]{2,1,0:T(8,128)(2,1)S(1)}, u32[]{:S(2)}, u32[]{:S(2)}) async-start(bf16[64,8,1152]{2,1,0:T(8,128)(2,1)} %bitcast.22), calls=%async_computation | async-start | bytes 2359296 | tf_op jit(solution)/shard_map/all_to_all | solution.py:464
  21.7 0.0 copy-done.2
  21.8 0.0 copy-done.3
  21.8 0.1 prepare.1.lookup_ref
  21.9 0.0 copy-done.4
  21.9 26.5 %all_gather.3.volume_ref = bf16[256,1024]{1,0:T(8,128)(2,1)S(1)} all-gather(bf16[32,1024]{1,0:T(8,128)(2,1)S(1)} %bitcast.23), channel_id=1, replica_groups=mesh['img'=64,'vol'=8] {'vol'}, dimensions={0}, use_global_device_ids=true | all-gather | bytes 589824 | tf_op jit(solution)/shard_map/all_gather | solution.py:467
  48.4 4.5 %all-to-all-done = bf16[64,8,1152]{2,1,0:T(8,128)(2,1)S(1)} async-done(((bf16[64,8,1152]{2,1,0:T(8,128)(2,1)}), bf16[64,8,1152]{2,1,0:T(8,128)(2,1)S(1)}, u32[]{:S(2)}, u32[]{:S(2)}) %all-to-all-start) | async-done | bytes 1179680 | tf_op jit(solution)/shard_map/all_to_all | solution.py:464
  52.9 4.3 %compare.4 = (bf16[512,1024]{1,0:T(8,128)(2,1)S(1)}, bf16[256,256]{1,0:T(8,128)(2,1)S(1)}, f32[128,128]{1,0:T(8,128)}, f32[64,128]{1,0:T(8,128)S(1)}) custom-call(s32[1]{0:T(128)} %bitcast.1.slot_ref, bf16[512,1152]{1,0:T(8,128)(2,1)S(1)} %bitcast.16, bf16[256,768]{1,0:T(8,128)(2,1)S(1)} %prepare.1.lookup_ref, bf16[256,1024]{1,0:T(8,128)(2,1)S(1)} %all_gather.3.volume_ref), custom_call_target="tpu_custom_call" | custom-call | flops 2147483648 | bytes 5242880 | tf_op jit(solution)/shard_map/compare/pallas_call | solution.py:296
  57.2 6.8 %all-to-all-start.1 = ((f32[64,2,128]{2,1,0:T(2,128)}), f32[64,2,128]{2,1,0:T(2,128)S(1)}, u32[]{:S(2)}, u32[]{:S(2)}) async-start(f32[64,2,128]{2,1,0:T(2,128)} %bitcast.8), calls=%async_computation.1 | async-start | bytes 131072 | tf_op jit(solution)/shard_map/all_to_all | solution.py:471
  64.0 1.3 %squares.1 = (bf16[512,512]{1,0:T(8,128)(2,1)S(1)}, f32[1,128]{1,0:T(1,128)S(1)}) custom-call(s32[1]{0:T(128)} %bitcast.1.slot_ref, f32[64,128]{1,0:T(8,128)S(1)} %get-tuple-element.19.about_ref), custom_call_target="tpu_custom_call" | custom-call | flops 134217728 | bytes 1048576 | tf_op jit(solution)/shard_map/squares/pallas_call | solution.py:337
  65.3 8.1 %all-to-all-done.1 = f32[64,2,128]{2,1,0:T(2,128)S(1)} async-done(((f32[64,2,128]{2,1,0:T(2,128)}), f32[64,2,128]{2,1,0:T(2,128)S(1)}, u32[]{:S(2)}, u32[]{:S(2)}) %all-to-all-start.1) | async-done | bytes 65568 | tf_op jit(solution)/shard_map/all_to_all | solution.py:471
  73.3 0.0 copy-start
  73.3 0.0 copy-start.1
  73.3 1.1 %project.1 = (f32[8,128]{1,0:T(8,128)S(1)}, bf16[4,32,1536]{2,1,0:T(8,128)(2,1)S(1)}, bf16[4,32,1536]{2,1,0:T(8,128)(2,1)S(1)}) custom-call(s32[1]{0:T(128)} %bitcast.core_ref, f32[128,128]{1,0:T(8,128)S(1)} %bitcast.18, f32[1,128]{1,0:T(1,128)S(1)} %get-tuple-element.20.noise_ref, bf16[256,256]{1,0:T(8,128)(2,1)S(1)} %get-tuple-element.21.picks_ref, ...), custom_call_target="tpu_custom_call" | custom-call | flops 536870912 | bytes 4194304 | tf_op jit(solution)/shard_map/project/pallas_call | solution.py:391
  74.5 3.8 %collective-permute-start = (bf16[4,32,1536]{2,1,0:T(8,128)(2,1)S(1)}, bf16[4,32,1536]{2,1,0:T(8,128)(2,1)S(1)}, u32[]{:S(2)}, u32[]{:S(2)}) collective-permute-start(bf16[4,32,1536]{2,1,0:T(8,128)(2,1)S(1)} %get-tuple-element.26), channel_id=1, source_target_pairs={{0,1},{1,0},{2,3},{3,2},{4,5},{5,4},{6,7},{7,6},{8,9},{9,8},{10,11... | collective-permute-start | bytes 1179656 | tf_op jit(solution)/shard_map/ppermute | solution.py:480
  78.3 0.1 reshape.55
  78.4 1.2 %collective-permute-done.got_ref = bf16[4,32,1536]{2,1,0:T(8,128)(2,1)S(1)} collective-permute-done((bf16[4,32,1536]{2,1,0:T(8,128)(2,1)S(1)}, bf16[4,32,1536]{2,1,0:T(8,128)(2,1)S(1)}, u32[]{:S(2)}, u32[]{:S(2)}) %collective-permute-start) | collective-permute-done | bytes 393248 | tf_op jit(solution)/shard_map/ppermute | solution.py:480
  79.6 0.1 middle.1
  79.7 4.2 %collective-permute-start.1 = (bf16[32,1536]{1,0:T(8,128)(2,1)S(1)}, bf16[32,1536]{1,0:T(8,128)(2,1)S(1)}, u32[]{:S(2)}, u32[]{:S(2)}) collective-permute-start(bf16[32,1536]{1,0:T(8,128)(2,1)S(1)} %get-tuple-element.28), channel_id=1, source_target_pairs={{0,2},{1,3},{2,4},{3,5},{4,6},{5,7},{6,0},{7,1},{8,10},{9,11},{10,... | collective-permute-start | bytes 294920 | tf_op jit(solution)/shard_map/ppermute | solution.py:483
  83.9 4.8 %collective-permute-start.2 = (bf16[32,1536]{1,0:T(8,128)(2,1)S(1)}, bf16[32,1536]{1,0:T(8,128)(2,1)S(1)}, u32[]{:S(2)}, u32[]{:S(2)}) collective-permute-start(bf16[32,1536]{1,0:T(8,128)(2,1)S(1)} %get-tuple-element.29), channel_id=1, source_target_pairs={{0,4},{1,5},{2,6},{3,7},{4,0},{5,1},{6,2},{7,3},{8,12},{9,13},{10,... | collective-permute-start | bytes 294920 | tf_op jit(solution)/shard_map/ppermute | solution.py:483
  88.7 5.0 %collective-permute-start.3 = (bf16[32,1536]{1,0:T(8,128)(2,1)S(1)}, bf16[32,1536]{1,0:T(8,128)(2,1)S(1)}, u32[]{:S(2)}, u32[]{:S(2)}) collective-permute-start(bf16[32,1536]{1,0:T(8,128)(2,1)S(1)} %get-tuple-element.30), channel_id=1, source_target_pairs={{0,6},{1,7},{2,0},{3,1},{4,2},{5,3},{6,4},{7,5},{8,14},{9,15},{10,... | collective-permute-start | bytes 294920 | tf_op jit(solution)/shard_map/ppermute | solution.py:483
  93.7 0.1 constant_dynamic-slice_fusion
  93.8 0.6 copy.14
  94.4 0.0 collective-permute-done.1.refs_0_
  94.4 1.3 %collective-permute-done.2.refs_1_ = bf16[32,1536]{1,0:T(8,128)(2,1)S(1)} collective-permute-done((bf16[32,1536]{1,0:T(8,128)(2,1)S(1)}, bf16[32,1536]{1,0:T(8,128)(2,1)S(1)}, u32[]{:S(2)}, u32[]{:S(2)}) %collective-permute-start.2) | collective-permute-done | bytes 98336 | tf_op jit(solution)/shard_map/ppermute | solution.py:483
  95.6 3.6 %collective-permute-done.3.refs_2_ = bf16[32,1536]{1,0:T(8,128)(2,1)S(1)} collective-permute-done((bf16[32,1536]{1,0:T(8,128)(2,1)S(1)}, bf16[32,1536]{1,0:T(8,128)(2,1)S(1)}, u32[]{:S(2)}, u32[]{:S(2)}) %collective-permute-start.3) | collective-permute-done | bytes 98336 | tf_op jit(solution)/shard_map/ppermute | solution.py:483
  99.2 0.0 copy-done
  99.2 0.0 copy-done.1
  99.2 0.7 finish.1
  (1 shorter events, 0.0 us)
Async XLA Ops:
  6.2 15.5 %copy-start.2 = (s32[2,768,8]{1,2,0:T(8,128)S(1)}, s32[2,768,8]{1,2,0:T(8,128)}, u32[]{:S(2)}) copy-start(s32[2,768,8]{1,2,0:T(8,128)} %param.14) | copy-start | bytes 147460
  6.2 15.5 %copy-start.3 = (bf16[2,768,8]{1,2,0:T(8,128)(2,1)S(1)}, bf16[2,768,8]{1,2,0:T(8,128)(2,1)}, u32[]{:S(2)}) copy-start(bf16[2,768,8]{1,2,0:T(8,128)(2,1)} %param.15) | copy-start | bytes 73732
  6.2 15.7 %copy-start.4 = (bf16[4,8,1024]{2,1,0:T(8,128)(2,1)S(1)}, bf16[4,8,1024]{2,1,0:T(8,128)(2,1)}, u32[]{:S(2)}) copy-start(bf16[4,8,1024]{2,1,0:T(8,128)(2,1)} %param.16) | copy-start | bytes 196612
  6.2 46.6 %all-to-all-start = ((bf16[64,8,1152]{2,1,0:T(8,128)(2,1)}), bf16[64,8,1152]{2,1,0:T(8,128)(2,1)S(1)}, u32[]{:S(2)}, u32[]{:S(2)}) async-start(bf16[64,8,1152]{2,1,0:T(8,128)(2,1)} %bitcast.22), calls=%async_computation | async-start | bytes 2359296 | tf_op jit(solution)/shard_map/all_to_all | solution.py:464
  57.2 16.1 %all-to-all-start.1 = ((f32[64,2,128]{2,1,0:T(2,128)}), f32[64,2,128]{2,1,0:T(2,128)S(1)}, u32[]{:S(2)}, u32[]{:S(2)}) async-start(f32[64,2,128]{2,1,0:T(2,128)} %bitcast.8), calls=%async_computation.1 | async-start | bytes 131072 | tf_op jit(solution)/shard_map/all_to_all | solution.py:471
  73.3 25.9 %copy-start = (f32[4,8,1024]{2,1,0:T(8,128)S(1)}, f32[4,8,1024]{2,1,0:T(8,128)}, u32[]{:S(2)}) copy-start(f32[4,8,1024]{2,1,0:T(8,128)} %param.17) | copy-start | bytes 393220
  73.3 25.9 %copy-start.1 = (f32[4,8,512]{2,1,0:T(8,128)S(1)}, f32[4,8,512]{2,1,0:T(8,128)}, u32[]{:S(2)}) copy-start(f32[4,8,512]{2,1,0:T(8,128)} %param.18) | copy-start | bytes 196612
  74.5 5.2 %collective-permute-start = (bf16[4,32,1536]{2,1,0:T(8,128)(2,1)S(1)}, bf16[4,32,1536]{2,1,0:T(8,128)(2,1)S(1)}, u32[]{:S(2)}, u32[]{:S(2)}) collective-permute-start(bf16[4,32,1536]{2,1,0:T(8,128)(2,1)S(1)} %get-tuple-element.26), channel_id=1, source_target_pairs={{0,1},{1,0},{2,3},{3,2},{4,5},{5,4},{6,7},{7,6},{8,9},{9,8},{10,11... | collective-permute-start | bytes 1179656 | tf_op jit(solution)/shard_map/ppermute | solution.py:480
  79.7 14.6 %collective-permute-start.1 = (bf16[32,1536]{1,0:T(8,128)(2,1)S(1)}, bf16[32,1536]{1,0:T(8,128)(2,1)S(1)}, u32[]{:S(2)}, u32[]{:S(2)}) collective-permute-start(bf16[32,1536]{1,0:T(8,128)(2,1)S(1)} %get-tuple-element.28), channel_id=1, source_target_pairs={{0,2},{1,3},{2,4},{3,5},{4,6},{5,7},{6,0},{7,1},{8,10},{9,11},{10,... | collective-permute-start | bytes 294920 | tf_op jit(solution)/shard_map/ppermute | solution.py:483
  83.9 11.7 %collective-permute-start.2 = (bf16[32,1536]{1,0:T(8,128)(2,1)S(1)}, bf16[32,1536]{1,0:T(8,128)(2,1)S(1)}, u32[]{:S(2)}, u32[]{:S(2)}) collective-permute-start(bf16[32,1536]{1,0:T(8,128)(2,1)S(1)} %get-tuple-element.29), channel_id=1, source_target_pairs={{0,4},{1,5},{2,6},{3,7},{4,0},{5,1},{6,2},{7,3},{8,12},{9,13},{10,... | collective-permute-start | bytes 294920 | tf_op jit(solution)/shard_map/ppermute | solution.py:483
  88.7 10.5 %collective-permute-start.3 = (bf16[32,1536]{1,0:T(8,128)(2,1)S(1)}, bf16[32,1536]{1,0:T(8,128)(2,1)S(1)}, u32[]{:S(2)}, u32[]{:S(2)}) collective-permute-start(bf16[32,1536]{1,0:T(8,128)(2,1)S(1)} %get-tuple-element.30), channel_id=1, source_target_pairs={{0,6},{1,7},{2,0},{3,1},{4,2},{5,3},{6,4},{7,5},{8,14},{9,15},{10,... | collective-permute-start | bytes 294920 | tf_op jit(solution)/shard_map/ppermute | solution.py:483

commit v5 on v4

--- a/solution.py
+++ b/solution.py
@@ -35,12 +35,16 @@
 META = 128
 
 
-def dft_table(npix):
+def dft_tables(npix):
     index = np.arange(npix)
     angle = (index[:, None] * index[None, :] % npix) * (2.0 * math.pi / npix)
     scale = 1.0 / math.sqrt(npix)
-    both = np.concatenate([np.cos(angle) * scale, np.sin(angle) * scale], 1)
-    return both.astype(np.float32).astype(ml_dtypes.bfloat16)
+    parts = [np.cos(angle) * scale, np.sin(angle) * scale]
+    halves = [part[: npix // 2, parity::2] for parity in range(2) for part in parts]
+    return tuple(
+        jnp.asarray(np.concatenate(table, 1).astype(np.float32).astype(ml_dtypes.bfloat16))
+        for table in (parts, halves)
+    )
 
 
 def frequency(index, npix):
@@ -94,30 +98,45 @@
     return jnp.where((sublane == lane)[None], values.reshape(height // rows, rows, width), 0.0)
 
 
-def transform_kernel(chunk, orient_hbm, defocus_hbm, noise_hbm, image_hbm, table_hbm, out_hbm, orient_ref, defocus_ref, noise_ref, image_ref, table_ref, both_ref, out_ref, in_sems, out_sems):
+def transform_kernel(chunk, orient_hbm, defocus_hbm, noise_hbm, image_hbm, table_hbm, halves_hbm, out_hbm, orient_ref, defocus_ref, noise_ref, image_ref, wide_ref, table_ref, halves_ref, both_ref, out_ref, in_sems, out_sems):
     npix = image_ref.shape[0]
+    half = npix // 2
     ori = orient_ref.shape[1]
     starts = list(range(0, 2 * npix, chunk))
     pairs = [(image_hbm, image_ref)]
     pairs += [(table_hbm.at[:, pl.ds(start, chunk)], table_ref.at[:, pl.ds(start, chunk)]) for start in starts]
-    pairs += [(orient_hbm, orient_ref), (defocus_hbm, defocus_ref), (noise_hbm, noise_ref)]
+    pairs += [(halves_hbm, halves_ref), (orient_hbm, orient_ref), (defocus_hbm, defocus_ref), (noise_hbm, noise_ref)]
     loads = []
     for number, (source, target) in enumerate(pairs):
         load = pltpu.make_async_copy(source, target, in_sems.at[number])
         load.start()
         loads.append(load)
     loads[0].wait()
+    tiles = range(npix // 128)
+    for tile in tiles:
+        wide_ref[tile] = image_ref[:, tile * 128 : (tile + 1) * 128].astype(jnp.float32)
+    image = jnp.concatenate(
+        [
+            jnp.concatenate([wide_ref[tile, pl.ds(parity, half, 2), :] for tile in tiles], 1)
+            for parity in range(2)
+        ],
+        0,
+    ).astype(jnp.bfloat16)
     for number, start in enumerate(starts):
         loads[1 + number].wait()
         first = jnp.dot(
-            image_ref[...], table_ref[:, start : start + chunk], preferred_element_type=jnp.float32
+            image, table_ref[:, start : start + chunk], preferred_element_type=jnp.float32
         ).astype(jnp.bfloat16)
-        if start < npix:
-            both_ref[:npix, start : start + chunk] = first
-            both_ref[npix:, npix + start : npix + start + chunk] = -first
-        else:
-            both_ref[:npix, start : start + chunk] = -first
-            both_ref[npix:, start - npix : start - npix + chunk] = -first
+        for parity in range(2):
+            part = first[parity * half : (parity + 1) * half]
+            upper = slice(parity * npix, parity * npix + half)
+            lower = slice(parity * npix + half, (parity + 1) * npix)
+            if start < npix:
+                both_ref[upper, start : start + chunk] = part
+                both_ref[lower, npix + start : npix + start + chunk] = -part
+            else:
+                both_ref[upper, start : start + chunk] = -part
+                both_ref[lower, start - npix : start - npix + chunk] = -part
     for load in loads[1 + len(starts) :]:
         load.wait()
     saves = []
@@ -143,21 +162,28 @@
     out_ref[:, 2 * npix :] = jnp.broadcast_to(about[:1], (npix, META)).astype(jnp.bfloat16)
     save(2 * npix, META)
     for start in starts:
-        out_ref[:, start : start + chunk] = jnp.dot(
-            table_ref[...], both_ref[:, start : start + chunk], preferred_element_type=jnp.float32
-        ).astype(jnp.bfloat16)
+        even, odd = (
+            jnp.dot(
+                halves_ref[:, parity * npix : (parity + 1) * npix],
+                both_ref[parity * npix : (parity + 1) * npix, start : start + chunk],
+                preferred_element_type=jnp.float32,
+            )
+            for parity in range(2)
+        )
+        out_ref[:half, start : start + chunk] = (even + odd).astype(jnp.bfloat16)
+        out_ref[half:, start : start + chunk] = (even - odd).astype(jnp.bfloat16)
         save(start, chunk)
     for copy in saves:
         copy.wait()
 
 
-def transform(orient, defocus, noise, image, table):
+def transform(orient, defocus, noise, image, table, halves):
     npix = image.shape[0]
     chunk = npix
     pieces = 2 * npix // chunk
     return pl.pallas_call(
         functools.partial(transform_kernel, chunk),
-        in_specs=[pl.BlockSpec(memory_space=pl.ANY)] * 5,
+        in_specs=[pl.BlockSpec(memory_space=pl.ANY)] * 6,
         out_specs=pl.BlockSpec(memory_space=pl.ANY),
         out_shape=jax.ShapeDtypeStruct((npix, 2 * npix + META), jnp.bfloat16),
         scratch_shapes=[
@@ -165,16 +191,18 @@
             pltpu.SMEM(defocus.shape, jnp.float32),
             pltpu.SMEM(noise.shape, jnp.float32),
             pltpu.VMEM((npix, npix), jnp.bfloat16),
+            pltpu.VMEM((npix // 128, npix, 128), jnp.float32),
             pltpu.VMEM((npix, 2 * npix), jnp.bfloat16),
+            pltpu.VMEM((npix // 2, 2 * npix), jnp.bfloat16),
             pltpu.VMEM((2 * npix, 2 * npix), jnp.bfloat16),
             pltpu.VMEM((npix, 2 * npix + META), jnp.bfloat16),
-            pltpu.SemaphoreType.DMA((pieces + 4,)),
+            pltpu.SemaphoreType.DMA((pieces + 5,)),
             pltpu.SemaphoreType.DMA((pieces + 1,)),
         ],
         compiler_params=params(HUGE),
         cost_estimate=cost(12 * npix**3, 10 * npix * npix),
         name="transform",
-    )(orient, defocus, noise, image, table)
+    )(orient, defocus, noise, image, table, halves)
 
 
 def prepare_kernel(planes_ref, weights_ref, lookup_ref):
@@ -314,8 +342,8 @@
     )(slot, fourier, lookup, volume)
 
 
-def squares_kernel(ori, rows, slot_ref, about_ref, square_ref, noise_ref):
-    many, npix = square_ref.shape
+def squares_kernel(ori, rows, npix, slot_ref, about_ref, square_ref, noise_ref):
+    many = square_ref.shape[0]
     images = many // rows
     about = about_ref[...]
     meta = jnp.dot(
@@ -324,7 +352,7 @@
         preferred_element_type=jnp.float32,
     )
     defocus, row_square = line_geometry(meta, ori, rows, many, npix, slot_ref[0])
-    for start in range(0, npix, 128):
+    for start in range(0, square_ref.shape[1], 128):
         ctf = contrast(defocus, row_square, start, 128, npix)
         square_ref[:, start : start + 128] = (ctf * ctf).astype(jnp.bfloat16)
     place = 2 * ori + 3
@@ -335,11 +363,11 @@
 def squares(slot, about, ori, rows, npix):
     images = about.shape[0]
     return pl.pallas_call(
-        functools.partial(squares_kernel, ori, rows),
+        functools.partial(squares_kernel, ori, rows, npix),
         in_specs=[scalar(), whole()],
         out_specs=(whole(), whole()),
         out_shape=(
-            jax.ShapeDtypeStruct((images * rows, npix), jnp.bfloat16),
+            jax.ShapeDtypeStruct((images * rows, npix // 2 + 128), jnp.bfloat16),
             jax.ShapeDtypeStruct((1, 2 * images), jnp.float32),
         ),
         compiler_params=params(SMALL),
@@ -377,17 +405,32 @@
     )
     share = own_row(share, rows).reshape(deep, many).astype(jnp.bfloat16)
     first = core_ref[0] == 0
-    for source_ref, start, size in ((filtered_ref, 0, wide), (square_ref, wide, wide // 2)):
+    pairs = keep_ref.shape[0]
+    slab = deep // (2 * pairs)
+    tiles = (wide + square_ref.shape[1]) // 128 - 1
+    for source_ref, start in ((filtered_ref, 0), (square_ref, wide // 128)):
         sums = jnp.dot(share, source_ref[...], preferred_element_type=jnp.float32)
-        sums = sums.reshape(keep_ref.shape[0], 2, keep_ref.shape[1], size)
-        keep_ref[:, :, start : start + size] = jnp.where(first, sums[:, 0], sums[:, 1]).astype(jnp.bfloat16)
-        send_ref[:, :, start : start + size] = jnp.where(first, sums[:, 1], sums[:, 0]).astype(jnp.bfloat16)
+        for number in range(sums.shape[1] // 128):
+            tile = sums[:, number * 128 : (number + 1) * 128].reshape(pairs, 2, slab, 128)
+            ours, theirs = tile[:, 0], tile[:, 1]
+            ours, theirs = jnp.where(first, ours, theirs), jnp.where(first, theirs, ours)
+            at = (start + number) * slab
+            for target_ref, value in ((keep_ref, ours), (send_ref, theirs)):
+                if start + number < tiles:
+                    target_ref[:, at : at + slab, :] = value.astype(jnp.bfloat16)
+                else:
+                    lane = lax.broadcasted_iota(jnp.int32, (pairs, slab // 2, 128), 2)
+                    lower = jnp.broadcast_to(value[:, slab // 2 :, :1], lane.shape)
+                    value = jnp.where(lane == 0, value[:, : slab // 2], lower)
+                    target_ref[:, at : at + slab // 2, :] = value.astype(jnp.bfloat16)
 
 
 def project(core, part, noise, picks, filtered, square, rows, ori, pairs):
     many, wide = filtered.shape
     deep = picks.shape[1]
-    half = jax.ShapeDtypeStruct((pairs, deep // (2 * pairs), wide + wide // 2), jnp.bfloat16)
+    slab = deep // (2 * pairs)
+    lines = (wide + square.shape[1]) // 128 * slab - slab // 2
+    half = jax.ShapeDtypeStruct((pairs, lines, 128), jnp.bfloat16)
     return pl.pallas_call(
         functools.partial(project_kernel, rows, ori),
         in_specs=[scalar()] + [whole()] * 5,
@@ -426,12 +469,32 @@
 
 def finish_kernel(own_ref, *refs):
     data_ref, weight_ref, data_out, weight_out = refs[-4:]
-    wide = data_ref.shape[1]
+    slab, npix = weight_ref.shape
+    half = npix // 2
     total = own_ref[...]
     for part_ref in refs[:-4]:
         total = total + part_ref[...].astype(jnp.float32)
-    data_out[...] = data_ref[...] + total[:, :wide]
-    weight_out[...] = weight_ref[...] + total[:, wide:]
+    for start in range(0, 2 * npix, 128):
+        at = start // 128 * slab
+        data_out[:, start : start + 128] = data_ref[:, start : start + 128] + total[at : at + slab]
+    lower = []
+    for start in range(0, half, 128):
+        at = (2 * npix + start) // 128 * slab
+        lower.append(total[at : at + slab])
+    lower = jnp.concatenate(lower, 1)
+    weight_out[:, :half] = weight_ref[:, :half] + lower
+    source = lax.broadcasted_iota(jnp.int32, (half, half), 0)
+    target = lax.broadcasted_iota(jnp.int32, (half, half), 1)
+    upper = jnp.dot(
+        lower,
+        jnp.where(source + target == half, 1.0, 0.0),
+        preferred_element_type=jnp.float32,
+        precision=lax.Precision.HIGHEST,
+    )
+    last = total[total.shape[0] - slab // 2 :]
+    last = jnp.concatenate([last[:, :1], last[:, 1:2]], 0)
+    lane = lax.broadcasted_iota(jnp.int32, (slab, half), 1)
+    weight_out[:, half:] = weight_ref[:, half:] + jnp.where(lane == 0, last, upper)
 
 
 def finish(own, parts, data_old, weight_old):
@@ -460,7 +523,7 @@
     slot = lax.axis_index("img").astype(jnp.int32).reshape(1)
     place = lax.axis_index("vol").astype(jnp.int32)
 
-    fourier = transform(orient, defocus, noise, images[0], jnp.asarray(dft_table(npix)))
+    fourier = transform(orient, defocus, noise, images[0], *dft_tables(npix))
     fourier = lax.all_to_all(
         fourier.reshape(n_img, rows, 2 * npix + META), "img", split_axis=0, concat_axis=0, tiled=True
     ).reshape(many, 2 * npix + META)

time: 100 us -> 99.2 us (level)
  no operation moved by 1% of the time
where the time goes in v5:
time: 99.2 us; the launch traced here: 98.8 us
  starting transfers between devices  40 us (40%)
  blocking collectives  26.5 us (27%)
  waiting for transfers between devices  18 us (18%)
  Pallas kernels  11.4 us (11%)
  between operations  2.09 us (2%)
    all_gather x1, blocking collectives, on_device(): lax.all_gather(volume.reshape(slab * rows, 2 * npix), 'vol', axis=0, tile...  26.5 us
    all_to_all x1, starting transfers between devices, on_device(): lax.all_to_all(fourier.reshape(n_img, rows, 2 * npix + META), 'img', spli...  15.5 us
    ppermute x3, starting transfers between devices, on_device(): lax.ppermute(part, 'vol', [(v, (v + 2 * ahead) % n_vol) for v in range(n_...  13.9 us
    all_to_all x1, waiting for transfers between devices, on_device(): lax.all_to_all(part.reshape(n_img, 2, 2 * n_img), 'img', split_axis=0, co...  8.28 us
    all_to_all x1, starting transfers between devices, on_device(): lax.all_to_all(part.reshape(n_img, 2, 2 * n_img), 'img', split_axis=0, co...  6.77 us
    all_to_all x1, waiting for transfers between devices, on_device(): lax.all_to_all(fourier.reshape(n_img, rows, 2 * npix + META), 'img', spli...  4.49 us
    pallas_call x1, Pallas kernels, compare(): pl.pallas_call(functools.partial(compare_kernel, ori, rows), in_specs=[sc...  4.31 us
    ppermute x3, waiting for transfers between devices, on_device(): lax.ppermute(part, 'vol', [(v, (v + 2 * ahead) % n_vol) for v in range(n_...  4.11 us
  transfers between devices with their start and end apart: 6, of which 5 were waited for; matrix products, arithmetic and copies ran while one was open for 1% of the time, Pallas kernels for 1%

profile of v5, /device:TPU:1, one launch (start us, length us, event | category | flops | bytes accessed | tf_op | source)
XLA Modules:
  0.0 98.8 jit_solution(1881064497060247488)
XLA Ops:
  1.9 3.8 %transform.1 = bf16[512,1152]{1,0:T(8,128)(2,1)} custom-call(s32[1,4]{1,0:T(1,128)} %orient_hbm.1, f32[1]{0:T(128)S(6)} %copy.16.defocus_hbm, f32[1]{0:T(128)S(6)} %copy.17.noise_hbm, bf16[512,512]{1,0:T(8,128)(2,1)} %bitcast.25, bf16[512,1024]{1,0:T(8,128)(2,1)} %constant.40.clone.table_hbm, bf16[256,1024]{1,0:T(8,128)(2,1)} %constant.41.clone.halves_hbm), custom_call_target="tpu_custom_call" | custom-call | flops 1610612736 | bytes 2621440 | tf_op jit(solution)/shard_map/transform/pallas_call | solution.py:184
  5.7 0.0 copy-start.2
  5.7 0.0 copy-start.3
  5.7 0.0 copy-start.4
  5.7 15.5 %all-to-all-start = ((bf16[64,8,1152]{2,1,0:T(8,128)(2,1)}), bf16[64,8,1152]{2,1,0:T(8,128)(2,1)S(1)}, u32[]{:S(2)}, u32[]{:S(2)}) async-start(bf16[64,8,1152]{2,1,0:T(8,128)(2,1)} %bitcast.22), calls=%async_computation | async-start | bytes 2359296 | tf_op jit(solution)/shard_map/all_to_all | solution.py:527
  21.2 0.0 copy-done.2
  21.2 0.0 copy-done.3
  21.2 0.1 prepare.1.lookup_ref
  21.4 0.0 copy-done.4
  21.4 26.5 %all_gather.3.volume_ref = bf16[256,1024]{1,0:T(8,128)(2,1)S(1)} all-gather(bf16[32,1024]{1,0:T(8,128)(2,1)S(1)} %bitcast.23), channel_id=1, replica_groups=mesh['img'=64,'vol'=8] {'vol'}, dimensions={0}, use_global_device_ids=true | all-gather | bytes 589824 | tf_op jit(solution)/shard_map/all_gather | solution.py:530
  47.9 4.5 %all-to-all-done = bf16[64,8,1152]{2,1,0:T(8,128)(2,1)S(1)} async-done(((bf16[64,8,1152]{2,1,0:T(8,128)(2,1)}), bf16[64,8,1152]{2,1,0:T(8,128)(2,1)S(1)}, u32[]{:S(2)}, u32[]{:S(2)}) %all-to-all-start) | async-done | bytes 1179680 | tf_op jit(solution)/shard_map/all_to_all | solution.py:527
  52.4 4.3 %compare.4 = (bf16[512,1024]{1,0:T(8,128)(2,1)S(1)}, bf16[256,256]{1,0:T(8,128)(2,1)S(1)}, f32[128,128]{1,0:T(8,128)}, f32[64,128]{1,0:T(8,128)S(1)}) custom-call(s32[1]{0:T(128)} %bitcast.1.slot_ref, bf16[512,1152]{1,0:T(8,128)(2,1)S(1)} %bitcast.16, bf16[256,768]{1,0:T(8,128)(2,1)S(1)} %prepare.1.lookup_ref, bf16[256,1024]{1,0:T(8,128)(2,1)S(1)} %all_gather.3.volume_ref), custom_call_target="tpu_custom_call" | custom-call | flops 2147483648 | bytes 5242880 | tf_op jit(solution)/shard_map/compare/pallas_call | solution.py:324
  56.7 6.8 %all-to-all-start.1 = ((f32[64,2,128]{2,1,0:T(2,128)}), f32[64,2,128]{2,1,0:T(2,128)S(1)}, u32[]{:S(2)}, u32[]{:S(2)}) async-start(f32[64,2,128]{2,1,0:T(2,128)} %bitcast.8), calls=%async_computation.1 | async-start | bytes 131072 | tf_op jit(solution)/shard_map/all_to_all | solution.py:534
  63.5 1.1 %squares.1 = (bf16[512,384]{1,0:T(8,128)(2,1)S(1)}, f32[1,128]{1,0:T(1,128)S(1)}) custom-call(s32[1]{0:T(128)} %bitcast.1.slot_ref, f32[64,128]{1,0:T(8,128)S(1)} %get-tuple-element.19.about_ref), custom_call_target="tpu_custom_call" | custom-call | flops 134217728 | bytes 1048576 | tf_op jit(solution)/shard_map/squares/pallas_call | solution.py:365
  64.5 8.3 %all-to-all-done.1 = f32[64,2,128]{2,1,0:T(2,128)S(1)} async-done(((f32[64,2,128]{2,1,0:T(2,128)}), f32[64,2,128]{2,1,0:T(2,128)S(1)}, u32[]{:S(2)}, u32[]{:S(2)}) %all-to-all-start.1) | async-done | bytes 65568 | tf_op jit(solution)/shard_map/all_to_all | solution.py:534
  72.8 0.0 copy-start
  72.8 0.0 copy-start.1
  72.8 1.2 %project.1 = (f32[8,128]{1,0:T(8,128)S(1)}, bf16[4,336,128]{2,1,0:T(8,128)(2,1)S(1)}, bf16[4,336,128]{2,1,0:T(8,128)(2,1)S(1)}) custom-call(s32[1]{0:T(128)} %bitcast.core_ref, f32[128,128]{1,0:T(8,128)S(1)} %bitcast.19, f32[1,128]{1,0:T(1,128)S(1)} %get-tuple-element.20.noise_ref, bf16[256,256]{1,0:T(8,128)(2,1)S(1)} %get-tuple-element.21.picks_ref, ...), custom_call_target="tpu_custom_call" | custom-call | flops 536870912 | bytes 4194304 | tf_op jit(solution)/shard_map/project/pallas_call | solution.py:434
  74.0 3.8 %collective-permute-start = (bf16[4,336,128]{2,1,0:T(8,128)(2,1)S(1)}, bf16[4,336,128]{2,1,0:T(8,128)(2,1)S(1)}, u32[]{:S(2)}, u32[]{:S(2)}) collective-permute-start(bf16[4,336,128]{2,1,0:T(8,128)(2,1)S(1)} %get-tuple-element.26), channel_id=1, source_target_pairs={{0,1},{1,0},{2,3},{3,2},{4,5},{5,4},{6,7},{7,6},{8,9},{9,8},{10,11... | collective-permute-start | bytes 1032200 | tf_op jit(solution)/shard_map/ppermute | solution.py:543
  77.9 0.1 reshape.55
  77.9 1.1 %collective-permute-done.got_ref = bf16[4,336,128]{2,1,0:T(8,128)(2,1)S(1)} collective-permute-done((bf16[4,336,128]{2,1,0:T(8,128)(2,1)S(1)}, bf16[4,336,128]{2,1,0:T(8,128)(2,1)S(1)}, u32[]{:S(2)}, u32[]{:S(2)}) %collective-permute-start) | collective-permute-done | bytes 344096 | tf_op jit(solution)/shard_map/ppermute | solution.py:543
  79.1 0.1 middle.1
  79.2 4.2 %collective-permute-start.1 = (bf16[336,128]{1,0:T(8,128)(2,1)S(1)}, bf16[336,128]{1,0:T(8,128)(2,1)S(1)}, u32[]{:S(2)}, u32[]{:S(2)}) collective-permute-start(bf16[336,128]{1,0:T(8,128)(2,1)S(1)} %get-tuple-element.28), channel_id=1, source_target_pairs={{0,2},{1,3},{2,4},{3,5},{4,6},{5,7},{6,0},{7,1},{8,10},{9,11},{10,... | collective-permute-start | bytes 258056 | tf_op jit(solution)/shard_map/ppermute | solution.py:546
  83.4 4.7 %collective-permute-start.2 = (bf16[336,128]{1,0:T(8,128)(2,1)S(1)}, bf16[336,128]{1,0:T(8,128)(2,1)S(1)}, u32[]{:S(2)}, u32[]{:S(2)}) collective-permute-start(bf16[336,128]{1,0:T(8,128)(2,1)S(1)} %get-tuple-element.29), channel_id=1, source_target_pairs={{0,4},{1,5},{2,6},{3,7},{4,0},{5,1},{6,2},{7,3},{8,12},{9,13},{10,... | collective-permute-start | bytes 258056 | tf_op jit(solution)/shard_map/ppermute | solution.py:546
  88.2 5.0 %collective-permute-start.3 = (bf16[336,128]{1,0:T(8,128)(2,1)S(1)}, bf16[336,128]{1,0:T(8,128)(2,1)S(1)}, u32[]{:S(2)}, u32[]{:S(2)}) collective-permute-start(bf16[336,128]{1,0:T(8,128)(2,1)S(1)} %get-tuple-element.30), channel_id=1, source_target_pairs={{0,6},{1,7},{2,0},{3,1},{4,2},{5,3},{6,4},{7,5},{8,14},{9,15},{10,... | collective-permute-start | bytes 258056 | tf_op jit(solution)/shard_map/ppermute | solution.py:546
  93.1 0.1 constant_dynamic-slice_fusion
  93.2 0.6 copy.15
  93.8 0.0 collective-permute-done.1.refs_0_
  93.8 1.2 %collective-permute-done.2.refs_1_ = bf16[336,128]{1,0:T(8,128)(2,1)S(1)} collective-permute-done((bf16[336,128]{1,0:T(8,128)(2,1)S(1)}, bf16[336,128]{1,0:T(8,128)(2,1)S(1)}, u32[]{:S(2)}, u32[]{:S(2)}) %collective-permute-start.2) | collective-permute-done | bytes 86048 | tf_op jit(solution)/shard_map/ppermute | solution.py:546
  95.0 2.9 %collective-permute-done.3.refs_2_ = bf16[336,128]{1,0:T(8,128)(2,1)S(1)} collective-permute-done((bf16[336,128]{1,0:T(8,128)(2,1)S(1)}, bf16[336,128]{1,0:T(8,128)(2,1)S(1)}, u32[]{:S(2)}, u32[]{:S(2)}) %collective-permute-start.3) | collective-permute-done | bytes 86048 | tf_op jit(solution)/shard_map/ppermute | solution.py:546
  97.9 0.0 copy-done
  97.9 0.0 copy-done.1
  97.9 0.9 finish.1
  (1 shorter events, 0.0 us)
Async XLA Ops:
  5.7 15.5 %copy-start.2 = (s32[2,768,8]{1,2,0:T(8,128)S(1)}, s32[2,768,8]{1,2,0:T(8,128)}, u32[]{:S(2)}) copy-start(s32[2,768,8]{1,2,0:T(8,128)} %param.15) | copy-start | bytes 147460
  5.7 15.5 %copy-start.3 = (bf16[2,768,8]{1,2,0:T(8,128)(2,1)S(1)}, bf16[2,768,8]{1,2,0:T(8,128)(2,1)}, u32[]{:S(2)}) copy-start(bf16[2,768,8]{1,2,0:T(8,128)(2,1)} %param.16) | copy-start | bytes 73732
  5.7 15.7 %copy-start.4 = (bf16[4,8,1024]{2,1,0:T(8,128)(2,1)S(1)}, bf16[4,8,1024]{2,1,0:T(8,128)(2,1)}, u32[]{:S(2)}) copy-start(bf16[4,8,1024]{2,1,0:T(8,128)(2,1)} %param.17) | copy-start | bytes 196612
  5.7 46.6 %all-to-all-start = ((bf16[64,8,1152]{2,1,0:T(8,128)(2,1)}), bf16[64,8,1152]{2,1,0:T(8,128)(2,1)S(1)}, u32[]{:S(2)}, u32[]{:S(2)}) async-start(bf16[64,8,1152]{2,1,0:T(8,128)(2,1)} %bitcast.22), calls=%async_computation | async-start | bytes 2359296 | tf_op jit(solution)/shard_map/all_to_all | solution.py:527
  56.7 16.1 %all-to-all-start.1 = ((f32[64,2,128]{2,1,0:T(2,128)}), f32[64,2,128]{2,1,0:T(2,128)S(1)}, u32[]{:S(2)}, u32[]{:S(2)}) async-start(f32[64,2,128]{2,1,0:T(2,128)} %bitcast.8), calls=%async_computation.1 | async-start | bytes 131072 | tf_op jit(solution)/shard_map/all_to_all | solution.py:534
  72.8 25.1 %copy-start = (f32[4,8,1024]{2,1,0:T(8,128)S(1)}, f32[4,8,1024]{2,1,0:T(8,128)}, u32[]{:S(2)}) copy-start(f32[4,8,1024]{2,1,0:T(8,128)} %param.18) | copy-start | bytes 393220
  72.8 25.1 %copy-start.1 = (f32[4,8,512]{2,1,0:T(8,128)S(1)}, f32[4,8,512]{2,1,0:T(8,128)}, u32[]{:S(2)}) copy-start(f32[4,8,512]{2,1,0:T(8,128)} %param.19) | copy-start | bytes 196612
  74.0 5.1 %collective-permute-start = (bf16[4,336,128]{2,1,0:T(8,128)(2,1)S(1)}, bf16[4,336,128]{2,1,0:T(8,128)(2,1)S(1)}, u32[]{:S(2)}, u32[]{:S(2)}) collective-permute-start(bf16[4,336,128]{2,1,0:T(8,128)(2,1)S(1)} %get-tuple-element.26), channel_id=1, source_target_pairs={{0,1},{1,0},{2,3},{3,2},{4,5},{5,4},{6,7},{7,6},{8,9},{9,8},{10,11... | collective-permute-start | bytes 1032200 | tf_op jit(solution)/shard_map/ppermute | solution.py:543
  79.2 14.7 %collective-permute-start.1 = (bf16[336,128]{1,0:T(8,128)(2,1)S(1)}, bf16[336,128]{1,0:T(8,128)(2,1)S(1)}, u32[]{:S(2)}, u32[]{:S(2)}) collective-permute-start(bf16[336,128]{1,0:T(8,128)(2,1)S(1)} %get-tuple-element.28), channel_id=1, source_target_pairs={{0,2},{1,3},{2,4},{3,5},{4,6},{5,7},{6,0},{7,1},{8,10},{9,11},{10,... | collective-permute-start | bytes 258056 | tf_op jit(solution)/shard_map/ppermute | solution.py:546
  83.4 11.6 %collective-permute-start.2 = (bf16[336,128]{1,0:T(8,128)(2,1)S(1)}, bf16[336,128]{1,0:T(8,128)(2,1)S(1)}, u32[]{:S(2)}, u32[]{:S(2)}) collective-permute-start(bf16[336,128]{1,0:T(8,128)(2,1)S(1)} %get-tuple-element.29), channel_id=1, source_target_pairs={{0,4},{1,5},{2,6},{3,7},{4,0},{5,1},{6,2},{7,3},{8,12},{9,13},{10,... | collective-permute-start | bytes 258056 | tf_op jit(solution)/shard_map/ppermute | solution.py:546
  88.2 9.8 %collective-permute-start.3 = (bf16[336,128]{1,0:T(8,128)(2,1)S(1)}, bf16[336,128]{1,0:T(8,128)(2,1)S(1)}, u32[]{:S(2)}, u32[]{:S(2)}) collective-permute-start(bf16[336,128]{1,0:T(8,128)(2,1)S(1)} %get-tuple-element.30), channel_id=1, source_target_pairs={{0,6},{1,7},{2,0},{3,1},{4,2},{5,3},{6,4},{7,5},{8,14},{9,15},{10,... | collective-permute-start | bytes 258056 | tf_op jit(solution)/shard_map/ppermute | solution.py:546

commit v6 on v5

--- a/solution.py
+++ b/solution.py
@@ -161,7 +161,8 @@
             place += 1
     out_ref[:, 2 * npix :] = jnp.broadcast_to(about[:1], (npix, META)).astype(jnp.bfloat16)
     save(2 * npix, META)
-    for start in starts:
+    chunk = chunk // 2
+    for start in range(0, 2 * npix, chunk):
         even, odd = (
             jnp.dot(
                 halves_ref[:, parity * npix : (parity + 1) * npix],
@@ -197,7 +198,7 @@
             pltpu.VMEM((2 * npix, 2 * npix), jnp.bfloat16),
             pltpu.VMEM((npix, 2 * npix + META), jnp.bfloat16),
             pltpu.SemaphoreType.DMA((pieces + 5,)),
-            pltpu.SemaphoreType.DMA((pieces + 1,)),
+            pltpu.SemaphoreType.DMA((2 * pieces + 1,)),
         ],
         compiler_params=params(HUGE),
         cost_estimate=cost(12 * npix**3, 10 * npix * npix),
@@ -250,7 +251,7 @@
     return defocus, freq_y * freq_y
 
 
-def compare_kernel(ori, rows, slot_ref, fourier_ref, lookup_ref, volume_ref, filtered_ref, picks_ref, part_ref, about_ref, mix_ref, section_ref, power_ref):
+def compare_kernel(ori, rows, slot_ref, fourier_ref, lookup_ref, volume_ref, filtered_ref, picks_ref, part_ref, about_ref, mix_ref, power_ref):
     many, wide = filtered_ref.shape
     npix = wide // 2
     deep = volume_ref.shape[0]
@@ -281,20 +282,17 @@
     for number, start in enumerate(range(0, npix, 128)):
         real = slice(start, start + 128)
         imag = slice(npix + start, npix + start + 128)
-        slot = number % 2
-        section_ref[slot] = jnp.dot(
-            mix_ref[...],
-            jnp.concatenate([volume_ref[:, real], volume_ref[:, imag]], 1),
-            preferred_element_type=jnp.float32,
-        )
+        planes = jnp.concatenate([volume_ref[:, real], volume_ref[:, imag]], 1)
         ctf = contrast(defocus, row_square, start, 128, npix)
         for part in (real, imag):
             filtered_ref[:, part] = (ctf * fourier_ref[:, part].astype(jnp.float32)).astype(jnp.bfloat16)
         square = ctf * ctf
         for o in range(ori):
-            s_real = section_ref[slot, o * many : (o + 1) * many, :128]
-            s_imag = section_ref[slot, o * many : (o + 1) * many, 128:]
-            power = square * (s_real * s_real + s_imag * s_imag)
+            section = jnp.dot(
+                mix_ref[o * many : (o + 1) * many, :], planes, preferred_element_type=jnp.float32
+            )
+            section = section * section
+            power = square * (section[:, :128] + section[:, 128:])
             if number:
                 power = power + power_ref[o]
             power_ref[o] = power
@@ -333,7 +331,6 @@
         ),
         scratch_shapes=[
             pltpu.VMEM((ori * many, deep), jnp.bfloat16),
-            pltpu.VMEM((2, ori * many, 256), jnp.float32),
             pltpu.VMEM((ori, many, 128), jnp.float32),
         ],
         compiler_params=params(LARGE),
@@ -376,8 +373,31 @@
     )(slot, about)
 
 
-def project_kernel(rows, ori, core_ref, part_ref, noise_ref, picks_ref, filtered_ref, square_ref, probs_ref, keep_ref, send_ref):
-    many, wide = filtered_ref.shape
+def pack(target_ref, share, source_ref, start, last):
+    pairs = target_ref.shape[0]
+    slab = share.shape[0] // pairs
+    sums = jnp.dot(share, source_ref[...], preferred_element_type=jnp.float32)
+    for number in range(sums.shape[1] // 128):
+        value = sums[:, number * 128 : (number + 1) * 128].reshape(pairs, slab, 128)
+        at = (start + number) * slab
+        if start + number < last:
+            target_ref[:, at : at + slab, :] = value.astype(jnp.bfloat16)
+        else:
+            lane = lax.broadcasted_iota(jnp.int32, (pairs, slab // 2, 128), 2)
+            lower = jnp.broadcast_to(value[:, slab // 2 :, :1], lane.shape)
+            value = jnp.where(lane == 0, value[:, : slab // 2], lower)
+            target_ref[:, at : at + slab // 2, :] = value.astype(jnp.bfloat16)
+
+
+def pack_both(target_ref, share, filtered_ref, square_ref):
+    tiles = filtered_ref.shape[1] // 128
+    last = tiles + square_ref.shape[1] // 128 - 1
+    pack(target_ref, share, filtered_ref, 0, last)
+    pack(target_ref, share, square_ref, tiles, last)
+
+
+def project_kernel(rows, ori, core_ref, part_ref, noise_ref, picks_ref, filtered_ref, square_ref, probs_ref, share_ref, send_ref):
+    many = filtered_ref.shape[0]
     deep = picks_ref.shape[1]
     lanes = part_ref.shape[1]
     images = lanes // 2
@@ -403,43 +423,51 @@
         spread_over(rows, (images, many), 0),
         preferred_element_type=jnp.float32,
     )
-    share = own_row(share, rows).reshape(deep, many).astype(jnp.bfloat16)
+    pairs = send_ref.shape[0]
+    share = own_row(share, rows).reshape(pairs, 2, deep // (2 * pairs), many)
     first = core_ref[0] == 0
-    pairs = keep_ref.shape[0]
+    ours = jnp.where(first, share[:, 0], share[:, 1]).reshape(deep // 2, many)
+    theirs = jnp.where(first, share[:, 1], share[:, 0]).reshape(deep // 2, many)
+    share_ref[...] = ours.astype(jnp.bfloat16)
+    pack_both(send_ref, theirs.astype(jnp.bfloat16), filtered_ref, square_ref)
+
+
+def packed(deep, filtered, square, pairs):
     slab = deep // (2 * pairs)
-    tiles = (wide + square_ref.shape[1]) // 128 - 1
-    for source_ref, start in ((filtered_ref, 0), (square_ref, wide // 128)):
-        sums = jnp.dot(share, source_ref[...], preferred_element_type=jnp.float32)
-        for number in range(sums.shape[1] // 128):
-            tile = sums[:, number * 128 : (number + 1) * 128].reshape(pairs, 2, slab, 128)
-            ours, theirs = tile[:, 0], tile[:, 1]
-            ours, theirs = jnp.where(first, ours, theirs), jnp.where(first, theirs, ours)
-            at = (start + number) * slab
-            for target_ref, value in ((keep_ref, ours), (send_ref, theirs)):
-                if start + number < tiles:
-                    target_ref[:, at : at + slab, :] = value.astype(jnp.bfloat16)
-                else:
-                    lane = lax.broadcasted_iota(jnp.int32, (pairs, slab // 2, 128), 2)
-                    lower = jnp.broadcast_to(value[:, slab // 2 :, :1], lane.shape)
-                    value = jnp.where(lane == 0, value[:, : slab // 2], lower)
-                    target_ref[:, at : at + slab // 2, :] = value.astype(jnp.bfloat16)
+    lines = (filtered.shape[1] + square.shape[1]) // 128 * slab - slab // 2
+    return jax.ShapeDtypeStruct((pairs, lines, 128), jnp.bfloat16)
 
 
 def project(core, part, noise, picks, filtered, square, rows, ori, pairs):
-    many, wide = filtered.shape
+    many = filtered.shape[0]
     deep = picks.shape[1]
-    slab = deep // (2 * pairs)
-    lines = (wide + square.shape[1]) // 128 * slab - slab // 2
-    half = jax.ShapeDtypeStruct((pairs, lines, 128), jnp.bfloat16)
     return pl.pallas_call(
         functools.partial(project_kernel, rows, ori),
         in_specs=[scalar()] + [whole()] * 5,
         out_specs=(whole(), whole(), whole()),
-        out_shape=(jax.ShapeDtypeStruct((8, part.shape[1]), jnp.float32), half, half),
+        out_shape=(
+            jax.ShapeDtypeStruct((8, part.shape[1]), jnp.float32),
+            jax.ShapeDtypeStruct((deep // 2, many), jnp.bfloat16),
+            packed(deep, filtered, square, pairs),
+        ),
         compiler_params=params(LARGE),
-        cost_estimate=cost(1 << 29, 4 << 20),
+        cost_estimate=cost(1 << 28, 4 << 20),
         name="project",
     )(core, part, noise, picks, filtered, square)
+
+
+def keep_kernel(share_ref, filtered_ref, square_ref, keep_ref):
+    pack_both(keep_ref, share_ref[...], filtered_ref, square_ref)
+
+
+def keep_own(share, filtered, square, pairs):
+    return pl.pallas_call(
+        keep_kernel,
+        out_shape=packed(2 * share.shape[0], filtered, square, pairs),
+        compiler_params=params(SMALL),
+        cost_estimate=cost(1 << 28, 2 << 20),
+        name="keep_own",
+    )(share, filtered, square)
 
 
 def middle_kernel(high_ref, keep_ref, got_ref, own_ref, *send_refs):
@@ -467,47 +495,46 @@
     )(high, keep, got)
 
 
-def finish_kernel(own_ref, *refs):
+def spread_lines(total, slab, npix, precision):
+    half = npix // 2
+    tiles = [total[at : at + slab] for at in range(0, total.shape[0] - slab // 2, slab)]
+    data = jnp.concatenate(tiles[: 2 * npix // 128], 1)
+    lower = jnp.concatenate(tiles[2 * npix // 128 :], 1)
+    source = lax.broadcasted_iota(jnp.int32, (half, half), 0)
+    target = lax.broadcasted_iota(jnp.int32, (half, half), 1)
+    mirror = jnp.where(source + target == half, 1.0, 0.0).astype(total.dtype)
+    upper = jnp.dot(lower, mirror, preferred_element_type=jnp.float32, precision=precision)
+    last = total[total.shape[0] - slab // 2 :].astype(jnp.float32)
+    last = jnp.concatenate([last[:, :1], last[:, 1:2]], 0)
+    lane = lax.broadcasted_iota(jnp.int32, (slab, half), 1)
+    upper = jnp.where(lane == 0, last, upper)
+    return data.astype(jnp.float32), lower.astype(jnp.float32), upper
+
+
+def finish_kernel(precision, first_ref, *refs):
     data_ref, weight_ref, data_out, weight_out = refs[-4:]
     slab, npix = weight_ref.shape
-    half = npix // 2
-    total = own_ref[...]
+    total = first_ref[...]
     for part_ref in refs[:-4]:
         total = total + part_ref[...].astype(jnp.float32)
-    for start in range(0, 2 * npix, 128):
-        at = start // 128 * slab
-        data_out[:, start : start + 128] = data_ref[:, start : start + 128] + total[at : at + slab]
-    lower = []
-    for start in range(0, half, 128):
-        at = (2 * npix + start) // 128 * slab
-        lower.append(total[at : at + slab])
-    lower = jnp.concatenate(lower, 1)
-    weight_out[:, :half] = weight_ref[:, :half] + lower
-    source = lax.broadcasted_iota(jnp.int32, (half, half), 0)
-    target = lax.broadcasted_iota(jnp.int32, (half, half), 1)
-    upper = jnp.dot(
-        lower,
-        jnp.where(source + target == half, 1.0, 0.0),
-        preferred_element_type=jnp.float32,
-        precision=lax.Precision.HIGHEST,
-    )
-    last = total[total.shape[0] - slab // 2 :]
-    last = jnp.concatenate([last[:, :1], last[:, 1:2]], 0)
-    lane = lax.broadcasted_iota(jnp.int32, (slab, half), 1)
-    weight_out[:, half:] = weight_ref[:, half:] + jnp.where(lane == 0, last, upper)
-
-
-def finish(own, parts, data_old, weight_old):
-    return pl.pallas_call(
-        finish_kernel,
+    data, lower, upper = spread_lines(total, slab, npix, precision)
+    data_out[...] = data_ref[...] + data
+    weight_out[:, : npix // 2] = weight_ref[:, : npix // 2] + lower
+    weight_out[:, npix // 2 :] = weight_ref[:, npix // 2 :] + upper
+
+
+def finish(first, parts, data_old, weight_old):
+    exact = first.dtype == jnp.bfloat16
+    return pl.pallas_call(
+        functools.partial(finish_kernel, None if exact else lax.Precision.HIGHEST),
         out_shape=(
             jax.ShapeDtypeStruct(data_old.shape, jnp.float32),
             jax.ShapeDtypeStruct(weight_old.shape, jnp.float32),
         ),
         compiler_params=params(SMALL),
         cost_estimate=cost(1 << 20, 2 << 20),
-        name="finish",
-    )(own, *parts, data_old, weight_old)
+        name="finish" if exact else "collect",
+    )(first, *parts, data_old, weight_old)
 
 
 def on_device(images, defocus, noise, orient, planes, weights, volume, data_old, weight_old):
@@ -534,13 +561,14 @@
     part = lax.all_to_all(
         part.reshape(n_img, 2, 2 * n_img), "img", split_axis=0, concat_axis=0, tiled=True
     ).reshape(2 * n_img, 2 * n_img)
-    probs, keep, send = project(
+    probs, share, send = project(
         (place % 2).reshape(1), part, noise_all, picks, filtered, square, rows, ori, pairs
     )
     mine = lax.dynamic_slice_in_dim(
         probs[:2].reshape(2 * 2, n_img), lax.axis_index("img"), 1, 1
     ).reshape(1, ori)
     got = lax.ppermute(send, "vol", [(v, v ^ 1) for v in range(n_vol)])
+    keep = keep_own(share, filtered, square, pairs)
     own, *sends = middle((place // 2).reshape(1), keep, got)
     parts = [
         lax.ppermute(part, "vol", [(v, (v + 2 * ahead) % n_vol) for v in range(n_vol)])
@@ -548,10 +576,11 @@
     ]
     data, weight = finish(
         own,
-        parts,
+        parts[:-1],
         data_old.reshape(slab * rows, 2 * npix),
         weight_old.reshape(slab * rows, npix),
     )
+    data, weight = finish(parts[-1], [], data, weight)
     return (mine, data.reshape(data_old.shape), weight.reshape(weight_old.shape))
 
 

time: 99.2 us -> 98.7 us (level)
  starting transfers between devices: 40 us -> 38.8 us
    ppermute x3, starting transfers between devices: 13.9 us -> 12.7 us  [on_device(): lax.ppermute(part, 'vol', [(v, (v + 2 * ahead) % n_vol) for v in range(n_...]
  transfers between devices with their start and end apart: 6 -> 6, of which waited for: 5 -> 4; matrix products, arithmetic and copies ran while one was open for 1% -> 1% of each run, Pallas kernels for 1% -> 2%
where the time goes in v6:
time: 98.7 us; the launch traced here: 97.9 us
  starting transfers between devices  38.8 us (39%)
  blocking collectives  26.5 us (27%)
  waiting for transfers between devices  18.1 us (18%)
  Pallas kernels  11.6 us (12%)
  between operations  2.1 us (2%)
    all_gather x1, blocking collectives, on_device(): lax.all_gather(volume.reshape(slab * rows, 2 * npix), 'vol', axis=0, tile...  26.5 us
    all_to_all x1, starting transfers between devices, on_device(): lax.all_to_all(fourier.reshape(n_img, rows, 2 * npix + META), 'img', spli...  15.5 us
    ppermute x3, starting transfers between devices, on_device(): lax.ppermute(part, 'vol', [(v, (v + 2 * ahead) % n_vol) for v in range(n_...  12.7 us
    all_to_all x1, waiting for transfers between devices, on_device(): lax.all_to_all(part.reshape(n_img, 2, 2 * n_img), 'img', split_axis=0, co...  8.28 us
    all_to_all x1, starting transfers between devices, on_device(): lax.all_to_all(part.reshape(n_img, 2, 2 * n_img), 'img', split_axis=0, co...  6.77 us
    ppermute x3, waiting for transfers between devices, on_device(): lax.ppermute(part, 'vol', [(v, (v + 2 * ahead) % n_vol) for v in range(n_...  4.62 us
    all_to_all x1, waiting for transfers between devices, on_device(): lax.all_to_all(fourier.reshape(n_img, rows, 2 * npix + META), 'img', spli...  4.48 us
    pallas_call x1, Pallas kernels, compare(): pl.pallas_call(functools.partial(compare_kernel, ori, rows), in_specs=[sc...  4.21 us
  transfers between devices with their start and end apart: 6, of which 4 were waited for; matrix products, arithmetic and copies ran while one was open for 1% of the time, Pallas kernels for 2%

profile of v6, /device:TPU:1, one launch (start us, length us, event | category | flops | bytes accessed | tf_op | source)
XLA Modules:
  0.0 97.9 jit_solution(2204945738616848741)
XLA Ops:
  1.9 3.7 %transform.1 = bf16[512,1152]{1,0:T(8,128)(2,1)} custom-call(s32[1,4]{1,0:T(1,128)} %orient_hbm.1, f32[1]{0:T(128)S(6)} %copy.16.defocus_hbm, f32[1]{0:T(128)S(6)} %copy.17.noise_hbm, bf16[512,512]{1,0:T(8,128)(2,1)} %bitcast.25, bf16[512,1024]{1,0:T(8,128)(2,1)} %constant.40.clone.table_hbm, bf16[256,1024]{1,0:T(8,128)(2,1)} %constant.41.clone.halves_hbm), custom_call_target="tpu_custom_call" | custom-call | flops 1610612736 | bytes 2621440 | tf_op jit(solution)/shard_map/transform/pallas_call | solution.py:185
  5.6 0.0 copy-start.2
  5.6 0.0 copy-start.3
  5.6 0.0 copy-start.4
  5.6 15.5 %all-to-all-start = ((bf16[64,8,1152]{2,1,0:T(8,128)(2,1)}), bf16[64,8,1152]{2,1,0:T(8,128)(2,1)S(1)}, u32[]{:S(2)}, u32[]{:S(2)}) async-start(bf16[64,8,1152]{2,1,0:T(8,128)(2,1)} %bitcast.22), calls=%async_computation | async-start | bytes 2359296 | tf_op jit(solution)/shard_map/all_to_all | solution.py:554
  21.1 0.0 copy-done.2
  21.1 0.0 copy-done.3
  21.2 0.1 prepare.1.lookup_ref
  21.3 0.0 copy-done.4
  21.3 26.5 %all_gather.3.volume_ref = bf16[256,1024]{1,0:T(8,128)(2,1)S(1)} all-gather(bf16[32,1024]{1,0:T(8,128)(2,1)S(1)} %bitcast.23), channel_id=1, replica_groups=mesh['img'=64,'vol'=8] {'vol'}, dimensions={0}, use_global_device_ids=true | all-gather | bytes 589824 | tf_op jit(solution)/shard_map/all_gather | solution.py:557
  47.8 4.5 %all-to-all-done = bf16[64,8,1152]{2,1,0:T(8,128)(2,1)S(1)} async-done(((bf16[64,8,1152]{2,1,0:T(8,128)(2,1)}), bf16[64,8,1152]{2,1,0:T(8,128)(2,1)S(1)}, u32[]{:S(2)}, u32[]{:S(2)}) %all-to-all-start) | async-done | bytes 1179680 | tf_op jit(solution)/shard_map/all_to_all | solution.py:554
  52.3 4.2 %compare.4 = (bf16[512,1024]{1,0:T(8,128)(2,1)S(1)}, bf16[256,256]{1,0:T(8,128)(2,1)S(1)}, f32[128,128]{1,0:T(8,128)}, f32[64,128]{1,0:T(8,128)S(1)}) custom-call(s32[1]{0:T(128)} %bitcast.1.slot_ref, bf16[512,1152]{1,0:T(8,128)(2,1)S(1)} %bitcast.16, bf16[256,768]{1,0:T(8,128)(2,1)S(1)} %prepare.1.lookup_ref, bf16[256,1024]{1,0:T(8,128)(2,1)S(1)} %all_gather.3.volume_ref), custom_call_target="tpu_custom_call" | custom-call | flops 2147483648 | bytes 5242880 | tf_op jit(solution)/shard_map/compare/pallas_call | solution.py:322
  56.5 6.8 %all-to-all-start.1 = ((f32[64,2,128]{2,1,0:T(2,128)}), f32[64,2,128]{2,1,0:T(2,128)S(1)}, u32[]{:S(2)}, u32[]{:S(2)}) async-start(f32[64,2,128]{2,1,0:T(2,128)} %bitcast.8), calls=%async_computation.1 | async-start | bytes 131072 | tf_op jit(solution)/shard_map/all_to_all | solution.py:561
  63.3 1.1 %squares.1 = (bf16[512,384]{1,0:T(8,128)(2,1)S(1)}, f32[1,128]{1,0:T(1,128)S(1)}) custom-call(s32[1]{0:T(128)} %bitcast.1.slot_ref, f32[64,128]{1,0:T(8,128)S(1)} %get-tuple-element.21.about_ref), custom_call_target="tpu_custom_call" | custom-call | flops 134217728 | bytes 1048576 | tf_op jit(solution)/shard_map/squares/pallas_call | solution.py:362
  64.3 8.3 %all-to-all-done.1 = f32[64,2,128]{2,1,0:T(2,128)S(1)} async-done(((f32[64,2,128]{2,1,0:T(2,128)}), f32[64,2,128]{2,1,0:T(2,128)S(1)}, u32[]{:S(2)}, u32[]{:S(2)}) %all-to-all-start.1) | async-done | bytes 65568 | tf_op jit(solution)/shard_map/all_to_all | solution.py:561
  72.6 1.0 %project.1 = (f32[8,128]{1,0:T(8,128)S(1)}, bf16[128,512]{1,0:T(8,128)(2,1)S(1)}, bf16[4,336,128]{2,1,0:T(8,128)(2,1)S(1)}) custom-call(s32[1]{0:T(128)} %bitcast.core_ref, f32[128,128]{1,0:T(8,128)S(1)} %bitcast.17, f32[1,128]{1,0:T(1,128)S(1)} %get-tuple-element.22.noise_ref, bf16[256,256]{1,0:T(8,128)(2,1)S(1)} %get-tuple-element.23.picks_ref, ...), custom_call_target="tpu_custom_call" | custom-call | flops 268435456 | bytes 4194304 | tf_op jit(solution)/shard_map/project/pallas_call | solution.py:444
  73.6 3.8 %collective-permute-start = (bf16[4,336,128]{2,1,0:T(8,128)(2,1)S(1)}, bf16[4,336,128]{2,1,0:T(8,128)(2,1)S(1)}, u32[]{:S(2)}, u32[]{:S(2)}) collective-permute-start(bf16[4,336,128]{2,1,0:T(8,128)(2,1)S(1)} %get-tuple-element.28), channel_id=1, source_target_pairs={{0,1},{1,0},{2,3},{3,2},{4,5},{5,4},{6,7},{7,6},{8,9},{9,8},{10,11... | collective-permute-start | bytes 1032200 | tf_op jit(solution)/shard_map/ppermute | solution.py:570
  77.5 0.1 reshape.55
  77.6 0.0 copy-start
  77.6 0.0 copy-start.1
  77.6 0.4 keep_own.1.keep_ref
  78.0 0.7 collective-permute-done.got_ref
  78.7 0.1 middle.1
  78.8 5.0 %collective-permute-start.1 = (bf16[336,128]{1,0:T(8,128)(2,1)S(1)}, bf16[336,128]{1,0:T(8,128)(2,1)S(1)}, u32[]{:S(2)}, u32[]{:S(2)}) collective-permute-start(bf16[336,128]{1,0:T(8,128)(2,1)S(1)} %get-tuple-element.29), channel_id=1, source_target_pairs={{0,6},{1,7},{2,0},{3,1},{4,2},{5,3},{6,4},{7,5},{8,14},{9,15},{10,... | collective-permute-start | bytes 258056 | tf_op jit(solution)/shard_map/ppermute | solution.py:574
  83.8 1.9 %collective-permute-start.2 = (bf16[336,128]{1,0:T(8,128)(2,1)S(1)}, bf16[336,128]{1,0:T(8,128)(2,1)S(1)}, u32[]{:S(2)}, u32[]{:S(2)}) collective-permute-start(bf16[336,128]{1,0:T(8,128)(2,1)S(1)} %get-tuple-element.31), channel_id=1, source_target_pairs={{0,2},{1,3},{2,4},{3,5},{4,6},{5,7},{6,0},{7,1},{8,10},{9,11},{10,... | collective-permute-start | bytes 258056 | tf_op jit(solution)/shard_map/ppermute | solution.py:574
  85.7 5.8 %collective-permute-start.3 = (bf16[336,128]{1,0:T(8,128)(2,1)S(1)}, bf16[336,128]{1,0:T(8,128)(2,1)S(1)}, u32[]{:S(2)}, u32[]{:S(2)}) collective-permute-start(bf16[336,128]{1,0:T(8,128)(2,1)S(1)} %get-tuple-element.32), channel_id=1, source_target_pairs={{0,4},{1,5},{2,6},{3,7},{4,0},{5,1},{6,2},{7,3},{8,12},{9,13},{10,... | collective-permute-start | bytes 258056 | tf_op jit(solution)/shard_map/ppermute | solution.py:574
  91.6 0.1 constant_dynamic-slice_fusion
  91.6 0.6 copy.15
  92.2 0.0 collective-permute-done.2.refs_0_
  92.3 4.6 %collective-permute-done.3.refs_1_ = bf16[336,128]{1,0:T(8,128)(2,1)S(1)} collective-permute-done((bf16[336,128]{1,0:T(8,128)(2,1)S(1)}, bf16[336,128]{1,0:T(8,128)(2,1)S(1)}, u32[]{:S(2)}, u32[]{:S(2)}) %collective-permute-start.3) | collective-permute-done | bytes 86048 | tf_op jit(solution)/shard_map/ppermute | solution.py:574
  96.9 0.0 copy-done
  96.9 0.0 copy-done.1
  96.9 0.2 collect.1
  97.1 0.0 collective-permute-done.1.first_ref
  97.1 0.8 finish.1
  (1 shorter events, 0.0 us)
Async XLA Ops:
  5.6 15.5 %copy-start.2 = (s32[2,768,8]{1,2,0:T(8,128)S(1)}, s32[2,768,8]{1,2,0:T(8,128)}, u32[]{:S(2)}) copy-start(s32[2,768,8]{1,2,0:T(8,128)} %param.15) | copy-start | bytes 147460
  5.6 15.5 %copy-start.3 = (bf16[2,768,8]{1,2,0:T(8,128)(2,1)S(1)}, bf16[2,768,8]{1,2,0:T(8,128)(2,1)}, u32[]{:S(2)}) copy-start(bf16[2,768,8]{1,2,0:T(8,128)(2,1)} %param.16) | copy-start | bytes 73732
  5.6 15.7 %copy-start.4 = (bf16[4,8,1024]{2,1,0:T(8,128)(2,1)S(1)}, bf16[4,8,1024]{2,1,0:T(8,128)(2,1)}, u32[]{:S(2)}) copy-start(bf16[4,8,1024]{2,1,0:T(8,128)(2,1)} %param.17) | copy-start | bytes 196612
  5.6 46.6 %all-to-all-start = ((bf16[64,8,1152]{2,1,0:T(8,128)(2,1)}), bf16[64,8,1152]{2,1,0:T(8,128)(2,1)S(1)}, u32[]{:S(2)}, u32[]{:S(2)}) async-start(bf16[64,8,1152]{2,1,0:T(8,128)(2,1)} %bitcast.22), calls=%async_computation | async-start | bytes 2359296 | tf_op jit(solution)/shard_map/all_to_all | solution.py:554
  56.5 16.1 %all-to-all-start.1 = ((f32[64,2,128]{2,1,0:T(2,128)}), f32[64,2,128]{2,1,0:T(2,128)S(1)}, u32[]{:S(2)}, u32[]{:S(2)}) async-start(f32[64,2,128]{2,1,0:T(2,128)} %bitcast.8), calls=%async_computation.1 | async-start | bytes 131072 | tf_op jit(solution)/shard_map/all_to_all | solution.py:561
  73.6 5.1 %collective-permute-start = (bf16[4,336,128]{2,1,0:T(8,128)(2,1)S(1)}, bf16[4,336,128]{2,1,0:T(8,128)(2,1)S(1)}, u32[]{:S(2)}, u32[]{:S(2)}) collective-permute-start(bf16[4,336,128]{2,1,0:T(8,128)(2,1)S(1)} %get-tuple-element.28), channel_id=1, source_target_pairs={{0,1},{1,0},{2,3},{3,2},{4,5},{5,4},{6,7},{7,6},{8,9},{9,8},{10,11... | collective-permute-start | bytes 1032200 | tf_op jit(solution)/shard_map/ppermute | solution.py:570
  77.6 19.3 %copy-start = (f32[4,8,1024]{2,1,0:T(8,128)S(1)}, f32[4,8,1024]{2,1,0:T(8,128)}, u32[]{:S(2)}) copy-start(f32[4,8,1024]{2,1,0:T(8,128)} %param.18) | copy-start | bytes 393220
  77.6 19.3 %copy-start.1 = (f32[4,8,512]{2,1,0:T(8,128)S(1)}, f32[4,8,512]{2,1,0:T(8,128)}, u32[]{:S(2)}) copy-start(f32[4,8,512]{2,1,0:T(8,128)} %param.19) | copy-start | bytes 196612
  78.8 18.3 %collective-permute-start.1 = (bf16[336,128]{1,0:T(8,128)(2,1)S(1)}, bf16[336,128]{1,0:T(8,128)(2,1)S(1)}, u32[]{:S(2)}, u32[]{:S(2)}) collective-permute-start(bf16[336,128]{1,0:T(8,128)(2,1)S(1)} %get-tuple-element.29), channel_id=1, source_target_pairs={{0,6},{1,7},{2,0},{3,1},{4,2},{5,3},{6,4},{7,5},{8,14},{9,15},{10,... | collective-permute-start | bytes 258056 | tf_op jit(solution)/shard_map/ppermute | solution.py:574
  83.8 8.5 %collective-permute-start.2 = (bf16[336,128]{1,0:T(8,128)(2,1)S(1)}, bf16[336,128]{1,0:T(8,128)(2,1)S(1)}, u32[]{:S(2)}, u32[]{:S(2)}) collective-permute-start(bf16[336,128]{1,0:T(8,128)(2,1)S(1)} %get-tuple-element.31), channel_id=1, source_target_pairs={{0,2},{1,3},{2,4},{3,5},{4,6},{5,7},{6,0},{7,1},{8,10},{9,11},{10,... | collective-permute-start | bytes 258056 | tf_op jit(solution)/shard_map/ppermute | solution.py:574
  85.7 11.1 %collective-permute-start.3 = (bf16[336,128]{1,0:T(8,128)(2,1)S(1)}, bf16[336,128]{1,0:T(8,128)(2,1)S(1)}, u32[]{:S(2)}, u32[]{:S(2)}) collective-permute-start(bf16[336,128]{1,0:T(8,128)(2,1)S(1)} %get-tuple-element.32), channel_id=1, source_target_pairs={{0,4},{1,5},{2,6},{3,7},{4,0},{5,1},{6,2},{7,3},{8,12},{9,13},{10,... | collective-permute-start | bytes 258056 | tf_op jit(solution)/shard_map/ppermute | solution.py:574

commit v7 on v6

--- a/solution.py
+++ b/solution.py
@@ -139,13 +139,9 @@
                 both_ref[lower, start - npix : start - npix + chunk] = -part
     for load in loads[1 + len(starts) :]:
         load.wait()
-    saves = []
-
-    def save(start, size):
-        at = pl.ds(start, size)
-        copy = pltpu.make_async_copy(out_ref.at[:, at], out_hbm.at[:, at], out_sems.at[len(saves)])
-        copy.start()
-        saves.append(copy)
+
+    def save(at, number):
+        return pltpu.make_async_copy(out_ref.at[:, at], out_hbm.at[:, at], out_sems.at[number])
 
     lane = lax.broadcasted_iota(jnp.int32, (8, META), 1)
     codes = jnp.zeros((8, META), jnp.int32)
@@ -160,22 +156,28 @@
             about = jnp.where(lane == place, part, about)
             place += 1
     out_ref[:, 2 * npix :] = jnp.broadcast_to(about[:1], (npix, META)).astype(jnp.bfloat16)
-    save(2 * npix, META)
     chunk = chunk // 2
-    for start in range(0, 2 * npix, chunk):
+    steps = 2 * npix // chunk
+    save(pl.ds(2 * npix, META), steps).start()
+
+    @pl.loop(0, steps)
+    def _(step):
+        at = pl.ds(pl.multiple_of(step * chunk, chunk), chunk)
         even, odd = (
             jnp.dot(
                 halves_ref[:, parity * npix : (parity + 1) * npix],
-                both_ref[parity * npix : (parity + 1) * npix, start : start + chunk],
+                both_ref[parity * npix : (parity + 1) * npix, at],
                 preferred_element_type=jnp.float32,
             )
             for parity in range(2)
         )
-        out_ref[:half, start : start + chunk] = (even + odd).astype(jnp.bfloat16)
-        out_ref[half:, start : start + chunk] = (even - odd).astype(jnp.bfloat16)
-        save(start, chunk)
-    for copy in saves:
-        copy.wait()
+        out_ref[:half, at] = (even + odd).astype(jnp.bfloat16)
+        out_ref[half:, at] = (even - odd).astype(jnp.bfloat16)
+        save(at, step).start()
+
+    for step in range(steps):
+        save(pl.ds(step * chunk, chunk), step).wait()
+    save(pl.ds(2 * npix, META), steps).wait()
 
 
 def transform(orient, defocus, noise, image, table, halves):
@@ -279,9 +281,13 @@
             own_row(every, rows).reshape(many, deep).astype(jnp.bfloat16)
         )
     defocus, row_square = line_geometry(meta.astype(jnp.float32), ori, rows, many, npix, slot_ref[0])
-    for number, start in enumerate(range(0, npix, 128)):
-        real = slice(start, start + 128)
-        imag = slice(npix + start, npix + start + 128)
+    power_ref[...] = jnp.zeros(power_ref.shape, jnp.float32)
+
+    @pl.loop(0, npix // 128)
+    def _(number):
+        start = pl.multiple_of(number * 128, 128)
+        real = pl.ds(start, 128)
+        imag = pl.ds(pl.multiple_of(npix + start, 128), 128)
         planes = jnp.concatenate([volume_ref[:, real], volume_ref[:, imag]], 1)
         ctf = contrast(defocus, row_square, start, 128, npix)
         for part in (real, imag):
@@ -292,10 +298,7 @@
                 mix_ref[o * many : (o + 1) * many, :], planes, preferred_element_type=jnp.float32
             )
             section = section * section
-            power = square * (section[:, :128] + section[:, 128:])
-            if number:
-                power = power + power_ref[o]
-            power_ref[o] = power
+            power_ref[o] += square * (section[:, :128] + section[:, 128:])
 
     found = own_row(same(filtered_ref[...], volume_ref[...]), rows)
     found = jnp.sum(found, axis=1)
@@ -495,46 +498,45 @@
     )(high, keep, got)
 
 
-def spread_lines(total, slab, npix, precision):
+def spread_lines(total, slab, npix):
     half = npix // 2
     tiles = [total[at : at + slab] for at in range(0, total.shape[0] - slab // 2, slab)]
     data = jnp.concatenate(tiles[: 2 * npix // 128], 1)
     lower = jnp.concatenate(tiles[2 * npix // 128 :], 1)
     source = lax.broadcasted_iota(jnp.int32, (half, half), 0)
     target = lax.broadcasted_iota(jnp.int32, (half, half), 1)
-    mirror = jnp.where(source + target == half, 1.0, 0.0).astype(total.dtype)
-    upper = jnp.dot(lower, mirror, preferred_element_type=jnp.float32, precision=precision)
-    last = total[total.shape[0] - slab // 2 :].astype(jnp.float32)
+    mirror = jnp.where(source + target == half, 1.0, 0.0)
+    upper = jnp.dot(lower, mirror, preferred_element_type=jnp.float32, precision=lax.Precision.HIGHEST)
+    last = total[total.shape[0] - slab // 2 :]
     last = jnp.concatenate([last[:, :1], last[:, 1:2]], 0)
     lane = lax.broadcasted_iota(jnp.int32, (slab, half), 1)
     upper = jnp.where(lane == 0, last, upper)
-    return data.astype(jnp.float32), lower.astype(jnp.float32), upper
-
-
-def finish_kernel(precision, first_ref, *refs):
+    return data, lower, upper
+
+
+def finish_kernel(own_ref, *refs):
     data_ref, weight_ref, data_out, weight_out = refs[-4:]
     slab, npix = weight_ref.shape
-    total = first_ref[...]
+    total = own_ref[...]
     for part_ref in refs[:-4]:
         total = total + part_ref[...].astype(jnp.float32)
-    data, lower, upper = spread_lines(total, slab, npix, precision)
+    data, lower, upper = spread_lines(total, slab, npix)
     data_out[...] = data_ref[...] + data
     weight_out[:, : npix // 2] = weight_ref[:, : npix // 2] + lower
     weight_out[:, npix // 2 :] = weight_ref[:, npix // 2 :] + upper
 
 
-def finish(first, parts, data_old, weight_old):
-    exact = first.dtype == jnp.bfloat16
-    return pl.pallas_call(
-        functools.partial(finish_kernel, None if exact else lax.Precision.HIGHEST),
+def finish(own, parts, data_old, weight_old):
+    return pl.pallas_call(
+        finish_kernel,
         out_shape=(
             jax.ShapeDtypeStruct(data_old.shape, jnp.float32),
             jax.ShapeDtypeStruct(weight_old.shape, jnp.float32),
         ),
         compiler_params=params(SMALL),
         cost_estimate=cost(1 << 20, 2 << 20),
-        name="finish" if exact else "collect",
-    )(first, *parts, data_old, weight_old)
+        name="finish",
+    )(own, *parts, data_old, weight_old)
 
 
 def on_device(images, defocus, noise, orient, planes, weights, volume, data_old, weight_old):
@@ -572,15 +574,14 @@
     own, *sends = middle((place // 2).reshape(1), keep, got)
     parts = [
         lax.ppermute(part, "vol", [(v, (v + 2 * ahead) % n_vol) for v in range(n_vol)])
-        for ahead, part in enumerate(sends, 1)
+        for ahead, part in ((2, sends[1]), (1, sends[0]), (3, sends[2]))
     ]
     data, weight = finish(
         own,
-        parts[:-1],
+        parts,
         data_old.reshape(slab * rows, 2 * npix),
         weight_old.reshape(slab * rows, npix),
     )
-    data, weight = finish(parts[-1], [], data, weight)
     return (mine, data.reshape(data_old.shape), weight.reshape(weight_old.shape))
 
 

time: 98.7 us -> 99.1 us (level)
  waiting for transfers between devices: 18.1 us -> 16.4 us
  Pallas kernels: 11.6 us -> 12.9 us
  starting transfers between devices: 38.8 us -> 40 us
    ppermute x3, waiting for transfers between devices: 4.62 us -> 2.98 us  [on_device(): lax.ppermute(part, 'vol', [(v, (v + 2 * ahead) % n_vol) for v in range(n_...]
    ppermute x3, starting transfers between devices: 12.7 us -> 14 us  [on_device(): lax.ppermute(part, 'vol', [(v, (v + 2 * ahead) % n_vol) for v in range(n_...]
where the time goes in v7:
time: 99.1 us; the launch traced here: 98.7 us
  starting transfers between devices  40 us (40%)
  blocking collectives  26.5 us (27%)
  waiting for transfers between devices  16.4 us (17%)
  Pallas kernels  12.9 us (13%)
  between operations  2.09 us (2%)
    all_gather x1, blocking collectives, on_device(): lax.all_gather(volume.reshape(slab * rows, 2 * npix), 'vol', axis=0, tile...  26.5 us
    all_to_all x1, starting transfers between devices, on_device(): lax.all_to_all(fourier.reshape(n_img, rows, 2 * npix + META), 'img', spli...  15.5 us
    ppermute x3, starting transfers between devices, on_device(): lax.ppermute(part, 'vol', [(v, (v + 2 * ahead) % n_vol) for v in range(n_...  14 us
    all_to_all x1, waiting for transfers between devices, on_device(): lax.all_to_all(part.reshape(n_img, 2, 2 * n_img), 'img', split_axis=0, co...  8.29 us
    all_to_all x1, starting transfers between devices, on_device(): lax.all_to_all(part.reshape(n_img, 2, 2 * n_img), 'img', split_axis=0, co...  6.77 us
    pallas_call x1, Pallas kernels, compare(): pl.pallas_call(functools.partial(compare_kernel, ori, rows), in_specs=[sc...  5 us
    all_to_all x1, waiting for transfers between devices, on_device(): lax.all_to_all(fourier.reshape(n_img, rows, 2 * npix + META), 'img', spli...  4.48 us
    pallas_call x1, Pallas kernels, transform(): pl.pallas_call(functools.partial(transform_kernel, chunk), in_specs=[pl.B...  4.26 us
  transfers between devices with their start and end apart: 6, of which 4 were waited for; matrix products, arithmetic and copies ran while one was open for 1% of the time, Pallas kernels for 2%

profile of v7, /device:TPU:1, one launch (start us, length us, event | category | flops | bytes accessed | tf_op | source)
XLA Modules:
  0.0 98.7 jit_solution(10607870456671517651)
XLA Ops:
  1.9 4.3 %transform.1 = bf16[512,1152]{1,0:T(8,128)(2,1)} custom-call(s32[1,4]{1,0:T(1,128)} %orient_hbm.1, f32[1]{0:T(128)S(6)} %copy.16.defocus_hbm, f32[1]{0:T(128)S(6)} %copy.17.noise_hbm, bf16[512,512]{1,0:T(8,128)(2,1)} %bitcast.25, bf16[512,1024]{1,0:T(8,128)(2,1)} %constant.40.clone.table_hbm, bf16[256,1024]{1,0:T(8,128)(2,1)} %constant.41.clone.halves_hbm), custom_call_target="tpu_custom_call" | custom-call | flops 1610612736 | bytes 2621440 | tf_op jit(solution)/shard_map/transform/pallas_call | solution.py:187
  6.2 0.0 copy-start.2
  6.2 0.0 copy-start.3
  6.2 0.0 copy-start.4
  6.2 15.5 %all-to-all-start = ((bf16[64,8,1152]{2,1,0:T(8,128)(2,1)}), bf16[64,8,1152]{2,1,0:T(8,128)(2,1)S(1)}, u32[]{:S(2)}, u32[]{:S(2)}) async-start(bf16[64,8,1152]{2,1,0:T(8,128)(2,1)} %bitcast.22), calls=%async_computation | async-start | bytes 2359296 | tf_op jit(solution)/shard_map/all_to_all | solution.py:556
  21.7 0.0 copy-done.2
  21.7 0.0 copy-done.3
  21.7 0.1 prepare.1.lookup_ref
  21.9 0.0 copy-done.4
  21.9 26.5 %all_gather.3.volume_ref = bf16[256,1024]{1,0:T(8,128)(2,1)S(1)} all-gather(bf16[32,1024]{1,0:T(8,128)(2,1)S(1)} %bitcast.23), channel_id=1, replica_groups=mesh['img'=64,'vol'=8] {'vol'}, dimensions={0}, use_global_device_ids=true | all-gather | bytes 589824 | tf_op jit(solution)/shard_map/all_gather | solution.py:559
  48.4 4.5 %all-to-all-done = bf16[64,8,1152]{2,1,0:T(8,128)(2,1)S(1)} async-done(((bf16[64,8,1152]{2,1,0:T(8,128)(2,1)}), bf16[64,8,1152]{2,1,0:T(8,128)(2,1)S(1)}, u32[]{:S(2)}, u32[]{:S(2)}) %all-to-all-start) | async-done | bytes 1179680 | tf_op jit(solution)/shard_map/all_to_all | solution.py:556
  52.9 5.0 %compare.4 = (bf16[512,1024]{1,0:T(8,128)(2,1)S(1)}, bf16[256,256]{1,0:T(8,128)(2,1)S(1)}, f32[128,128]{1,0:T(8,128)}, f32[64,128]{1,0:T(8,128)S(1)}) custom-call(s32[1]{0:T(128)} %bitcast.1.slot_ref, bf16[512,1152]{1,0:T(8,128)(2,1)S(1)} %bitcast.16, bf16[256,768]{1,0:T(8,128)(2,1)S(1)} %prepare.1.lookup_ref, bf16[256,1024]{1,0:T(8,128)(2,1)S(1)} %all_gather.3.volume_ref), custom_call_target="tpu_custom_call" | custom-call | flops 2147483648 | bytes 5242880 | tf_op jit(solution)/shard_map/compare/pallas_call | solution.py:325
  57.9 6.8 %all-to-all-start.1 = ((f32[64,2,128]{2,1,0:T(2,128)}), f32[64,2,128]{2,1,0:T(2,128)S(1)}, u32[]{:S(2)}, u32[]{:S(2)}) async-start(f32[64,2,128]{2,1,0:T(2,128)} %bitcast.8), calls=%async_computation.1 | async-start | bytes 131072 | tf_op jit(solution)/shard_map/all_to_all | solution.py:563
  64.7 1.1 %squares.1 = (bf16[512,384]{1,0:T(8,128)(2,1)S(1)}, f32[1,128]{1,0:T(1,128)S(1)}) custom-call(s32[1]{0:T(128)} %bitcast.1.slot_ref, f32[64,128]{1,0:T(8,128)S(1)} %get-tuple-element.19.about_ref), custom_call_target="tpu_custom_call" | custom-call | flops 134217728 | bytes 1048576 | tf_op jit(solution)/shard_map/squares/pallas_call | solution.py:365
  65.7 8.3 %all-to-all-done.1 = f32[64,2,128]{2,1,0:T(2,128)S(1)} async-done(((f32[64,2,128]{2,1,0:T(2,128)}), f32[64,2,128]{2,1,0:T(2,128)S(1)}, u32[]{:S(2)}, u32[]{:S(2)}) %all-to-all-start.1) | async-done | bytes 65568 | tf_op jit(solution)/shard_map/all_to_all | solution.py:563
  74.0 1.0 %project.1 = (f32[8,128]{1,0:T(8,128)S(1)}, bf16[128,512]{1,0:T(8,128)(2,1)S(1)}, bf16[4,336,128]{2,1,0:T(8,128)(2,1)S(1)}) custom-call(s32[1]{0:T(128)} %bitcast.core_ref, f32[128,128]{1,0:T(8,128)S(1)} %bitcast.17, f32[1,128]{1,0:T(1,128)S(1)} %get-tuple-element.20.noise_ref, bf16[256,256]{1,0:T(8,128)(2,1)S(1)} %get-tuple-element.21.picks_ref, ...), custom_call_target="tpu_custom_call" | custom-call | flops 268435456 | bytes 4194304 | tf_op jit(solution)/shard_map/project/pallas_call | solution.py:447
  75.0 3.8 %collective-permute-start = (bf16[4,336,128]{2,1,0:T(8,128)(2,1)S(1)}, bf16[4,336,128]{2,1,0:T(8,128)(2,1)S(1)}, u32[]{:S(2)}, u32[]{:S(2)}) collective-permute-start(bf16[4,336,128]{2,1,0:T(8,128)(2,1)S(1)} %get-tuple-element.26), channel_id=1, source_target_pairs={{0,1},{1,0},{2,3},{3,2},{4,5},{5,4},{6,7},{7,6},{8,9},{9,8},{10,11... | collective-permute-start | bytes 1032200 | tf_op jit(solution)/shard_map/ppermute | solution.py:572
  78.9 0.1 reshape.55
  79.0 0.0 copy-start
  79.0 0.0 copy-start.1
  79.0 0.4 keep_own.1.keep_ref
  79.4 0.7 collective-permute-done.got_ref
  80.1 0.1 middle.1
  80.2 6.6 %collective-permute-start.1 = (bf16[336,128]{1,0:T(8,128)(2,1)S(1)}, bf16[336,128]{1,0:T(8,128)(2,1)S(1)}, u32[]{:S(2)}, u32[]{:S(2)}) collective-permute-start(bf16[336,128]{1,0:T(8,128)(2,1)S(1)} %get-tuple-element.28), channel_id=1, source_target_pairs={{0,4},{1,5},{2,6},{3,7},{4,0},{5,1},{6,2},{7,3},{8,12},{9,13},{10,... | collective-permute-start | bytes 258056 | tf_op jit(solution)/shard_map/ppermute | solution.py:576
  86.8 2.4 %collective-permute-start.2 = (bf16[336,128]{1,0:T(8,128)(2,1)S(1)}, bf16[336,128]{1,0:T(8,128)(2,1)S(1)}, u32[]{:S(2)}, u32[]{:S(2)}) collective-permute-start(bf16[336,128]{1,0:T(8,128)(2,1)S(1)} %get-tuple-element.29), channel_id=1, source_target_pairs={{0,2},{1,3},{2,4},{3,5},{4,6},{5,7},{6,0},{7,1},{8,10},{9,11},{10,... | collective-permute-start | bytes 258056 | tf_op jit(solution)/shard_map/ppermute | solution.py:576
  89.2 5.0 %collective-permute-start.3 = (bf16[336,128]{1,0:T(8,128)(2,1)S(1)}, bf16[336,128]{1,0:T(8,128)(2,1)S(1)}, u32[]{:S(2)}, u32[]{:S(2)}) collective-permute-start(bf16[336,128]{1,0:T(8,128)(2,1)S(1)} %get-tuple-element.30), channel_id=1, source_target_pairs={{0,6},{1,7},{2,0},{3,1},{4,2},{5,3},{6,4},{7,5},{8,14},{9,15},{10,... | collective-permute-start | bytes 258056 | tf_op jit(solution)/shard_map/ppermute | solution.py:576
  94.2 0.1 constant_dynamic-slice_fusion
  94.2 0.6 copy.15
  94.8 0.0 collective-permute-done.1.refs_0_
  94.8 0.0 collective-permute-done.2.refs_1_
  94.8 3.0 %collective-permute-done.3.refs_2_ = bf16[336,128]{1,0:T(8,128)(2,1)S(1)} collective-permute-done((bf16[336,128]{1,0:T(8,128)(2,1)S(1)}, bf16[336,128]{1,0:T(8,128)(2,1)S(1)}, u32[]{:S(2)}, u32[]{:S(2)}) %collective-permute-start.3) | collective-permute-done | bytes 86048 | tf_op jit(solution)/shard_map/ppermute | solution.py:576
  97.8 0.0 copy-done
  97.8 0.0 copy-done.1
  97.8 0.9 finish.1
  (1 shorter events, 0.0 us)
Async XLA Ops:
  6.2 15.5 %copy-start.2 = (s32[2,768,8]{1,2,0:T(8,128)S(1)}, s32[2,768,8]{1,2,0:T(8,128)}, u32[]{:S(2)}) copy-start(s32[2,768,8]{1,2,0:T(8,128)} %param.15) | copy-start | bytes 147460
  6.2 15.5 %copy-start.3 = (bf16[2,768,8]{1,2,0:T(8,128)(2,1)S(1)}, bf16[2,768,8]{1,2,0:T(8,128)(2,1)}, u32[]{:S(2)}) copy-start(bf16[2,768,8]{1,2,0:T(8,128)(2,1)} %param.16) | copy-start | bytes 73732
  6.2 15.7 %copy-start.4 = (bf16[4,8,1024]{2,1,0:T(8,128)(2,1)S(1)}, bf16[4,8,1024]{2,1,0:T(8,128)(2,1)}, u32[]{:S(2)}) copy-start(bf16[4,8,1024]{2,1,0:T(8,128)(2,1)} %param.17) | copy-start | bytes 196612
  6.2 46.6 %all-to-all-start = ((bf16[64,8,1152]{2,1,0:T(8,128)(2,1)}), bf16[64,8,1152]{2,1,0:T(8,128)(2,1)S(1)}, u32[]{:S(2)}, u32[]{:S(2)}) async-start(bf16[64,8,1152]{2,1,0:T(8,128)(2,1)} %bitcast.22), calls=%async_computation | async-start | bytes 2359296 | tf_op jit(solution)/shard_map/all_to_all | solution.py:556
  57.9 16.2 %all-to-all-start.1 = ((f32[64,2,128]{2,1,0:T(2,128)}), f32[64,2,128]{2,1,0:T(2,128)S(1)}, u32[]{:S(2)}, u32[]{:S(2)}) async-start(f32[64,2,128]{2,1,0:T(2,128)} %bitcast.8), calls=%async_computation.1 | async-start | bytes 131072 | tf_op jit(solution)/shard_map/all_to_all | solution.py:563
  75.0 5.1 %collective-permute-start = (bf16[4,336,128]{2,1,0:T(8,128)(2,1)S(1)}, bf16[4,336,128]{2,1,0:T(8,128)(2,1)S(1)}, u32[]{:S(2)}, u32[]{:S(2)}) collective-permute-start(bf16[4,336,128]{2,1,0:T(8,128)(2,1)S(1)} %get-tuple-element.26), channel_id=1, source_target_pairs={{0,1},{1,0},{2,3},{3,2},{4,5},{5,4},{6,7},{7,6},{8,9},{9,8},{10,11... | collective-permute-start | bytes 1032200 | tf_op jit(solution)/shard_map/ppermute | solution.py:572
  79.0 18.9 %copy-start = (f32[4,8,1024]{2,1,0:T(8,128)S(1)}, f32[4,8,1024]{2,1,0:T(8,128)}, u32[]{:S(2)}) copy-start(f32[4,8,1024]{2,1,0:T(8,128)} %param.18) | copy-start | bytes 393220
  79.0 18.9 %copy-start.1 = (f32[4,8,512]{2,1,0:T(8,128)S(1)}, f32[4,8,512]{2,1,0:T(8,128)}, u32[]{:S(2)}) copy-start(f32[4,8,512]{2,1,0:T(8,128)} %param.19) | copy-start | bytes 196612
  80.2 14.7 %collective-permute-start.1 = (bf16[336,128]{1,0:T(8,128)(2,1)S(1)}, bf16[336,128]{1,0:T(8,128)(2,1)S(1)}, u32[]{:S(2)}, u32[]{:S(2)}) collective-permute-start(bf16[336,128]{1,0:T(8,128)(2,1)S(1)} %get-tuple-element.28), channel_id=1, source_target_pairs={{0,4},{1,5},{2,6},{3,7},{4,0},{5,1},{6,2},{7,3},{8,12},{9,13},{10,... | collective-permute-start | bytes 258056 | tf_op jit(solution)/shard_map/ppermute | solution.py:576
  86.8 8.1 %collective-permute-start.2 = (bf16[336,128]{1,0:T(8,128)(2,1)S(1)}, bf16[336,128]{1,0:T(8,128)(2,1)S(1)}, u32[]{:S(2)}, u32[]{:S(2)}) collective-permute-start(bf16[336,128]{1,0:T(8,128)(2,1)S(1)} %get-tuple-element.29), channel_id=1, source_target_pairs={{0,2},{1,3},{2,4},{3,5},{4,6},{5,7},{6,0},{7,1},{8,10},{9,11},{10,... | collective-permute-start | bytes 258056 | tf_op jit(solution)/shard_map/ppermute | solution.py:576
  89.2 8.7 %collective-permute-start.3 = (bf16[336,128]{1,0:T(8,128)(2,1)S(1)}, bf16[336,128]{1,0:T(8,128)(2,1)S(1)}, u32[]{:S(2)}, u32[]{:S(2)}) collective-permute-start(bf16[336,128]{1,0:T(8,128)(2,1)S(1)} %get-tuple-element.30), channel_id=1, source_target_pairs={{0,6},{1,7},{2,0},{3,1},{4,2},{5,3},{6,4},{7,5},{8,14},{9,15},{10,... | collective-permute-start | bytes 258056 | tf_op jit(solution)/shard_map/ppermute | solution.py:576

commit v8 on v7

--- a/solution.py
+++ b/solution.py
@@ -139,10 +139,6 @@
                 both_ref[lower, start - npix : start - npix + chunk] = -part
     for load in loads[1 + len(starts) :]:
         load.wait()
-
-    def save(at, number):
-        return pltpu.make_async_copy(out_ref.at[:, at], out_hbm.at[:, at], out_sems.at[number])
-
     lane = lax.broadcasted_iota(jnp.int32, (8, META), 1)
     codes = jnp.zeros((8, META), jnp.int32)
     for o in range(ori):
@@ -156,28 +152,25 @@
             about = jnp.where(lane == place, part, about)
             place += 1
     out_ref[:, 2 * npix :] = jnp.broadcast_to(about[:1], (npix, META)).astype(jnp.bfloat16)
-    chunk = chunk // 2
-    steps = 2 * npix // chunk
-    save(pl.ds(2 * npix, META), steps).start()
-
-    @pl.loop(0, steps)
-    def _(step):
-        at = pl.ds(pl.multiple_of(step * chunk, chunk), chunk)
-        even, odd = (
-            jnp.dot(
-                halves_ref[:, parity * npix : (parity + 1) * npix],
-                both_ref[parity * npix : (parity + 1) * npix, at],
-                preferred_element_type=jnp.float32,
-            )
-            for parity in range(2)
+    even, odd = (
+        jnp.dot(
+            halves_ref[:, parity * npix : (parity + 1) * npix],
+            both_ref[parity * npix : (parity + 1) * npix, :],
+            preferred_element_type=jnp.float32,
         )
-        out_ref[:half, at] = (even + odd).astype(jnp.bfloat16)
-        out_ref[half:, at] = (even - odd).astype(jnp.bfloat16)
-        save(at, step).start()
-
-    for step in range(steps):
-        save(pl.ds(step * chunk, chunk), step).wait()
-    save(pl.ds(2 * npix, META), steps).wait()
+        for parity in range(2)
+    )
+    saves = []
+    for part, value in enumerate((even + odd, even - odd)):
+        at = slice(part * half, (part + 1) * half)
+        out_ref[at, : 2 * npix] = value.astype(jnp.bfloat16)
+        copy = pltpu.make_async_copy(
+            out_ref.at[pl.ds(part * half, half)], out_hbm.at[pl.ds(part * half, half)], out_sems.at[part]
+        )
+        copy.start()
+        saves.append(copy)
+    for copy in saves:
+        copy.wait()
 
 
 def transform(orient, defocus, noise, image, table, halves):
@@ -200,7 +193,7 @@
             pltpu.VMEM((2 * npix, 2 * npix), jnp.bfloat16),
             pltpu.VMEM((npix, 2 * npix + META), jnp.bfloat16),
             pltpu.SemaphoreType.DMA((pieces + 5,)),
-            pltpu.SemaphoreType.DMA((2 * pieces + 1,)),
+            pltpu.SemaphoreType.DMA((2,)),
         ],
         compiler_params=params(HUGE),
         cost_estimate=cost(12 * npix**3, 10 * npix * npix),
@@ -253,7 +246,7 @@
     return defocus, freq_y * freq_y
 
 
-def compare_kernel(ori, rows, slot_ref, fourier_ref, lookup_ref, volume_ref, filtered_ref, picks_ref, part_ref, about_ref, mix_ref, power_ref):
+def compare_kernel(ori, rows, slot_ref, fourier_ref, lookup_ref, volume_ref, filtered_ref, picks_ref, part_ref, about_ref, mix_ref, square_ref):
     many, wide = filtered_ref.shape
     npix = wide // 2
     deep = volume_ref.shape[0]
@@ -281,24 +274,24 @@
             own_row(every, rows).reshape(many, deep).astype(jnp.bfloat16)
         )
     defocus, row_square = line_geometry(meta.astype(jnp.float32), ori, rows, many, npix, slot_ref[0])
-    power_ref[...] = jnp.zeros(power_ref.shape, jnp.float32)
-
-    @pl.loop(0, npix // 128)
-    def _(number):
-        start = pl.multiple_of(number * 128, 128)
-        real = pl.ds(start, 128)
-        imag = pl.ds(pl.multiple_of(npix + start, 128), 128)
-        planes = jnp.concatenate([volume_ref[:, real], volume_ref[:, imag]], 1)
+    for start in range(0, npix, 128):
         ctf = contrast(defocus, row_square, start, 128, npix)
-        for part in (real, imag):
-            filtered_ref[:, part] = (ctf * fourier_ref[:, part].astype(jnp.float32)).astype(jnp.bfloat16)
-        square = ctf * ctf
-        for o in range(ori):
-            section = jnp.dot(
-                mix_ref[o * many : (o + 1) * many, :], planes, preferred_element_type=jnp.float32
-            )
-            section = section * section
-            power_ref[o] += square * (section[:, :128] + section[:, 128:])
+        for at in (start, npix + start):
+            filtered_ref[:, at : at + 128] = (
+                ctf * fourier_ref[:, at : at + 128].astype(jnp.float32)
+            ).astype(jnp.bfloat16)
+        square_ref[:, start : start + 128] = ctf * ctf
+    powers = []
+    for o in range(ori):
+        section = jnp.dot(
+            mix_ref[o * many : (o + 1) * many, :], volume_ref[...], preferred_element_type=jnp.float32
+        )
+        section = section * section
+        power = jnp.zeros((many, 128), jnp.float32)
+        for start in range(0, npix, 128):
+            both = section[:, start : start + 128] + section[:, npix + start : npix + start + 128]
+            power = power + square_ref[:, start : start + 128] * both
+        powers.append(jnp.sum(power.reshape(images, rows, 128), axis=1))
 
     found = own_row(same(filtered_ref[...], volume_ref[...]), rows)
     found = jnp.sum(found, axis=1)
@@ -308,8 +301,7 @@
         lanes = cross[:, :128]
         for start in range(128, deep, 128):
             lanes = lanes + cross[:, start : start + 128]
-        power = jnp.sum(power_ref[o].reshape(images, rows, 128), axis=1)
-        halves.append(lanes - 0.5 * power)
+        halves.append(lanes - 0.5 * powers[o])
     upper = jnp.concatenate(halves[: ori // 2], 0)
     lower = jnp.concatenate(halves[ori // 2 :], 0)
     upper = jnp.sum(jnp.transpose(upper), axis=0, keepdims=True)
@@ -334,7 +326,7 @@
         ),
         scratch_shapes=[
             pltpu.VMEM((ori * many, deep), jnp.bfloat16),
-            pltpu.VMEM((ori, many, 128), jnp.float32),
+            pltpu.VMEM((many, wide // 2), jnp.float32),
         ],
         compiler_params=params(LARGE),
         cost_estimate=cost(1 << 31, 5 << 20),

time: 99.1 us -> 98.1 us (0.990)
  Pallas kernels: 12.9 us -> 11.8 us
where the time goes in v8:
time: 98.1 us; the launch traced here: 97.7 us
  starting transfers between devices  40 us (41%)
  blocking collectives  26.5 us (27%)
  waiting for transfers between devices  16.5 us (17%)
  Pallas kernels  11.8 us (12%)
  between operations  2.09 us (2%)
    all_gather x1, blocking collectives, on_device(): lax.all_gather(volume.reshape(slab * rows, 2 * npix), 'vol', axis=0, tile...  26.5 us
    all_to_all x1, starting transfers between devices, on_device(): lax.all_to_all(fourier.reshape(n_img, rows, 2 * npix + META), 'img', spli...  15.5 us
    ppermute x3, starting transfers between devices, on_device(): lax.ppermute(part, 'vol', [(v, (v + 2 * ahead) % n_vol) for v in range(n_...  13.9 us
    all_to_all x1, waiting for transfers between devices, on_device(): lax.all_to_all(part.reshape(n_img, 2, 2 * n_img), 'img', split_axis=0, co...  8.28 us
    all_to_all x1, starting transfers between devices, on_device(): lax.all_to_all(part.reshape(n_img, 2, 2 * n_img), 'img', split_axis=0, co...  6.76 us
    all_to_all x1, waiting for transfers between devices, on_device(): lax.all_to_all(fourier.reshape(n_img, rows, 2 * npix + META), 'img', spli...  4.5 us
    pallas_call x1, Pallas kernels, compare(): pl.pallas_call(functools.partial(compare_kernel, ori, rows), in_specs=[sc...  4.3 us
    pallas_call x1, Pallas kernels, transform(): pl.pallas_call(functools.partial(transform_kernel, chunk), in_specs=[pl.B...  3.95 us
  transfers between devices with their start and end apart: 6, of which 4 were waited for; matrix products, arithmetic and copies ran while one was open for 1% of the time, Pallas kernels for 2%

profile of v8, /device:TPU:1, one launch (start us, length us, event | category | flops | bytes accessed | tf_op | source)
XLA Modules:
  0.0 97.7 jit_solution(5037323155218825682)
XLA Ops:
  1.9 4.0 %transform.1 = bf16[512,1152]{1,0:T(8,128)(2,1)} custom-call(s32[1,4]{1,0:T(1,128)} %orient_hbm.1, f32[1]{0:T(128)S(6)} %copy.16.defocus_hbm, f32[1]{0:T(128)S(6)} %copy.17.noise_hbm, bf16[512,512]{1,0:T(8,128)(2,1)} %bitcast.25, bf16[512,1024]{1,0:T(8,128)(2,1)} %constant.40.clone.table_hbm, bf16[256,1024]{1,0:T(8,128)(2,1)} %constant.41.clone.halves_hbm), custom_call_target="tpu_custom_call" | custom-call | flops 1610612736 | bytes 2621440 | tf_op jit(solution)/shard_map/transform/pallas_call | solution.py:180
  5.9 0.0 copy-start.2
  5.9 0.0 copy-start.3
  5.9 0.0 copy-start.4
  5.9 15.5 %all-to-all-start = ((bf16[64,8,1152]{2,1,0:T(8,128)(2,1)}), bf16[64,8,1152]{2,1,0:T(8,128)(2,1)S(1)}, u32[]{:S(2)}, u32[]{:S(2)}) async-start(bf16[64,8,1152]{2,1,0:T(8,128)(2,1)} %bitcast.22), calls=%async_computation | async-start | bytes 2359296 | tf_op jit(solution)/shard_map/all_to_all | solution.py:548
  21.4 0.0 copy-done.2
  21.4 0.0 copy-done.3
  21.4 0.1 prepare.1.lookup_ref
  21.6 0.0 copy-done.4
  21.6 26.5 %all_gather.3.volume_ref = bf16[256,1024]{1,0:T(8,128)(2,1)S(1)} all-gather(bf16[32,1024]{1,0:T(8,128)(2,1)S(1)} %bitcast.23), channel_id=1, replica_groups=mesh['img'=64,'vol'=8] {'vol'}, dimensions={0}, use_global_device_ids=true | all-gather | bytes 589824 | tf_op jit(solution)/shard_map/all_gather | solution.py:551
  48.1 4.5 %all-to-all-done = bf16[64,8,1152]{2,1,0:T(8,128)(2,1)S(1)} async-done(((bf16[64,8,1152]{2,1,0:T(8,128)(2,1)}), bf16[64,8,1152]{2,1,0:T(8,128)(2,1)S(1)}, u32[]{:S(2)}, u32[]{:S(2)}) %all-to-all-start) | async-done | bytes 1179680 | tf_op jit(solution)/shard_map/all_to_all | solution.py:548
  52.6 4.3 %compare.4 = (bf16[512,1024]{1,0:T(8,128)(2,1)S(1)}, bf16[256,256]{1,0:T(8,128)(2,1)S(1)}, f32[128,128]{1,0:T(8,128)}, f32[64,128]{1,0:T(8,128)S(1)}) custom-call(s32[1]{0:T(128)} %bitcast.1.slot_ref, bf16[512,1152]{1,0:T(8,128)(2,1)S(1)} %bitcast.16, bf16[256,768]{1,0:T(8,128)(2,1)S(1)} %prepare.1.lookup_ref, bf16[256,1024]{1,0:T(8,128)(2,1)S(1)} %all_gather.3.volume_ref), custom_call_target="tpu_custom_call" | custom-call | flops 2147483648 | bytes 5242880 | tf_op jit(solution)/shard_map/compare/pallas_call | solution.py:317
  56.9 6.8 %all-to-all-start.1 = ((f32[64,2,128]{2,1,0:T(2,128)}), f32[64,2,128]{2,1,0:T(2,128)S(1)}, u32[]{:S(2)}, u32[]{:S(2)}) async-start(f32[64,2,128]{2,1,0:T(2,128)} %bitcast.8), calls=%async_computation.1 | async-start | bytes 131072 | tf_op jit(solution)/shard_map/all_to_all | solution.py:555
  63.6 1.1 %squares.1 = (bf16[512,384]{1,0:T(8,128)(2,1)S(1)}, f32[1,128]{1,0:T(1,128)S(1)}) custom-call(s32[1]{0:T(128)} %bitcast.1.slot_ref, f32[64,128]{1,0:T(8,128)S(1)} %get-tuple-element.19.about_ref), custom_call_target="tpu_custom_call" | custom-call | flops 134217728 | bytes 1048576 | tf_op jit(solution)/shard_map/squares/pallas_call | solution.py:357
  64.7 8.3 %all-to-all-done.1 = f32[64,2,128]{2,1,0:T(2,128)S(1)} async-done(((f32[64,2,128]{2,1,0:T(2,128)}), f32[64,2,128]{2,1,0:T(2,128)S(1)}, u32[]{:S(2)}, u32[]{:S(2)}) %all-to-all-start.1) | async-done | bytes 65568 | tf_op jit(solution)/shard_map/all_to_all | solution.py:555
  73.0 1.0 %project.1 = (f32[8,128]{1,0:T(8,128)S(1)}, bf16[128,512]{1,0:T(8,128)(2,1)S(1)}, bf16[4,336,128]{2,1,0:T(8,128)(2,1)S(1)}) custom-call(s32[1]{0:T(128)} %bitcast.core_ref, f32[128,128]{1,0:T(8,128)S(1)} %bitcast.17, f32[1,128]{1,0:T(1,128)S(1)} %get-tuple-element.20.noise_ref, bf16[256,256]{1,0:T(8,128)(2,1)S(1)} %get-tuple-element.21.picks_ref, ...), custom_call_target="tpu_custom_call" | custom-call | flops 268435456 | bytes 4194304 | tf_op jit(solution)/shard_map/project/pallas_call | solution.py:439
  74.0 3.8 %collective-permute-start = (bf16[4,336,128]{2,1,0:T(8,128)(2,1)S(1)}, bf16[4,336,128]{2,1,0:T(8,128)(2,1)S(1)}, u32[]{:S(2)}, u32[]{:S(2)}) collective-permute-start(bf16[4,336,128]{2,1,0:T(8,128)(2,1)S(1)} %get-tuple-element.26), channel_id=1, source_target_pairs={{0,1},{1,0},{2,3},{3,2},{4,5},{5,4},{6,7},{7,6},{8,9},{9,8},{10,11... | collective-permute-start | bytes 1032200 | tf_op jit(solution)/shard_map/ppermute | solution.py:564
  77.9 0.1 reshape.55
  77.9 0.0 copy-start
  77.9 0.0 copy-start.1
  77.9 0.5 keep_own.1.keep_ref
  78.4 0.7 collective-permute-done.got_ref
  79.1 0.1 middle.1
  79.2 6.6 %collective-permute-start.1 = (bf16[336,128]{1,0:T(8,128)(2,1)S(1)}, bf16[336,128]{1,0:T(8,128)(2,1)S(1)}, u32[]{:S(2)}, u32[]{:S(2)}) collective-permute-start(bf16[336,128]{1,0:T(8,128)(2,1)S(1)} %get-tuple-element.28), channel_id=1, source_target_pairs={{0,4},{1,5},{2,6},{3,7},{4,0},{5,1},{6,2},{7,3},{8,12},{9,13},{10,... | collective-permute-start | bytes 258056 | tf_op jit(solution)/shard_map/ppermute | solution.py:568
  85.7 2.4 %collective-permute-start.2 = (bf16[336,128]{1,0:T(8,128)(2,1)S(1)}, bf16[336,128]{1,0:T(8,128)(2,1)S(1)}, u32[]{:S(2)}, u32[]{:S(2)}) collective-permute-start(bf16[336,128]{1,0:T(8,128)(2,1)S(1)} %get-tuple-element.29), channel_id=1, source_target_pairs={{0,2},{1,3},{2,4},{3,5},{4,6},{5,7},{6,0},{7,1},{8,10},{9,11},{10,... | collective-permute-start | bytes 258056 | tf_op jit(solution)/shard_map/ppermute | solution.py:568
  88.2 5.0 %collective-permute-start.3 = (bf16[336,128]{1,0:T(8,128)(2,1)S(1)}, bf16[336,128]{1,0:T(8,128)(2,1)S(1)}, u32[]{:S(2)}, u32[]{:S(2)}) collective-permute-start(bf16[336,128]{1,0:T(8,128)(2,1)S(1)} %get-tuple-element.30), channel_id=1, source_target_pairs={{0,6},{1,7},{2,0},{3,1},{4,2},{5,3},{6,4},{7,5},{8,14},{9,15},{10,... | collective-permute-start | bytes 258056 | tf_op jit(solution)/shard_map/ppermute | solution.py:568
  93.1 0.1 constant_dynamic-slice_fusion
  93.2 0.6 copy.15
  93.8 0.0 collective-permute-done.1.refs_0_
  93.8 0.0 collective-permute-done.2.refs_1_
  93.8 3.0 %collective-permute-done.3.refs_2_ = bf16[336,128]{1,0:T(8,128)(2,1)S(1)} collective-permute-done((bf16[336,128]{1,0:T(8,128)(2,1)S(1)}, bf16[336,128]{1,0:T(8,128)(2,1)S(1)}, u32[]{:S(2)}, u32[]{:S(2)}) %collective-permute-start.3) | collective-permute-done | bytes 86048 | tf_op jit(solution)/shard_map/ppermute | solution.py:568
  96.8 0.0 copy-done
  96.8 0.0 copy-done.1
  96.8 0.9 finish.1
  (1 shorter events, 0.0 us)
Async XLA Ops:
  5.9 15.5 %copy-start.2 = (s32[2,768,8]{1,2,0:T(8,128)S(1)}, s32[2,768,8]{1,2,0:T(8,128)}, u32[]{:S(2)}) copy-start(s32[2,768,8]{1,2,0:T(8,128)} %param.15) | copy-start | bytes 147460
  5.9 15.5 %copy-start.3 = (bf16[2,768,8]{1,2,0:T(8,128)(2,1)S(1)}, bf16[2,768,8]{1,2,0:T(8,128)(2,1)}, u32[]{:S(2)}) copy-start(bf16[2,768,8]{1,2,0:T(8,128)(2,1)} %param.16) | copy-start | bytes 73732
  5.9 15.7 %copy-start.4 = (bf16[4,8,1024]{2,1,0:T(8,128)(2,1)S(1)}, bf16[4,8,1024]{2,1,0:T(8,128)(2,1)}, u32[]{:S(2)}) copy-start(bf16[4,8,1024]{2,1,0:T(8,128)(2,1)} %param.17) | copy-start | bytes 196612
  5.9 46.7 %all-to-all-start = ((bf16[64,8,1152]{2,1,0:T(8,128)(2,1)}), bf16[64,8,1152]{2,1,0:T(8,128)(2,1)S(1)}, u32[]{:S(2)}, u32[]{:S(2)}) async-start(bf16[64,8,1152]{2,1,0:T(8,128)(2,1)} %bitcast.22), calls=%async_computation | async-start | bytes 2359296 | tf_op jit(solution)/shard_map/all_to_all | solution.py:548
  56.9 16.1 %all-to-all-start.1 = ((f32[64,2,128]{2,1,0:T(2,128)}), f32[64,2,128]{2,1,0:T(2,128)S(1)}, u32[]{:S(2)}, u32[]{:S(2)}) async-start(f32[64,2,128]{2,1,0:T(2,128)} %bitcast.8), calls=%async_computation.1 | async-start | bytes 131072 | tf_op jit(solution)/shard_map/all_to_all | solution.py:555
  74.0 5.1 %collective-permute-start = (bf16[4,336,128]{2,1,0:T(8,128)(2,1)S(1)}, bf16[4,336,128]{2,1,0:T(8,128)(2,1)S(1)}, u32[]{:S(2)}, u32[]{:S(2)}) collective-permute-start(bf16[4,336,128]{2,1,0:T(8,128)(2,1)S(1)} %get-tuple-element.26), channel_id=1, source_target_pairs={{0,1},{1,0},{2,3},{3,2},{4,5},{5,4},{6,7},{7,6},{8,9},{9,8},{10,11... | collective-permute-start | bytes 1032200 | tf_op jit(solution)/shard_map/ppermute | solution.py:564
  77.9 18.9 %copy-start = (f32[4,8,1024]{2,1,0:T(8,128)S(1)}, f32[4,8,1024]{2,1,0:T(8,128)}, u32[]{:S(2)}) copy-start(f32[4,8,1024]{2,1,0:T(8,128)} %param.18) | copy-start | bytes 393220
  77.9 18.9 %copy-start.1 = (f32[4,8,512]{2,1,0:T(8,128)S(1)}, f32[4,8,512]{2,1,0:T(8,128)}, u32[]{:S(2)}) copy-start(f32[4,8,512]{2,1,0:T(8,128)} %param.19) | copy-start | bytes 196612
  79.2 14.7 %collective-permute-start.1 = (bf16[336,128]{1,0:T(8,128)(2,1)S(1)}, bf16[336,128]{1,0:T(8,128)(2,1)S(1)}, u32[]{:S(2)}, u32[]{:S(2)}) collective-permute-start(bf16[336,128]{1,0:T(8,128)(2,1)S(1)} %get-tuple-element.28), channel_id=1, source_target_pairs={{0,4},{1,5},{2,6},{3,7},{4,0},{5,1},{6,2},{7,3},{8,12},{9,13},{10,... | collective-permute-start | bytes 258056 | tf_op jit(solution)/shard_map/ppermute | solution.py:568
  85.7 8.1 %collective-permute-start.2 = (bf16[336,128]{1,0:T(8,128)(2,1)S(1)}, bf16[336,128]{1,0:T(8,128)(2,1)S(1)}, u32[]{:S(2)}, u32[]{:S(2)}) collective-permute-start(bf16[336,128]{1,0:T(8,128)(2,1)S(1)} %get-tuple-element.29), channel_id=1, source_target_pairs={{0,2},{1,3},{2,4},{3,5},{4,6},{5,7},{6,0},{7,1},{8,10},{9,11},{10,... | collective-permute-start | bytes 258056 | tf_op jit(solution)/shard_map/ppermute | solution.py:568
  88.2 8.7 %collective-permute-start.3 = (bf16[336,128]{1,0:T(8,128)(2,1)S(1)}, bf16[336,128]{1,0:T(8,128)(2,1)S(1)}, u32[]{:S(2)}, u32[]{:S(2)}) collective-permute-start(bf16[336,128]{1,0:T(8,128)(2,1)S(1)} %get-tuple-element.30), channel_id=1, source_target_pairs={{0,6},{1,7},{2,0},{3,1},{4,2},{5,3},{6,4},{7,5},{8,14},{9,15},{10,... | collective-permute-start | bytes 258056 | tf_op jit(solution)/shard_map/ppermute | solution.py:568

commit v9 on v6

--- a/solution.py
+++ b/solution.py
@@ -472,13 +472,13 @@
 
 def middle_kernel(high_ref, keep_ref, got_ref, own_ref, *send_refs):
     pairs = keep_ref.shape[0]
-    for ahead in range(pairs):
-        at = (high_ref[0] + ahead) % pairs
+    for apart in range(pairs):
+        at = high_ref[0] ^ apart
         total = keep_ref[at].astype(jnp.float32) + got_ref[at].astype(jnp.float32)
-        if ahead == 0:
+        if apart == 0:
             own_ref[...] = total
         else:
-            send_refs[ahead - 1][...] = total.astype(jnp.bfloat16)
+            send_refs[apart - 1][...] = total.astype(jnp.bfloat16)
 
 
 def middle(high, keep, got):
@@ -495,46 +495,45 @@
     )(high, keep, got)
 
 
-def spread_lines(total, slab, npix, precision):
+def spread_lines(total, slab, npix):
     half = npix // 2
     tiles = [total[at : at + slab] for at in range(0, total.shape[0] - slab // 2, slab)]
     data = jnp.concatenate(tiles[: 2 * npix // 128], 1)
     lower = jnp.concatenate(tiles[2 * npix // 128 :], 1)
     source = lax.broadcasted_iota(jnp.int32, (half, half), 0)
     target = lax.broadcasted_iota(jnp.int32, (half, half), 1)
-    mirror = jnp.where(source + target == half, 1.0, 0.0).astype(total.dtype)
-    upper = jnp.dot(lower, mirror, preferred_element_type=jnp.float32, precision=precision)
-    last = total[total.shape[0] - slab // 2 :].astype(jnp.float32)
+    mirror = jnp.where(source + target == half, 1.0, 0.0)
+    upper = jnp.dot(lower, mirror, preferred_element_type=jnp.float32, precision=lax.Precision.HIGHEST)
+    last = total[total.shape[0] - slab // 2 :]
     last = jnp.concatenate([last[:, :1], last[:, 1:2]], 0)
     lane = lax.broadcasted_iota(jnp.int32, (slab, half), 1)
     upper = jnp.where(lane == 0, last, upper)
-    return data.astype(jnp.float32), lower.astype(jnp.float32), upper
-
-
-def finish_kernel(precision, first_ref, *refs):
+    return data, lower, upper
+
+
+def finish_kernel(own_ref, *refs):
     data_ref, weight_ref, data_out, weight_out = refs[-4:]
     slab, npix = weight_ref.shape
-    total = first_ref[...]
+    total = own_ref[...]
     for part_ref in refs[:-4]:
         total = total + part_ref[...].astype(jnp.float32)
-    data, lower, upper = spread_lines(total, slab, npix, precision)
+    data, lower, upper = spread_lines(total, slab, npix)
     data_out[...] = data_ref[...] + data
     weight_out[:, : npix // 2] = weight_ref[:, : npix // 2] + lower
     weight_out[:, npix // 2 :] = weight_ref[:, npix // 2 :] + upper
 
 
-def finish(first, parts, data_old, weight_old):
-    exact = first.dtype == jnp.bfloat16
-    return pl.pallas_call(
-        functools.partial(finish_kernel, None if exact else lax.Precision.HIGHEST),
+def finish(own, parts, data_old, weight_old):
+    return pl.pallas_call(
+        finish_kernel,
         out_shape=(
             jax.ShapeDtypeStruct(data_old.shape, jnp.float32),
             jax.ShapeDtypeStruct(weight_old.shape, jnp.float32),
         ),
         compiler_params=params(SMALL),
         cost_estimate=cost(1 << 20, 2 << 20),
-        name="finish" if exact else "collect",
-    )(first, *parts, data_old, weight_old)
+        name="finish",
+    )(own, *parts, data_old, weight_old)
 
 
 def on_device(images, defocus, noise, orient, planes, weights, volume, data_old, weight_old):
@@ -571,16 +570,15 @@
     keep = keep_own(share, filtered, square, pairs)
     own, *sends = middle((place // 2).reshape(1), keep, got)
     parts = [
-        lax.ppermute(part, "vol", [(v, (v + 2 * ahead) % n_vol) for v in range(n_vol)])
-        for ahead, part in enumerate(sends, 1)
+        lax.ppermute(sends[apart - 1], "vol", [(v, v ^ (2 * apart)) for v in range(n_vol)])
+        for apart in (2, 3, 1)
     ]
     data, weight = finish(
         own,
-        parts[:-1],
+        parts,
         data_old.reshape(slab * rows, 2 * npix),
         weight_old.reshape(slab * rows, npix),
     )
-    data, weight = finish(parts[-1], [], data, weight)
     return (mine, data.reshape(data_old.shape), weight.reshape(weight_old.shape))
 
 

time: 98.7 us -> 96.9 us (0.982)
  starting transfers between devices: 38.8 us -> 37.5 us
    ppermute x3, starting transfers between devices: 12.7 us -> 11.4 us  [on_device(): lax.ppermute(sends[apart - 1], 'vol', [(v, v ^ 2 * apart) for v in range(...]
  transfers between devices with their start and end apart: 6 -> 6, of which waited for: 4 -> 5; matrix products, arithmetic and copies ran while one was open for 1% -> 1% of each run, Pallas kernels for 2% -> 2%
where the time goes in v9:
time: 96.9 us; the launch traced here: 96.4 us
  starting transfers between devices  37.5 us (39%)
  blocking collectives  26.5 us (27%)
  waiting for transfers between devices  18.1 us (19%)
  Pallas kernels  11.5 us (12%)
  between operations  2.09 us (2%)
    all_gather x1, blocking collectives, on_device(): lax.all_gather(volume.reshape(slab * rows, 2 * npix), 'vol', axis=0, tile...  26.5 us
    all_to_all x1, starting transfers between devices, on_device(): lax.all_to_all(fourier.reshape(n_img, rows, 2 * npix + META), 'img', spli...  15.5 us
    ppermute x3, starting transfers between devices, on_device(): lax.ppermute(sends[apart - 1], 'vol', [(v, v ^ 2 * apart) for v in range(...  11.4 us
    all_to_all x1, waiting for transfers between devices, on_device(): lax.all_to_all(part.reshape(n_img, 2, 2 * n_img), 'img', split_axis=0, co...  8.28 us
    all_to_all x1, starting transfers between devices, on_device(): lax.all_to_all(part.reshape(n_img, 2, 2 * n_img), 'img', split_axis=0, co...  6.76 us
    ppermute x3, waiting for transfers between devices, on_device(): lax.ppermute(sends[apart - 1], 'vol', [(v, v ^ 2 * apart) for v in range(...  4.65 us
    all_to_all x1, waiting for transfers between devices, on_device(): lax.all_to_all(fourier.reshape(n_img, rows, 2 * npix + META), 'img', spli...  4.49 us
    pallas_call x1, Pallas kernels, compare(): pl.pallas_call(functools.partial(compare_kernel, ori, rows), in_specs=[sc...  4.21 us
  transfers between devices with their start and end apart: 6, of which 5 were waited for; matrix products, arithmetic and copies ran while one was open for 1% of the time, Pallas kernels for 2%

profile of v9, /device:TPU:1, one launch (start us, length us, event | category | flops | bytes accessed | tf_op | source)
XLA Modules:
  0.0 96.4 jit_solution(10551730568825617534)
XLA Ops:
  1.9 3.7 %transform.1 = bf16[512,1152]{1,0:T(8,128)(2,1)} custom-call(s32[1,4]{1,0:T(1,128)} %orient_hbm.1, f32[1]{0:T(128)S(6)} %copy.16.defocus_hbm, f32[1]{0:T(128)S(6)} %copy.17.noise_hbm, bf16[512,512]{1,0:T(8,128)(2,1)} %bitcast.25, bf16[512,1024]{1,0:T(8,128)(2,1)} %constant.40.clone.table_hbm, bf16[256,1024]{1,0:T(8,128)(2,1)} %constant.41.clone.halves_hbm), custom_call_target="tpu_custom_call" | custom-call | flops 1610612736 | bytes 2621440 | tf_op jit(solution)/shard_map/transform/pallas_call | solution.py:185
  5.6 0.0 copy-start.2
  5.6 0.0 copy-start.3
  5.6 0.0 copy-start.4
  5.6 15.5 %all-to-all-start = ((bf16[64,8,1152]{2,1,0:T(8,128)(2,1)}), bf16[64,8,1152]{2,1,0:T(8,128)(2,1)S(1)}, u32[]{:S(2)}, u32[]{:S(2)}) async-start(bf16[64,8,1152]{2,1,0:T(8,128)(2,1)} %bitcast.22), calls=%async_computation | async-start | bytes 2359296 | tf_op jit(solution)/shard_map/all_to_all | solution.py:553
  21.1 0.0 copy-done.2
  21.1 0.0 copy-done.3
  21.1 0.1 prepare.1.lookup_ref
  21.3 0.0 copy-done.4
  21.3 26.5 %all_gather.3.volume_ref = bf16[256,1024]{1,0:T(8,128)(2,1)S(1)} all-gather(bf16[32,1024]{1,0:T(8,128)(2,1)S(1)} %bitcast.23), channel_id=1, replica_groups=mesh['img'=64,'vol'=8] {'vol'}, dimensions={0}, use_global_device_ids=true | all-gather | bytes 589824 | tf_op jit(solution)/shard_map/all_gather | solution.py:556
  47.8 4.5 %all-to-all-done = bf16[64,8,1152]{2,1,0:T(8,128)(2,1)S(1)} async-done(((bf16[64,8,1152]{2,1,0:T(8,128)(2,1)}), bf16[64,8,1152]{2,1,0:T(8,128)(2,1)S(1)}, u32[]{:S(2)}, u32[]{:S(2)}) %all-to-all-start) | async-done | bytes 1179680 | tf_op jit(solution)/shard_map/all_to_all | solution.py:553
  52.3 4.2 %compare.4 = (bf16[512,1024]{1,0:T(8,128)(2,1)S(1)}, bf16[256,256]{1,0:T(8,128)(2,1)S(1)}, f32[128,128]{1,0:T(8,128)}, f32[64,128]{1,0:T(8,128)S(1)}) custom-call(s32[1]{0:T(128)} %bitcast.1.slot_ref, bf16[512,1152]{1,0:T(8,128)(2,1)S(1)} %bitcast.16, bf16[256,768]{1,0:T(8,128)(2,1)S(1)} %prepare.1.lookup_ref, bf16[256,1024]{1,0:T(8,128)(2,1)S(1)} %all_gather.3.volume_ref), custom_call_target="tpu_custom_call" | custom-call | flops 2147483648 | bytes 5242880 | tf_op jit(solution)/shard_map/compare/pallas_call | solution.py:322
  56.5 6.8 %all-to-all-start.1 = ((f32[64,2,128]{2,1,0:T(2,128)}), f32[64,2,128]{2,1,0:T(2,128)S(1)}, u32[]{:S(2)}, u32[]{:S(2)}) async-start(f32[64,2,128]{2,1,0:T(2,128)} %bitcast.8), calls=%async_computation.1 | async-start | bytes 131072 | tf_op jit(solution)/shard_map/all_to_all | solution.py:560
  63.3 1.1 %squares.1 = (bf16[512,384]{1,0:T(8,128)(2,1)S(1)}, f32[1,128]{1,0:T(1,128)S(1)}) custom-call(s32[1]{0:T(128)} %bitcast.1.slot_ref, f32[64,128]{1,0:T(8,128)S(1)} %get-tuple-element.19.about_ref), custom_call_target="tpu_custom_call" | custom-call | flops 134217728 | bytes 1048576 | tf_op jit(solution)/shard_map/squares/pallas_call | solution.py:362
  64.3 8.3 %all-to-all-done.1 = f32[64,2,128]{2,1,0:T(2,128)S(1)} async-done(((f32[64,2,128]{2,1,0:T(2,128)}), f32[64,2,128]{2,1,0:T(2,128)S(1)}, u32[]{:S(2)}, u32[]{:S(2)}) %all-to-all-start.1) | async-done | bytes 65568 | tf_op jit(solution)/shard_map/all_to_all | solution.py:560
  72.6 1.0 %project.1 = (f32[8,128]{1,0:T(8,128)S(1)}, bf16[128,512]{1,0:T(8,128)(2,1)S(1)}, bf16[4,336,128]{2,1,0:T(8,128)(2,1)S(1)}) custom-call(s32[1]{0:T(128)} %bitcast.core_ref, f32[128,128]{1,0:T(8,128)S(1)} %bitcast.17, f32[1,128]{1,0:T(1,128)S(1)} %get-tuple-element.20.noise_ref, bf16[256,256]{1,0:T(8,128)(2,1)S(1)} %get-tuple-element.21.picks_ref, ...), custom_call_target="tpu_custom_call" | custom-call | flops 268435456 | bytes 4194304 | tf_op jit(solution)/shard_map/project/pallas_call | solution.py:444
  73.6 3.8 %collective-permute-start = (bf16[4,336,128]{2,1,0:T(8,128)(2,1)S(1)}, bf16[4,336,128]{2,1,0:T(8,128)(2,1)S(1)}, u32[]{:S(2)}, u32[]{:S(2)}) collective-permute-start(bf16[4,336,128]{2,1,0:T(8,128)(2,1)S(1)} %get-tuple-element.26), channel_id=1, source_target_pairs={{0,1},{1,0},{2,3},{3,2},{4,5},{5,4},{6,7},{7,6},{8,9},{9,8},{10,11... | collective-permute-start | bytes 1032200 | tf_op jit(solution)/shard_map/ppermute | solution.py:569
  77.5 0.1 reshape.55
  77.6 0.0 copy-start
  77.6 0.0 copy-start.1
  77.6 0.5 keep_own.1.keep_ref
  78.0 0.7 collective-permute-done.got_ref
  78.7 0.1 middle.1
  78.8 6.6 %collective-permute-start.1 = (bf16[336,128]{1,0:T(8,128)(2,1)S(1)}, bf16[336,128]{1,0:T(8,128)(2,1)S(1)}, u32[]{:S(2)}, u32[]{:S(2)}) collective-permute-start(bf16[336,128]{1,0:T(8,128)(2,1)S(1)} %get-tuple-element.28), channel_id=1, source_target_pairs={{0,4},{1,5},{2,6},{3,7},{4,0},{5,1},{6,2},{7,3},{8,12},{9,13},{10,... | collective-permute-start | bytes 258056 | tf_op jit(solution)/shard_map/ppermute | solution.py:573
  85.4 2.9 %collective-permute-start.2 = (bf16[336,128]{1,0:T(8,128)(2,1)S(1)}, bf16[336,128]{1,0:T(8,128)(2,1)S(1)}, u32[]{:S(2)}, u32[]{:S(2)}) collective-permute-start(bf16[336,128]{1,0:T(8,128)(2,1)S(1)} %get-tuple-element.29), channel_id=1, source_target_pairs={{0,6},{1,7},{2,4},{3,5},{4,2},{5,3},{6,0},{7,1},{8,14},{9,15},{10,... | collective-permute-start | bytes 258056 | tf_op jit(solution)/shard_map/ppermute | solution.py:573
  88.2 1.9 %collective-permute-start.3 = (bf16[336,128]{1,0:T(8,128)(2,1)S(1)}, bf16[336,128]{1,0:T(8,128)(2,1)S(1)}, u32[]{:S(2)}, u32[]{:S(2)}) collective-permute-start(bf16[336,128]{1,0:T(8,128)(2,1)S(1)} %get-tuple-element.30), channel_id=1, source_target_pairs={{0,2},{1,3},{2,0},{3,1},{4,6},{5,7},{6,4},{7,5},{8,10},{9,11},{10,... | collective-permute-start | bytes 258056 | tf_op jit(solution)/shard_map/ppermute | solution.py:573
  90.2 0.1 constant_dynamic-slice_fusion
  90.3 0.6 copy.15
  90.9 0.0 collective-permute-done.1.refs_0_
  90.9 2.8 %collective-permute-done.2.refs_1_ = bf16[336,128]{1,0:T(8,128)(2,1)S(1)} collective-permute-done((bf16[336,128]{1,0:T(8,128)(2,1)S(1)}, bf16[336,128]{1,0:T(8,128)(2,1)S(1)}, u32[]{:S(2)}, u32[]{:S(2)}) %collective-permute-start.2) | collective-permute-done | bytes 86048 | tf_op jit(solution)/shard_map/ppermute | solution.py:573
  93.7 1.8 %collective-permute-done.3.refs_2_ = bf16[336,128]{1,0:T(8,128)(2,1)S(1)} collective-permute-done((bf16[336,128]{1,0:T(8,128)(2,1)S(1)}, bf16[336,128]{1,0:T(8,128)(2,1)S(1)}, u32[]{:S(2)}, u32[]{:S(2)}) %collective-permute-start.3) | collective-permute-done | bytes 86048 | tf_op jit(solution)/shard_map/ppermute | solution.py:573
  95.5 0.0 copy-done
  95.5 0.0 copy-done.1
  95.5 0.9 finish.1
  (1 shorter events, 0.0 us)
Async XLA Ops:
  5.6 15.5 %copy-start.2 = (s32[2,768,8]{1,2,0:T(8,128)S(1)}, s32[2,768,8]{1,2,0:T(8,128)}, u32[]{:S(2)}) copy-start(s32[2,768,8]{1,2,0:T(8,128)} %param.15) | copy-start | bytes 147460
  5.6 15.5 %copy-start.3 = (bf16[2,768,8]{1,2,0:T(8,128)(2,1)S(1)}, bf16[2,768,8]{1,2,0:T(8,128)(2,1)}, u32[]{:S(2)}) copy-start(bf16[2,768,8]{1,2,0:T(8,128)(2,1)} %param.16) | copy-start | bytes 73732
  5.6 15.7 %copy-start.4 = (bf16[4,8,1024]{2,1,0:T(8,128)(2,1)S(1)}, bf16[4,8,1024]{2,1,0:T(8,128)(2,1)}, u32[]{:S(2)}) copy-start(bf16[4,8,1024]{2,1,0:T(8,128)(2,1)} %param.17) | copy-start | bytes 196612
  5.6 46.6 %all-to-all-start = ((bf16[64,8,1152]{2,1,0:T(8,128)(2,1)}), bf16[64,8,1152]{2,1,0:T(8,128)(2,1)S(1)}, u32[]{:S(2)}, u32[]{:S(2)}) async-start(bf16[64,8,1152]{2,1,0:T(8,128)(2,1)} %bitcast.22), calls=%async_computation | async-start | bytes 2359296 | tf_op jit(solution)/shard_map/all_to_all | solution.py:553
  56.5 16.1 %all-to-all-start.1 = ((f32[64,2,128]{2,1,0:T(2,128)}), f32[64,2,128]{2,1,0:T(2,128)S(1)}, u32[]{:S(2)}, u32[]{:S(2)}) async-start(f32[64,2,128]{2,1,0:T(2,128)} %bitcast.8), calls=%async_computation.1 | async-start | bytes 131072 | tf_op jit(solution)/shard_map/all_to_all | solution.py:560
  73.6 5.1 %collective-permute-start = (bf16[4,336,128]{2,1,0:T(8,128)(2,1)S(1)}, bf16[4,336,128]{2,1,0:T(8,128)(2,1)S(1)}, u32[]{:S(2)}, u32[]{:S(2)}) collective-permute-start(bf16[4,336,128]{2,1,0:T(8,128)(2,1)S(1)} %get-tuple-element.26), channel_id=1, source_target_pairs={{0,1},{1,0},{2,3},{3,2},{4,5},{5,4},{6,7},{7,6},{8,9},{9,8},{10,11... | collective-permute-start | bytes 1032200 | tf_op jit(solution)/shard_map/ppermute | solution.py:569
  77.6 18.0 %copy-start = (f32[4,8,1024]{2,1,0:T(8,128)S(1)}, f32[4,8,1024]{2,1,0:T(8,128)}, u32[]{:S(2)}) copy-start(f32[4,8,1024]{2,1,0:T(8,128)} %param.18) | copy-start | bytes 393220
  77.6 18.0 %copy-start.1 = (f32[4,8,512]{2,1,0:T(8,128)S(1)}, f32[4,8,512]{2,1,0:T(8,128)}, u32[]{:S(2)}) copy-start(f32[4,8,512]{2,1,0:T(8,128)} %param.19) | copy-start | bytes 196612
  78.8 12.1 %collective-permute-start.1 = (bf16[336,128]{1,0:T(8,128)(2,1)S(1)}, bf16[336,128]{1,0:T(8,128)(2,1)S(1)}, u32[]{:S(2)}, u32[]{:S(2)}) collective-permute-start(bf16[336,128]{1,0:T(8,128)(2,1)S(1)} %get-tuple-element.28), channel_id=1, source_target_pairs={{0,4},{1,5},{2,6},{3,7},{4,0},{5,1},{6,2},{7,3},{8,12},{9,13},{10,... | collective-permute-start | bytes 258056 | tf_op jit(solution)/shard_map/ppermute | solution.py:573
  85.4 8.3 %collective-permute-start.2 = (bf16[336,128]{1,0:T(8,128)(2,1)S(1)}, bf16[336,128]{1,0:T(8,128)(2,1)S(1)}, u32[]{:S(2)}, u32[]{:S(2)}) collective-permute-start(bf16[336,128]{1,0:T(8,128)(2,1)S(1)} %get-tuple-element.29), channel_id=1, source_target_pairs={{0,6},{1,7},{2,4},{3,5},{4,2},{5,3},{6,0},{7,1},{8,14},{9,15},{10,... | collective-permute-start | bytes 258056 | tf_op jit(solution)/shard_map/ppermute | solution.py:573
  88.2 7.3 %collective-permute-start.3 = (bf16[336,128]{1,0:T(8,128)(2,1)S(1)}, bf16[336,128]{1,0:T(8,128)(2,1)S(1)}, u32[]{:S(2)}, u32[]{:S(2)}) collective-permute-start(bf16[336,128]{1,0:T(8,128)(2,1)S(1)} %get-tuple-element.30), channel_id=1, source_target_pairs={{0,2},{1,3},{2,0},{3,1},{4,6},{5,7},{6,4},{7,5},{8,10},{9,11},{10,... | collective-permute-start | bytes 258056 | tf_op jit(solution)/shard_map/ppermute | solution.py:573

commit v10 on v9

--- a/solution.py
+++ b/solution.py
@@ -279,23 +279,33 @@
             own_row(every, rows).reshape(many, deep).astype(jnp.bfloat16)
         )
     defocus, row_square = line_geometry(meta.astype(jnp.float32), ori, rows, many, npix, slot_ref[0])
-    for number, start in enumerate(range(0, npix, 128)):
-        real = slice(start, start + 128)
-        imag = slice(npix + start, npix + start + 128)
-        planes = jnp.concatenate([volume_ref[:, real], volume_ref[:, imag]], 1)
-        ctf = contrast(defocus, row_square, start, 128, npix)
-        for part in (real, imag):
-            filtered_ref[:, part] = (ctf * fourier_ref[:, part].astype(jnp.float32)).astype(jnp.bfloat16)
-        square = ctf * ctf
-        for o in range(ori):
-            section = jnp.dot(
+    def sections(start):
+        planes = jnp.concatenate(
+            [volume_ref[:, at : at + 128] for at in (start, npix + start)], 1
+        )
+        return [
+            jnp.dot(
                 mix_ref[o * many : (o + 1) * many, :], planes, preferred_element_type=jnp.float32
             )
-            section = section * section
+            for o in range(ori)
+        ]
+
+    current = sections(0)
+    for start in range(0, npix, 128):
+        ctf = contrast(defocus, row_square, start, 128, npix)
+        for at in (start, npix + start):
+            filtered_ref[:, at : at + 128] = (
+                ctf * fourier_ref[:, at : at + 128].astype(jnp.float32)
+            ).astype(jnp.bfloat16)
+        square = ctf * ctf
+        following = sections(start + 128) if start + 128 < npix else None
+        for o in range(ori):
+            section = current[o] * current[o]
             power = square * (section[:, :128] + section[:, 128:])
-            if number:
+            if start:
                 power = power + power_ref[o]
             power_ref[o] = power
+        current = following
 
     found = own_row(same(filtered_ref[...], volume_ref[...]), rows)
     found = jnp.sum(found, axis=1)
@@ -495,45 +505,68 @@
     )(high, keep, got)
 
 
-def spread_lines(total, slab, npix):
-    half = npix // 2
-    tiles = [total[at : at + slab] for at in range(0, total.shape[0] - slab // 2, slab)]
-    data = jnp.concatenate(tiles[: 2 * npix // 128], 1)
-    lower = jnp.concatenate(tiles[2 * npix // 128 :], 1)
+def mirror_columns(lower, last, precision=None):
+    slab, half = lower.shape
     source = lax.broadcasted_iota(jnp.int32, (half, half), 0)
     target = lax.broadcasted_iota(jnp.int32, (half, half), 1)
-    mirror = jnp.where(source + target == half, 1.0, 0.0)
-    upper = jnp.dot(lower, mirror, preferred_element_type=jnp.float32, precision=lax.Precision.HIGHEST)
-    last = total[total.shape[0] - slab // 2 :]
+    mirror = jnp.where(source + target == half, 1.0, 0.0).astype(lower.dtype)
+    upper = jnp.dot(lower, mirror, preferred_element_type=jnp.float32, precision=precision)
+    lane = lax.broadcasted_iota(jnp.int32, (slab, half), 1)
+    return jnp.where(lane == 0, last, upper)
+
+
+def spread_lines(lines, slab, npix):
+    tiles = [lines[at : at + slab] for at in range(0, lines.shape[0] - slab // 2, slab)]
+    last = lines[lines.shape[0] - slab // 2 :].astype(jnp.float32)
     last = jnp.concatenate([last[:, :1], last[:, 1:2]], 0)
-    lane = lax.broadcasted_iota(jnp.int32, (slab, half), 1)
-    upper = jnp.where(lane == 0, last, upper)
-    return data, lower, upper
-
-
-def finish_kernel(own_ref, *refs):
-    data_ref, weight_ref, data_out, weight_out = refs[-4:]
+    count = 2 * npix // 128
+    return jnp.concatenate(tiles[:count], 1), jnp.concatenate(tiles[count:], 1), last
+
+
+def collect_kernel(own_ref, data_ref, weight_ref, data_out, weight_out):
     slab, npix = weight_ref.shape
-    total = own_ref[...]
-    for part_ref in refs[:-4]:
-        total = total + part_ref[...].astype(jnp.float32)
-    data, lower, upper = spread_lines(total, slab, npix)
+    half = npix // 2
+    data, lower, last = spread_lines(own_ref[...], slab, npix)
     data_out[...] = data_ref[...] + data
-    weight_out[:, : npix // 2] = weight_ref[:, : npix // 2] + lower
-    weight_out[:, npix // 2 :] = weight_ref[:, npix // 2 :] + upper
-
-
-def finish(own, parts, data_old, weight_old):
-    return pl.pallas_call(
-        finish_kernel,
+    weight_out[:, :half] = weight_ref[:, :half] + lower
+    weight_out[:, half:] = weight_ref[:, half:] + mirror_columns(
+        lower, last, lax.Precision.HIGHEST
+    )
+
+
+def finish_kernel(*refs):
+    *part_refs, data_ref, weight_ref, data_out, weight_out = refs
+    slab, npix = weight_ref.shape
+    half = npix // 2
+    data = data_ref[...]
+    weight = weight_ref[:, :half]
+    lowers, lasts = [], []
+    for part_ref in part_refs:
+        part, lower, last = spread_lines(part_ref[...], slab, npix)
+        data = data + part.astype(jnp.float32)
+        weight = weight + lower.astype(jnp.float32)
+        lowers.append(lower)
+        lasts.append(last)
+    uppers = mirror_columns(jnp.concatenate(lowers, 0), jnp.concatenate(lasts, 0))
+    upper = weight_ref[:, half:]
+    for number in range(len(part_refs)):
+        upper = upper + uppers[number * slab : (number + 1) * slab]
+    data_out[...] = data
+    weight_out[:, :half] = weight
+    weight_out[:, half:] = upper
+
+
+def add_lines(kernel, name, lines, data, weight):
+    return pl.pallas_call(
+        kernel,
         out_shape=(
-            jax.ShapeDtypeStruct(data_old.shape, jnp.float32),
-            jax.ShapeDtypeStruct(weight_old.shape, jnp.float32),
+            jax.ShapeDtypeStruct(data.shape, jnp.float32),
+            jax.ShapeDtypeStruct(weight.shape, jnp.float32),
         ),
         compiler_params=params(SMALL),
         cost_estimate=cost(1 << 20, 2 << 20),
-        name="finish",
-    )(own, *parts, data_old, weight_old)
+        name=name,
+    )(*lines, data, weight)
 
 
 def on_device(images, defocus, noise, orient, planes, weights, volume, data_old, weight_old):
@@ -571,14 +604,16 @@
     own, *sends = middle((place // 2).reshape(1), keep, got)
     parts = [
         lax.ppermute(sends[apart - 1], "vol", [(v, v ^ (2 * apart)) for v in range(n_vol)])
-        for apart in (2, 3, 1)
+        for apart in (2, 1, 3)
     ]
-    data, weight = finish(
-        own,
-        parts,
+    data, weight = add_lines(
+        collect_kernel,
+        "collect",
+        [own],
         data_old.reshape(slab * rows, 2 * npix),
         weight_old.reshape(slab * rows, npix),
     )
+    data, weight = add_lines(finish_kernel, "finish", parts, data, weight)
     return (mine, data.reshape(data_old.shape), weight.reshape(weight_old.shape))
 
 

time: 96.9 us -> 98.5 us (1.017)
  waiting for transfers between devices: 18.1 us -> 19.6 us
    ppermute x3, waiting for transfers between devices: 4.65 us -> 6.13 us  [on_device(): lax.ppermute(sends[apart - 1], 'vol', [(v, v ^ 2 * apart) for v in range(...]
where the time goes in v10:
time: 98.5 us; the launch traced here: 98.1 us
  starting transfers between devices  37.5 us (38%)
  blocking collectives  26.5 us (27%)
  waiting for transfers between devices  19.6 us (20%)
  Pallas kernels  11.6 us (12%)
  between operations  2.13 us (2%)
    all_gather x1, blocking collectives, on_device(): lax.all_gather(volume.reshape(slab * rows, 2 * npix), 'vol', axis=0, tile...  26.5 us
    all_to_all x1, starting transfers between devices, on_device(): lax.all_to_all(fourier.reshape(n_img, rows, 2 * npix + META), 'img', spli...  15.5 us
    ppermute x3, starting transfers between devices, on_device(): lax.ppermute(sends[apart - 1], 'vol', [(v, v ^ 2 * apart) for v in range(...  11.4 us
    all_to_all x1, waiting for transfers between devices, on_device(): lax.all_to_all(part.reshape(n_img, 2, 2 * n_img), 'img', split_axis=0, co...  8.28 us
    all_to_all x1, starting transfers between devices, on_device(): lax.all_to_all(part.reshape(n_img, 2, 2 * n_img), 'img', split_axis=0, co...  6.77 us
    ppermute x3, waiting for transfers between devices, on_device(): lax.ppermute(sends[apart - 1], 'vol', [(v, v ^ 2 * apart) for v in range(...  6.13 us
    all_to_all x1, waiting for transfers between devices, on_device(): lax.all_to_all(fourier.reshape(n_img, rows, 2 * npix + META), 'img', spli...  4.49 us
    pallas_call x1, Pallas kernels, compare(): pl.pallas_call(functools.partial(compare_kernel, ori, rows), in_specs=[sc...  4.21 us
  transfers between devices with their start and end apart: 6, of which 5 were waited for; matrix products, arithmetic and copies ran while one was open for 1% of the time, Pallas kernels for 2%

profile of v10, /device:TPU:1, one launch (start us, length us, event | category | flops | bytes accessed | tf_op | source)
XLA Modules:
  0.0 98.1 jit_solution(16410954880752953165)
XLA Ops:
  1.9 3.7 %transform.1 = bf16[512,1152]{1,0:T(8,128)(2,1)} custom-call(s32[1,4]{1,0:T(1,128)} %orient_hbm.1, f32[1]{0:T(128)S(6)} %copy.16.defocus_hbm, f32[1]{0:T(128)S(6)} %copy.17.noise_hbm, bf16[512,512]{1,0:T(8,128)(2,1)} %bitcast.25, bf16[512,1024]{1,0:T(8,128)(2,1)} %constant.40.clone.table_hbm, bf16[256,1024]{1,0:T(8,128)(2,1)} %constant.41.clone.halves_hbm), custom_call_target="tpu_custom_call" | custom-call | flops 1610612736 | bytes 2621440 | tf_op jit(solution)/shard_map/transform/pallas_call | solution.py:185
  5.6 0.0 copy-start.2
  5.6 0.0 copy-start.3
  5.6 0.0 copy-start.4
  5.6 15.5 %all-to-all-start = ((bf16[64,8,1152]{2,1,0:T(8,128)(2,1)}), bf16[64,8,1152]{2,1,0:T(8,128)(2,1)S(1)}, u32[]{:S(2)}, u32[]{:S(2)}) async-start(bf16[64,8,1152]{2,1,0:T(8,128)(2,1)} %bitcast.22), calls=%async_computation | async-start | bytes 2359296 | tf_op jit(solution)/shard_map/all_to_all | solution.py:586
  21.1 0.0 copy-done.2
  21.1 0.0 copy-done.3
  21.2 0.1 prepare.1.lookup_ref
  21.3 0.0 copy-done.4
  21.3 26.5 %all_gather.3.volume_ref = bf16[256,1024]{1,0:T(8,128)(2,1)S(1)} all-gather(bf16[32,1024]{1,0:T(8,128)(2,1)S(1)} %bitcast.23), channel_id=1, replica_groups=mesh['img'=64,'vol'=8] {'vol'}, dimensions={0}, use_global_device_ids=true | all-gather | bytes 589824 | tf_op jit(solution)/shard_map/all_gather | solution.py:589
  47.8 4.5 %all-to-all-done = bf16[64,8,1152]{2,1,0:T(8,128)(2,1)S(1)} async-done(((bf16[64,8,1152]{2,1,0:T(8,128)(2,1)}), bf16[64,8,1152]{2,1,0:T(8,128)(2,1)S(1)}, u32[]{:S(2)}, u32[]{:S(2)}) %all-to-all-start) | async-done | bytes 1179680 | tf_op jit(solution)/shard_map/all_to_all | solution.py:586
  52.3 4.2 %compare.4 = (bf16[512,1024]{1,0:T(8,128)(2,1)S(1)}, bf16[256,256]{1,0:T(8,128)(2,1)S(1)}, f32[128,128]{1,0:T(8,128)}, f32[64,128]{1,0:T(8,128)S(1)}) custom-call(s32[1]{0:T(128)} %bitcast.1.slot_ref, bf16[512,1152]{1,0:T(8,128)(2,1)S(1)} %bitcast.16, bf16[256,768]{1,0:T(8,128)(2,1)S(1)} %prepare.1.lookup_ref, bf16[256,1024]{1,0:T(8,128)(2,1)S(1)} %all_gather.3.volume_ref), custom_call_target="tpu_custom_call" | custom-call | flops 2147483648 | bytes 5242880 | tf_op jit(solution)/shard_map/compare/pallas_call | solution.py:332
  56.5 6.8 %all-to-all-start.1 = ((f32[64,2,128]{2,1,0:T(2,128)}), f32[64,2,128]{2,1,0:T(2,128)S(1)}, u32[]{:S(2)}, u32[]{:S(2)}) async-start(f32[64,2,128]{2,1,0:T(2,128)} %bitcast.8), calls=%async_computation.1 | async-start | bytes 131072 | tf_op jit(solution)/shard_map/all_to_all | solution.py:593
  63.3 1.1 %squares.1 = (bf16[512,384]{1,0:T(8,128)(2,1)S(1)}, f32[1,128]{1,0:T(1,128)S(1)}) custom-call(s32[1]{0:T(128)} %bitcast.1.slot_ref, f32[64,128]{1,0:T(8,128)S(1)} %get-tuple-element.21.about_ref), custom_call_target="tpu_custom_call" | custom-call | flops 134217728 | bytes 1048576 | tf_op jit(solution)/shard_map/squares/pallas_call | solution.py:372
  64.3 8.3 %all-to-all-done.1 = f32[64,2,128]{2,1,0:T(2,128)S(1)} async-done(((f32[64,2,128]{2,1,0:T(2,128)}), f32[64,2,128]{2,1,0:T(2,128)S(1)}, u32[]{:S(2)}, u32[]{:S(2)}) %all-to-all-start.1) | async-done | bytes 65568 | tf_op jit(solution)/shard_map/all_to_all | solution.py:593
  72.6 1.0 %project.1 = (f32[8,128]{1,0:T(8,128)S(1)}, bf16[128,512]{1,0:T(8,128)(2,1)S(1)}, bf16[4,336,128]{2,1,0:T(8,128)(2,1)S(1)}) custom-call(s32[1]{0:T(128)} %bitcast.core_ref, f32[128,128]{1,0:T(8,128)S(1)} %bitcast.17, f32[1,128]{1,0:T(1,128)S(1)} %get-tuple-element.22.noise_ref, bf16[256,256]{1,0:T(8,128)(2,1)S(1)} %get-tuple-element.23.picks_ref, ...), custom_call_target="tpu_custom_call" | custom-call | flops 268435456 | bytes 4194304 | tf_op jit(solution)/shard_map/project/pallas_call | solution.py:454
  73.6 3.8 %collective-permute-start = (bf16[4,336,128]{2,1,0:T(8,128)(2,1)S(1)}, bf16[4,336,128]{2,1,0:T(8,128)(2,1)S(1)}, u32[]{:S(2)}, u32[]{:S(2)}) collective-permute-start(bf16[4,336,128]{2,1,0:T(8,128)(2,1)S(1)} %get-tuple-element.28), channel_id=1, source_target_pairs={{0,1},{1,0},{2,3},{3,2},{4,5},{5,4},{6,7},{7,6},{8,9},{9,8},{10,11... | collective-permute-start | bytes 1032200 | tf_op jit(solution)/shard_map/ppermute | solution.py:602
  77.5 0.1 reshape.55
  77.6 0.0 copy-start
  77.6 0.0 copy-start.1
  77.6 0.4 keep_own.1.keep_ref
  78.0 0.7 collective-permute-done.got_ref
  78.7 0.1 middle.1
  78.8 6.6 %collective-permute-start.1 = (bf16[336,128]{1,0:T(8,128)(2,1)S(1)}, bf16[336,128]{1,0:T(8,128)(2,1)S(1)}, u32[]{:S(2)}, u32[]{:S(2)}) collective-permute-start(bf16[336,128]{1,0:T(8,128)(2,1)S(1)} %get-tuple-element.29), channel_id=1, source_target_pairs={{0,4},{1,5},{2,6},{3,7},{4,0},{5,1},{6,2},{7,3},{8,12},{9,13},{10,... | collective-permute-start | bytes 258056 | tf_op jit(solution)/shard_map/ppermute | solution.py:606
  85.4 2.4 %collective-permute-start.2 = (bf16[336,128]{1,0:T(8,128)(2,1)S(1)}, bf16[336,128]{1,0:T(8,128)(2,1)S(1)}, u32[]{:S(2)}, u32[]{:S(2)}) collective-permute-start(bf16[336,128]{1,0:T(8,128)(2,1)S(1)} %get-tuple-element.30), channel_id=1, source_target_pairs={{0,2},{1,3},{2,0},{3,1},{4,6},{5,7},{6,4},{7,5},{8,10},{9,11},{10,... | collective-permute-start | bytes 258056 | tf_op jit(solution)/shard_map/ppermute | solution.py:606
  87.8 2.4 %collective-permute-start.3 = (bf16[336,128]{1,0:T(8,128)(2,1)S(1)}, bf16[336,128]{1,0:T(8,128)(2,1)S(1)}, u32[]{:S(2)}, u32[]{:S(2)}) collective-permute-start(bf16[336,128]{1,0:T(8,128)(2,1)S(1)} %get-tuple-element.31), channel_id=1, source_target_pairs={{0,6},{1,7},{2,4},{3,5},{4,2},{5,3},{6,0},{7,1},{8,14},{9,15},{10,... | collective-permute-start | bytes 258056 | tf_op jit(solution)/shard_map/ppermute | solution.py:606
  90.2 0.1 constant_dynamic-slice_fusion
  90.3 0.6 copy.15
  90.9 0.0 copy-done
  90.9 0.0 copy-done.1
  90.9 0.2 collect.1
  91.1 0.0 collective-permute-done.1.refs_0_
  91.1 3.6 %collective-permute-done.2.refs_1_ = bf16[336,128]{1,0:T(8,128)(2,1)S(1)} collective-permute-done((bf16[336,128]{1,0:T(8,128)(2,1)S(1)}, bf16[336,128]{1,0:T(8,128)(2,1)S(1)}, u32[]{:S(2)}, u32[]{:S(2)}) %collective-permute-start.2) | collective-permute-done | bytes 86048 | tf_op jit(solution)/shard_map/ppermute | solution.py:606
  94.7 2.5 %collective-permute-done.3.refs_2_ = bf16[336,128]{1,0:T(8,128)(2,1)S(1)} collective-permute-done((bf16[336,128]{1,0:T(8,128)(2,1)S(1)}, bf16[336,128]{1,0:T(8,128)(2,1)S(1)}, u32[]{:S(2)}, u32[]{:S(2)}) %collective-permute-start.3) | collective-permute-done | bytes 86048 | tf_op jit(solution)/shard_map/ppermute | solution.py:606
  97.3 0.8 finish.1
  (1 shorter events, 0.0 us)
Async XLA Ops:
  5.6 15.5 %copy-start.2 = (s32[2,768,8]{1,2,0:T(8,128)S(1)}, s32[2,768,8]{1,2,0:T(8,128)}, u32[]{:S(2)}) copy-start(s32[2,768,8]{1,2,0:T(8,128)} %param.15) | copy-start | bytes 147460
  5.6 15.5 %copy-start.3 = (bf16[2,768,8]{1,2,0:T(8,128)(2,1)S(1)}, bf16[2,768,8]{1,2,0:T(8,128)(2,1)}, u32[]{:S(2)}) copy-start(bf16[2,768,8]{1,2,0:T(8,128)(2,1)} %param.16) | copy-start | bytes 73732
  5.6 15.7 %copy-start.4 = (bf16[4,8,1024]{2,1,0:T(8,128)(2,1)S(1)}, bf16[4,8,1024]{2,1,0:T(8,128)(2,1)}, u32[]{:S(2)}) copy-start(bf16[4,8,1024]{2,1,0:T(8,128)(2,1)} %param.17) | copy-start | bytes 196612
  5.6 46.6 %all-to-all-start = ((bf16[64,8,1152]{2,1,0:T(8,128)(2,1)}), bf16[64,8,1152]{2,1,0:T(8,128)(2,1)S(1)}, u32[]{:S(2)}, u32[]{:S(2)}) async-start(bf16[64,8,1152]{2,1,0:T(8,128)(2,1)} %bitcast.22), calls=%async_computation | async-start | bytes 2359296 | tf_op jit(solution)/shard_map/all_to_all | solution.py:586
  56.5 16.1 %all-to-all-start.1 = ((f32[64,2,128]{2,1,0:T(2,128)}), f32[64,2,128]{2,1,0:T(2,128)S(1)}, u32[]{:S(2)}, u32[]{:S(2)}) async-start(f32[64,2,128]{2,1,0:T(2,128)} %bitcast.8), calls=%async_computation.1 | async-start | bytes 131072 | tf_op jit(solution)/shard_map/all_to_all | solution.py:593
  73.6 5.1 %collective-permute-start = (bf16[4,336,128]{2,1,0:T(8,128)(2,1)S(1)}, bf16[4,336,128]{2,1,0:T(8,128)(2,1)S(1)}, u32[]{:S(2)}, u32[]{:S(2)}) collective-permute-start(bf16[4,336,128]{2,1,0:T(8,128)(2,1)S(1)} %get-tuple-element.28), channel_id=1, source_target_pairs={{0,1},{1,0},{2,3},{3,2},{4,5},{5,4},{6,7},{7,6},{8,9},{9,8},{10,11... | collective-permute-start | bytes 1032200 | tf_op jit(solution)/shard_map/ppermute | solution.py:602
  77.6 13.3 %copy-start = (f32[4,8,1024]{2,1,0:T(8,128)S(1)}, f32[4,8,1024]{2,1,0:T(8,128)}, u32[]{:S(2)}) copy-start(f32[4,8,1024]{2,1,0:T(8,128)} %param.18) | copy-start | bytes 393220
  77.6 13.3 %copy-start.1 = (f32[4,8,512]{2,1,0:T(8,128)S(1)}, f32[4,8,512]{2,1,0:T(8,128)}, u32[]{:S(2)}) copy-start(f32[4,8,512]{2,1,0:T(8,128)} %param.19) | copy-start | bytes 196612
  78.8 12.3 %collective-permute-start.1 = (bf16[336,128]{1,0:T(8,128)(2,1)S(1)}, bf16[336,128]{1,0:T(8,128)(2,1)S(1)}, u32[]{:S(2)}, u32[]{:S(2)}) collective-permute-start(bf16[336,128]{1,0:T(8,128)(2,1)S(1)} %get-tuple-element.29), channel_id=1, source_target_pairs={{0,4},{1,5},{2,6},{3,7},{4,0},{5,1},{6,2},{7,3},{8,12},{9,13},{10,... | collective-permute-start | bytes 258056 | tf_op jit(solution)/shard_map/ppermute | solution.py:606
  85.4 9.4 %collective-permute-start.2 = (bf16[336,128]{1,0:T(8,128)(2,1)S(1)}, bf16[336,128]{1,0:T(8,128)(2,1)S(1)}, u32[]{:S(2)}, u32[]{:S(2)}) collective-permute-start(bf16[336,128]{1,0:T(8,128)(2,1)S(1)} %get-tuple-element.30), channel_id=1, source_target_pairs={{0,2},{1,3},{2,0},{3,1},{4,6},{5,7},{6,4},{7,5},{8,10},{9,11},{10,... | collective-permute-start | bytes 258056 | tf_op jit(solution)/shard_map/ppermute | solution.py:606
  87.8 9.5 %collective-permute-start.3 = (bf16[336,128]{1,0:T(8,128)(2,1)S(1)}, bf16[336,128]{1,0:T(8,128)(2,1)S(1)}, u32[]{:S(2)}, u32[]{:S(2)}) collective-permute-start(bf16[336,128]{1,0:T(8,128)(2,1)S(1)} %get-tuple-element.31), channel_id=1, source_target_pairs={{0,6},{1,7},{2,4},{3,5},{4,2},{5,3},{6,0},{7,1},{8,14},{9,15},{10,... | collective-permute-start | bytes 258056 | tf_op jit(solution)/shard_map/ppermute | solution.py:606

commit v11 on v10

--- a/solution.py
+++ b/solution.py
@@ -604,7 +604,7 @@
     own, *sends = middle((place // 2).reshape(1), keep, got)
     parts = [
         lax.ppermute(sends[apart - 1], "vol", [(v, v ^ (2 * apart)) for v in range(n_vol)])
-        for apart in (2, 1, 3)
+        for apart in (2, 3, 1)
     ]
     data, weight = add_lines(
         collect_kernel,

time: 98.5 us -> 96.8 us (0.983)
  waiting for transfers between devices: 19.6 us -> 17.9 us
    ppermute x3, waiting for transfers between devices: 6.13 us -> 4.4 us  [on_device(): lax.ppermute(sends[apart - 1], 'vol', [(v, v ^ 2 * apart) for v in range(...]
where the time goes in v11:
time: 96.8 us; the launch traced here: 96.3 us
  starting transfers between devices  37.5 us (39%)
  blocking collectives  26.5 us (27%)
  waiting for transfers between devices  17.9 us (18%)
  Pallas kernels  11.6 us (12%)
  between operations  2.13 us (2%)
    all_gather x1, blocking collectives, on_device(): lax.all_gather(volume.reshape(slab * rows, 2 * npix), 'vol', axis=0, tile...  26.5 us
    all_to_all x1, starting transfers between devices, on_device(): lax.all_to_all(fourier.reshape(n_img, rows, 2 * npix + META), 'img', spli...  15.5 us
    ppermute x3, starting transfers between devices, on_device(): lax.ppermute(sends[apart - 1], 'vol', [(v, v ^ 2 * apart) for v in range(...  11.4 us
    all_to_all x1, waiting for transfers between devices, on_device(): lax.all_to_all(part.reshape(n_img, 2, 2 * n_img), 'img', split_axis=0, co...  8.28 us
    all_to_all x1, starting transfers between devices, on_device(): lax.all_to_all(part.reshape(n_img, 2, 2 * n_img), 'img', split_axis=0, co...  6.77 us
    all_to_all x1, waiting for transfers between devices, on_device(): lax.all_to_all(fourier.reshape(n_img, rows, 2 * npix + META), 'img', spli...  4.49 us
    ppermute x3, waiting for transfers between devices, on_device(): lax.ppermute(sends[apart - 1], 'vol', [(v, v ^ 2 * apart) for v in range(...  4.4 us
    pallas_call x1, Pallas kernels, compare(): pl.pallas_call(functools.partial(compare_kernel, ori, rows), in_specs=[sc...  4.21 us
  transfers between devices with their start and end apart: 6, of which 5 were waited for; matrix products, arithmetic and copies ran while one was open for 1% of the time, Pallas kernels for 2%

profile of v11, /device:TPU:1, one launch (start us, length us, event | category | flops | bytes accessed | tf_op | source)
XLA Modules:
  0.0 96.3 jit_solution(7959503039541252142)
XLA Ops:
  1.9 3.7 %transform.1 = bf16[512,1152]{1,0:T(8,128)(2,1)} custom-call(s32[1,4]{1,0:T(1,128)} %orient_hbm.1, f32[1]{0:T(128)S(6)} %copy.16.defocus_hbm, f32[1]{0:T(128)S(6)} %copy.17.noise_hbm, bf16[512,512]{1,0:T(8,128)(2,1)} %bitcast.25, bf16[512,1024]{1,0:T(8,128)(2,1)} %constant.40.clone.table_hbm, bf16[256,1024]{1,0:T(8,128)(2,1)} %constant.41.clone.halves_hbm), custom_call_target="tpu_custom_call" | custom-call | flops 1610612736 | bytes 2621440 | tf_op jit(solution)/shard_map/transform/pallas_call | solution.py:185
  5.6 0.0 copy-start.2
  5.6 0.0 copy-start.3
  5.6 0.0 copy-start.4
  5.6 15.5 %all-to-all-start = ((bf16[64,8,1152]{2,1,0:T(8,128)(2,1)}), bf16[64,8,1152]{2,1,0:T(8,128)(2,1)S(1)}, u32[]{:S(2)}, u32[]{:S(2)}) async-start(bf16[64,8,1152]{2,1,0:T(8,128)(2,1)} %bitcast.22), calls=%async_computation | async-start | bytes 2359296 | tf_op jit(solution)/shard_map/all_to_all | solution.py:586
  21.1 0.0 copy-done.2
  21.1 0.0 copy-done.3
  21.2 0.1 prepare.1.lookup_ref
  21.3 0.0 copy-done.4
  21.3 26.5 %all_gather.3.volume_ref = bf16[256,1024]{1,0:T(8,128)(2,1)S(1)} all-gather(bf16[32,1024]{1,0:T(8,128)(2,1)S(1)} %bitcast.23), channel_id=1, replica_groups=mesh['img'=64,'vol'=8] {'vol'}, dimensions={0}, use_global_device_ids=true | all-gather | bytes 589824 | tf_op jit(solution)/shard_map/all_gather | solution.py:589
  47.8 4.5 %all-to-all-done = bf16[64,8,1152]{2,1,0:T(8,128)(2,1)S(1)} async-done(((bf16[64,8,1152]{2,1,0:T(8,128)(2,1)}), bf16[64,8,1152]{2,1,0:T(8,128)(2,1)S(1)}, u32[]{:S(2)}, u32[]{:S(2)}) %all-to-all-start) | async-done | bytes 1179680 | tf_op jit(solution)/shard_map/all_to_all | solution.py:586
  52.3 4.2 %compare.4 = (bf16[512,1024]{1,0:T(8,128)(2,1)S(1)}, bf16[256,256]{1,0:T(8,128)(2,1)S(1)}, f32[128,128]{1,0:T(8,128)}, f32[64,128]{1,0:T(8,128)S(1)}) custom-call(s32[1]{0:T(128)} %bitcast.1.slot_ref, bf16[512,1152]{1,0:T(8,128)(2,1)S(1)} %bitcast.16, bf16[256,768]{1,0:T(8,128)(2,1)S(1)} %prepare.1.lookup_ref, bf16[256,1024]{1,0:T(8,128)(2,1)S(1)} %all_gather.3.volume_ref), custom_call_target="tpu_custom_call" | custom-call | flops 2147483648 | bytes 5242880 | tf_op jit(solution)/shard_map/compare/pallas_call | solution.py:332
  56.5 6.8 %all-to-all-start.1 = ((f32[64,2,128]{2,1,0:T(2,128)}), f32[64,2,128]{2,1,0:T(2,128)S(1)}, u32[]{:S(2)}, u32[]{:S(2)}) async-start(f32[64,2,128]{2,1,0:T(2,128)} %bitcast.8), calls=%async_computation.1 | async-start | bytes 131072 | tf_op jit(solution)/shard_map/all_to_all | solution.py:593
  63.3 1.1 %squares.1 = (bf16[512,384]{1,0:T(8,128)(2,1)S(1)}, f32[1,128]{1,0:T(1,128)S(1)}) custom-call(s32[1]{0:T(128)} %bitcast.1.slot_ref, f32[64,128]{1,0:T(8,128)S(1)} %get-tuple-element.21.about_ref), custom_call_target="tpu_custom_call" | custom-call | flops 134217728 | bytes 1048576 | tf_op jit(solution)/shard_map/squares/pallas_call | solution.py:372
  64.3 8.3 %all-to-all-done.1 = f32[64,2,128]{2,1,0:T(2,128)S(1)} async-done(((f32[64,2,128]{2,1,0:T(2,128)}), f32[64,2,128]{2,1,0:T(2,128)S(1)}, u32[]{:S(2)}, u32[]{:S(2)}) %all-to-all-start.1) | async-done | bytes 65568 | tf_op jit(solution)/shard_map/all_to_all | solution.py:593
  72.6 1.0 %project.1 = (f32[8,128]{1,0:T(8,128)S(1)}, bf16[128,512]{1,0:T(8,128)(2,1)S(1)}, bf16[4,336,128]{2,1,0:T(8,128)(2,1)S(1)}) custom-call(s32[1]{0:T(128)} %bitcast.core_ref, f32[128,128]{1,0:T(8,128)S(1)} %bitcast.17, f32[1,128]{1,0:T(1,128)S(1)} %get-tuple-element.22.noise_ref, bf16[256,256]{1,0:T(8,128)(2,1)S(1)} %get-tuple-element.23.picks_ref, ...), custom_call_target="tpu_custom_call" | custom-call | flops 268435456 | bytes 4194304 | tf_op jit(solution)/shard_map/project/pallas_call | solution.py:454
  73.6 3.8 %collective-permute-start = (bf16[4,336,128]{2,1,0:T(8,128)(2,1)S(1)}, bf16[4,336,128]{2,1,0:T(8,128)(2,1)S(1)}, u32[]{:S(2)}, u32[]{:S(2)}) collective-permute-start(bf16[4,336,128]{2,1,0:T(8,128)(2,1)S(1)} %get-tuple-element.28), channel_id=1, source_target_pairs={{0,1},{1,0},{2,3},{3,2},{4,5},{5,4},{6,7},{7,6},{8,9},{9,8},{10,11... | collective-permute-start | bytes 1032200 | tf_op jit(solution)/shard_map/ppermute | solution.py:602
  77.5 0.1 reshape.55
  77.6 0.0 copy-start
  77.6 0.0 copy-start.1
  77.6 0.4 keep_own.1.keep_ref
  78.0 0.7 collective-permute-done.got_ref
  78.7 0.1 middle.1
  78.8 6.6 %collective-permute-start.1 = (bf16[336,128]{1,0:T(8,128)(2,1)S(1)}, bf16[336,128]{1,0:T(8,128)(2,1)S(1)}, u32[]{:S(2)}, u32[]{:S(2)}) collective-permute-start(bf16[336,128]{1,0:T(8,128)(2,1)S(1)} %get-tuple-element.29), channel_id=1, source_target_pairs={{0,4},{1,5},{2,6},{3,7},{4,0},{5,1},{6,2},{7,3},{8,12},{9,13},{10,... | collective-permute-start | bytes 258056 | tf_op jit(solution)/shard_map/ppermute | solution.py:606
  85.4 2.9 %collective-permute-start.2 = (bf16[336,128]{1,0:T(8,128)(2,1)S(1)}, bf16[336,128]{1,0:T(8,128)(2,1)S(1)}, u32[]{:S(2)}, u32[]{:S(2)}) collective-permute-start(bf16[336,128]{1,0:T(8,128)(2,1)S(1)} %get-tuple-element.30), channel_id=1, source_target_pairs={{0,6},{1,7},{2,4},{3,5},{4,2},{5,3},{6,0},{7,1},{8,14},{9,15},{10,... | collective-permute-start | bytes 258056 | tf_op jit(solution)/shard_map/ppermute | solution.py:606
  88.2 2.0 %collective-permute-start.3 = (bf16[336,128]{1,0:T(8,128)(2,1)S(1)}, bf16[336,128]{1,0:T(8,128)(2,1)S(1)}, u32[]{:S(2)}, u32[]{:S(2)}) collective-permute-start(bf16[336,128]{1,0:T(8,128)(2,1)S(1)} %get-tuple-element.31), channel_id=1, source_target_pairs={{0,2},{1,3},{2,0},{3,1},{4,6},{5,7},{6,4},{7,5},{8,10},{9,11},{10,... | collective-permute-start | bytes 258056 | tf_op jit(solution)/shard_map/ppermute | solution.py:606
  90.2 0.1 constant_dynamic-slice_fusion
  90.3 0.6 copy.15
  90.9 0.0 copy-done
  90.9 0.0 copy-done.1
  90.9 0.2 collect.1
  91.1 0.0 collective-permute-done.1.refs_0_
  91.1 2.6 %collective-permute-done.2.refs_1_ = bf16[336,128]{1,0:T(8,128)(2,1)S(1)} collective-permute-done((bf16[336,128]{1,0:T(8,128)(2,1)S(1)}, bf16[336,128]{1,0:T(8,128)(2,1)S(1)}, u32[]{:S(2)}, u32[]{:S(2)}) %collective-permute-start.2) | collective-permute-done | bytes 86048 | tf_op jit(solution)/shard_map/ppermute | solution.py:606
  93.7 1.8 %collective-permute-done.3.refs_2_ = bf16[336,128]{1,0:T(8,128)(2,1)S(1)} collective-permute-done((bf16[336,128]{1,0:T(8,128)(2,1)S(1)}, bf16[336,128]{1,0:T(8,128)(2,1)S(1)}, u32[]{:S(2)}, u32[]{:S(2)}) %collective-permute-start.3) | collective-permute-done | bytes 86048 | tf_op jit(solution)/shard_map/ppermute | solution.py:606
  95.5 0.8 finish.1
  (1 shorter events, 0.0 us)
Async XLA Ops:
  5.6 15.5 %copy-start.2 = (s32[2,768,8]{1,2,0:T(8,128)S(1)}, s32[2,768,8]{1,2,0:T(8,128)}, u32[]{:S(2)}) copy-start(s32[2,768,8]{1,2,0:T(8,128)} %param.15) | copy-start | bytes 147460
  5.6 15.5 %copy-start.3 = (bf16[2,768,8]{1,2,0:T(8,128)(2,1)S(1)}, bf16[2,768,8]{1,2,0:T(8,128)(2,1)}, u32[]{:S(2)}) copy-start(bf16[2,768,8]{1,2,0:T(8,128)(2,1)} %param.16) | copy-start | bytes 73732
  5.6 15.7 %copy-start.4 = (bf16[4,8,1024]{2,1,0:T(8,128)(2,1)S(1)}, bf16[4,8,1024]{2,1,0:T(8,128)(2,1)}, u32[]{:S(2)}) copy-start(bf16[4,8,1024]{2,1,0:T(8,128)(2,1)} %param.17) | copy-start | bytes 196612
  5.6 46.6 %all-to-all-start = ((bf16[64,8,1152]{2,1,0:T(8,128)(2,1)}), bf16[64,8,1152]{2,1,0:T(8,128)(2,1)S(1)}, u32[]{:S(2)}, u32[]{:S(2)}) async-start(bf16[64,8,1152]{2,1,0:T(8,128)(2,1)} %bitcast.22), calls=%async_computation | async-start | bytes 2359296 | tf_op jit(solution)/shard_map/all_to_all | solution.py:586
  56.5 16.1 %all-to-all-start.1 = ((f32[64,2,128]{2,1,0:T(2,128)}), f32[64,2,128]{2,1,0:T(2,128)S(1)}, u32[]{:S(2)}, u32[]{:S(2)}) async-start(f32[64,2,128]{2,1,0:T(2,128)} %bitcast.8), calls=%async_computation.1 | async-start | bytes 131072 | tf_op jit(solution)/shard_map/all_to_all | solution.py:593
  73.6 5.1 %collective-permute-start = (bf16[4,336,128]{2,1,0:T(8,128)(2,1)S(1)}, bf16[4,336,128]{2,1,0:T(8,128)(2,1)S(1)}, u32[]{:S(2)}, u32[]{:S(2)}) collective-permute-start(bf16[4,336,128]{2,1,0:T(8,128)(2,1)S(1)} %get-tuple-element.28), channel_id=1, source_target_pairs={{0,1},{1,0},{2,3},{3,2},{4,5},{5,4},{6,7},{7,6},{8,9},{9,8},{10,11... | collective-permute-start | bytes 1032200 | tf_op jit(solution)/shard_map/ppermute | solution.py:602
  77.6 13.3 %copy-start = (f32[4,8,1024]{2,1,0:T(8,128)S(1)}, f32[4,8,1024]{2,1,0:T(8,128)}, u32[]{:S(2)}) copy-start(f32[4,8,1024]{2,1,0:T(8,128)} %param.18) | copy-start | bytes 393220
  77.6 13.3 %copy-start.1 = (f32[4,8,512]{2,1,0:T(8,128)S(1)}, f32[4,8,512]{2,1,0:T(8,128)}, u32[]{:S(2)}) copy-start(f32[4,8,512]{2,1,0:T(8,128)} %param.19) | copy-start | bytes 196612
  78.8 12.3 %collective-permute-start.1 = (bf16[336,128]{1,0:T(8,128)(2,1)S(1)}, bf16[336,128]{1,0:T(8,128)(2,1)S(1)}, u32[]{:S(2)}, u32[]{:S(2)}) collective-permute-start(bf16[336,128]{1,0:T(8,128)(2,1)S(1)} %get-tuple-element.29), channel_id=1, source_target_pairs={{0,4},{1,5},{2,6},{3,7},{4,0},{5,1},{6,2},{7,3},{8,12},{9,13},{10,... | collective-permute-start | bytes 258056 | tf_op jit(solution)/shard_map/ppermute | solution.py:606
  85.4 8.3 %collective-permute-start.2 = (bf16[336,128]{1,0:T(8,128)(2,1)S(1)}, bf16[336,128]{1,0:T(8,128)(2,1)S(1)}, u32[]{:S(2)}, u32[]{:S(2)}) collective-permute-start(bf16[336,128]{1,0:T(8,128)(2,1)S(1)} %get-tuple-element.30), channel_id=1, source_target_pairs={{0,6},{1,7},{2,4},{3,5},{4,2},{5,3},{6,0},{7,1},{8,14},{9,15},{10,... | collective-permute-start | bytes 258056 | tf_op jit(solution)/shard_map/ppermute | solution.py:606
  88.2 7.3 %collective-permute-start.3 = (bf16[336,128]{1,0:T(8,128)(2,1)S(1)}, bf16[336,128]{1,0:T(8,128)(2,1)S(1)}, u32[]{:S(2)}, u32[]{:S(2)}) collective-permute-start(bf16[336,128]{1,0:T(8,128)(2,1)S(1)} %get-tuple-element.31), channel_id=1, source_target_pairs={{0,2},{1,3},{2,0},{3,1},{4,6},{5,7},{6,4},{7,5},{8,10},{9,11},{10,... | collective-permute-start | bytes 258056 | tf_op jit(solution)/shard_map/ppermute | solution.py:606

commit v12 on v11

--- a/solution.py
+++ b/solution.py
@@ -98,14 +98,14 @@
     return jnp.where((sublane == lane)[None], values.reshape(height // rows, rows, width), 0.0)
 
 
-def transform_kernel(chunk, orient_hbm, defocus_hbm, noise_hbm, image_hbm, table_hbm, halves_hbm, out_hbm, orient_ref, defocus_ref, noise_ref, image_ref, wide_ref, table_ref, halves_ref, both_ref, out_ref, in_sems, out_sems):
+def transform_kernel(chunk, orient_hbm, defocus_hbm, image_hbm, table_hbm, halves_hbm, out_hbm, orient_ref, defocus_ref, image_ref, wide_ref, table_ref, halves_ref, both_ref, out_ref, in_sems, out_sems):
     npix = image_ref.shape[0]
     half = npix // 2
     ori = orient_ref.shape[1]
     starts = list(range(0, 2 * npix, chunk))
     pairs = [(image_hbm, image_ref)]
     pairs += [(table_hbm.at[:, pl.ds(start, chunk)], table_ref.at[:, pl.ds(start, chunk)]) for start in starts]
-    pairs += [(halves_hbm, halves_ref), (orient_hbm, orient_ref), (defocus_hbm, defocus_ref), (noise_hbm, noise_ref)]
+    pairs += [(halves_hbm, halves_ref), (orient_hbm, orient_ref), (defocus_hbm, defocus_ref)]
     loads = []
     for number, (source, target) in enumerate(pairs):
         load = pltpu.make_async_copy(source, target, in_sems.at[number])
@@ -154,11 +154,9 @@
         codes = jnp.where(lane == o, label & 255, codes)
         codes = jnp.where(lane == ori + o, label >> 8, codes)
     about = codes.astype(jnp.float32)
-    place = 2 * ori
-    for scalar_ref in (defocus_ref, noise_ref):
-        for part in three_parts(jnp.full((8, META), scalar_ref[0], jnp.float32)):
-            about = jnp.where(lane == place, part, about)
-            place += 1
+    parts = three_parts(jnp.full((8, META), defocus_ref[0], jnp.float32))
+    for place, part in enumerate(parts, 2 * ori):
+        about = jnp.where(lane == place, part, about)
     out_ref[:, 2 * npix :] = jnp.broadcast_to(about[:1], (npix, META)).astype(jnp.bfloat16)
     save(2 * npix, META)
     chunk = chunk // 2
@@ -178,32 +176,31 @@
         copy.wait()
 
 
-def transform(orient, defocus, noise, image, table, halves):
+def transform(orient, defocus, image, table, halves):
     npix = image.shape[0]
     chunk = npix
     pieces = 2 * npix // chunk
     return pl.pallas_call(
         functools.partial(transform_kernel, chunk),
-        in_specs=[pl.BlockSpec(memory_space=pl.ANY)] * 6,
+        in_specs=[pl.BlockSpec(memory_space=pl.ANY)] * 5,
         out_specs=pl.BlockSpec(memory_space=pl.ANY),
         out_shape=jax.ShapeDtypeStruct((npix, 2 * npix + META), jnp.bfloat16),
         scratch_shapes=[
             pltpu.SMEM(orient.shape, jnp.int32),
             pltpu.SMEM(defocus.shape, jnp.float32),
-            pltpu.SMEM(noise.shape, jnp.float32),
             pltpu.VMEM((npix, npix), jnp.bfloat16),
             pltpu.VMEM((npix // 128, npix, 128), jnp.float32),
             pltpu.VMEM((npix, 2 * npix), jnp.bfloat16),
             pltpu.VMEM((npix // 2, 2 * npix), jnp.bfloat16),
             pltpu.VMEM((2 * npix, 2 * npix), jnp.bfloat16),
             pltpu.VMEM((npix, 2 * npix + META), jnp.bfloat16),
-            pltpu.SemaphoreType.DMA((pieces + 5,)),
+            pltpu.SemaphoreType.DMA((pieces + 4,)),
             pltpu.SemaphoreType.DMA((2 * pieces + 1,)),
         ],
         compiler_params=params(HUGE),
         cost_estimate=cost(12 * npix**3, 10 * npix * npix),
         name="transform",
-    )(orient, defocus, noise, image, table, halves)
+    )(orient, defocus, image, table, halves)
 
 
 def prepare_kernel(planes_ref, weights_ref, lookup_ref):
@@ -251,7 +248,7 @@
     return defocus, freq_y * freq_y
 
 
-def compare_kernel(ori, rows, slot_ref, fourier_ref, lookup_ref, volume_ref, filtered_ref, picks_ref, part_ref, about_ref, mix_ref, power_ref):
+def compare_kernel(ori, rows, slot_ref, noise_ref, fourier_ref, lookup_ref, volume_ref, filtered_ref, picks_ref, part_ref, about_ref, mix_ref, power_ref):
     many, wide = filtered_ref.shape
     npix = wide // 2
     deep = volume_ref.shape[0]
@@ -317,6 +314,10 @@
             lanes = lanes + cross[:, start : start + 128]
         power = jnp.sum(power_ref[o].reshape(images, rows, 128), axis=1)
         halves.append(lanes - 0.5 * power)
+    lane = lax.broadcasted_iota(jnp.int32, (images, 128), 1)
+    image = lax.broadcasted_iota(jnp.int32, (images, 128), 0)
+    noise = jnp.where((image == slot_ref[0]) & (lane == 0), noise_ref[0], 0.0)
+    halves = [part - halves[0] for part in halves[1:]] + [noise]
     upper = jnp.concatenate(halves[: ori // 2], 0)
     lower = jnp.concatenate(halves[ori // 2 :], 0)
     upper = jnp.sum(jnp.transpose(upper), axis=0, keepdims=True)
@@ -325,13 +326,13 @@
     part_ref[...] = jnp.where(even, upper, lower)
 
 
-def compare(slot, fourier, lookup, volume, ori, rows, copies):
+def compare(slot, noise, fourier, lookup, volume, ori, rows, copies):
     many = fourier.shape[0]
     deep, wide = volume.shape
     images = many // rows
     return pl.pallas_call(
         functools.partial(compare_kernel, ori, rows),
-        in_specs=[scalar()] + [whole()] * 3,
+        in_specs=[scalar()] * 2 + [whole()] * 3,
         out_specs=(whole(),) * 4,
         out_shape=(
             jax.ShapeDtypeStruct((many, wide), jnp.bfloat16),
@@ -346,10 +347,10 @@
         compiler_params=params(LARGE),
         cost_estimate=cost(1 << 31, 5 << 20),
         name="compare",
-    )(slot, fourier, lookup, volume)
-
-
-def squares_kernel(ori, rows, npix, slot_ref, about_ref, square_ref, noise_ref):
+    )(slot, noise, fourier, lookup, volume)
+
+
+def squares_kernel(ori, rows, npix, slot_ref, about_ref, square_ref):
     many = square_ref.shape[0]
     images = many // rows
     about = about_ref[...]
@@ -362,9 +363,6 @@
     for start in range(0, square_ref.shape[1], 128):
         ctf = contrast(defocus, row_square, start, 128, npix)
         square_ref[:, start : start + 128] = (ctf * ctf).astype(jnp.bfloat16)
-    place = 2 * ori + 3
-    turned = jnp.transpose(jnp.concatenate([about, about], 0))
-    noise_ref[...] = turned[place : place + 1] + turned[place + 1 : place + 2] + turned[place + 2 : place + 3]
 
 
 def squares(slot, about, ori, rows, npix):
@@ -372,11 +370,8 @@
     return pl.pallas_call(
         functools.partial(squares_kernel, ori, rows, npix),
         in_specs=[scalar(), whole()],
-        out_specs=(whole(), whole()),
-        out_shape=(
-            jax.ShapeDtypeStruct((images * rows, npix // 2 + 128), jnp.bfloat16),
-            jax.ShapeDtypeStruct((1, 2 * images), jnp.float32),
-        ),
+        out_specs=whole(),
+        out_shape=jax.ShapeDtypeStruct((images * rows, npix // 2 + 128), jnp.bfloat16),
         compiler_params=params(SMALL),
         cost_estimate=cost(1 << 27, 1 << 20),
         name="squares",
@@ -406,7 +401,7 @@
     pack(target_ref, share, square_ref, tiles, last)
 
 
-def project_kernel(rows, ori, core_ref, part_ref, noise_ref, picks_ref, filtered_ref, square_ref, probs_ref, share_ref, send_ref):
+def project_kernel(rows, ori, core_ref, part_ref, picks_ref, filtered_ref, square_ref, probs_ref, share_ref, send_ref):
     many = filtered_ref.shape[0]
     deep = picks_ref.shape[1]
     lanes = part_ref.shape[1]
@@ -414,7 +409,11 @@
     sums = jnp.sum(part_ref[...].reshape(part_ref.shape[0] // 8, 8, lanes), axis=0)
     sums = sums + pltpu.roll(sums, 4, 0)
     sums = sums + pltpu.roll(sums, 2, 0)
-    score = sums / noise_ref[...]
+    line = lax.broadcasted_iota(jnp.int32, sums.shape, 0) & 1
+    lane = lax.broadcasted_iota(jnp.int32, sums.shape, 1)
+    noise = jnp.where(line == 1, sums, pltpu.roll(sums, 1, 0))
+    noise = jnp.where(lane >= images, noise, pltpu.roll(noise, images, 1))
+    score = jnp.where((line == 1) & (lane >= images), 0.0, sums / noise)
     top = jnp.maximum(score, pltpu.roll(score, 1, 0))
     top = jnp.maximum(top, pltpu.roll(top, images, 1))
     power = jnp.exp(score - top)
@@ -425,8 +424,9 @@
     column = jnp.transpose(jnp.concatenate([probs] * (lanes // 8), 0))
     share = jnp.zeros((images, deep), jnp.float32)
     for o in range(ori):
-        half = o % 2
-        chance = column[half * images : (half + 1) * images, o // 2 : o // 2 + 1]
+        place = (o - 1) % ori
+        half, line = place % 2, place // 2
+        chance = column[half * images : (half + 1) * images, line : line + 1]
         share = share + chance * picks_ref[o * images : (o + 1) * images, :].astype(jnp.float32)
     share = jnp.dot(
         jnp.transpose(share).astype(jnp.bfloat16),
@@ -448,12 +448,12 @@
     return jax.ShapeDtypeStruct((pairs, lines, 128), jnp.bfloat16)
 
 
-def project(core, part, noise, picks, filtered, square, rows, ori, pairs):
+def project(core, part, picks, filtered, square, rows, ori, pairs):
     many = filtered.shape[0]
     deep = picks.shape[1]
     return pl.pallas_call(
         functools.partial(project_kernel, rows, ori),
-        in_specs=[scalar()] + [whole()] * 5,
+        in_specs=[scalar()] + [whole()] * 4,
         out_specs=(whole(), whole(), whole()),
         out_shape=(
             jax.ShapeDtypeStruct((8, part.shape[1]), jnp.float32),
@@ -463,7 +463,7 @@
         compiler_params=params(LARGE),
         cost_estimate=cost(1 << 28, 4 << 20),
         name="project",
-    )(core, part, noise, picks, filtered, square)
+    )(core, part, picks, filtered, square)
 
 
 def keep_kernel(share_ref, filtered_ref, square_ref, keep_ref):
@@ -582,23 +582,26 @@
     slot = lax.axis_index("img").astype(jnp.int32).reshape(1)
     place = lax.axis_index("vol").astype(jnp.int32)
 
-    fourier = transform(orient, defocus, noise, images[0], *dft_tables(npix))
+    fourier = transform(orient, defocus, images[0], *dft_tables(npix))
     fourier = lax.all_to_all(
         fourier.reshape(n_img, rows, 2 * npix + META), "img", split_axis=0, concat_axis=0, tiled=True
     ).reshape(many, 2 * npix + META)
     vol_rows = lax.all_gather(volume.reshape(slab * rows, 2 * npix), "vol", axis=0, tiled=True)
     lookup = prepare(jnp.swapaxes(planes, 1, 2), jnp.swapaxes(weights, 1, 2), deep)
-    filtered, picks, part, about = compare(slot, fourier, lookup, vol_rows, ori, rows, n_img)
-    square, noise_all = squares(slot, about, ori, rows, npix)
+    filtered, picks, part, about = compare(
+        slot, noise, fourier, lookup, vol_rows, ori, rows, n_img
+    )
+    square = squares(slot, about, ori, rows, npix)
     part = lax.all_to_all(
         part.reshape(n_img, 2, 2 * n_img), "img", split_axis=0, concat_axis=0, tiled=True
     ).reshape(2 * n_img, 2 * n_img)
     probs, share, send = project(
-        (place % 2).reshape(1), part, noise_all, picks, filtered, square, rows, ori, pairs
+        (place % 2).reshape(1), part, picks, filtered, square, rows, ori, pairs
     )
     mine = lax.dynamic_slice_in_dim(
         probs[:2].reshape(2 * 2, n_img), lax.axis_index("img"), 1, 1
     ).reshape(1, ori)
+    mine = jnp.concatenate([mine[:, ori - 1 :], mine[:, : ori - 1]], 1)
     got = lax.ppermute(send, "vol", [(v, v ^ 1) for v in range(n_vol)])
     keep = keep_own(share, filtered, square, pairs)
     own, *sends = middle((place // 2).reshape(1), keep, got)

time: 96.8 us -> 96.3 us (level)
  other arithmetic: 0 us -> 1.23 us
  waiting for transfers between devices: 17.9 us -> 16.7 us
    concatenate x0 -> x1, other arithmetic: none -> 1.23 us  [on_device(): mine = jnp.concatenate([mine[:, ori - 1:], mine[:, :ori - 1]], 1)]
  transfers between devices with their start and end apart: 6 -> 6, of which waited for: 5 -> 4; matrix products, arithmetic and copies ran while one was open for 1% -> 2% of each run, Pallas kernels for 2% -> 2%
where the time goes in v12:
time: 96.3 us; the launch traced here: 95.8 us
  starting transfers between devices  37.4 us (39%)
  blocking collectives  25.8 us (27%)
  waiting for transfers between devices  16.7 us (17%)
  Pallas kernels  11.7 us (12%)
  between operations  2.14 us (2%)
  other arithmetic  1.23 us (1%)
    all_gather x1, blocking collectives, on_device(): lax.all_gather(volume.reshape(slab * rows, 2 * npix), 'vol', axis=0, tile...  25.8 us
    all_to_all x1, starting transfers between devices, on_device(): lax.all_to_all(fourier.reshape(n_img, rows, 2 * npix + META), 'img', spli...  15.5 us
    ppermute x3, starting transfers between devices, on_device(): lax.ppermute(sends[apart - 1], 'vol', [(v, v ^ 2 * apart) for v in range(...  11.4 us
    all_to_all x1, waiting for transfers between devices, on_device(): lax.all_to_all(part.reshape(n_img, 2, 2 * n_img), 'img', split_axis=0, co...  8.28 us
    all_to_all x1, starting transfers between devices, on_device(): lax.all_to_all(part.reshape(n_img, 2, 2 * n_img), 'img', split_axis=0, co...  6.68 us
    all_to_all x1, waiting for transfers between devices, on_device(): lax.all_to_all(fourier.reshape(n_img, rows, 2 * npix + META), 'img', spli...  4.63 us
    pallas_call x1, Pallas kernels, compare(): pl.pallas_call(functools.partial(compare_kernel, ori, rows), in_specs=[sc...  4.22 us
    ppermute x1, starting transfers between devices, on_device(): got = lax.ppermute(send, 'vol', [(v, v ^ 1) for v in range(n_vol)])  3.82 us
  transfers between devices with their start and end apart: 6, of which 4 were waited for; matrix products, arithmetic and copies ran while one was open for 2% of the time, Pallas kernels for 2%

profile of v12, /device:TPU:1, one launch (start us, length us, event | category | flops | bytes accessed | tf_op | source)
XLA Modules:
  0.0 95.8 jit_solution(4081064021300665821)
XLA Ops:
  1.3 3.6 %transform.1 = bf16[512,1152]{1,0:T(8,128)(2,1)} custom-call(s32[1,4]{1,0:T(1,128)} %orient_hbm.1, f32[1]{0:T(128)S(6)} %copy.16.defocus_hbm, bf16[512,512]{1,0:T(8,128)(2,1)} %bitcast.27, bf16[512,1024]{1,0:T(8,128)(2,1)} %constant.40.clone.table_hbm, bf16[256,1024]{1,0:T(8,128)(2,1)} %constant.41.clone.halves_hbm), custom_call_target="tpu_custom_call" | custom-call | flops 1610612736 | bytes 2621440 | tf_op jit(solution)/shard_map/transform/pallas_call | solution.py:183
  4.9 0.0 copy-start.2
  4.9 0.0 copy-start.3
  4.9 0.0 copy-start.4
  5.0 15.5 %all-to-all-start = ((bf16[64,8,1152]{2,1,0:T(8,128)(2,1)}), bf16[64,8,1152]{2,1,0:T(8,128)(2,1)S(1)}, u32[]{:S(2)}, u32[]{:S(2)}) async-start(bf16[64,8,1152]{2,1,0:T(8,128)(2,1)} %bitcast.23), calls=%async_computation | async-start | bytes 2359296 | tf_op jit(solution)/shard_map/all_to_all | solution.py:586
  21.1 0.0 copy-done.2
  21.1 0.0 copy-done.3
  21.1 0.1 prepare.1.lookup_ref
  21.3 0.0 copy-done.4
  21.3 25.8 %all_gather.3.volume_ref = bf16[256,1024]{1,0:T(8,128)(2,1)S(1)} all-gather(bf16[32,1024]{1,0:T(8,128)(2,1)S(1)} %bitcast.24), channel_id=1, replica_groups=mesh['img'=64,'vol'=8] {'vol'}, dimensions={0}, use_global_device_ids=true | all-gather | bytes 589824 | tf_op jit(solution)/shard_map/all_gather | solution.py:589
  47.1 4.6 %all-to-all-done = bf16[64,8,1152]{2,1,0:T(8,128)(2,1)S(1)} async-done(((bf16[64,8,1152]{2,1,0:T(8,128)(2,1)}), bf16[64,8,1152]{2,1,0:T(8,128)(2,1)S(1)}, u32[]{:S(2)}, u32[]{:S(2)}) %all-to-all-start) | async-done | bytes 1179680 | tf_op jit(solution)/shard_map/all_to_all | solution.py:586
  51.7 4.2 %compare.4 = (bf16[512,1024]{1,0:T(8,128)(2,1)S(1)}, bf16[256,256]{1,0:T(8,128)(2,1)S(1)}, f32[128,128]{1,0:T(8,128)}, f32[64,128]{1,0:T(8,128)S(1)}) custom-call(s32[1]{0:T(128)} %bitcast.1.slot_ref, f32[1]{0:T(128)S(6)} %copy.17.noise_ref, bf16[512,1152]{1,0:T(8,128)(2,1)S(1)} %bitcast.17, bf16[256,768]{1,0:T(8,128)(2,1)S(1)} %prepare.1.lookup_ref, ...), custom_call_target="tpu_custom_call" | custom-call | flops 2147483648 | bytes 5242880 | tf_op jit(solution)/shard_map/compare/pallas_call | solution.py:333
  55.9 6.7 %all-to-all-start.1 = ((f32[64,2,128]{2,1,0:T(2,128)}), f32[64,2,128]{2,1,0:T(2,128)S(1)}, u32[]{:S(2)}, u32[]{:S(2)}) async-start(f32[64,2,128]{2,1,0:T(2,128)} %bitcast.8), calls=%async_computation.1 | async-start | bytes 131072 | tf_op jit(solution)/shard_map/all_to_all | solution.py:595
  62.6 1.1 %squares.1.square_ref = bf16[512,384]{1,0:T(8,128)(2,1)S(1)} custom-call(s32[1]{0:T(128)} %bitcast.1.slot_ref, f32[64,128]{1,0:T(8,128)S(1)} %get-tuple-element.21.about_ref), custom_call_target="tpu_custom_call" | custom-call | flops 134217728 | bytes 1048576 | tf_op jit(solution)/shard_map/squares/pallas_call | solution.py:370
  63.7 8.3 %all-to-all-done.1 = f32[64,2,128]{2,1,0:T(2,128)S(1)} async-done(((f32[64,2,128]{2,1,0:T(2,128)}), f32[64,2,128]{2,1,0:T(2,128)S(1)}, u32[]{:S(2)}, u32[]{:S(2)}) %all-to-all-start.1) | async-done | bytes 65568 | tf_op jit(solution)/shard_map/all_to_all | solution.py:595
  72.0 1.1 %project.1 = (f32[8,128]{1,0:T(8,128)S(1)}, bf16[128,512]{1,0:T(8,128)(2,1)S(1)}, bf16[4,336,128]{2,1,0:T(8,128)(2,1)S(1)}) custom-call(s32[1]{0:T(128)} %bitcast.core_ref, f32[128,128]{1,0:T(8,128)S(1)} %bitcast.18, bf16[256,256]{1,0:T(8,128)(2,1)S(1)} %get-tuple-element.19.picks_ref, bf16[512,1024]{1,0:T(8,128)(2,1)S(1)} %get-tuple-element.20.filtered_ref, ...), custom_call_target="tpu_custom_call" | custom-call | flops 268435456 | bytes 4194304 | tf_op jit(solution)/shard_map/project/pallas_call | solution.py:454
  73.1 3.8 %collective-permute-start = (bf16[4,336,128]{2,1,0:T(8,128)(2,1)S(1)}, bf16[4,336,128]{2,1,0:T(8,128)(2,1)S(1)}, u32[]{:S(2)}, u32[]{:S(2)}) collective-permute-start(bf16[4,336,128]{2,1,0:T(8,128)(2,1)S(1)} %get-tuple-element.24), channel_id=1, source_target_pairs={{0,1},{1,0},{2,3},{3,2},{4,5},{5,4},{6,7},{7,6},{8,9},{9,8},{10,11... | collective-permute-start | bytes 1032200 | tf_op jit(solution)/shard_map/ppermute | solution.py:605
  76.9 0.1 reshape.55
  77.0 0.1 constant_dynamic-slice_fusion
  77.1 0.1 copy.15
  77.2 0.6 slice.10
  77.7 0.0 copy-start
  77.7 0.0 copy-start.1
  77.8 0.4 keep_own.1.keep_ref
  78.2 0.0 collective-permute-done.got_ref
  78.2 0.1 middle.1
  78.3 6.6 %collective-permute-start.1 = (bf16[336,128]{1,0:T(8,128)(2,1)S(1)}, bf16[336,128]{1,0:T(8,128)(2,1)S(1)}, u32[]{:S(2)}, u32[]{:S(2)}) collective-permute-start(bf16[336,128]{1,0:T(8,128)(2,1)S(1)} %get-tuple-element.25), channel_id=1, source_target_pairs={{0,4},{1,5},{2,6},{3,7},{4,0},{5,1},{6,2},{7,3},{8,12},{9,13},{10,... | collective-permute-start | bytes 258056 | tf_op jit(solution)/shard_map/ppermute | solution.py:609
  84.9 2.8 %collective-permute-start.2 = (bf16[336,128]{1,0:T(8,128)(2,1)S(1)}, bf16[336,128]{1,0:T(8,128)(2,1)S(1)}, u32[]{:S(2)}, u32[]{:S(2)}) collective-permute-start(bf16[336,128]{1,0:T(8,128)(2,1)S(1)} %get-tuple-element.26), channel_id=1, source_target_pairs={{0,6},{1,7},{2,4},{3,5},{4,2},{5,3},{6,0},{7,1},{8,14},{9,15},{10,... | collective-permute-start | bytes 258056 | tf_op jit(solution)/shard_map/ppermute | solution.py:609
  87.7 2.0 %collective-permute-start.3 = (bf16[336,128]{1,0:T(8,128)(2,1)S(1)}, bf16[336,128]{1,0:T(8,128)(2,1)S(1)}, u32[]{:S(2)}, u32[]{:S(2)}) collective-permute-start(bf16[336,128]{1,0:T(8,128)(2,1)S(1)} %get-tuple-element.27), channel_id=1, source_target_pairs={{0,2},{1,3},{2,0},{3,1},{4,6},{5,7},{6,4},{7,5},{8,10},{9,11},{10,... | collective-permute-start | bytes 258056 | tf_op jit(solution)/shard_map/ppermute | solution.py:609
  89.7 1.2 %pad_maximum_fusion = f32[1,4]{1,0:T(1,128)} fusion(f32[1,3]{1,0:T(1,128)S(1)} %bitcast.26, f32[1,1]{1,0:T(1,128)} %slice.10), kind=kLoop, calls=%fused_computation | loop fusion | flops 4 | bytes 32 | tf_op jit(solution)/shard_map/concatenate | solution.py:604
  90.9 0.0 copy-done
  90.9 0.0 copy-done.1
  90.9 0.2 collect.1
  91.2 0.0 collective-permute-done.1.refs_0_
  91.2 2.0 %collective-permute-done.2.refs_1_ = bf16[336,128]{1,0:T(8,128)(2,1)S(1)} collective-permute-done((bf16[336,128]{1,0:T(8,128)(2,1)S(1)}, bf16[336,128]{1,0:T(8,128)(2,1)S(1)}, u32[]{:S(2)}, u32[]{:S(2)}) %collective-permute-start.2) | collective-permute-done | bytes 86048 | tf_op jit(solution)/shard_map/ppermute | solution.py:609
  93.2 1.8 %collective-permute-done.3.refs_2_ = bf16[336,128]{1,0:T(8,128)(2,1)S(1)} collective-permute-done((bf16[336,128]{1,0:T(8,128)(2,1)S(1)}, bf16[336,128]{1,0:T(8,128)(2,1)S(1)}, u32[]{:S(2)}, u32[]{:S(2)}) %collective-permute-start.3) | collective-permute-done | bytes 86048 | tf_op jit(solution)/shard_map/ppermute | solution.py:609
  95.0 0.8 finish.1
  (1 shorter events, 0.0 us)
Async XLA Ops:
  4.9 16.2 %copy-start.2 = (s32[2,768,8]{1,2,0:T(8,128)S(1)}, s32[2,768,8]{1,2,0:T(8,128)}, u32[]{:S(2)}) copy-start(s32[2,768,8]{1,2,0:T(8,128)} %param.15) | copy-start | bytes 147460
  4.9 16.2 %copy-start.3 = (bf16[2,768,8]{1,2,0:T(8,128)(2,1)S(1)}, bf16[2,768,8]{1,2,0:T(8,128)(2,1)}, u32[]{:S(2)}) copy-start(bf16[2,768,8]{1,2,0:T(8,128)(2,1)} %param.16) | copy-start | bytes 73732
  4.9 16.3 %copy-start.4 = (bf16[4,8,1024]{2,1,0:T(8,128)(2,1)S(1)}, bf16[4,8,1024]{2,1,0:T(8,128)(2,1)}, u32[]{:S(2)}) copy-start(bf16[4,8,1024]{2,1,0:T(8,128)(2,1)} %param.17) | copy-start | bytes 196612
  5.0 46.7 %all-to-all-start = ((bf16[64,8,1152]{2,1,0:T(8,128)(2,1)}), bf16[64,8,1152]{2,1,0:T(8,128)(2,1)S(1)}, u32[]{:S(2)}, u32[]{:S(2)}) async-start(bf16[64,8,1152]{2,1,0:T(8,128)(2,1)} %bitcast.23), calls=%async_computation | async-start | bytes 2359296 | tf_op jit(solution)/shard_map/all_to_all | solution.py:586
  55.9 16.1 %all-to-all-start.1 = ((f32[64,2,128]{2,1,0:T(2,128)}), f32[64,2,128]{2,1,0:T(2,128)S(1)}, u32[]{:S(2)}, u32[]{:S(2)}) async-start(f32[64,2,128]{2,1,0:T(2,128)} %bitcast.8), calls=%async_computation.1 | async-start | bytes 131072 | tf_op jit(solution)/shard_map/all_to_all | solution.py:595
  73.1 5.1 %collective-permute-start = (bf16[4,336,128]{2,1,0:T(8,128)(2,1)S(1)}, bf16[4,336,128]{2,1,0:T(8,128)(2,1)S(1)}, u32[]{:S(2)}, u32[]{:S(2)}) collective-permute-start(bf16[4,336,128]{2,1,0:T(8,128)(2,1)S(1)} %get-tuple-element.24), channel_id=1, source_target_pairs={{0,1},{1,0},{2,3},{3,2},{4,5},{5,4},{6,7},{7,6},{8,9},{9,8},{10,11... | collective-permute-start | bytes 1032200 | tf_op jit(solution)/shard_map/ppermute | solution.py:605
  77.7 13.2 %copy-start = (f32[4,8,1024]{2,1,0:T(8,128)S(1)}, f32[4,8,1024]{2,1,0:T(8,128)}, u32[]{:S(2)}) copy-start(f32[4,8,1024]{2,1,0:T(8,128)} %param.18) | copy-start | bytes 393220
  77.7 13.2 %copy-start.1 = (f32[4,8,512]{2,1,0:T(8,128)S(1)}, f32[4,8,512]{2,1,0:T(8,128)}, u32[]{:S(2)}) copy-start(f32[4,8,512]{2,1,0:T(8,128)} %param.19) | copy-start | bytes 196612
  78.3 12.9 %collective-permute-start.1 = (bf16[336,128]{1,0:T(8,128)(2,1)S(1)}, bf16[336,128]{1,0:T(8,128)(2,1)S(1)}, u32[]{:S(2)}, u32[]{:S(2)}) collective-permute-start(bf16[336,128]{1,0:T(8,128)(2,1)S(1)} %get-tuple-element.25), channel_id=1, source_target_pairs={{0,4},{1,5},{2,6},{3,7},{4,0},{5,1},{6,2},{7,3},{8,12},{9,13},{10,... | collective-permute-start | bytes 258056 | tf_op jit(solution)/shard_map/ppermute | solution.py:609
  84.9 8.3 %collective-permute-start.2 = (bf16[336,128]{1,0:T(8,128)(2,1)S(1)}, bf16[336,128]{1,0:T(8,128)(2,1)S(1)}, u32[]{:S(2)}, u32[]{:S(2)}) collective-permute-start(bf16[336,128]{1,0:T(8,128)(2,1)S(1)} %get-tuple-element.26), channel_id=1, source_target_pairs={{0,6},{1,7},{2,4},{3,5},{4,2},{5,3},{6,0},{7,1},{8,14},{9,15},{10,... | collective-permute-start | bytes 258056 | tf_op jit(solution)/shard_map/ppermute | solution.py:609
  87.7 7.2 %collective-permute-start.3 = (bf16[336,128]{1,0:T(8,128)(2,1)S(1)}, bf16[336,128]{1,0:T(8,128)(2,1)S(1)}, u32[]{:S(2)}, u32[]{:S(2)}) collective-permute-start(bf16[336,128]{1,0:T(8,128)(2,1)S(1)} %get-tuple-element.27), channel_id=1, source_target_pairs={{0,2},{1,3},{2,0},{3,1},{4,6},{5,7},{6,4},{7,5},{8,10},{9,11},{10,... | collective-permute-start | bytes 258056 | tf_op jit(solution)/shard_map/ppermute | solution.py:609

commit v13 on v12

--- a/solution.py
+++ b/solution.py
@@ -317,7 +317,7 @@
     lane = lax.broadcasted_iota(jnp.int32, (images, 128), 1)
     image = lax.broadcasted_iota(jnp.int32, (images, 128), 0)
     noise = jnp.where((image == slot_ref[0]) & (lane == 0), noise_ref[0], 0.0)
-    halves = [part - halves[0] for part in halves[1:]] + [noise]
+    halves = [noise] + [part - halves[0] for part in halves[1:]]
     upper = jnp.concatenate(halves[: ori // 2], 0)
     lower = jnp.concatenate(halves[ori // 2 :], 0)
     upper = jnp.sum(jnp.transpose(upper), axis=0, keepdims=True)
@@ -411,9 +411,9 @@
     sums = sums + pltpu.roll(sums, 2, 0)
     line = lax.broadcasted_iota(jnp.int32, sums.shape, 0) & 1
     lane = lax.broadcasted_iota(jnp.int32, sums.shape, 1)
-    noise = jnp.where(line == 1, sums, pltpu.roll(sums, 1, 0))
-    noise = jnp.where(lane >= images, noise, pltpu.roll(noise, images, 1))
-    score = jnp.where((line == 1) & (lane >= images), 0.0, sums / noise)
+    noise = jnp.where(line == 0, sums, pltpu.roll(sums, 1, 0))
+    noise = jnp.where(lane < images, noise, pltpu.roll(noise, images, 1))
+    score = jnp.where((line == 0) & (lane < images), 0.0, sums / noise)
     top = jnp.maximum(score, pltpu.roll(score, 1, 0))
     top = jnp.maximum(top, pltpu.roll(top, images, 1))
     power = jnp.exp(score - top)
@@ -424,9 +424,8 @@
     column = jnp.transpose(jnp.concatenate([probs] * (lanes // 8), 0))
     share = jnp.zeros((images, deep), jnp.float32)
     for o in range(ori):
-        place = (o - 1) % ori
-        half, line = place % 2, place // 2
-        chance = column[half * images : (half + 1) * images, line : line + 1]
+        half = o % 2
+        chance = column[half * images : (half + 1) * images, o // 2 : o // 2 + 1]
         share = share + chance * picks_ref[o * images : (o + 1) * images, :].astype(jnp.float32)
     share = jnp.dot(
         jnp.transpose(share).astype(jnp.bfloat16),
@@ -601,7 +600,6 @@
     mine = lax.dynamic_slice_in_dim(
         probs[:2].reshape(2 * 2, n_img), lax.axis_index("img"), 1, 1
     ).reshape(1, ori)
-    mine = jnp.concatenate([mine[:, ori - 1 :], mine[:, : ori - 1]], 1)
     got = lax.ppermute(send, "vol", [(v, v ^ 1) for v in range(n_vol)])
     keep = keep_own(share, filtered, square, pairs)
     own, *sends = middle((place // 2).reshape(1), keep, got)

time: 96.3 us -> 96.3 us (level)
  waiting for transfers between devices: 16.7 us -> 18 us
  other arithmetic: 1.23 us -> 0 us
    concatenate x1 -> x0, other arithmetic: 1.23 us -> none  [on_device(): mine = jnp.concatenate([mine[:, ori - 1:], mine[:, :ori - 1]], 1)]
  transfers between devices with their start and end apart: 6 -> 6, of which waited for: 4 -> 5; matrix products, arithmetic and copies ran while one was open for 2% -> 1% of each run, Pallas kernels for 2% -> 2%
where the time goes in v13:
time: 96.3 us; the launch traced here: 95.8 us
  starting transfers between devices  37.4 us (39%)
  blocking collectives  25.8 us (27%)
  waiting for transfers between devices  18 us (19%)
  Pallas kernels  11.7 us (12%)
  between operations  2.14 us (2%)
    all_gather x1, blocking collectives, on_device(): lax.all_gather(volume.reshape(slab * rows, 2 * npix), 'vol', axis=0, tile...  25.8 us
    all_to_all x1, starting transfers between devices, on_device(): lax.all_to_all(fourier.reshape(n_img, rows, 2 * npix + META), 'img', spli...  15.5 us
    ppermute x3, starting transfers between devices, on_device(): lax.ppermute(sends[apart - 1], 'vol', [(v, v ^ 2 * apart) for v in range(...  11.4 us
    all_to_all x1, waiting for transfers between devices, on_device(): lax.all_to_all(part.reshape(n_img, 2, 2 * n_img), 'img', split_axis=0, co...  8.28 us
    all_to_all x1, starting transfers between devices, on_device(): lax.all_to_all(part.reshape(n_img, 2, 2 * n_img), 'img', split_axis=0, co...  6.69 us
    all_to_all x1, waiting for transfers between devices, on_device(): lax.all_to_all(fourier.reshape(n_img, rows, 2 * npix + META), 'img', spli...  4.62 us
    ppermute x3, waiting for transfers between devices, on_device(): lax.ppermute(sends[apart - 1], 'vol', [(v, v ^ 2 * apart) for v in range(...  4.41 us
    pallas_call x1, Pallas kernels, compare(): pl.pallas_call(functools.partial(compare_kernel, ori, rows), in_specs=[sc...  4.22 us
  transfers between devices with their start and end apart: 6, of which 5 were waited for; matrix products, arithmetic and copies ran while one was open for 1% of the time, Pallas kernels for 2%

profile of v13, /device:TPU:1, one launch (start us, length us, event | category | flops | bytes accessed | tf_op | source)
XLA Modules:
  0.0 95.8 jit_solution(14208202357378080282)
XLA Ops:
  1.3 3.6 %transform.1 = bf16[512,1152]{1,0:T(8,128)(2,1)} custom-call(s32[1,4]{1,0:T(1,128)} %orient_hbm.1, f32[1]{0:T(128)S(6)} %copy.16.defocus_hbm, bf16[512,512]{1,0:T(8,128)(2,1)} %bitcast.25, bf16[512,1024]{1,0:T(8,128)(2,1)} %constant.40.clone.table_hbm, bf16[256,1024]{1,0:T(8,128)(2,1)} %constant.41.clone.halves_hbm), custom_call_target="tpu_custom_call" | custom-call | flops 1610612736 | bytes 2621440 | tf_op jit(solution)/shard_map/transform/pallas_call | solution.py:183
  4.9 0.0 copy-start.2
  4.9 0.0 copy-start.3
  4.9 0.0 copy-start.4
  5.0 15.5 %all-to-all-start = ((bf16[64,8,1152]{2,1,0:T(8,128)(2,1)}), bf16[64,8,1152]{2,1,0:T(8,128)(2,1)S(1)}, u32[]{:S(2)}, u32[]{:S(2)}) async-start(bf16[64,8,1152]{2,1,0:T(8,128)(2,1)} %bitcast.22), calls=%async_computation | async-start | bytes 2359296 | tf_op jit(solution)/shard_map/all_to_all | solution.py:585
  21.1 0.0 copy-done.2
  21.1 0.0 copy-done.3
  21.1 0.1 prepare.1.lookup_ref
  21.3 0.0 copy-done.4
  21.3 25.8 %all_gather.3.volume_ref = bf16[256,1024]{1,0:T(8,128)(2,1)S(1)} all-gather(bf16[32,1024]{1,0:T(8,128)(2,1)S(1)} %bitcast.23), channel_id=1, replica_groups=mesh['img'=64,'vol'=8] {'vol'}, dimensions={0}, use_global_device_ids=true | all-gather | bytes 589824 | tf_op jit(solution)/shard_map/all_gather | solution.py:588
  47.1 4.6 %all-to-all-done = bf16[64,8,1152]{2,1,0:T(8,128)(2,1)S(1)} async-done(((bf16[64,8,1152]{2,1,0:T(8,128)(2,1)}), bf16[64,8,1152]{2,1,0:T(8,128)(2,1)S(1)}, u32[]{:S(2)}, u32[]{:S(2)}) %all-to-all-start) | async-done | bytes 1179680 | tf_op jit(solution)/shard_map/all_to_all | solution.py:585
  51.7 4.2 %compare.4 = (bf16[512,1024]{1,0:T(8,128)(2,1)S(1)}, bf16[256,256]{1,0:T(8,128)(2,1)S(1)}, f32[128,128]{1,0:T(8,128)}, f32[64,128]{1,0:T(8,128)S(1)}) custom-call(s32[1]{0:T(128)} %bitcast.1.slot_ref, f32[1]{0:T(128)S(6)} %copy.17.noise_ref, bf16[512,1152]{1,0:T(8,128)(2,1)S(1)} %bitcast.16, bf16[256,768]{1,0:T(8,128)(2,1)S(1)} %prepare.1.lookup_ref, ...), custom_call_target="tpu_custom_call" | custom-call | flops 2147483648 | bytes 5242880 | tf_op jit(solution)/shard_map/compare/pallas_call | solution.py:333
  55.9 6.7 %all-to-all-start.1 = ((f32[64,2,128]{2,1,0:T(2,128)}), f32[64,2,128]{2,1,0:T(2,128)S(1)}, u32[]{:S(2)}, u32[]{:S(2)}) async-start(f32[64,2,128]{2,1,0:T(2,128)} %bitcast.8), calls=%async_computation.1 | async-start | bytes 131072 | tf_op jit(solution)/shard_map/all_to_all | solution.py:594
  62.6 1.1 %squares.1.square_ref = bf16[512,384]{1,0:T(8,128)(2,1)S(1)} custom-call(s32[1]{0:T(128)} %bitcast.1.slot_ref, f32[64,128]{1,0:T(8,128)S(1)} %get-tuple-element.21.about_ref), custom_call_target="tpu_custom_call" | custom-call | flops 134217728 | bytes 1048576 | tf_op jit(solution)/shard_map/squares/pallas_call | solution.py:370
  63.7 8.3 %all-to-all-done.1 = f32[64,2,128]{2,1,0:T(2,128)S(1)} async-done(((f32[64,2,128]{2,1,0:T(2,128)}), f32[64,2,128]{2,1,0:T(2,128)S(1)}, u32[]{:S(2)}, u32[]{:S(2)}) %all-to-all-start.1) | async-done | bytes 65568 | tf_op jit(solution)/shard_map/all_to_all | solution.py:594
  72.0 1.1 %project.1 = (f32[8,128]{1,0:T(8,128)S(1)}, bf16[128,512]{1,0:T(8,128)(2,1)S(1)}, bf16[4,336,128]{2,1,0:T(8,128)(2,1)S(1)}) custom-call(s32[1]{0:T(128)} %bitcast.core_ref, f32[128,128]{1,0:T(8,128)S(1)} %bitcast.17, bf16[256,256]{1,0:T(8,128)(2,1)S(1)} %get-tuple-element.19.picks_ref, bf16[512,1024]{1,0:T(8,128)(2,1)S(1)} %get-tuple-element.20.filtered_ref, ...), custom_call_target="tpu_custom_call" | custom-call | flops 268435456 | bytes 4194304 | tf_op jit(solution)/shard_map/project/pallas_call | solution.py:453
  73.1 3.8 %collective-permute-start = (bf16[4,336,128]{2,1,0:T(8,128)(2,1)S(1)}, bf16[4,336,128]{2,1,0:T(8,128)(2,1)S(1)}, u32[]{:S(2)}, u32[]{:S(2)}) collective-permute-start(bf16[4,336,128]{2,1,0:T(8,128)(2,1)S(1)} %get-tuple-element.24), channel_id=1, source_target_pairs={{0,1},{1,0},{2,3},{3,2},{4,5},{5,4},{6,7},{7,6},{8,9},{9,8},{10,11... | collective-permute-start | bytes 1032200 | tf_op jit(solution)/shard_map/ppermute | solution.py:603
  76.9 0.1 reshape.55
  77.0 0.0 copy-start
  77.0 0.0 copy-start.1
  77.0 0.5 keep_own.1.keep_ref
  77.4 0.7 collective-permute-done.got_ref
  78.1 0.1 middle.1
  78.2 6.6 %collective-permute-start.1 = (bf16[336,128]{1,0:T(8,128)(2,1)S(1)}, bf16[336,128]{1,0:T(8,128)(2,1)S(1)}, u32[]{:S(2)}, u32[]{:S(2)}) collective-permute-start(bf16[336,128]{1,0:T(8,128)(2,1)S(1)} %get-tuple-element.25), channel_id=1, source_target_pairs={{0,4},{1,5},{2,6},{3,7},{4,0},{5,1},{6,2},{7,3},{8,12},{9,13},{10,... | collective-permute-start | bytes 258056 | tf_op jit(solution)/shard_map/ppermute | solution.py:607
  84.8 2.8 %collective-permute-start.2 = (bf16[336,128]{1,0:T(8,128)(2,1)S(1)}, bf16[336,128]{1,0:T(8,128)(2,1)S(1)}, u32[]{:S(2)}, u32[]{:S(2)}) collective-permute-start(bf16[336,128]{1,0:T(8,128)(2,1)S(1)} %get-tuple-element.26), channel_id=1, source_target_pairs={{0,6},{1,7},{2,4},{3,5},{4,2},{5,3},{6,0},{7,1},{8,14},{9,15},{10,... | collective-permute-start | bytes 258056 | tf_op jit(solution)/shard_map/ppermute | solution.py:607
  87.7 2.0 %collective-permute-start.3 = (bf16[336,128]{1,0:T(8,128)(2,1)S(1)}, bf16[336,128]{1,0:T(8,128)(2,1)S(1)}, u32[]{:S(2)}, u32[]{:S(2)}) collective-permute-start(bf16[336,128]{1,0:T(8,128)(2,1)S(1)} %get-tuple-element.27), channel_id=1, source_target_pairs={{0,2},{1,3},{2,0},{3,1},{4,6},{5,7},{6,4},{7,5},{8,10},{9,11},{10,... | collective-permute-start | bytes 258056 | tf_op jit(solution)/shard_map/ppermute | solution.py:607
  89.6 0.1 constant_dynamic-slice_fusion
  89.7 0.6 copy.15
  90.3 0.0 copy-done
  90.3 0.0 copy-done.1
  90.3 0.2 collect.1
  90.5 0.0 collective-permute-done.1.refs_0_
  90.6 2.6 %collective-permute-done.2.refs_1_ = bf16[336,128]{1,0:T(8,128)(2,1)S(1)} collective-permute-done((bf16[336,128]{1,0:T(8,128)(2,1)S(1)}, bf16[336,128]{1,0:T(8,128)(2,1)S(1)}, u32[]{:S(2)}, u32[]{:S(2)}) %collective-permute-start.2) | collective-permute-done | bytes 86048 | tf_op jit(solution)/shard_map/ppermute | solution.py:607
  93.1 1.8 %collective-permute-done.3.refs_2_ = bf16[336,128]{1,0:T(8,128)(2,1)S(1)} collective-permute-done((bf16[336,128]{1,0:T(8,128)(2,1)S(1)}, bf16[336,128]{1,0:T(8,128)(2,1)S(1)}, u32[]{:S(2)}, u32[]{:S(2)}) %collective-permute-start.3) | collective-permute-done | bytes 86048 | tf_op jit(solution)/shard_map/ppermute | solution.py:607
  95.0 0.8 finish.1
  (1 shorter events, 0.0 us)
Async XLA Ops:
  4.9 16.2 %copy-start.2 = (s32[2,768,8]{1,2,0:T(8,128)S(1)}, s32[2,768,8]{1,2,0:T(8,128)}, u32[]{:S(2)}) copy-start(s32[2,768,8]{1,2,0:T(8,128)} %param.15) | copy-start | bytes 147460
  4.9 16.2 %copy-start.3 = (bf16[2,768,8]{1,2,0:T(8,128)(2,1)S(1)}, bf16[2,768,8]{1,2,0:T(8,128)(2,1)}, u32[]{:S(2)}) copy-start(bf16[2,768,8]{1,2,0:T(8,128)(2,1)} %param.16) | copy-start | bytes 73732
  4.9 16.3 %copy-start.4 = (bf16[4,8,1024]{2,1,0:T(8,128)(2,1)S(1)}, bf16[4,8,1024]{2,1,0:T(8,128)(2,1)}, u32[]{:S(2)}) copy-start(bf16[4,8,1024]{2,1,0:T(8,128)(2,1)} %param.17) | copy-start | bytes 196612
  5.0 46.7 %all-to-all-start = ((bf16[64,8,1152]{2,1,0:T(8,128)(2,1)}), bf16[64,8,1152]{2,1,0:T(8,128)(2,1)S(1)}, u32[]{:S(2)}, u32[]{:S(2)}) async-start(bf16[64,8,1152]{2,1,0:T(8,128)(2,1)} %bitcast.22), calls=%async_computation | async-start | bytes 2359296 | tf_op jit(solution)/shard_map/all_to_all | solution.py:585
  55.9 16.1 %all-to-all-start.1 = ((f32[64,2,128]{2,1,0:T(2,128)}), f32[64,2,128]{2,1,0:T(2,128)S(1)}, u32[]{:S(2)}, u32[]{:S(2)}) async-start(f32[64,2,128]{2,1,0:T(2,128)} %bitcast.8), calls=%async_computation.1 | async-start | bytes 131072 | tf_op jit(solution)/shard_map/all_to_all | solution.py:594
  73.1 5.1 %collective-permute-start = (bf16[4,336,128]{2,1,0:T(8,128)(2,1)S(1)}, bf16[4,336,128]{2,1,0:T(8,128)(2,1)S(1)}, u32[]{:S(2)}, u32[]{:S(2)}) collective-permute-start(bf16[4,336,128]{2,1,0:T(8,128)(2,1)S(1)} %get-tuple-element.24), channel_id=1, source_target_pairs={{0,1},{1,0},{2,3},{3,2},{4,5},{5,4},{6,7},{7,6},{8,9},{9,8},{10,11... | collective-permute-start | bytes 1032200 | tf_op jit(solution)/shard_map/ppermute | solution.py:603
  77.0 13.3 %copy-start = (f32[4,8,1024]{2,1,0:T(8,128)S(1)}, f32[4,8,1024]{2,1,0:T(8,128)}, u32[]{:S(2)}) copy-start(f32[4,8,1024]{2,1,0:T(8,128)} %param.18) | copy-start | bytes 393220
  77.0 13.3 %copy-start.1 = (f32[4,8,512]{2,1,0:T(8,128)S(1)}, f32[4,8,512]{2,1,0:T(8,128)}, u32[]{:S(2)}) copy-start(f32[4,8,512]{2,1,0:T(8,128)} %param.19) | copy-start | bytes 196612
  78.2 12.3 %collective-permute-start.1 = (bf16[336,128]{1,0:T(8,128)(2,1)S(1)}, bf16[336,128]{1,0:T(8,128)(2,1)S(1)}, u32[]{:S(2)}, u32[]{:S(2)}) collective-permute-start(bf16[336,128]{1,0:T(8,128)(2,1)S(1)} %get-tuple-element.25), channel_id=1, source_target_pairs={{0,4},{1,5},{2,6},{3,7},{4,0},{5,1},{6,2},{7,3},{8,12},{9,13},{10,... | collective-permute-start | bytes 258056 | tf_op jit(solution)/shard_map/ppermute | solution.py:607
  84.8 8.3 %collective-permute-start.2 = (bf16[336,128]{1,0:T(8,128)(2,1)S(1)}, bf16[336,128]{1,0:T(8,128)(2,1)S(1)}, u32[]{:S(2)}, u32[]{:S(2)}) collective-permute-start(bf16[336,128]{1,0:T(8,128)(2,1)S(1)} %get-tuple-element.26), channel_id=1, source_target_pairs={{0,6},{1,7},{2,4},{3,5},{4,2},{5,3},{6,0},{7,1},{8,14},{9,15},{10,... | collective-permute-start | bytes 258056 | tf_op jit(solution)/shard_map/ppermute | solution.py:607
  87.7 7.3 %collective-permute-start.3 = (bf16[336,128]{1,0:T(8,128)(2,1)S(1)}, bf16[336,128]{1,0:T(8,128)(2,1)S(1)}, u32[]{:S(2)}, u32[]{:S(2)}) collective-permute-start(bf16[336,128]{1,0:T(8,128)(2,1)S(1)} %get-tuple-element.27), channel_id=1, source_target_pairs={{0,2},{1,3},{2,0},{3,1},{4,6},{5,7},{6,4},{7,5},{8,10},{9,11},{10,... | collective-permute-start | bytes 258056 | tf_op jit(solution)/shard_map/ppermute | solution.py:607

commit v14 on v13

--- a/solution.py
+++ b/solution.py
@@ -65,10 +65,6 @@
 
 def scalar():
     return pl.BlockSpec(memory_space=pltpu.SMEM)
-
-
-def same(a, b):
-    return lax.dot_general(a, b, (((1,), (1,)), ((), ())), preferred_element_type=jnp.float32)
 
 
 def three_parts(value):
@@ -204,14 +200,14 @@
 
 
 def prepare_kernel(planes_ref, weights_ref, lookup_ref):
-    deep, labels = lookup_ref.shape
+    labels, deep = lookup_ref.shape
     rows = planes_ref.shape[1]
     level = lax.broadcasted_iota(jnp.int32, (deep // rows, rows, labels), 0)
     total = jnp.zeros((deep // rows, rows, labels), jnp.float32)
     for k in range(2):
         weight = weights_ref[k].astype(jnp.float32)
         total = total + jnp.where(level == planes_ref[k][None], weight[None], 0.0)
-    lookup_ref[...] = total.reshape(deep, labels).astype(jnp.bfloat16)
+    lookup_ref[...] = jnp.transpose(total.reshape(deep, labels)).astype(jnp.bfloat16)
 
 
 def prepare(planes, weights, deep):
@@ -220,11 +216,25 @@
         prepare_kernel,
         in_specs=[whole(), whole()],
         out_specs=whole(),
-        out_shape=jax.ShapeDtypeStruct((deep, labels), jnp.bfloat16),
+        out_shape=jax.ShapeDtypeStruct((labels, deep), jnp.bfloat16),
         compiler_params=params(SMALL),
         cost_estimate=cost(1 << 22, 1 << 20),
         name="prepare",
     )(planes, weights)
+
+
+def turn_kernel(volume_ref, turned_ref):
+    turned_ref[...] = jnp.transpose(volume_ref[...].astype(jnp.float32)).astype(jnp.bfloat16)
+
+
+def turn(volume):
+    return pl.pallas_call(
+        turn_kernel,
+        out_shape=jax.ShapeDtypeStruct(volume.shape[::-1], jnp.bfloat16),
+        compiler_params=params(SMALL),
+        cost_estimate=cost(1 << 22, 1 << 20),
+        name="turn",
+    )(volume)
 
 
 def contrast(defocus, row_square, start, width, npix):
@@ -248,7 +258,7 @@
     return defocus, freq_y * freq_y
 
 
-def compare_kernel(ori, rows, slot_ref, noise_ref, fourier_ref, lookup_ref, volume_ref, filtered_ref, picks_ref, part_ref, about_ref, mix_ref, power_ref):
+def compare_kernel(ori, rows, slot_ref, noise_ref, fourier_ref, lookup_ref, volume_ref, turned_ref, filtered_ref, picks_ref, part_ref, about_ref, mix_ref, power_ref):
     many, wide = filtered_ref.shape
     npix = wide // 2
     deep = volume_ref.shape[0]
@@ -260,12 +270,14 @@
     pick = jnp.where(here == there, 1.0, 0.0).astype(jnp.bfloat16)
     about = jnp.dot(pick, meta, preferred_element_type=jnp.float32)
     about_ref[...] = about
-    label = lax.broadcasted_iota(jnp.int32, (images, lookup_ref.shape[1]), 1).astype(jnp.float32)
+    label = lax.broadcasted_iota(jnp.int32, (images, lookup_ref.shape[0]), 1).astype(jnp.float32)
     found = []
     for o in range(ori):
         mine = about[:, o : o + 1] + 256.0 * about[:, ori + o : ori + o + 1]
         found.append(jnp.where(label == mine, 1.0, 0.0).astype(jnp.bfloat16))
-    found = same(jnp.concatenate(found, 0), lookup_ref[...]).astype(jnp.bfloat16)
+    found = jnp.dot(
+        jnp.concatenate(found, 0), lookup_ref[...], preferred_element_type=jnp.float32
+    ).astype(jnp.bfloat16)
     picks_ref[...] = found
     spread = spread_over(rows, (many, images), 1)
     for o in range(ori):
@@ -304,7 +316,9 @@
             power_ref[o] = power
         current = following
 
-    found = own_row(same(filtered_ref[...], volume_ref[...]), rows)
+    found = own_row(
+        jnp.dot(filtered_ref[...], turned_ref[...], preferred_element_type=jnp.float32), rows
+    )
     found = jnp.sum(found, axis=1)
     halves = []
     for o in range(ori):
@@ -326,13 +340,13 @@
     part_ref[...] = jnp.where(even, upper, lower)
 
 
-def compare(slot, noise, fourier, lookup, volume, ori, rows, copies):
+def compare(slot, noise, fourier, lookup, volume, turned, ori, rows, copies):
     many = fourier.shape[0]
     deep, wide = volume.shape
     images = many // rows
     return pl.pallas_call(
         functools.partial(compare_kernel, ori, rows),
-        in_specs=[scalar()] * 2 + [whole()] * 3,
+        in_specs=[scalar()] * 2 + [whole()] * 4,
         out_specs=(whole(),) * 4,
         out_shape=(
             jax.ShapeDtypeStruct((many, wide), jnp.bfloat16),
@@ -347,7 +361,7 @@
         compiler_params=params(LARGE),
         cost_estimate=cost(1 << 31, 5 << 20),
         name="compare",
-    )(slot, noise, fourier, lookup, volume)
+    )(slot, noise, fourier, lookup, volume, turned)
 
 
 def squares_kernel(ori, rows, npix, slot_ref, about_ref, square_ref):
@@ -588,7 +602,7 @@
     vol_rows = lax.all_gather(volume.reshape(slab * rows, 2 * npix), "vol", axis=0, tiled=True)
     lookup = prepare(jnp.swapaxes(planes, 1, 2), jnp.swapaxes(weights, 1, 2), deep)
     filtered, picks, part, about = compare(
-        slot, noise, fourier, lookup, vol_rows, ori, rows, n_img
+        slot, noise, fourier, lookup, vol_rows, turn(vol_rows), ori, rows, n_img
     )
     square = squares(slot, about, ori, rows, npix)
     part = lax.all_to_all(

time: 96.3 us -> 97.4 us (1.011)
  local copies, waits for them, and re-layouts: 0.79 us -> 2.52 us
  waiting for transfers between devices: 18 us -> 16.5 us
    unnamed x11 -> x15, local copies, waits for them, and re-layouts: 0.63 us -> 2.36 us
    all_to_all x1, waiting for transfers between devices: 4.62 us -> 3.38 us  [on_device(): lax.all_to_all(fourier.reshape(n_img, rows, 2 * npix + META), 'img', spli...]
where the time goes in v14:
time: 97.4 us; the launch traced here: 96.6 us
  starting transfers between devices  37.5 us (39%)
  blocking collectives  25.9 us (27%)
  waiting for transfers between devices  16.5 us (17%)
  Pallas kernels  12 us (12%)
  local copies, waits for them, and re-layouts  2.52 us (3%)
  between operations  2.17 us (2%)
    all_gather x1, blocking collectives, on_device(): lax.all_gather(volume.reshape(slab * rows, 2 * npix), 'vol', axis=0, tile...  25.9 us
    all_to_all x1, starting transfers between devices, on_device(): lax.all_to_all(fourier.reshape(n_img, rows, 2 * npix + META), 'img', spli...  15.5 us
    ppermute x3, starting transfers between devices, on_device(): lax.ppermute(sends[apart - 1], 'vol', [(v, v ^ 2 * apart) for v in range(...  11.5 us
    all_to_all x1, waiting for transfers between devices, on_device(): lax.all_to_all(part.reshape(n_img, 2, 2 * n_img), 'img', split_axis=0, co...  8.28 us
    all_to_all x1, starting transfers between devices, on_device(): lax.all_to_all(part.reshape(n_img, 2, 2 * n_img), 'img', split_axis=0, co...  6.72 us
    pallas_call x1, Pallas kernels, compare(): pl.pallas_call(functools.partial(compare_kernel, ori, rows), in_specs=[sc...  4.22 us
    ppermute x3, waiting for transfers between devices, on_device(): lax.ppermute(sends[apart - 1], 'vol', [(v, v ^ 2 * apart) for v in range(...  4.18 us
    ppermute x1, starting transfers between devices, on_device(): got = lax.ppermute(send, 'vol', [(v, v ^ 1) for v in range(n_vol)])  3.83 us
  transfers between devices with their start and end apart: 6, of which 5 were waited for; matrix products, arithmetic and copies ran while one was open for 1% of the time, Pallas kernels for 2%

profile of v14, /device:TPU:1, one launch (start us, length us, event | category | flops | bytes accessed | tf_op | source)
XLA Modules:
  0.0 96.6 jit_solution(1379185469859244614)
XLA Ops:
  1.3 3.7 %transform.1 = bf16[512,1152]{1,0:T(8,128)(2,1)} custom-call(s32[1,4]{1,0:T(1,128)} %orient_hbm.1, f32[1]{0:T(128)S(6)} %copy.16.defocus_hbm, bf16[512,512]{1,0:T(8,128)(2,1)} %bitcast.25, bf16[512,1024]{1,0:T(8,128)(2,1)} %constant.40.clone.table_hbm, bf16[256,1024]{1,0:T(8,128)(2,1)} %constant.41.clone.halves_hbm), custom_call_target="tpu_custom_call" | custom-call | flops 1610612736 | bytes 2621440 | tf_op jit(solution)/shard_map/transform/pallas_call | solution.py:179
  4.9 0.0 copy-start.6
  4.9 15.5 %all-to-all-start = ((bf16[64,8,1152]{2,1,0:T(8,128)(2,1)}), bf16[64,8,1152]{2,1,0:T(8,128)(2,1)S(1)}, u32[]{:S(2)}, u32[]{:S(2)}) async-start(bf16[64,8,1152]{2,1,0:T(8,128)(2,1)} %bitcast.22), calls=%async_computation | async-start | bytes 2359296 | tf_op jit(solution)/shard_map/all_to_all | solution.py:599
  20.4 0.0 copy-start.4
  20.5 0.0 copy-start.5
  21.1 0.0 copy-done.6
  21.1 25.9 %all_gather.3.volume_ref = bf16[256,1024]{1,0:T(8,128)(2,1)S(1)} all-gather(bf16[32,1024]{1,0:T(8,128)(2,1)S(1)} %bitcast.23), channel_id=1, replica_groups=mesh['img'=64,'vol'=8] {'vol'}, dimensions={0}, use_global_device_ids=true | all-gather | bytes 589824 | tf_op jit(solution)/shard_map/all_gather | solution.py:602
  47.1 0.2 turn.1.turned_ref
  47.3 0.0 copy-done.4
  47.3 0.0 copy-done.5
  47.3 0.2 prepare.1.lookup_ref
  47.5 0.0 copy-start
  47.5 0.7 copy-done
  48.3 3.4 %all-to-all-done = bf16[64,8,1152]{2,1,0:T(8,128)(2,1)S(1)} async-done(((bf16[64,8,1152]{2,1,0:T(8,128)(2,1)}), bf16[64,8,1152]{2,1,0:T(8,128)(2,1)S(1)}, u32[]{:S(2)}, u32[]{:S(2)}) %all-to-all-start) | async-done | bytes 1179680 | tf_op jit(solution)/shard_map/all_to_all | solution.py:599
  51.6 0.0 copy-start.1
  51.6 1.0 %copy-done.1 = bf16[768,256]{1,0:T(8,128)(2,1)S(1)} copy-done((bf16[768,256]{1,0:T(8,128)(2,1)S(1)}, bf16[768,256]{1,0:T(8,128)(2,1)}, u32[]{:S(2)}) %copy-start.1) | copy-done | bytes 393240
  52.6 4.2 %compare.4 = (bf16[512,1024]{1,0:T(8,128)(2,1)S(1)}, bf16[256,256]{1,0:T(8,128)(2,1)S(1)}, f32[128,128]{1,0:T(8,128)}, f32[64,128]{1,0:T(8,128)S(1)}) custom-call(s32[1]{0:T(128)} %bitcast.1.slot_ref, f32[1]{0:T(128)S(6)} %copy.17.noise_ref, bf16[512,1152]{1,0:T(8,128)(2,1)S(1)} %bitcast.16, bf16[768,256]{1,0:T(8,128)(2,1)S(1)} %copy-done.1, ...), custom_call_target="tpu_custom_call" | custom-call | flops 2147483648 | bytes 5242880 | tf_op jit(solution)/shard_map/compare/pallas_call | solution.py:347
  56.9 6.7 %all-to-all-start.1 = ((f32[64,2,128]{2,1,0:T(2,128)}), f32[64,2,128]{2,1,0:T(2,128)S(1)}, u32[]{:S(2)}, u32[]{:S(2)}) async-start(f32[64,2,128]{2,1,0:T(2,128)} %bitcast.8), calls=%async_computation.1 | async-start | bytes 131072 | tf_op jit(solution)/shard_map/all_to_all | solution.py:608
  63.6 1.1 %squares.1.square_ref = bf16[512,384]{1,0:T(8,128)(2,1)S(1)} custom-call(s32[1]{0:T(128)} %bitcast.1.slot_ref, f32[64,128]{1,0:T(8,128)S(1)} %get-tuple-element.21.about_ref), custom_call_target="tpu_custom_call" | custom-call | flops 134217728 | bytes 1048576 | tf_op jit(solution)/shard_map/squares/pallas_call | solution.py:384
  64.7 8.3 %all-to-all-done.1 = f32[64,2,128]{2,1,0:T(2,128)S(1)} async-done(((f32[64,2,128]{2,1,0:T(2,128)}), f32[64,2,128]{2,1,0:T(2,128)S(1)}, u32[]{:S(2)}, u32[]{:S(2)}) %all-to-all-start.1) | async-done | bytes 65568 | tf_op jit(solution)/shard_map/all_to_all | solution.py:608
  73.0 1.1 %project.1 = (f32[8,128]{1,0:T(8,128)S(1)}, bf16[128,512]{1,0:T(8,128)(2,1)S(1)}, bf16[4,336,128]{2,1,0:T(8,128)(2,1)S(1)}) custom-call(s32[1]{0:T(128)} %bitcast.core_ref, f32[128,128]{1,0:T(8,128)S(1)} %bitcast.17, bf16[256,256]{1,0:T(8,128)(2,1)S(1)} %get-tuple-element.19.picks_ref, bf16[512,1024]{1,0:T(8,128)(2,1)S(1)} %get-tuple-element.20.filtered_ref, ...), custom_call_target="tpu_custom_call" | custom-call | flops 268435456 | bytes 4194304 | tf_op jit(solution)/shard_map/project/pallas_call | solution.py:467
  74.0 3.8 %collective-permute-start = (bf16[4,336,128]{2,1,0:T(8,128)(2,1)S(1)}, bf16[4,336,128]{2,1,0:T(8,128)(2,1)S(1)}, u32[]{:S(2)}, u32[]{:S(2)}) collective-permute-start(bf16[4,336,128]{2,1,0:T(8,128)(2,1)S(1)} %get-tuple-element.24), channel_id=1, source_target_pairs={{0,1},{1,0},{2,3},{3,2},{4,5},{5,4},{6,7},{7,6},{8,9},{9,8},{10,11... | collective-permute-start | bytes 1032200 | tf_op jit(solution)/shard_map/ppermute | solution.py:617
  77.9 0.1 reshape.55
  78.0 0.0 copy-start.2
  78.0 0.0 copy-start.3
  78.0 0.5 keep_own.1.keep_ref
  78.4 0.7 collective-permute-done.got_ref
  79.1 0.1 middle.1
  79.2 6.6 %collective-permute-start.1 = (bf16[336,128]{1,0:T(8,128)(2,1)S(1)}, bf16[336,128]{1,0:T(8,128)(2,1)S(1)}, u32[]{:S(2)}, u32[]{:S(2)}) collective-permute-start(bf16[336,128]{1,0:T(8,128)(2,1)S(1)} %get-tuple-element.25), channel_id=1, source_target_pairs={{0,4},{1,5},{2,6},{3,7},{4,0},{5,1},{6,2},{7,3},{8,12},{9,13},{10,... | collective-permute-start | bytes 258056 | tf_op jit(solution)/shard_map/ppermute | solution.py:621
  85.8 2.9 %collective-permute-start.2 = (bf16[336,128]{1,0:T(8,128)(2,1)S(1)}, bf16[336,128]{1,0:T(8,128)(2,1)S(1)}, u32[]{:S(2)}, u32[]{:S(2)}) collective-permute-start(bf16[336,128]{1,0:T(8,128)(2,1)S(1)} %get-tuple-element.26), channel_id=1, source_target_pairs={{0,6},{1,7},{2,4},{3,5},{4,2},{5,3},{6,0},{7,1},{8,14},{9,15},{10,... | collective-permute-start | bytes 258056 | tf_op jit(solution)/shard_map/ppermute | solution.py:621
  88.8 1.9 %collective-permute-start.3 = (bf16[336,128]{1,0:T(8,128)(2,1)S(1)}, bf16[336,128]{1,0:T(8,128)(2,1)S(1)}, u32[]{:S(2)}, u32[]{:S(2)}) collective-permute-start(bf16[336,128]{1,0:T(8,128)(2,1)S(1)} %get-tuple-element.27), channel_id=1, source_target_pairs={{0,2},{1,3},{2,0},{3,1},{4,6},{5,7},{6,4},{7,5},{8,10},{9,11},{10,... | collective-permute-start | bytes 258056 | tf_op jit(solution)/shard_map/ppermute | solution.py:621
  90.7 0.1 constant_dynamic-slice_fusion
  90.8 0.6 copy.15
  91.4 0.0 copy-done.2
  91.4 0.0 copy-done.3
  91.4 0.2 collect.1
  91.6 0.0 collective-permute-done.1.refs_0_
  91.7 2.5 %collective-permute-done.2.refs_1_ = bf16[336,128]{1,0:T(8,128)(2,1)S(1)} collective-permute-done((bf16[336,128]{1,0:T(8,128)(2,1)S(1)}, bf16[336,128]{1,0:T(8,128)(2,1)S(1)}, u32[]{:S(2)}, u32[]{:S(2)}) %collective-permute-start.2) | collective-permute-done | bytes 86048 | tf_op jit(solution)/shard_map/ppermute | solution.py:621
  94.1 1.7 %collective-permute-done.3.refs_2_ = bf16[336,128]{1,0:T(8,128)(2,1)S(1)} collective-permute-done((bf16[336,128]{1,0:T(8,128)(2,1)S(1)}, bf16[336,128]{1,0:T(8,128)(2,1)S(1)}, u32[]{:S(2)}, u32[]{:S(2)}) %collective-permute-start.3) | collective-permute-done | bytes 86048 | tf_op jit(solution)/shard_map/ppermute | solution.py:621
  95.8 0.8 finish.1
  (1 shorter events, 0.0 us)
Async XLA Ops:
  4.9 16.2 %copy-start.6 = (bf16[4,8,1024]{2,1,0:T(8,128)(2,1)S(1)}, bf16[4,8,1024]{2,1,0:T(8,128)(2,1)}, u32[]{:S(2)}) copy-start(bf16[4,8,1024]{2,1,0:T(8,128)(2,1)} %param.17) | copy-start | bytes 196612
  4.9 46.7 %all-to-all-start = ((bf16[64,8,1152]{2,1,0:T(8,128)(2,1)}), bf16[64,8,1152]{2,1,0:T(8,128)(2,1)S(1)}, u32[]{:S(2)}, u32[]{:S(2)}) async-start(bf16[64,8,1152]{2,1,0:T(8,128)(2,1)} %bitcast.22), calls=%async_computation | async-start | bytes 2359296 | tf_op jit(solution)/shard_map/all_to_all | solution.py:599
  20.4 26.8 %copy-start.4 = (s32[2,768,8]{1,2,0:T(8,128)S(1)}, s32[2,768,8]{1,2,0:T(8,128)}, u32[]{:S(2)}) copy-start(s32[2,768,8]{1,2,0:T(8,128)} %param.15) | copy-start | bytes 147460
  20.5 26.8 %copy-start.5 = (bf16[2,768,8]{1,2,0:T(8,128)(2,1)S(1)}, bf16[2,768,8]{1,2,0:T(8,128)(2,1)}, u32[]{:S(2)}) copy-start(bf16[2,768,8]{1,2,0:T(8,128)(2,1)} %param.16) | copy-start | bytes 73732
  47.5 0.7 copy-start
  51.6 1.0 %copy-start.1 = (bf16[768,256]{1,0:T(8,128)(2,1)S(1)}, bf16[768,256]{1,0:T(8,128)(2,1)}, u32[]{:S(2)}) copy-start(bf16[768,256]{1,0:T(8,128)(2,1)} %copy-done) | copy-start | bytes 1179652
  56.9 16.1 %all-to-all-start.1 = ((f32[64,2,128]{2,1,0:T(2,128)}), f32[64,2,128]{2,1,0:T(2,128)S(1)}, u32[]{:S(2)}, u32[]{:S(2)}) async-start(f32[64,2,128]{2,1,0:T(2,128)} %bitcast.8), calls=%async_computation.1 | async-start | bytes 131072 | tf_op jit(solution)/shard_map/all_to_all | solution.py:608
  74.0 5.1 %collective-permute-start = (bf16[4,336,128]{2,1,0:T(8,128)(2,1)S(1)}, bf16[4,336,128]{2,1,0:T(8,128)(2,1)S(1)}, u32[]{:S(2)}, u32[]{:S(2)}) collective-permute-start(bf16[4,336,128]{2,1,0:T(8,128)(2,1)S(1)} %get-tuple-element.24), channel_id=1, source_target_pairs={{0,1},{1,0},{2,3},{3,2},{4,5},{5,4},{6,7},{7,6},{8,9},{9,8},{10,11... | collective-permute-start | bytes 1032200 | tf_op jit(solution)/shard_map/ppermute | solution.py:617
  78.0 13.4 %copy-start.2 = (f32[4,8,1024]{2,1,0:T(8,128)S(1)}, f32[4,8,1024]{2,1,0:T(8,128)}, u32[]{:S(2)}) copy-start(f32[4,8,1024]{2,1,0:T(8,128)} %param.18) | copy-start | bytes 393220
  78.0 13.4 %copy-start.3 = (f32[4,8,512]{2,1,0:T(8,128)S(1)}, f32[4,8,512]{2,1,0:T(8,128)}, u32[]{:S(2)}) copy-start(f32[4,8,512]{2,1,0:T(8,128)} %param.19) | copy-start | bytes 196612
  79.2 12.4 %collective-permute-start.1 = (bf16[336,128]{1,0:T(8,128)(2,1)S(1)}, bf16[336,128]{1,0:T(8,128)(2,1)S(1)}, u32[]{:S(2)}, u32[]{:S(2)}) collective-permute-start(bf16[336,128]{1,0:T(8,128)(2,1)S(1)} %get-tuple-element.25), channel_id=1, source_target_pairs={{0,4},{1,5},{2,6},{3,7},{4,0},{5,1},{6,2},{7,3},{8,12},{9,13},{10,... | collective-permute-start | bytes 258056 | tf_op jit(solution)/shard_map/ppermute | solution.py:621
  85.8 8.3 %collective-permute-start.2 = (bf16[336,128]{1,0:T(8,128)(2,1)S(1)}, bf16[336,128]{1,0:T(8,128)(2,1)S(1)}, u32[]{:S(2)}, u32[]{:S(2)}) collective-permute-start(bf16[336,128]{1,0:T(8,128)(2,1)S(1)} %get-tuple-element.26), channel_id=1, source_target_pairs={{0,6},{1,7},{2,4},{3,5},{4,2},{5,3},{6,0},{7,1},{8,14},{9,15},{10,... | collective-permute-start | bytes 258056 | tf_op jit(solution)/shard_map/ppermute | solution.py:621
  88.8 7.0 %collective-permute-start.3 = (bf16[336,128]{1,0:T(8,128)(2,1)S(1)}, bf16[336,128]{1,0:T(8,128)(2,1)S(1)}, u32[]{:S(2)}, u32[]{:S(2)}) collective-permute-start(bf16[336,128]{1,0:T(8,128)(2,1)S(1)} %get-tuple-element.27), channel_id=1, source_target_pairs={{0,2},{1,3},{2,0},{3,1},{4,6},{5,7},{6,4},{7,5},{8,10},{9,11},{10,... | collective-permute-start | bytes 258056 | tf_op jit(solution)/shard_map/ppermute | solution.py:621

commit v15 on v13

--- a/solution.py
+++ b/solution.py
@@ -102,7 +102,7 @@
     npix = image_ref.shape[0]
     half = npix // 2
     ori = orient_ref.shape[1]
-    starts = list(range(0, 2 * npix, chunk))
+    starts = [at + start for start in range(0, npix, chunk) for at in (0, npix)]
     pairs = [(image_hbm, image_ref)]
     pairs += [(table_hbm.at[:, pl.ds(start, chunk)], table_ref.at[:, pl.ds(start, chunk)]) for start in starts]
     pairs += [(halves_hbm, halves_ref), (orient_hbm, orient_ref), (defocus_hbm, defocus_ref)]
@@ -122,7 +122,29 @@
         ],
         0,
     ).astype(jnp.bfloat16)
-    for number, start in enumerate(starts):
+    for load in loads[1 + len(starts) :]:
+        load.wait()
+    saves = []
+
+    def save(start, size):
+        at = pl.ds(start, size)
+        copy = pltpu.make_async_copy(out_ref.at[:, at], out_hbm.at[:, at], out_sems.at[len(saves)])
+        copy.start()
+        saves.append(copy)
+
+    lane = lax.broadcasted_iota(jnp.int32, (8, META), 1)
+    codes = jnp.zeros((8, META), jnp.int32)
+    for o in range(ori):
+        label = orient_ref[0, o]
+        codes = jnp.where(lane == o, label & 255, codes)
+        codes = jnp.where(lane == ori + o, label >> 8, codes)
+    about = codes.astype(jnp.float32)
+    parts = three_parts(jnp.full((8, META), defocus_ref[0], jnp.float32))
+    for place, part in enumerate(parts, 2 * ori):
+        about = jnp.where(lane == place, part, about)
+    out_ref[:, 2 * npix :] = jnp.broadcast_to(about[:1], (npix, META)).astype(jnp.bfloat16)
+    save(2 * npix, META)
+    def first_stage(number, start):
         loads[1 + number].wait()
         first = jnp.dot(
             image, table_ref[:, start : start + chunk], preferred_element_type=jnp.float32
@@ -137,30 +159,8 @@
             else:
                 both_ref[upper, start : start + chunk] = -part
                 both_ref[lower, start - npix : start - npix + chunk] = -part
-    for load in loads[1 + len(starts) :]:
-        load.wait()
-    saves = []
-
-    def save(start, size):
-        at = pl.ds(start, size)
-        copy = pltpu.make_async_copy(out_ref.at[:, at], out_hbm.at[:, at], out_sems.at[len(saves)])
-        copy.start()
-        saves.append(copy)
-
-    lane = lax.broadcasted_iota(jnp.int32, (8, META), 1)
-    codes = jnp.zeros((8, META), jnp.int32)
-    for o in range(ori):
-        label = orient_ref[0, o]
-        codes = jnp.where(lane == o, label & 255, codes)
-        codes = jnp.where(lane == ori + o, label >> 8, codes)
-    about = codes.astype(jnp.float32)
-    parts = three_parts(jnp.full((8, META), defocus_ref[0], jnp.float32))
-    for place, part in enumerate(parts, 2 * ori):
-        about = jnp.where(lane == place, part, about)
-    out_ref[:, 2 * npix :] = jnp.broadcast_to(about[:1], (npix, META)).astype(jnp.bfloat16)
-    save(2 * npix, META)
-    chunk = chunk // 2
-    for start in range(0, 2 * npix, chunk):
+
+    def second_stage(start):
         even, odd = (
             jnp.dot(
                 halves_ref[:, parity * npix : (parity + 1) * npix],
@@ -172,13 +172,19 @@
         out_ref[:half, start : start + chunk] = (even + odd).astype(jnp.bfloat16)
         out_ref[half:, start : start + chunk] = (even - odd).astype(jnp.bfloat16)
         save(start, chunk)
+
+    for number, start in enumerate(starts):
+        first_stage(number, start)
+        if number % 2:
+            second_stage(start - npix)
+            second_stage(start)
     for copy in saves:
         copy.wait()
 
 
 def transform(orient, defocus, image, table, halves):
     npix = image.shape[0]
-    chunk = npix
+    chunk = npix // 2
     pieces = 2 * npix // chunk
     return pl.pallas_call(
         functools.partial(transform_kernel, chunk),
@@ -195,7 +201,7 @@
             pltpu.VMEM((2 * npix, 2 * npix), jnp.bfloat16),
             pltpu.VMEM((npix, 2 * npix + META), jnp.bfloat16),
             pltpu.SemaphoreType.DMA((pieces + 4,)),
-            pltpu.SemaphoreType.DMA((2 * pieces + 1,)),
+            pltpu.SemaphoreType.DMA((pieces + 1,)),
         ],
         compiler_params=params(HUGE),
         cost_estimate=cost(12 * npix**3, 10 * npix * npix),

time: 96.3 us -> 97.4 us (1.011)
  Pallas kernels: 11.7 us -> 12.8 us
    pallas_call x1, Pallas kernels: 3.64 us -> 4.77 us  [transform(): pl.pallas_call(functools.partial(transform_kernel, chunk), in_specs=[pl.B...]
where the time goes in v15:
time: 97.4 us; the launch traced here: 96.9 us
  starting transfers between devices  37.4 us (38%)
  blocking collectives  25.8 us (26%)
  waiting for transfers between devices  18 us (18%)
  Pallas kernels  12.8 us (13%)
  between operations  2.14 us (2%)
    all_gather x1, blocking collectives, on_device(): lax.all_gather(volume.reshape(slab * rows, 2 * npix), 'vol', axis=0, tile...  25.8 us
    all_to_all x1, starting transfers between devices, on_device(): lax.all_to_all(fourier.reshape(n_img, rows, 2 * npix + META), 'img', spli...  15.5 us
    ppermute x3, starting transfers between devices, on_device(): lax.ppermute(sends[apart - 1], 'vol', [(v, v ^ 2 * apart) for v in range(...  11.4 us
    all_to_all x1, waiting for transfers between devices, on_device(): lax.all_to_all(part.reshape(n_img, 2, 2 * n_img), 'img', split_axis=0, co...  8.28 us
    all_to_all x1, starting transfers between devices, on_device(): lax.all_to_all(part.reshape(n_img, 2, 2 * n_img), 'img', split_axis=0, co...  6.69 us
    pallas_call x1, Pallas kernels, transform(): pl.pallas_call(functools.partial(transform_kernel, chunk), in_specs=[pl.B...  4.77 us
    all_to_all x1, waiting for transfers between devices, on_device(): lax.all_to_all(fourier.reshape(n_img, rows, 2 * npix + META), 'img', spli...  4.63 us
    ppermute x3, waiting for transfers between devices, on_device(): lax.ppermute(sends[apart - 1], 'vol', [(v, v ^ 2 * apart) for v in range(...  4.42 us
  transfers between devices with their start and end apart: 6, of which 5 were waited for; matrix products, arithmetic and copies ran while one was open for 1% of the time, Pallas kernels for 2%

profile of v15, /device:TPU:1, one launch (start us, length us, event | category | flops | bytes accessed | tf_op | source)
XLA Modules:
  0.0 96.9 jit_solution(14215861427069904360)
XLA Ops:
  1.3 4.8 %transform.1 = bf16[512,1152]{1,0:T(8,128)(2,1)} custom-call(s32[1,4]{1,0:T(1,128)} %orient_hbm.1, f32[1]{0:T(128)S(6)} %copy.16.defocus_hbm, bf16[512,512]{1,0:T(8,128)(2,1)} %bitcast.25, bf16[512,1024]{1,0:T(8,128)(2,1)} %constant.40.clone.table_hbm, bf16[256,1024]{1,0:T(8,128)(2,1)} %constant.41.clone.halves_hbm), custom_call_target="tpu_custom_call" | custom-call | flops 1610612736 | bytes 2621440 | tf_op jit(solution)/shard_map/transform/pallas_call | solution.py:189
  6.1 0.0 copy-start.2
  6.1 0.0 copy-start.3
  6.1 0.0 copy-start.4
  6.1 15.5 %all-to-all-start = ((bf16[64,8,1152]{2,1,0:T(8,128)(2,1)}), bf16[64,8,1152]{2,1,0:T(8,128)(2,1)S(1)}, u32[]{:S(2)}, u32[]{:S(2)}) async-start(bf16[64,8,1152]{2,1,0:T(8,128)(2,1)} %bitcast.22), calls=%async_computation | async-start | bytes 2359296 | tf_op jit(solution)/shard_map/all_to_all | solution.py:591
  22.2 0.0 copy-done.2
  22.3 0.0 copy-done.3
  22.3 0.1 prepare.1.lookup_ref
  22.4 0.0 copy-done.4
  22.4 25.8 %all_gather.3.volume_ref = bf16[256,1024]{1,0:T(8,128)(2,1)S(1)} all-gather(bf16[32,1024]{1,0:T(8,128)(2,1)S(1)} %bitcast.23), channel_id=1, replica_groups=mesh['img'=64,'vol'=8] {'vol'}, dimensions={0}, use_global_device_ids=true | all-gather | bytes 589824 | tf_op jit(solution)/shard_map/all_gather | solution.py:594
  48.2 4.6 %all-to-all-done = bf16[64,8,1152]{2,1,0:T(8,128)(2,1)S(1)} async-done(((bf16[64,8,1152]{2,1,0:T(8,128)(2,1)}), bf16[64,8,1152]{2,1,0:T(8,128)(2,1)S(1)}, u32[]{:S(2)}, u32[]{:S(2)}) %all-to-all-start) | async-done | bytes 1179680 | tf_op jit(solution)/shard_map/all_to_all | solution.py:591
  52.8 4.2 %compare.4 = (bf16[512,1024]{1,0:T(8,128)(2,1)S(1)}, bf16[256,256]{1,0:T(8,128)(2,1)S(1)}, f32[128,128]{1,0:T(8,128)}, f32[64,128]{1,0:T(8,128)S(1)}) custom-call(s32[1]{0:T(128)} %bitcast.1.slot_ref, f32[1]{0:T(128)S(6)} %copy.17.noise_ref, bf16[512,1152]{1,0:T(8,128)(2,1)S(1)} %bitcast.16, bf16[256,768]{1,0:T(8,128)(2,1)S(1)} %prepare.1.lookup_ref, ...), custom_call_target="tpu_custom_call" | custom-call | flops 2147483648 | bytes 5242880 | tf_op jit(solution)/shard_map/compare/pallas_call | solution.py:339
  57.0 6.7 %all-to-all-start.1 = ((f32[64,2,128]{2,1,0:T(2,128)}), f32[64,2,128]{2,1,0:T(2,128)S(1)}, u32[]{:S(2)}, u32[]{:S(2)}) async-start(f32[64,2,128]{2,1,0:T(2,128)} %bitcast.8), calls=%async_computation.1 | async-start | bytes 131072 | tf_op jit(solution)/shard_map/all_to_all | solution.py:600
  63.8 1.1 %squares.1.square_ref = bf16[512,384]{1,0:T(8,128)(2,1)S(1)} custom-call(s32[1]{0:T(128)} %bitcast.1.slot_ref, f32[64,128]{1,0:T(8,128)S(1)} %get-tuple-element.21.about_ref), custom_call_target="tpu_custom_call" | custom-call | flops 134217728 | bytes 1048576 | tf_op jit(solution)/shard_map/squares/pallas_call | solution.py:376
  64.8 8.3 %all-to-all-done.1 = f32[64,2,128]{2,1,0:T(2,128)S(1)} async-done(((f32[64,2,128]{2,1,0:T(2,128)}), f32[64,2,128]{2,1,0:T(2,128)S(1)}, u32[]{:S(2)}, u32[]{:S(2)}) %all-to-all-start.1) | async-done | bytes 65568 | tf_op jit(solution)/shard_map/all_to_all | solution.py:600
  73.1 1.1 %project.1 = (f32[8,128]{1,0:T(8,128)S(1)}, bf16[128,512]{1,0:T(8,128)(2,1)S(1)}, bf16[4,336,128]{2,1,0:T(8,128)(2,1)S(1)}) custom-call(s32[1]{0:T(128)} %bitcast.core_ref, f32[128,128]{1,0:T(8,128)S(1)} %bitcast.17, bf16[256,256]{1,0:T(8,128)(2,1)S(1)} %get-tuple-element.19.picks_ref, bf16[512,1024]{1,0:T(8,128)(2,1)S(1)} %get-tuple-element.20.filtered_ref, ...), custom_call_target="tpu_custom_call" | custom-call | flops 268435456 | bytes 4194304 | tf_op jit(solution)/shard_map/project/pallas_call | solution.py:459
  74.2 3.8 %collective-permute-start = (bf16[4,336,128]{2,1,0:T(8,128)(2,1)S(1)}, bf16[4,336,128]{2,1,0:T(8,128)(2,1)S(1)}, u32[]{:S(2)}, u32[]{:S(2)}) collective-permute-start(bf16[4,336,128]{2,1,0:T(8,128)(2,1)S(1)} %get-tuple-element.24), channel_id=1, source_target_pairs={{0,1},{1,0},{2,3},{3,2},{4,5},{5,4},{6,7},{7,6},{8,9},{9,8},{10,11... | collective-permute-start | bytes 1032200 | tf_op jit(solution)/shard_map/ppermute | solution.py:609
  78.0 0.1 reshape.55
  78.1 0.0 copy-start
  78.1 0.0 copy-start.1
  78.1 0.5 keep_own.1.keep_ref
  78.6 0.7 collective-permute-done.got_ref
  79.3 0.1 middle.1
  79.4 6.6 %collective-permute-start.1 = (bf16[336,128]{1,0:T(8,128)(2,1)S(1)}, bf16[336,128]{1,0:T(8,128)(2,1)S(1)}, u32[]{:S(2)}, u32[]{:S(2)}) collective-permute-start(bf16[336,128]{1,0:T(8,128)(2,1)S(1)} %get-tuple-element.25), channel_id=1, source_target_pairs={{0,4},{1,5},{2,6},{3,7},{4,0},{5,1},{6,2},{7,3},{8,12},{9,13},{10,... | collective-permute-start | bytes 258056 | tf_op jit(solution)/shard_map/ppermute | solution.py:613
  85.9 2.8 %collective-permute-start.2 = (bf16[336,128]{1,0:T(8,128)(2,1)S(1)}, bf16[336,128]{1,0:T(8,128)(2,1)S(1)}, u32[]{:S(2)}, u32[]{:S(2)}) collective-permute-start(bf16[336,128]{1,0:T(8,128)(2,1)S(1)} %get-tuple-element.26), channel_id=1, source_target_pairs={{0,6},{1,7},{2,4},{3,5},{4,2},{5,3},{6,0},{7,1},{8,14},{9,15},{10,... | collective-permute-start | bytes 258056 | tf_op jit(solution)/shard_map/ppermute | solution.py:613
  88.8 2.0 %collective-permute-start.3 = (bf16[336,128]{1,0:T(8,128)(2,1)S(1)}, bf16[336,128]{1,0:T(8,128)(2,1)S(1)}, u32[]{:S(2)}, u32[]{:S(2)}) collective-permute-start(bf16[336,128]{1,0:T(8,128)(2,1)S(1)} %get-tuple-element.27), channel_id=1, source_target_pairs={{0,2},{1,3},{2,0},{3,1},{4,6},{5,7},{6,4},{7,5},{8,10},{9,11},{10,... | collective-permute-start | bytes 258056 | tf_op jit(solution)/shard_map/ppermute | solution.py:613
  90.8 0.1 constant_dynamic-slice_fusion
  90.8 0.6 copy.15
  91.4 0.0 copy-done
  91.4 0.0 copy-done.1
  91.4 0.2 collect.1
  91.7 0.0 collective-permute-done.1.refs_0_
  91.7 2.6 %collective-permute-done.2.refs_1_ = bf16[336,128]{1,0:T(8,128)(2,1)S(1)} collective-permute-done((bf16[336,128]{1,0:T(8,128)(2,1)S(1)}, bf16[336,128]{1,0:T(8,128)(2,1)S(1)}, u32[]{:S(2)}, u32[]{:S(2)}) %collective-permute-start.2) | collective-permute-done | bytes 86048 | tf_op jit(solution)/shard_map/ppermute | solution.py:613
  94.3 1.8 %collective-permute-done.3.refs_2_ = bf16[336,128]{1,0:T(8,128)(2,1)S(1)} collective-permute-done((bf16[336,128]{1,0:T(8,128)(2,1)S(1)}, bf16[336,128]{1,0:T(8,128)(2,1)S(1)}, u32[]{:S(2)}, u32[]{:S(2)}) %collective-permute-start.3) | collective-permute-done | bytes 86048 | tf_op jit(solution)/shard_map/ppermute | solution.py:613
  96.1 0.8 finish.1
  (1 shorter events, 0.0 us)
Async XLA Ops:
  6.1 16.2 %copy-start.2 = (s32[2,768,8]{1,2,0:T(8,128)S(1)}, s32[2,768,8]{1,2,0:T(8,128)}, u32[]{:S(2)}) copy-start(s32[2,768,8]{1,2,0:T(8,128)} %param.15) | copy-start | bytes 147460
  6.1 16.2 %copy-start.3 = (bf16[2,768,8]{1,2,0:T(8,128)(2,1)S(1)}, bf16[2,768,8]{1,2,0:T(8,128)(2,1)}, u32[]{:S(2)}) copy-start(bf16[2,768,8]{1,2,0:T(8,128)(2,1)} %param.16) | copy-start | bytes 73732
  6.1 16.3 %copy-start.4 = (bf16[4,8,1024]{2,1,0:T(8,128)(2,1)S(1)}, bf16[4,8,1024]{2,1,0:T(8,128)(2,1)}, u32[]{:S(2)}) copy-start(bf16[4,8,1024]{2,1,0:T(8,128)(2,1)} %param.17) | copy-start | bytes 196612
  6.1 46.7 %all-to-all-start = ((bf16[64,8,1152]{2,1,0:T(8,128)(2,1)}), bf16[64,8,1152]{2,1,0:T(8,128)(2,1)S(1)}, u32[]{:S(2)}, u32[]{:S(2)}) async-start(bf16[64,8,1152]{2,1,0:T(8,128)(2,1)} %bitcast.22), calls=%async_computation | async-start | bytes 2359296 | tf_op jit(solution)/shard_map/all_to_all | solution.py:591
  57.0 16.1 %all-to-all-start.1 = ((f32[64,2,128]{2,1,0:T(2,128)}), f32[64,2,128]{2,1,0:T(2,128)S(1)}, u32[]{:S(2)}, u32[]{:S(2)}) async-start(f32[64,2,128]{2,1,0:T(2,128)} %bitcast.8), calls=%async_computation.1 | async-start | bytes 131072 | tf_op jit(solution)/shard_map/all_to_all | solution.py:600
  74.2 5.1 %collective-permute-start = (bf16[4,336,128]{2,1,0:T(8,128)(2,1)S(1)}, bf16[4,336,128]{2,1,0:T(8,128)(2,1)S(1)}, u32[]{:S(2)}, u32[]{:S(2)}) collective-permute-start(bf16[4,336,128]{2,1,0:T(8,128)(2,1)S(1)} %get-tuple-element.24), channel_id=1, source_target_pairs={{0,1},{1,0},{2,3},{3,2},{4,5},{5,4},{6,7},{7,6},{8,9},{9,8},{10,11... | collective-permute-start | bytes 1032200 | tf_op jit(solution)/shard_map/ppermute | solution.py:609
  78.1 13.3 %copy-start = (f32[4,8,1024]{2,1,0:T(8,128)S(1)}, f32[4,8,1024]{2,1,0:T(8,128)}, u32[]{:S(2)}) copy-start(f32[4,8,1024]{2,1,0:T(8,128)} %param.18) | copy-start | bytes 393220
  78.1 13.3 %copy-start.1 = (f32[4,8,512]{2,1,0:T(8,128)S(1)}, f32[4,8,512]{2,1,0:T(8,128)}, u32[]{:S(2)}) copy-start(f32[4,8,512]{2,1,0:T(8,128)} %param.19) | copy-start | bytes 196612
  79.4 12.3 %collective-permute-start.1 = (bf16[336,128]{1,0:T(8,128)(2,1)S(1)}, bf16[336,128]{1,0:T(8,128)(2,1)S(1)}, u32[]{:S(2)}, u32[]{:S(2)}) collective-permute-start(bf16[336,128]{1,0:T(8,128)(2,1)S(1)} %get-tuple-element.25), channel_id=1, source_target_pairs={{0,4},{1,5},{2,6},{3,7},{4,0},{5,1},{6,2},{7,3},{8,12},{9,13},{10,... | collective-permute-start | bytes 258056 | tf_op jit(solution)/shard_map/ppermute | solution.py:613
  85.9 8.3 %collective-permute-start.2 = (bf16[336,128]{1,0:T(8,128)(2,1)S(1)}, bf16[336,128]{1,0:T(8,128)(2,1)S(1)}, u32[]{:S(2)}, u32[]{:S(2)}) collective-permute-start(bf16[336,128]{1,0:T(8,128)(2,1)S(1)} %get-tuple-element.26), channel_id=1, source_target_pairs={{0,6},{1,7},{2,4},{3,5},{4,2},{5,3},{6,0},{7,1},{8,14},{9,15},{10,... | collective-permute-start | bytes 258056 | tf_op jit(solution)/shard_map/ppermute | solution.py:613
  88.8 7.3 %collective-permute-start.3 = (bf16[336,128]{1,0:T(8,128)(2,1)S(1)}, bf16[336,128]{1,0:T(8,128)(2,1)S(1)}, u32[]{:S(2)}, u32[]{:S(2)}) collective-permute-start(bf16[336,128]{1,0:T(8,128)(2,1)S(1)} %get-tuple-element.27), channel_id=1, source_target_pairs={{0,2},{1,3},{2,0},{3,1},{4,6},{5,7},{6,4},{7,5},{8,10},{9,11},{10,... | collective-permute-start | bytes 258056 | tf_op jit(solution)/shard_map/ppermute | solution.py:613
